TPU v7x, 32 devices: a whole 2x2x4 slice. The times are simulated.
32 devices in a mesh: dp: 4 (over y, x), shard: 8 (over z, core).
Axes of the slice: x: 2, y: 2, z: 4, core: 2. Of those that a mesh axis runs over, the one named last changes fastest.
Arguments:
- grads: bfloat16 [4, 8, 1024, 1024], P('dp', 'shard'), may hold values from -6 to 6
- left_roots: bfloat16 [8, 1024, 1024], P('shard'), as said below
- right_roots: bfloat16 [8, 1024, 1024], P('shard'), as said below
- rows_valid: int32 [8], P('shard'), may hold values from 256 to 1024, as said below
- cols_valid: int32 [8], P('shard'), may hold values from 256 to 1024, as said below
Outputs:
- update: bfloat16 [8, 1024, 1024], P('shard', 'dp')
Inputs may be any that keep to these rules, and one draw needn't show every extreme that they name: `left_roots`: each entry is symmetric, with a diagonal between 0.5 and 2. `right_roots`: each entry is symmetric, with a diagonal between 0.5 and 2. A multiple of 256; no block has both rows_valid and cols_valid below 1024. A multiple of 256; no block has both rows_valid and cols_valid below 1024.
All inputs are finite; a program needn't handle non-finite values.
Results may differ from a plain program's by a relative error of at most 0.024.
Values may be sent and summed in bfloat16 or wider, within the bound.
No kernel may reach another device: no remote copies, remote signals or barrier semaphores. Data moves between devices by JAX's collectives and lax.ppermute only.
A program may use at most 64 MiB of HBM per device.

v0:
```python
import jax
import jax.numpy as jnp
from jax import lax
from jax.sharding import PartitionSpec as P


def shifted(value, axis, steps):
    count = lax.axis_size(axis)
    pairs = [(source, (source + steps) % count) for source in range(count)]
    return lax.ppermute(value, axis, pairs)


def precondition(masked, own_rows, right):
    half = jnp.einsum("bsk,bkj->bsj", masked, right, preferred_element_type=jnp.float32).astype(
        jnp.bfloat16
    )
    gathered = lax.psum_scatter(
        jnp.einsum("bsi,bsj->ibj", own_rows, half, preferred_element_type=jnp.float32).astype(
            jnp.bfloat16
        ),
        "dp",
        scatter_dimension=0,
        tiled=True,
    ).astype(jnp.float32)
    return jnp.transpose(gathered, (1, 0, 2))


def on_device(grads, left_roots, right_roots, rows_valid, cols_valid):
    width = grads.shape[3]
    groups = lax.axis_size("dp")
    strip = width // groups
    summed = lax.psum_scatter(
        grads[0].astype(jnp.float32).astype(jnp.bfloat16), "dp", scatter_dimension=1, tiled=True
    ).astype(jnp.float32)
    start_row = lax.axis_index("dp") * strip
    row_ids = start_row + jnp.arange(strip, dtype=jnp.int32)
    col_ids = jnp.arange(width, dtype=jnp.int32)
    mask = (row_ids[None, :, None] < rows_valid[:, None, None]) & (
        col_ids[None, None, :] < cols_valid[:, None, None]
    )
    masked = jnp.where(mask, summed, 0.0).astype(jnp.bfloat16)
    offset = lax.axis_size("shard") // 2
    left_full, right = shifted((left_roots, right_roots), "shard", offset)
    own_rows = lax.dynamic_slice_in_dim(left_full, start_row, strip, 1)
    result = precondition(masked, own_rows, right)
    return jnp.where(mask, result, 0.0).astype(jnp.bfloat16)


def solution(mesh):
    placed = (
        P("dp", "shard", None, None),
        P("shard", None, None),
        P("shard", None, None),
        P("shard"),
        P("shard"),
    )
    return jax.shard_map(
        on_device, mesh=mesh, in_specs=placed, out_specs=P("shard", "dp", None), check_vma=False
    )
```

profile of v0, /device:TPU:0, one launch (start us, length us, event | category | flops | bytes accessed | tf_op | source)
XLA Modules:
  0.0 247.0 jit_solution(11613496020633151469)
XLA Ops:
  6.5 0.0 reduce-scatter.3.cloned.1.call-start
  6.5 3.9 %copy.6 = bf16[1,1,1024,1024]{2,3,1,0:T(8,128)(2,1)} copy(bf16[1,1,1024,1024]{3,2,1,0:T(8,128)(2,1)} %param.5) | data formatting | bytes 4194304 | tf_op args[0]
  10.5 0.0 copy-start
  10.5 0.0 reduce-scatter.3.cloned.1.call-update
  10.5 0.0 reduce-scatter.5.cloned.1.call-start
  10.5 1.5 copy-done
  12.1 4.0 %collective-permute-start.1 = (bf16[1,1024,1024]{2,1,0:T(8,128)(2,1)S(1)}, bf16[1,1024,1024]{2,1,0:T(8,128)(2,1)}, u32[]{:S(2)}, u32[]{:S(2)}) collective-permute-start(bf16[1,1024,1024]{2,1,0:T(8,128)(2,1)S(1)} %copy-done), channel_id=1, source_target_pairs={{0,4},{1,5},{2,6},{3,7},{4,0},{5,1},{6,2},{7,3},{8,12},{9,13},{10,... | collective-permute-start | bytes 6291464 | tf_op jit(solution)/shard_map/ppermute | solution.py:10
  16.1 0.0 collective-permute-start
  17.4 135.1 %collective-permute-done.1 = bf16[1,1024,1024]{2,1,0:T(8,128)(2,1)} collective-permute-done((bf16[1,1024,1024]{2,1,0:T(8,128)(2,1)S(1)}, bf16[1,1024,1024]{2,1,0:T(8,128)(2,1)}, u32[]{:S(2)}, u32[]{:S(2)}) %collective-permute-start.1) | collective-permute-done | bytes 2097184 | tf_op jit(solution)/shard_map/ppermute | solution.py:10
  152.5 44.1 %collective-permute-done = bf16[1,1024,1024]{2,1,0:T(8,128)(2,1)} collective-permute-done((bf16[1,1024,1024]{2,1,0:T(8,128)(2,1)}, bf16[1,1024,1024]{2,1,0:T(8,128)(2,1)}, u32[]{:S(2)}, u32[]{:S(2)}) %collective-permute-start) | collective-permute-done | bytes 2097184 | tf_op jit(solution)/shard_map/ppermute | solution.py:10
  196.6 0.0 reduce-scatter.3.cloned.1.call-done
  196.6 4.6 %convert_bitcast_fusion = bf16[1024,1,1024]{0,2,1:T(8,128)(2,1)} fusion(bf16[1,1024,1024]{2,1,0:T(8,128)(2,1)} %collective-permute-done, bf16[1,256,1024]{1,2,0:T(8,128)(2,1)} %reduce-scatter.3.cloned.1.call-done, bf16[1,1024,1024]{2,1,0:T(8,128)(2,1)} %collective-permute-done.1, s32[]{:T(128)S(6)} %select_n.19, pred[256]{0:T(512)(128)(4,1)S(1)} %add_compare_fusion, ...), kind=kOutput, calls=%fused_computation.2 | convolution fusion | flops 1076101120 | bytes 5244164 | tf_op jit(solution)/shard_map/bsi,bsj->ibj/dot_general | solution.py:18
  201.3 0.0 reduce-scatter.5.cloned.1.call-update
  201.3 36.5 %reduce-scatter.5.cloned.1.call-done = bf16[256,1,1024]{0,2,1:T(8,128)(2,1)} async-done(((bf16[1024,1,1024]{0,2,1:T(8,128)(2,1)}), bf16[256,1,1024]{0,2,1:T(8,128)(2,1)}) %reduce-scatter.5.cloned.1.call-update) | async-done | bytes 524304 | tf_op jit(solution)/shard_map/reduce_scatter | solution.py:17
  237.8 1.3 fusion.6
  239.1 1.0 copy.7
  (2 shorter events, 0.0 us)
Async XLA Ops:
  6.5 190.1 %reduce-scatter.3.cloned.1.call-start = ((), (), s32[]{:S(2)}) async-start(), calls=%async_computation.2 | async-start | bytes 2621440 | tf_op jit(solution)/shard_map/reduce_scatter | solution.py:32
  10.5 1.6 copy-start
  10.5 227.4 %reduce-scatter.5.cloned.1.call-start = ((), (), s32[]{:S(2)}) async-start(), calls=%async_computation.3 | async-start | bytes 2621440 | tf_op jit(solution)/shard_map/reduce_scatter | solution.py:17
  12.1 140.5 %collective-permute-start.1 = (bf16[1,1024,1024]{2,1,0:T(8,128)(2,1)S(1)}, bf16[1,1024,1024]{2,1,0:T(8,128)(2,1)}, u32[]{:S(2)}, u32[]{:S(2)}) collective-permute-start(bf16[1,1024,1024]{2,1,0:T(8,128)(2,1)S(1)} %copy-done), channel_id=1, source_target_pairs={{0,4},{1,5},{2,6},{3,7},{4,0},{5,1},{6,2},{7,3},{8,12},{9,13},{10,... | collective-permute-start | bytes 6291464 | tf_op jit(solution)/shard_map/ppermute | solution.py:10
  16.1 180.6 %collective-permute-start = (bf16[1,1024,1024]{2,1,0:T(8,128)(2,1)}, bf16[1,1024,1024]{2,1,0:T(8,128)(2,1)}, u32[]{:S(2)}, u32[]{:S(2)}) collective-permute-start(bf16[1,1024,1024]{2,1,0:T(8,128)(2,1)} %param.7), channel_id=1, source_target_pairs={{0,4},{1,5},{2,6},{3,7},{4,0},{5,1},{6,2},{7,3},{8,12},{9,13},{10,... | collective-permute-start | bytes 6291464 | tf_op jit(solution)/shard_map/ppermute | solution.py:10
Sparse Core Ops, SparseCore 0:
  10.6 37.8 reduce-scatter.2
  201.4 36.3 reduce-scatter.4
where the time goes:
time: 247 us
  waiting for transfers between devices  216 us (87%)
  between operations  14.7 us (6%)
  local copies, waits for them, and re-layouts  6.44 us (3%)
  matrix products  4.65 us (2%)
  starting transfers between devices  4.11 us (2%)
    ppermute x2, waiting for transfers between devices, shifted(): return lax.ppermute(value, axis, pairs)  179 us
    reduce_scatter x1, waiting for transfers between devices, precondition(): lax.psum_scatter(jnp.einsum('bsi,bsj->ibj', own_rows, half, preferred_ele...  36.5 us
    unnamed x3, local copies, waits for them, and re-layouts  5.44 us
  transfers between devices with their start and end apart: 4, of which 3 were waited for; matrix products, arithmetic and copies ran while one was open for 0% of the time, Pallas kernels for 0%

commit v1 on v0

v1 whole, which is shorter than its diff:
```python
import functools

import jax
import jax.numpy as jnp
from jax import lax
from jax.experimental import pallas as pl
from jax.experimental.pallas import tpu as pltpu
from jax.sharding import PartitionSpec as P

TILE = 256
VMEM = 56 * 1024 * 1024


def shifted(value, axis, steps):
    count = lax.axis_size(axis)
    pairs = [(source, (source + steps) % count) for source in range(count)]
    return lax.ppermute(value, axis, pairs)


def swapped(value, axis, flip):
    count = lax.axis_size(axis)
    return lax.ppermute(value, axis, [(source, source ^ flip) for source in range(count)])


def pack_kernel(strip, me_ref, left_ref, right_ref, corner_ref, packed_ref, diag_ref):
    step = pl.program_id(0)
    rows = packed_ref.shape[0]
    width = packed_ref.shape[1]
    start = me_ref[0] * strip + step * rows
    row = lax.broadcasted_iota(jnp.int32, (rows, width), 0) + start
    column = lax.broadcasted_iota(jnp.int32, (rows, width), 1)
    packed_ref[...] = jnp.where(row <= column, left_ref[0], right_ref[0])
    tile = corner_ref.shape[1]
    on_diag = lax.broadcasted_iota(jnp.int32, (tile, tile), 0) == lax.broadcasted_iota(jnp.int32, (tile, tile), 1)
    line = jnp.sum(jnp.where(on_diag, corner_ref[0].astype(jnp.float32), 0.0), axis=0, keepdims=True)
    per = tile // 128
    for part in range(per):
        diag_ref[pl.ds(step * per + part, 1), :] = line[:, part * 128 : (part + 1) * 128]


def pack(me, left, right, strip):
    width = left.shape[-1]
    steps = width // TILE
    rows = strip // steps
    return pl.pallas_call(
        functools.partial(pack_kernel, strip),
        grid_spec=pltpu.PrefetchScalarGridSpec(
            num_scalar_prefetch=1,
            grid=(steps,),
            in_specs=[
                pl.BlockSpec((1, rows, width), lambda i, me: (0, me[0] * steps + i, 0)),
                pl.BlockSpec((1, rows, width), lambda i, me: (0, me[0] * steps + i, 0)),
                pl.BlockSpec((1, TILE, TILE), lambda i, me: (0, i, i)),
            ],
            out_specs=[
                pl.BlockSpec((rows, width), lambda i, me: (i, 0)),
                pl.BlockSpec((width // 128, 128), lambda i, me: (0, 0)),
            ],
        ),
        out_shape=[
            jax.ShapeDtypeStruct((strip, width), jnp.bfloat16),
            jax.ShapeDtypeStruct((width // 128, 128), jnp.float32),
        ],
        compiler_params=pltpu.CompilerParams(vmem_limit_bytes=VMEM),
        name="pack_roots",
    )(me, left, right, right)


def product_kernel(groups, me_ref, rows_ref, cols_ref, grad_ref, diag_ref, *refs):
    pieces, outs, (packed, left, right, half) = refs[:groups], refs[groups : 2 * groups], refs[2 * groups :]
    width = packed.shape[0]
    strip = width // groups
    tiles = width // TILE
    me = me_ref[0]
    for flip in range(groups):
        start = pl.multiple_of(jnp.bitwise_xor(me, flip) * strip, strip)
        packed[pl.ds(start, strip), :] = pieces[flip][...]

    row = lax.broadcasted_iota(jnp.int32, (TILE, TILE), 0)
    column = lax.broadcasted_iota(jnp.int32, (TILE, TILE), 1)
    for i in range(tiles):
        at_i = pl.ds(i * TILE, TILE)
        corner = packed[at_i, at_i].astype(jnp.float32)
        turned = corner.T
        line = jnp.concatenate(
            [diag_ref[pl.ds(i * (TILE // 128) + part, 1), :] for part in range(TILE // 128)], axis=1
        )
        left[at_i, at_i] = jnp.where(row <= column, corner, turned).astype(jnp.bfloat16)
        right[at_i, at_i] = jnp.where(
            row == column, jnp.broadcast_to(line, (TILE, TILE)), jnp.where(row > column, corner, turned)
        ).astype(jnp.bfloat16)
        for j in range(i):
            at_j = pl.ds(j * TILE, TILE)
            low, high = packed[at_i, at_j], packed[at_j, at_i]
            right[at_i, at_j] = low
            right[at_j, at_i] = low.T
            left[at_j, at_i] = high
            left[at_i, at_j] = high.T

    rows_valid, cols_valid = rows_ref[0], cols_ref[0]

    def mask_rows(i, carry):
        at = pl.ds(pl.multiple_of(i * TILE, TILE), TILE)
        rows = lax.broadcasted_iota(jnp.int32, (TILE, width), 0) + i * TILE
        columns = lax.broadcasted_iota(jnp.int32, (TILE, width), 1)
        keep = (rows < rows_valid) & (columns < cols_valid)
        value = jnp.where(keep, grad_ref[0, 0, at, :].astype(jnp.float32), 0.0).astype(jnp.bfloat16)
        half[at, :] = jnp.dot(value, right[...], preferred_element_type=jnp.float32).astype(jnp.bfloat16)
        return carry

    lax.fori_loop(0, tiles, mask_rows, 0)
    for flip in reversed(range(groups)):
        start = pl.multiple_of(jnp.bitwise_xor(me, flip) * strip, strip)
        outs[flip][...] = jnp.dot(
            left[pl.ds(start, strip), :], half[...], preferred_element_type=jnp.float32
        ).astype(jnp.bfloat16)


def product(me, rows_valid, cols_valid, grads, diag, pieces):
    groups = len(pieces)
    width = grads.shape[-1]
    strip = width // groups
    smem = pl.BlockSpec(memory_space=pltpu.SMEM)
    vmem = pl.BlockSpec(memory_space=pltpu.VMEM)
    return pl.pallas_call(
        functools.partial(product_kernel, groups),
        in_specs=[smem, smem, smem] + [vmem] * (2 + groups),
        out_specs=[vmem] * groups,
        out_shape=[jax.ShapeDtypeStruct((strip, width), jnp.bfloat16)] * groups,
        scratch_shapes=[pltpu.VMEM((width, width), jnp.bfloat16)] * 4,
        compiler_params=pltpu.CompilerParams(vmem_limit_bytes=VMEM),
        name="left_grad_right",
    )(me, rows_valid, cols_valid, grads, diag, *pieces)


def on_device(grads, left_roots, right_roots, rows_valid, cols_valid):
    width = grads.shape[3]
    groups = lax.axis_size("dp")
    strip = width // groups
    me = lax.axis_index("dp")
    me_arr = me.astype(jnp.int32).reshape(1)
    offset = lax.axis_size("shard") // 2

    packed, diag = pack(me_arr, left_roots, right_roots, strip)
    packed, diag = shifted((packed, diag), "shard", offset)
    pieces = [packed] + [swapped(packed, "dp", flip) for flip in range(1, groups)]
    terms = product(me_arr, rows_valid, cols_valid, grads, diag, pieces)
    got = [terms[0]] + [swapped(terms[flip], "dp", flip) for flip in range(1, groups)]

    row_ids = me * strip + jnp.arange(strip, dtype=jnp.int32)
    col_ids = jnp.arange(width, dtype=jnp.int32)
    mask = (row_ids[:, None] < rows_valid[0]) & (col_ids[None, :] < cols_valid[0])
    total = functools.reduce(lambda a, b: a + b, [term.astype(jnp.float32) for term in got])
    return jnp.where(mask, total, 0.0).astype(jnp.bfloat16)[None]


def solution(mesh):
    placed = (
        P("dp", "shard", None, None),
        P("shard", None, None),
        P("shard", None, None),
        P("shard"),
        P("shard"),
    )
    return jax.shard_map(
        on_device, mesh=mesh, in_specs=placed, out_specs=P("shard", "dp", None), check_vma=False
    )
```

time: 247 us -> 93.5 us (0.38)
  waiting for transfers between devices: 216 us -> 63.9 us
  between operations: 14.7 us -> 1.33 us
  Pallas kernels: 0 us -> 12.6 us
  starting transfers between devices: 4.11 us -> 11 us
  local copies, waits for them, and re-layouts: 6.44 us -> 1.59 us
  matrix products: 4.65 us -> 0 us
    ppermute x2, waiting for transfers between devices: 179 us -> 26.8 us  [shifted(): return lax.ppermute(value, axis, pairs)]
    ppermute x0 -> x6, waiting for transfers between devices: none -> 37.1 us  [swapped(): lax.ppermute(value, axis, [(source, source ^ flip) for source in range(co...]
    reduce_scatter x2 -> x0, waiting for transfers between devices: 36.5 us -> none  [the longest x1 36.5 us: precondition(): lax.psum_scatter(jnp.einsum('bsi,bsj->ibj', own_rows, half, preferred_ele...]
    pallas_call x0 -> x2, Pallas kernels: none -> 12.6 us  [the longest x1 9.16 us: product(): pl.pallas_call(functools.partial(product_kernel, groups), in_specs=[smem,...]
    ppermute x0 -> x6, starting transfers between devices: none -> 6.98 us  [swapped(): lax.ppermute(value, axis, [(source, source ^ flip) for source in range(co...]
    dot_general x1 -> x0, matrix products: 4.65 us -> none  [precondition(): jnp.einsum('bsi,bsj->ibj', own_rows, half, preferred_element_type=jnp.flo...]
    unnamed x3 -> x10, local copies, waits for them, and re-layouts: 5.44 us -> 1.59 us
  transfers between devices with their start and end apart: 4 -> 8, of which waited for: 3 -> 6; matrix products, arithmetic and copies ran while one was open for 0% -> 0% of each run, Pallas kernels for 0% -> 0%
where the time goes in v1:
time: 93.5 us; the launch traced here: 92.7 us
  waiting for transfers between devices  63.9 us (68%)
  Pallas kernels  12.6 us (13%)
  starting transfers between devices  11 us (12%)
  other arithmetic  2.21 us (2%)
  local copies, waits for them, and re-layouts  1.59 us (2%)
  between operations  1.33 us (1%)
    ppermute x6, waiting for transfers between devices, swapped(): lax.ppermute(value, axis, [(source, source ^ flip) for source in range(co...  37.1 us
    ppermute x2, waiting for transfers between devices, shifted(): return lax.ppermute(value, axis, pairs)  26.8 us
    pallas_call x1, Pallas kernels, product(): pl.pallas_call(functools.partial(product_kernel, groups), in_specs=[smem,...  9.16 us
    ppermute x6, starting transfers between devices, swapped(): lax.ppermute(value, axis, [(source, source ^ flip) for source in range(co...  6.98 us
    ppermute x2, starting transfers between devices, shifted(): return lax.ppermute(value, axis, pairs)  4.04 us
    pallas_call x1, Pallas kernels, pack(): pl.pallas_call(functools.partial(pack_kernel, strip), grid_spec=pltpu.Pre...  3.43 us
    broadcast_in_dim x1, other arithmetic, on_device(): return jnp.where(mask, total, 0.0).astype(jnp.bfloat16)[None]  2.19 us
  transfers between devices with their start and end apart: 8, of which 6 were waited for; matrix products, arithmetic and copies ran while one was open for 0% of the time, Pallas kernels for 0%

profile of v1, /device:TPU:0, one launch (start us, length us, event | category | flops | bytes accessed | tf_op | source)
XLA Modules:
  0.0 92.7 jit_solution(12480370818283279010)
XLA Ops:
  0.0 3.4 %pack_roots.1 = (bf16[256,1024]{1,0:T(8,128)(2,1)}, f32[8,128]{1,0:T(8,128)}) custom-call(s32[1]{0:T(128)} %bitcast.2.me_ref, bf16[1,1024,1024]{2,1,0:T(8,128)(2,1)} %left_ref.1, bf16[1,1024,1024]{2,1,0:T(8,128)(2,1)} %corner_ref.1, bf16[1,1024,1024]{2,1,0:T(8,128)(2,1)} %corner_ref.1), custom_call_target="tpu_custom_call" | custom-call | tf_op jit(solution)/shard_map/pack_roots/pallas_call | solution.py:45
  3.4 4.0 %collective-permute-start.1 = (bf16[256,1024]{1,0:T(8,128)(2,1)}, bf16[256,1024]{1,0:T(8,128)(2,1)S(1)}, u32[]{:S(2)}, u32[]{:S(2)}) collective-permute-start(bf16[256,1024]{1,0:T(8,128)(2,1)} %get-tuple-element.12), channel_id=1, source_target_pairs={{0,4},{1,5},{2,6},{3,7},{4,0},{5,1},{6,2},{7,3},{8,12},{9,13},{10,... | collective-permute-start | bytes 1572872 | tf_op jit(solution)/shard_map/ppermute | solution.py:17
  7.5 23.4 %collective-permute-done.1.refs_0_ = bf16[256,1024]{1,0:T(8,128)(2,1)S(1)} collective-permute-done((bf16[256,1024]{1,0:T(8,128)(2,1)}, bf16[256,1024]{1,0:T(8,128)(2,1)S(1)}, u32[]{:S(2)}, u32[]{:S(2)}) %collective-permute-start.1) | collective-permute-done | bytes 524320 | tf_op jit(solution)/shard_map/ppermute | solution.py:17
  30.8 0.0 copy-start
  30.8 1.5 %collective-permute-start.2 = (bf16[256,1024]{1,0:T(8,128)(2,1)S(1)}, bf16[256,1024]{1,0:T(8,128)(2,1)S(1)}, u32[]{:S(2)}, u32[]{:S(2)}) collective-permute-start(bf16[256,1024]{1,0:T(8,128)(2,1)S(1)} %collective-permute-done.1.refs_0_), channel_id=1, source_target_pairs={{0,8},{8,0},{16,24},{24,16},{1,9},{9,1},{17,25},{25,17},{2,10},{10... | collective-permute-start | bytes 1572872 | tf_op jit(solution)/shard_map/ppermute | solution.py:22
  32.4 1.5 %collective-permute-start.3 = (bf16[256,1024]{1,0:T(8,128)(2,1)S(1)}, bf16[256,1024]{1,0:T(8,128)(2,1)S(1)}, u32[]{:S(2)}, u32[]{:S(2)}) collective-permute-start(bf16[256,1024]{1,0:T(8,128)(2,1)S(1)} %collective-permute-done.1.refs_0_), channel_id=1, source_target_pairs={{0,16},{8,24},{16,0},{24,8},{1,17},{9,25},{17,1},{25,9},{2,18},{10... | collective-permute-start | bytes 1572872 | tf_op jit(solution)/shard_map/ppermute | solution.py:22
  33.9 0.4 collective-permute-start.4
  34.3 0.0 collective-permute-start
  35.6 3.4 %collective-permute-done.diag_ref = f32[8,128]{1,0:T(8,128)S(1)} collective-permute-done((f32[8,128]{1,0:T(8,128)}, f32[8,128]{1,0:T(8,128)S(1)}, u32[]{:S(2)}, u32[]{:S(2)}) %collective-permute-start) | collective-permute-done | bytes 4128 | tf_op jit(solution)/shard_map/ppermute | solution.py:17
  39.0 0.0 copy-start.4
  39.0 6.7 %collective-permute-done.2.refs_1_ = bf16[256,1024]{1,0:T(8,128)(2,1)S(1)} collective-permute-done((bf16[256,1024]{1,0:T(8,128)(2,1)S(1)}, bf16[256,1024]{1,0:T(8,128)(2,1)S(1)}, u32[]{:S(2)}, u32[]{:S(2)}) %collective-permute-start.2) | collective-permute-done | bytes 524320 | tf_op jit(solution)/shard_map/ppermute | solution.py:22
  45.7 0.0 copy-start.1
  45.7 10.5 %collective-permute-done.3.refs_2_ = bf16[256,1024]{1,0:T(8,128)(2,1)S(1)} collective-permute-done((bf16[256,1024]{1,0:T(8,128)(2,1)S(1)}, bf16[256,1024]{1,0:T(8,128)(2,1)S(1)}, u32[]{:S(2)}, u32[]{:S(2)}) %collective-permute-start.3) | collective-permute-done | bytes 524320 | tf_op jit(solution)/shard_map/ppermute | solution.py:22
  56.2 0.0 copy-start.2
  56.2 0.0 collective-permute-done.4.refs_3_
  56.2 0.0 copy-done
  56.2 0.0 copy-done.4
  56.2 0.0 copy-done.1
  56.2 0.8 copy-done.2
  57.0 0.0 copy-start.3
  57.0 0.8 copy-done.3
  57.8 9.2 %left_grad_right.1 = (bf16[256,1024]{1,0:T(8,128)(2,1)}, bf16[256,1024]{1,0:T(8,128)(2,1)}, bf16[256,1024]{1,0:T(8,128)(2,1)}, bf16[256,1024]{1,0:T(8,128)(2,1)}) custom-call(s32[1]{0:T(128)} %bitcast.2.me_ref, s32[1]{0:T(128)} %copy.6.rows_ref, s32[1]{0:T(128)} %copy.7.cols_ref, bf16[1,1,1024,1024]{3,2,1,0:T(8,128)(2,1)} %grad_ref.1, f32[8,128]{1,0:T(8,128)} %copy-done.4, ...), custom_call_target="tpu_custom_call" | custom-call | tf_op jit(solution)/shard_map/left_grad_right/pallas_call | solution.py:125
  66.9 0.5 collective-permute-start.5
  67.4 1.6 %collective-permute-start.6 = (bf16[256,1024]{1,0:T(8,128)(2,1)}, bf16[256,1024]{1,0:T(8,128)(2,1)S(1)}, u32[]{:S(2)}, u32[]{:S(2)}) collective-permute-start(bf16[256,1024]{1,0:T(8,128)(2,1)} %get-tuple-element.15), channel_id=1, source_target_pairs={{0,16},{8,24},{16,0},{24,8},{1,17},{9,25},{17,1},{25,9},{2,18},{10... | collective-permute-start | bytes 1572872 | tf_op jit(solution)/shard_map/ppermute | solution.py:22
  69.0 1.4 %collective-permute-start.7 = (bf16[256,1024]{1,0:T(8,128)(2,1)}, bf16[256,1024]{1,0:T(8,128)(2,1)S(1)}, u32[]{:S(2)}, u32[]{:S(2)}) collective-permute-start(bf16[256,1024]{1,0:T(8,128)(2,1)} %get-tuple-element.16), channel_id=1, source_target_pairs={{0,24},{8,16},{16,8},{24,0},{1,25},{9,17},{17,9},{25,1},{2,26},{10... | collective-permute-start | bytes 1572872 | tf_op jit(solution)/shard_map/ppermute | solution.py:22
  70.4 11.6 %collective-permute-done.5 = bf16[256,1024]{1,0:T(8,128)(2,1)S(1)} collective-permute-done((bf16[256,1024]{1,0:T(8,128)(2,1)}, bf16[256,1024]{1,0:T(8,128)(2,1)S(1)}, u32[]{:S(2)}, u32[]{:S(2)}) %collective-permute-start.5) | collective-permute-done | bytes 524320 | tf_op jit(solution)/shard_map/ppermute | solution.py:22
  82.0 8.5 %collective-permute-done.6 = bf16[256,1024]{1,0:T(8,128)(2,1)S(1)} collective-permute-done((bf16[256,1024]{1,0:T(8,128)(2,1)}, bf16[256,1024]{1,0:T(8,128)(2,1)S(1)}, u32[]{:S(2)}, u32[]{:S(2)}) %collective-permute-start.6) | collective-permute-done | bytes 524320 | tf_op jit(solution)/shard_map/ppermute | solution.py:22
  90.5 0.0 collective-permute-done.7
  90.5 2.2 %fusion = bf16[1,256,1024]{2,1,0:T(8,128)(2,1)} fusion(bf16[256,1024]{1,0:T(8,128)(2,1)S(1)} %collective-permute-done.7, bf16[256,1024]{1,0:T(8,128)(2,1)S(1)} %collective-permute-done.6, bf16[256,1024]{1,0:T(8,128)(2,1)S(1)} %collective-permute-done.5, bf16[256,1024]{1,0:T(8,128)(2,1)} %get-tuple-element.13, pred[1024]{0:T(1024)(128)(4,1)S(1)} %iota_compare_fusion, ...), kind=kLoop, calls=%fused_computation.1 | loop fusion | flops 2621440 | bytes 2622720 | tf_op jit(solution)/shard_map/broadcast_in_dim | solution.py:154
  (2 shorter events, 0.0 us)
Async XLA Ops:
  3.4 27.4 %collective-permute-start.1 = (bf16[256,1024]{1,0:T(8,128)(2,1)}, bf16[256,1024]{1,0:T(8,128)(2,1)S(1)}, u32[]{:S(2)}, u32[]{:S(2)}) collective-permute-start(bf16[256,1024]{1,0:T(8,128)(2,1)} %get-tuple-element.12), channel_id=1, source_target_pairs={{0,4},{1,5},{2,6},{3,7},{4,0},{5,1},{6,2},{7,3},{8,12},{9,13},{10,... | collective-permute-start | bytes 1572872 | tf_op jit(solution)/shard_map/ppermute | solution.py:17
  30.8 25.3 %copy-start = (bf16[256,1024]{1,0:T(8,128)(2,1)}, bf16[256,1024]{1,0:T(8,128)(2,1)S(1)}, u32[]{:S(2)}) copy-start(bf16[256,1024]{1,0:T(8,128)(2,1)S(1)} %collective-permute-done.1.refs_0_) | copy-start | bytes 1572868
  30.8 14.9 %collective-permute-start.2 = (bf16[256,1024]{1,0:T(8,128)(2,1)S(1)}, bf16[256,1024]{1,0:T(8,128)(2,1)S(1)}, u32[]{:S(2)}, u32[]{:S(2)}) collective-permute-start(bf16[256,1024]{1,0:T(8,128)(2,1)S(1)} %collective-permute-done.1.refs_0_), channel_id=1, source_target_pairs={{0,8},{8,0},{16,24},{24,16},{1,9},{9,1},{17,25},{25,17},{2,10},{10... | collective-permute-start | bytes 1572872 | tf_op jit(solution)/shard_map/ppermute | solution.py:22
  32.4 23.8 %collective-permute-start.3 = (bf16[256,1024]{1,0:T(8,128)(2,1)S(1)}, bf16[256,1024]{1,0:T(8,128)(2,1)S(1)}, u32[]{:S(2)}, u32[]{:S(2)}) collective-permute-start(bf16[256,1024]{1,0:T(8,128)(2,1)S(1)} %collective-permute-done.1.refs_0_), channel_id=1, source_target_pairs={{0,16},{8,24},{16,0},{24,8},{1,17},{9,25},{17,1},{25,9},{2,18},{10... | collective-permute-start | bytes 1572872 | tf_op jit(solution)/shard_map/ppermute | solution.py:22
  33.9 22.3 %collective-permute-start.4 = (bf16[256,1024]{1,0:T(8,128)(2,1)S(1)}, bf16[256,1024]{1,0:T(8,128)(2,1)S(1)}, u32[]{:S(2)}, u32[]{:S(2)}) collective-permute-start(bf16[256,1024]{1,0:T(8,128)(2,1)S(1)} %collective-permute-done.1.refs_0_), channel_id=1, source_target_pairs={{0,24},{8,16},{16,8},{24,0},{1,25},{9,17},{17,9},{25,1},{2,26},{10... | collective-permute-start | bytes 1572872 | tf_op jit(solution)/shard_map/ppermute | solution.py:22
  34.3 4.7 %collective-permute-start = (f32[8,128]{1,0:T(8,128)}, f32[8,128]{1,0:T(8,128)S(1)}, u32[]{:S(2)}, u32[]{:S(2)}) collective-permute-start(f32[8,128]{1,0:T(8,128)} %get-tuple-element.11), channel_id=1, source_target_pairs={{0,4},{1,5},{2,6},{3,7},{4,0},{5,1},{6,2},{7,3},{8,12},{9,13},{10,... | collective-permute-start | bytes 12296 | tf_op jit(solution)/shard_map/ppermute | solution.py:17
  39.0 17.1 %copy-start.4 = (f32[8,128]{1,0:T(8,128)}, f32[8,128]{1,0:T(8,128)S(1)}, u32[]{:S(2)}) copy-start(f32[8,128]{1,0:T(8,128)S(1)} %collective-permute-done.diag_ref) | copy-start | bytes 12292
  45.7 10.5 %copy-start.1 = (bf16[256,1024]{1,0:T(8,128)(2,1)}, bf16[256,1024]{1,0:T(8,128)(2,1)S(1)}, u32[]{:S(2)}) copy-start(bf16[256,1024]{1,0:T(8,128)(2,1)S(1)} %collective-permute-done.2.refs_1_) | copy-start | bytes 1572868
  56.2 0.8 copy-start.2
  57.0 0.8 copy-start.3
  66.9 15.1 %collective-permute-start.5 = (bf16[256,1024]{1,0:T(8,128)(2,1)}, bf16[256,1024]{1,0:T(8,128)(2,1)S(1)}, u32[]{:S(2)}, u32[]{:S(2)}) collective-permute-start(bf16[256,1024]{1,0:T(8,128)(2,1)} %get-tuple-element.14), channel_id=1, source_target_pairs={{0,8},{8,0},{16,24},{24,16},{1,9},{9,1},{17,25},{25,17},{2,10},{10... | collective-permute-start | bytes 1572872 | tf_op jit(solution)/shard_map/ppermute | solution.py:22
  67.4 23.1 %collective-permute-start.6 = (bf16[256,1024]{1,0:T(8,128)(2,1)}, bf16[256,1024]{1,0:T(8,128)(2,1)S(1)}, u32[]{:S(2)}, u32[]{:S(2)}) collective-permute-start(bf16[256,1024]{1,0:T(8,128)(2,1)} %get-tuple-element.15), channel_id=1, source_target_pairs={{0,16},{8,24},{16,0},{24,8},{1,17},{9,25},{17,1},{25,9},{2,18},{10... | collective-permute-start | bytes 1572872 | tf_op jit(solution)/shard_map/ppermute | solution.py:22
  69.0 21.5 %collective-permute-start.7 = (bf16[256,1024]{1,0:T(8,128)(2,1)}, bf16[256,1024]{1,0:T(8,128)(2,1)S(1)}, u32[]{:S(2)}, u32[]{:S(2)}) collective-permute-start(bf16[256,1024]{1,0:T(8,128)(2,1)} %get-tuple-element.16), channel_id=1, source_target_pairs={{0,24},{8,16},{16,8},{24,0},{1,25},{9,17},{17,9},{25,1},{2,26},{10... | collective-permute-start | bytes 1572872 | tf_op jit(solution)/shard_map/ppermute | solution.py:22

commit v2 on v0

v2 whole, which is shorter than its diff:
```python
import functools

import jax
import jax.numpy as jnp
from jax import lax
from jax.experimental import pallas as pl
from jax.experimental.pallas import tpu as pltpu
from jax.sharding import PartitionSpec as P

TILE = 256
VMEM = 24 * 1024 * 1024
PACK_VMEM = 60 * 1024 * 1024
SMEM_SPEC = pl.BlockSpec(memory_space=pltpu.SMEM)
VMEM_SPEC = pl.BlockSpec(memory_space=pltpu.VMEM)
BF16 = jnp.bfloat16
F32 = jnp.float32


def shifted(value, axis, steps):
    count = lax.axis_size(axis)
    pairs = [(source, (source + steps) % count) for source in range(count)]
    return lax.ppermute(value, axis, pairs)


def swapped(value, flip):
    count = lax.axis_size("dp")
    return lax.ppermute(value, "dp", [(source, source ^ flip) for source in range(count)])


def after(value, *earlier):
    return lax.optimization_barrier((value, *earlier))[0]


def gathered(value, turn):
    count = lax.axis_size("dp")
    if count != 4:
        return [value] + [swapped(value, flip) for flip in range(1, count)]
    near = [swapped(value, 1), swapped(value, 2)]
    return [value, *near, swapped(near[turn], 2 - turn)]


def layout(tiles):
    above = [(i, j) for i in range(tiles) for j in range(i + 1, tiles)]
    cut = len(above) // 2
    below = [(i, j) for j in range(tiles) for i in range(j + 1, tiles)]
    return {
        "left_a": above[:cut],
        "left_b": above[cut:],
        "corner": [(i, i) for i in range(tiles)],
        "right_a": below[:cut],
        "right_b": below[cut:],
    }


def block(index):
    return pl.ds(index * TILE, TILE)


def cost(flops, bytes_accessed):
    return pl.CostEstimate(flops=flops, bytes_accessed=bytes_accessed, transcendentals=0)


def pack_first_kernel(blocks, rows_of, tiles, me_ref, *refs):
    lefts, out = refs[: len(rows_of)], refs[-1]
    strip = out.shape[0] // len(blocks)
    for k, (i, j) in enumerate(blocks):
        out[pl.ds(k * strip, strip), :] = lefts[rows_of.index(i)][0, :, block(j)]


def strip_specs(rows_of, strip, width, groups):
    def index_map(i):
        return lambda step, me: (0, i * groups + me[0], 0)

    return [pl.BlockSpec((1, strip, width), index_map(i)) for i in rows_of]


def pack_first(me, left, groups, blocks):
    width = left.shape[-1]
    strip = TILE // groups
    rows_of = sorted({i for i, _ in blocks})
    return pl.pallas_call(
        functools.partial(pack_first_kernel, blocks, rows_of, width // TILE),
        grid_spec=pltpu.PrefetchScalarGridSpec(
            num_scalar_prefetch=1,
            grid=(1,),
            in_specs=strip_specs(rows_of, strip, width, groups),
            out_specs=pl.BlockSpec((len(blocks) * strip, TILE), lambda step, me: (0, 0)),
        ),
        out_shape=jax.ShapeDtypeStruct((len(blocks) * strip, TILE), BF16),
        compiler_params=pltpu.CompilerParams(vmem_limit_bytes=PACK_VMEM),
        name="pack_first",
    )(me, *[left] * len(rows_of))


def pack_rest_kernel(plan, tiles, me_ref, *refs):
    lefts, rights, outs = refs[:tiles], refs[tiles : 2 * tiles], refs[2 * tiles :]
    strip = lefts[0].shape[1]
    left_b, corner, right_a, right_b = outs
    for k, (i, j) in enumerate(plan["left_b"]):
        left_b[pl.ds(k * strip, strip), :] = lefts[i][0, :, block(j)]
    for out, name in ((right_a, "right_a"), (right_b, "right_b")):
        for k, (i, j) in enumerate(plan[name]):
            out[pl.ds(k * strip, strip), :] = rights[i][0, :, block(j)]
    row = lax.broadcasted_iota(jnp.int32, (strip, TILE), 0) + me_ref[0] * strip
    column = lax.broadcasted_iota(jnp.int32, (strip, TILE), 1)
    lines = []
    for i in range(tiles):
        mine = lefts[i][0, :, block(i)].astype(F32)
        other = rights[i][0, :, block(i)].astype(F32)
        corner[pl.ds(i * strip, strip), :] = jnp.where(row <= column, mine, other).astype(BF16)
        lines.append(jnp.sum(jnp.where(row == column, other, 0.0), axis=0, keepdims=True))
    extra = right_b.shape[0] - len(plan["right_b"]) * strip
    lines.append(jnp.zeros((extra - tiles, TILE), F32))
    right_b[pl.ds(len(plan["right_b"]) * strip, extra), :] = jnp.concatenate(lines, axis=0).astype(BF16)


def pack_rest(me, left, right, groups, plan):
    width = left.shape[-1]
    strip = TILE // groups
    tiles = width // TILE
    extra = -(-tiles // 16) * 16
    rows = [len(plan[name]) * strip for name in ("left_b", "corner", "right_a", "right_b")]
    rows[-1] += extra
    return pl.pallas_call(
        functools.partial(pack_rest_kernel, plan, tiles),
        grid_spec=pltpu.PrefetchScalarGridSpec(
            num_scalar_prefetch=1,
            grid=(1,),
            in_specs=strip_specs(range(tiles), strip, width, groups) * 2,
            out_specs=[pl.BlockSpec((count, TILE), lambda step, me: (0, 0)) for count in rows],
        ),
        out_shape=[jax.ShapeDtypeStruct((count, TILE), BF16) for count in rows],
        compiler_params=pltpu.CompilerParams(vmem_limit_bytes=PACK_VMEM),
        name="pack_rest",
    )(me, *[left] * tiles, *[right] * tiles)


def place(blocks, pieces, me, target, at=lambda i, j: (i * TILE, j * TILE)):
    strip = TILE // len(pieces)
    for k, (i, j) in enumerate(blocks):
        top, side = at(i, j)
        for flip, piece in enumerate(pieces):
            start = pl.multiple_of(top + jnp.bitwise_xor(me, flip) * strip, strip)
            target[pl.ds(start, strip), pl.ds(side, TILE)] = piece[pl.ds(k * strip, strip), :]


def whole_left_kernel(plan, groups, me_ref, *refs):
    left_a, left_b, corner = refs[:groups], refs[groups : 2 * groups], refs[2 * groups : 3 * groups]
    left, right_corner, mixed = refs[3 * groups :]
    me = me_ref[0]
    tiles = left.shape[0] // TILE
    place(plan["left_a"], left_a, me, left)
    place(plan["left_b"], left_b, me, left)
    place(plan["corner"], corner, me, mixed, lambda i, j: (i * TILE, 0))
    row = lax.broadcasted_iota(jnp.int32, (TILE, TILE), 0)
    column = lax.broadcasted_iota(jnp.int32, (TILE, TILE), 1)
    for i in range(tiles):
        value = mixed[block(i), :].astype(F32)
        turned = value.T
        left[block(i), block(i)] = jnp.where(row <= column, value, turned).astype(BF16)
        right_corner[block(i), :] = jnp.where(row > column, value, turned).astype(BF16)
        for j in range(i):
            left[block(i), block(j)] = left[block(j), block(i)].T


def whole_left(me, width, plan, left_a, left_b, corner):
    groups = len(left_a)
    return pl.pallas_call(
        functools.partial(whole_left_kernel, plan, groups),
        in_specs=[SMEM_SPEC] + [VMEM_SPEC] * (3 * groups),
        out_specs=[VMEM_SPEC] * 2,
        out_shape=[jax.ShapeDtypeStruct((width, width), BF16), jax.ShapeDtypeStruct((width, TILE), BF16)],
        scratch_shapes=[pltpu.VMEM((width, TILE), BF16)],
        compiler_params=pltpu.CompilerParams(vmem_limit_bytes=VMEM),
        cost_estimate=cost(width**2, 4 * width**2),
        name="whole_left",
    )(me, *left_a, *left_b, *corner)


def left_grad_kernel(rows_ref, cols_ref, left, grad_ref, out, grad):
    tiles = left.shape[0] // TILE
    rows_valid, cols_valid = rows_ref[0], cols_ref[0]
    for i in range(tiles):
        for j in range(tiles):
            keep = (i * TILE < rows_valid) & (j * TILE < cols_valid)

            @pl.when(keep)
            def _():
                grad[block(i), block(j)] = grad_ref[0, 0, block(i), block(j)]

            @pl.when(jnp.logical_not(keep))
            def _():
                grad[block(i), block(j)] = jnp.zeros((TILE, TILE), BF16)

    def step(i, carry):
        at = pl.ds(pl.multiple_of(i * TILE, TILE), TILE)
        out[at, :] = jnp.dot(left[at, :], grad[...], preferred_element_type=F32).astype(BF16)
        return carry

    lax.fori_loop(0, tiles, step, 0)


def left_grad(rows_valid, cols_valid, left, grads):
    width = grads.shape[-1]
    return pl.pallas_call(
        left_grad_kernel,
        in_specs=[SMEM_SPEC] * 2 + [VMEM_SPEC] * 2,
        out_specs=VMEM_SPEC,
        out_shape=jax.ShapeDtypeStruct((width, width), BF16),
        scratch_shapes=[pltpu.VMEM((width, width), BF16)],
        compiler_params=pltpu.CompilerParams(vmem_limit_bytes=VMEM),
        cost_estimate=cost(2 * width**3, 6 * width**2),
        name="left_grad",
    )(rows_valid, cols_valid, left, grads)


def far_kernel(plan, groups, me_ref, product_ref, corner_ref, *refs):
    right_a, right_b = refs[:groups], refs[groups : 2 * groups]
    far_first, far_second, right = refs[2 * groups :]
    me = me_ref[0]
    width = right.shape[0]
    tiles = width // TILE
    place(plan["right_a"], right_a, me, right)
    place(plan["right_b"], right_b, me, right)
    row = lax.broadcasted_iota(jnp.int32, (TILE, TILE), 0)
    column = lax.broadcasted_iota(jnp.int32, (TILE, TILE), 1)
    base = len(plan["right_b"]) * (TILE // groups)
    lines = functools.reduce(
        lambda a, b: a + b, [piece[pl.ds(base, piece.shape[0] - base), :].astype(F32) for piece in right_b]
    )
    for i in range(tiles):
        line = jnp.broadcast_to(lines[i : i + 1, :], (TILE, TILE))
        right[block(i), block(i)] = jnp.where(row == column, line, corner_ref[block(i), :].astype(F32)).astype(BF16)
        for j in range(i):
            right[block(j), block(i)] = right[block(i), block(j)].T
    strip = width // groups
    start = pl.multiple_of(jnp.bitwise_xor(me, groups - 1) * strip, strip)
    value = jnp.dot(product_ref[pl.ds(start, strip), :], right[...], preferred_element_type=F32).astype(BF16)
    far_first[...] = value[:, : width // 2]
    far_second[...] = value[:, width // 2 :]


def far(me, product, corner, plan, right_a, right_b):
    groups = len(right_a)
    width = product.shape[0]
    strip = width // groups
    part = jax.ShapeDtypeStruct((strip, width // 2), BF16)
    return pl.pallas_call(
        functools.partial(far_kernel, plan, groups),
        in_specs=[SMEM_SPEC] + [VMEM_SPEC] * (2 + 2 * groups),
        out_specs=[VMEM_SPEC] * 3,
        out_shape=[part, part, jax.ShapeDtypeStruct((width, width), BF16)],
        compiler_params=pltpu.CompilerParams(vmem_limit_bytes=VMEM),
        cost_estimate=cost(2 * strip * width**2, 8 * width**2),
        name="far_rows",
    )(me, product, corner, *right_a, *right_b)


def near_kernel(flips, me_ref, product_ref, right_ref, *outs):
    me = me_ref[0]
    strip = outs[0].shape[0]
    width = right_ref.shape[0]
    for (flip, first, last), out in zip(flips, outs):
        start = pl.multiple_of(jnp.bitwise_xor(me, flip) * strip, strip)
        out[...] = jnp.dot(
            product_ref[pl.ds(start, strip), :], right_ref[:, first:last], preferred_element_type=F32
        ).astype(out.dtype)


def near(me, product, right, groups, flips, name):
    width = product.shape[0]
    strip = width // groups
    return pl.pallas_call(
        functools.partial(near_kernel, flips),
        in_specs=[SMEM_SPEC] + [VMEM_SPEC] * 2,
        out_specs=[VMEM_SPEC] * len(flips),
        out_shape=[jax.ShapeDtypeStruct((strip, last - first), BF16) for _, first, last in flips],
        compiler_params=pltpu.CompilerParams(vmem_limit_bytes=VMEM),
        cost_estimate=cost(2 * strip * width * sum(last - first for _, first, last in flips), 4 * width**2),
        name=name,
    )(me, product, right)


def added(*terms):
    return functools.reduce(lambda a, b: a + b, [term.astype(F32) for term in terms])


def on_device(grads, left_roots, right_roots, rows_valid, cols_valid):
    width = grads.shape[3]
    groups = lax.axis_size("dp")
    strip = width // groups
    half = width // 2
    me = lax.axis_index("dp").astype(jnp.int32)
    me_arr = me.reshape(1)
    offset = lax.axis_size("shard") // 2
    plan = layout(width // TILE)

    messages = [pack_first(me_arr, left_roots, groups, plan["left_a"])]
    crossed = [shifted(messages[0], "shard", offset)]
    messages += pack_rest(me_arr, left_roots, right_roots, groups, plan)
    crossed.append(shifted(messages[1], "shard", offset))
    pieces = []
    for k in range(len(messages)):
        arrived = crossed[k]
        if k > 0:
            arrived = after(arrived, *pieces[-1][1:3], *[piece[3] for piece in pieces[-2:-1]])
        if k == 4:
            left, right_corner = whole_left(me_arr, width, plan, *pieces[:3])
            arrived = after(arrived, right_corner)
        if k + 2 < len(messages):
            crossed.append(shifted(after(messages[k + 2], crossed[k]), "shard", offset))
        pieces.append(gathered(arrived, k % 2))
    right_a, right_b = pieces[3:]
    product = left_grad(rows_valid, cols_valid, left, grads)
    far_first, far_second, right = far(me_arr, product, right_corner, plan, right_a, right_b)
    if groups == 4:
        far_first, far_second = swapped(far_first, 1), swapped(far_second, 2)
        near_first, near_second = near(
            me_arr, product, right, groups, [(1, 0, half), (2, half, width)], "near_rows"
        )
        via_first, via_second, own = near(
            me_arr, product, right, groups, [(2, 0, half), (1, half, width), (0, 0, width)], "own_rows"
        )
        near_first, near_second = swapped(near_first, 1), swapped(near_second, 2)
        via_first = swapped(added(via_first, far_first).astype(BF16), 2)
        via_second = swapped(added(via_second, far_second).astype(BF16), 1)
        total = jnp.concatenate(
            [added(own[:, :half], near_first, via_first), added(own[:, half:], near_second, via_second)], axis=1
        )
    else:
        last = groups - 1
        rest = near(me_arr, product, right, groups, [(flip, 0, width) for flip in range(last)], "near_rows")
        far_whole = swapped(jnp.concatenate([far_first, far_second], axis=1), last)
        total = added(rest[0], far_whole, *[swapped(rest[flip], flip) for flip in range(1, last)])

    row_ids = me * strip + jnp.arange(strip, dtype=jnp.int32)
    col_ids = jnp.arange(width, dtype=jnp.int32)
    mask = (row_ids[:, None] < rows_valid[0]) & (col_ids[None, :] < cols_valid[0])
    return jnp.where(mask, total, 0.0).astype(BF16)[None]


def solution(mesh):
    placed = (
        P("dp", "shard", None, None),
        P("shard", None, None),
        P("shard", None, None),
        P("shard"),
        P("shard"),
    )
    return jax.shard_map(
        on_device, mesh=mesh, in_specs=placed, out_specs=P("shard", "dp", None), check_vma=False
    )
```

time: 247 us -> 71.6 us (0.29)
  the two profiles are of different devices: /device:TPU:0 before, /device:TPU:12 now
where the time goes in v2:
time: 71.6 us; the launch traced here: 71.4 us
  starting transfers between devices  30.8 us (43%)
  waiting for transfers between devices  27.5 us (38%)
  Pallas kernels  10.3 us (14%)
  between operations  1.39 us (2%)
  other arithmetic  1.36 us (2%)
    ppermute x21, waiting for transfers between devices, swapped(): lax.ppermute(value, 'dp', [(source, source ^ flip) for source in range(co...  22.6 us
    ppermute x21, starting transfers between devices, swapped(): lax.ppermute(value, 'dp', [(source, source ^ flip) for source in range(co...  18.3 us
    ppermute x5, starting transfers between devices, shifted(): return lax.ppermute(value, axis, pairs)  12.6 us
    ppermute x5, waiting for transfers between devices, shifted(): return lax.ppermute(value, axis, pairs)  4.98 us
    pallas_call x1, Pallas kernels, left_grad(): pl.pallas_call(left_grad_kernel, in_specs=[SMEM_SPEC] * 2 + [VMEM_SPEC] *...  3.11 us
    pallas_call x1, Pallas kernels, pack_rest(): pl.pallas_call(functools.partial(pack_rest_kernel, plan, tiles), grid_spe...  2.06 us
    pallas_call x2, Pallas kernels, near(): pl.pallas_call(functools.partial(near_kernel, flips), in_specs=[SMEM_SPEC...  1.95 us
    pallas_call x1, Pallas kernels, pack_first(): pl.pallas_call(functools.partial(pack_first_kernel, blocks, rows_of, widt...  1.55 us
  transfers between devices with their start and end apart: 26, of which 18 were waited for; matrix products, arithmetic and copies ran while one was open for 0% of the time, Pallas kernels for 10%

profile of v2, /device:TPU:12, one launch (start us, length us, event | category | flops | bytes accessed | tf_op | source)
XLA Modules:
  0.0 71.4 jit_solution(13351097936371790101)
XLA Ops:
  0.0 1.5 %pack_first.1 = bf16[192,256]{1,0:T(8,128)(2,1)} custom-call(s32[1]{0:T(128)} %bitcast.2.me_ref, bf16[1,1024,1024]{2,1,0:T(8,128)(2,1)} %refs_3_.1), custom_call_target="tpu_custom_call" | custom-call | tf_op jit(solution)/shard_map/pack_first/pallas_call | solution.py:81
  1.6 2.6 %collective-permute-start = (bf16[192,256]{1,0:T(8,128)(2,1)}, bf16[192,256]{1,0:T(8,128)(2,1)S(1)}, u32[]{:S(2)}, u32[]{:S(2)}) collective-permute-start(bf16[192,256]{1,0:T(8,128)(2,1)} %pack_first.1), channel_id=1, source_target_pairs={{0,4},{1,5},{2,6},{3,7},{4,0},{5,1},{6,2},{7,3},{8,12},{9,13},{10,... | collective-permute-start | bytes 294920 | tf_op jit(solution)/shard_map/ppermute | solution.py:22
  4.1 2.1 %pack_rest.1 = (bf16[192,256]{1,0:T(8,128)(2,1)}, bf16[256,256]{1,0:T(8,128)(2,1)}, bf16[192,256]{1,0:T(8,128)(2,1)}, bf16[208,256]{1,0:T(8,128)(2,1)}) custom-call(s32[1]{0:T(128)} %bitcast.2.me_ref, bf16[1,1024,1024]{2,1,0:T(8,128)(2,1)} %refs_3_.1, bf16[1,1024,1024]{2,1,0:T(8,128)(2,1)} %refs_3_.1, bf16[1,1024,1024]{2,1,0:T(8,128)(2,1)} %refs_3_.1, ...), custom_call_target="tpu_custom_call" | custom-call | tf_op jit(solution)/shard_map/pack_rest/pallas_call | solution.py:124
  6.7 3.9 %collective-permute-done.refs_0_ = bf16[192,256]{1,0:T(8,128)(2,1)S(1)} collective-permute-done((bf16[192,256]{1,0:T(8,128)(2,1)}, bf16[192,256]{1,0:T(8,128)(2,1)S(1)}, u32[]{:S(2)}, u32[]{:S(2)}) %collective-permute-start) | collective-permute-done | bytes 98336 | tf_op jit(solution)/shard_map/ppermute | solution.py:22
  10.7 2.9 %collective-permute-start.1 = (bf16[192,256]{1,0:T(8,128)(2,1)S(1)}, bf16[192,256]{1,0:T(8,128)(2,1)S(1)}, u32[]{:S(2)}, u32[]{:S(2)}) collective-permute-start(bf16[192,256]{1,0:T(8,128)(2,1)S(1)} %collective-permute-done.refs_0_), channel_id=1, source_target_pairs={{0,8},{8,0},{16,24},{24,16},{1,9},{9,1},{17,25},{25,17},{2,10},{10... | collective-permute-start | bytes 294920 | tf_op jit(solution)/shard_map/ppermute | solution.py:27
  13.6 3.8 %collective-permute-start.8 = (bf16[256,256]{1,0:T(8,128)(2,1)}, bf16[256,256]{1,0:T(8,128)(2,1)S(1)}, u32[]{:S(2)}, u32[]{:S(2)}) collective-permute-start(bf16[256,256]{1,0:T(8,128)(2,1)} %get-tuple-element.30), channel_id=1, source_target_pairs={{0,4},{1,5},{2,6},{3,7},{4,0},{5,1},{6,2},{7,3},{8,12},{9,13},{10,... | collective-permute-start | bytes 393224 | tf_op jit(solution)/shard_map/ppermute | solution.py:22
  17.4 0.8 %collective-permute-done.2.refs_2_ = bf16[192,256]{1,0:T(8,128)(2,1)S(1)} collective-permute-done((bf16[192,256]{1,0:T(8,128)(2,1)S(1)}, bf16[192,256]{1,0:T(8,128)(2,1)S(1)}, u32[]{:S(2)}, u32[]{:S(2)}) %collective-permute-start.2) | collective-permute-done | bytes 98336 | tf_op jit(solution)/shard_map/ppermute | solution.py:27
  18.2 0.8 %collective-permute-start.6 = (bf16[192,256]{1,0:T(8,128)(2,1)S(1)}, bf16[192,256]{1,0:T(8,128)(2,1)S(1)}, u32[]{:S(2)}, u32[]{:S(2)}) collective-permute-start(bf16[192,256]{1,0:T(8,128)(2,1)S(1)} %collective-permute-done.4.refs_4_), channel_id=1, source_target_pairs={{0,16},{8,24},{16,0},{24,8},{1,17},{9,25},{17,1},{25,9},{2,18},{10... | collective-permute-start | bytes 294920 | tf_op jit(solution)/shard_map/ppermute | solution.py:27
  20.5 2.3 %collective-permute-done.6.refs_6_ = bf16[192,256]{1,0:T(8,128)(2,1)S(1)} collective-permute-done((bf16[192,256]{1,0:T(8,128)(2,1)S(1)}, bf16[192,256]{1,0:T(8,128)(2,1)S(1)}, u32[]{:S(2)}, u32[]{:S(2)}) %collective-permute-start.6) | collective-permute-done | bytes 98336 | tf_op jit(solution)/shard_map/ppermute | solution.py:27
  22.8 0.8 %collective-permute-done.5.refs_5_ = bf16[192,256]{1,0:T(8,128)(2,1)S(1)} collective-permute-done((bf16[192,256]{1,0:T(8,128)(2,1)S(1)}, bf16[192,256]{1,0:T(8,128)(2,1)S(1)}, u32[]{:S(2)}, u32[]{:S(2)}) %collective-permute-start.5) | collective-permute-done | bytes 98336 | tf_op jit(solution)/shard_map/ppermute | solution.py:27
  24.1 1.5 %collective-permute-start.9 = (bf16[256,256]{1,0:T(8,128)(2,1)S(1)}, bf16[256,256]{1,0:T(8,128)(2,1)S(1)}, u32[]{:S(2)}, u32[]{:S(2)}) collective-permute-start(bf16[256,256]{1,0:T(8,128)(2,1)S(1)} %collective-permute-done.8.refs_8_), channel_id=1, source_target_pairs={{0,8},{8,0},{16,24},{24,16},{1,9},{9,1},{17,25},{25,17},{2,10},{10... | collective-permute-start | bytes 393224 | tf_op jit(solution)/shard_map/ppermute | solution.py:27
  25.6 1.3 %collective-permute-start.10 = (bf16[256,256]{1,0:T(8,128)(2,1)S(1)}, bf16[256,256]{1,0:T(8,128)(2,1)S(1)}, u32[]{:S(2)}, u32[]{:S(2)}) collective-permute-start(bf16[256,256]{1,0:T(8,128)(2,1)S(1)} %collective-permute-done.8.refs_8_), channel_id=1, source_target_pairs={{0,16},{8,24},{16,0},{24,8},{1,17},{9,25},{17,1},{25,9},{2,18},{10... | collective-permute-start | bytes 393224 | tf_op jit(solution)/shard_map/ppermute | solution.py:27
  26.9 3.3 %collective-permute-start.12 = (bf16[192,256]{1,0:T(8,128)(2,1)}, bf16[192,256]{1,0:T(8,128)(2,1)S(1)}, u32[]{:S(2)}, u32[]{:S(2)}) collective-permute-start(bf16[192,256]{1,0:T(8,128)(2,1)} %get-tuple-element.35), channel_id=1, source_target_pairs={{0,4},{1,5},{2,6},{3,7},{4,0},{5,1},{6,2},{7,3},{8,12},{9,13},{10,... | collective-permute-start | bytes 294920 | tf_op jit(solution)/shard_map/ppermute | solution.py:22
  31.2 2.4 %collective-permute-start.16 = (bf16[208,256]{1,0:T(8,128)(2,1)}, bf16[208,256]{1,0:T(8,128)(2,1)S(1)}, u32[]{:S(2)}, u32[]{:S(2)}) collective-permute-start(bf16[208,256]{1,0:T(8,128)(2,1)} %get-tuple-element.38), channel_id=1, source_target_pairs={{0,4},{1,5},{2,6},{3,7},{4,0},{5,1},{6,2},{7,3},{8,12},{9,13},{10,... | collective-permute-start | bytes 319496 | tf_op jit(solution)/shard_map/ppermute | solution.py:22
  33.8 1.7 %collective-permute-done.7.refs_7_ = bf16[192,256]{1,0:T(8,128)(2,1)S(1)} collective-permute-done((bf16[192,256]{1,0:T(8,128)(2,1)S(1)}, bf16[192,256]{1,0:T(8,128)(2,1)S(1)}, u32[]{:S(2)}, u32[]{:S(2)}) %collective-permute-start.7) | collective-permute-done | bytes 98336 | tf_op jit(solution)/shard_map/ppermute | solution.py:27
  37.0 4.0 %collective-permute-done.13.refs_1_ = bf16[192,256]{1,0:T(8,128)(2,1)S(1)} collective-permute-done((bf16[192,256]{1,0:T(8,128)(2,1)S(1)}, bf16[192,256]{1,0:T(8,128)(2,1)S(1)}, u32[]{:S(2)}, u32[]{:S(2)}) %collective-permute-start.13) | collective-permute-done | bytes 98336 | tf_op jit(solution)/shard_map/ppermute | solution.py:27
  41.7 1.1 %collective-permute-start.17 = (bf16[208,256]{1,0:T(8,128)(2,1)S(1)}, bf16[208,256]{1,0:T(8,128)(2,1)S(1)}, u32[]{:S(2)}, u32[]{:S(2)}) collective-permute-start(bf16[208,256]{1,0:T(8,128)(2,1)S(1)} %collective-permute-done.16.refs_4_), channel_id=1, source_target_pairs={{0,8},{8,0},{16,24},{24,16},{1,9},{9,1},{17,25},{25,17},{2,10},{10... | collective-permute-start | bytes 319496 | tf_op jit(solution)/shard_map/ppermute | solution.py:27
  44.1 1.1 %collective-permute-start.15 = (bf16[192,256]{1,0:T(8,128)(2,1)S(1)}, bf16[192,256]{1,0:T(8,128)(2,1)S(1)}, u32[]{:S(2)}, u32[]{:S(2)}) collective-permute-start(bf16[192,256]{1,0:T(8,128)(2,1)S(1)} %collective-permute-done.14.refs_2_), channel_id=1, source_target_pairs={{0,8},{8,0},{16,24},{24,16},{1,9},{9,1},{17,25},{25,17},{2,10},{10... | collective-permute-start | bytes 294920 | tf_op jit(solution)/shard_map/ppermute | solution.py:27
  45.2 1.3 %collective-permute-done.17.refs_5_ = bf16[208,256]{1,0:T(8,128)(2,1)S(1)} collective-permute-done((bf16[208,256]{1,0:T(8,128)(2,1)S(1)}, bf16[208,256]{1,0:T(8,128)(2,1)S(1)}, u32[]{:S(2)}, u32[]{:S(2)}) %collective-permute-start.17) | collective-permute-done | bytes 106528 | tf_op jit(solution)/shard_map/ppermute | solution.py:27
  47.2 3.1 %left_grad.1.product_ref = bf16[1024,1024]{1,0:T(8,128)(2,1)S(1)} custom-call(s32[1]{0:T(128)} %copy.6.rows_ref, s32[1]{0:T(128)} %copy.7.cols_ref, bf16[1024,1024]{1,0:T(8,128)(2,1)S(1)} %get-tuple-element.32.left, bf16[1,1,1024,1024]{3,2,1,0:T(8,128)(2,1)S(1)} %copy-done), custom_call_target="tpu_custom_call" | custom-call | flops 2147483648 | bytes 6291456 | tf_op jit(solution)/shard_map/left_grad/pallas_call | solution.py:205
  50.9 2.3 %collective-permute-done.19.refs_7_ = bf16[208,256]{1,0:T(8,128)(2,1)S(1)} collective-permute-done((bf16[208,256]{1,0:T(8,128)(2,1)S(1)}, bf16[208,256]{1,0:T(8,128)(2,1)S(1)}, u32[]{:S(2)}, u32[]{:S(2)}) %collective-permute-start.19) | collective-permute-done | bytes 106528 | tf_op jit(solution)/shard_map/ppermute | solution.py:27
  53.2 1.0 %far_rows.1 = (bf16[256,512]{1,0:T(8,128)(2,1)S(1)}, bf16[256,512]{1,0:T(8,128)(2,1)S(1)}, bf16[1024,1024]{1,0:T(8,128)(2,1)S(1)}) custom-call(s32[1]{0:T(128)} %bitcast.2.me_ref, bf16[1024,1024]{1,0:T(8,128)(2,1)S(1)} %left_grad.1.product_ref, bf16[1024,256]{1,0:T(8,128)(2,1)S(1)} %get-tuple-element.33.corner_ref, ...), custom_call_target="tpu_custom_call" | custom-call | flops 536870912 | bytes 8388608 | tf_op jit(solution)/shard_map/far_rows/pallas_call | solution.py:248
  54.3 1.1 %collective-permute-start.21 = (bf16[256,512]{1,0:T(8,128)(2,1)S(1)}, bf16[256,512]{1,0:T(8,128)(2,1)S(1)}, u32[]{:S(2)}, u32[]{:S(2)}) collective-permute-start(bf16[256,512]{1,0:T(8,128)(2,1)S(1)} %get-tuple-element.45), channel_id=1, source_target_pairs={{0,8},{8,0},{16,24},{24,16},{1,9},{9,1},{17,25},{25,17},{2,10},{10... | collective-permute-start | bytes 786440 | tf_op jit(solution)/shard_map/ppermute | solution.py:27
  55.4 1.2 %own_rows.1 = (bf16[256,512]{1,0:T(8,128)(2,1)S(1)}, bf16[256,512]{1,0:T(8,128)(2,1)S(1)}, bf16[256,1024]{1,0:T(8,128)(2,1)S(1)}) custom-call(s32[1]{0:T(128)} %bitcast.2.me_ref, bf16[1024,1024]{1,0:T(8,128)(2,1)S(1)} %left_grad.1.product_ref, bf16[1024,1024]{1,0:T(8,128)(2,1)S(1)} %get-tuple-element.41.right_ref), custom_call_target="tpu_custom_call" | custom-call | flops 1073741824 | bytes 4194304 | tf_op jit(solution)/shard_map/own_rows/pallas_call | solution.py:273
  57.4 1.1 %collective-permute-start.20 = (bf16[256,512]{1,0:T(8,128)(2,1)S(1)}, bf16[256,512]{1,0:T(8,128)(2,1)S(1)}, u32[]{:S(2)}, u32[]{:S(2)}) collective-permute-start(bf16[256,512]{1,0:T(8,128)(2,1)S(1)} %get-tuple-element.43), channel_id=1, source_target_pairs={{0,8},{8,0},{16,24},{24,16},{1,9},{9,1},{17,25},{25,17},{2,10},{10... | collective-permute-start | bytes 786440 | tf_op jit(solution)/shard_map/ppermute | solution.py:27
  58.4 2.0 %collective-permute-start.23 = (bf16[256,512]{1,0:T(8,128)(2,1)S(1)}, bf16[256,512]{1,0:T(8,128)(2,1)S(1)}, u32[]{:S(2)}, u32[]{:S(2)}) collective-permute-start(bf16[256,512]{1,0:T(8,128)(2,1)S(1)} %get-tuple-element.46), channel_id=1, source_target_pairs={{0,16},{8,24},{16,0},{24,8},{1,17},{9,25},{17,1},{25,9},{2,18},{10... | collective-permute-start | bytes 786440 | tf_op jit(solution)/shard_map/ppermute | solution.py:27
  60.4 2.2 %collective-permute-done.24 = bf16[256,512]{1,0:T(8,128)(2,1)S(1)} collective-permute-done((bf16[256,512]{1,0:T(8,128)(2,1)S(1)}, bf16[256,512]{1,0:T(8,128)(2,1)S(1)}, u32[]{:S(2)}, u32[]{:S(2)}) %collective-permute-start.24) | collective-permute-done | bytes 262176 | tf_op jit(solution)/shard_map/ppermute | solution.py:27
  62.6 1.1 %collective-permute-start.25 = (bf16[256,512]{1,0:T(8,128)(2,1)S(1)}, bf16[256,512]{1,0:T(8,128)(2,1)S(1)}, u32[]{:S(2)}, u32[]{:S(2)}) collective-permute-start(bf16[256,512]{1,0:T(8,128)(2,1)S(1)} %add_convert_fusion), channel_id=1, source_target_pairs={{0,8},{8,0},{16,24},{24,16},{1,9},{9,1},{17,25},{25,17},{2,10},{10... | collective-permute-start | bytes 786440 | tf_op jit(solution)/shard_map/ppermute | solution.py:27
  64.5 0.9 %collective-permute-done.23 = bf16[256,512]{1,0:T(8,128)(2,1)S(1)} collective-permute-done((bf16[256,512]{1,0:T(8,128)(2,1)S(1)}, bf16[256,512]{1,0:T(8,128)(2,1)S(1)}, u32[]{:S(2)}, u32[]{:S(2)}) %collective-permute-start.23) | collective-permute-done | bytes 262176 | tf_op jit(solution)/shard_map/ppermute | solution.py:27
  65.4 3.7 %collective-permute-done.25 = bf16[256,512]{1,0:T(8,128)(2,1)S(1)} collective-permute-done((bf16[256,512]{1,0:T(8,128)(2,1)S(1)}, bf16[256,512]{1,0:T(8,128)(2,1)S(1)}, u32[]{:S(2)}, u32[]{:S(2)}) %collective-permute-start.25) | collective-permute-done | bytes 262176 | tf_op jit(solution)/shard_map/ppermute | solution.py:27
  69.1 1.1 %collective-permute-done.22 = bf16[256,512]{1,0:T(8,128)(2,1)S(1)} collective-permute-done((bf16[256,512]{1,0:T(8,128)(2,1)S(1)}, bf16[256,512]{1,0:T(8,128)(2,1)S(1)}, u32[]{:S(2)}, u32[]{:S(2)}) %collective-permute-start.22) | collective-permute-done | bytes 262176 | tf_op jit(solution)/shard_map/ppermute | solution.py:27
  70.4 1.0 %fusion = bf16[1,256,1024]{2,1,0:T(8,128)(2,1)} fusion(bf16[1,256,512]{2,1,0:T(8,128)(2,1)S(1)} %get-tuple-element.50, bf16[1,256,512]{2,1,0:T(8,128)(2,1)S(1)} %get-tuple-element.49, pred[1024]{0:T(1024)(128)(4,1)S(1)} %iota_compare_fusion, pred[256]{0:T(512)(128)(4,1)S(1)} %add_compare_fusion), kind=kLoop, calls=%fused_computation.1 | loop fusion | flops 1572864 | bytes 1049856 | tf_op jit(solution)/shard_map/convert_element_type | solution.py:339
  (35 shorter events, 9.1 us)
Async XLA Ops:
  1.5 45.7 %copy-start = (bf16[1,1,1024,1024]{3,2,1,0:T(8,128)(2,1)S(1)}, bf16[1,1,1024,1024]{3,2,1,0:T(8,128)(2,1)}, u32[]{:S(2)}) copy-start(bf16[1,1,1024,1024]{3,2,1,0:T(8,128)(2,1)} %grad_ref.1) | copy-start | bytes 6291460
  1.6 9.1 %collective-permute-start = (bf16[192,256]{1,0:T(8,128)(2,1)}, bf16[192,256]{1,0:T(8,128)(2,1)S(1)}, u32[]{:S(2)}, u32[]{:S(2)}) collective-permute-start(bf16[192,256]{1,0:T(8,128)(2,1)} %pack_first.1), channel_id=1, source_target_pairs={{0,4},{1,5},{2,6},{3,7},{4,0},{5,1},{6,2},{7,3},{8,12},{9,13},{10,... | collective-permute-start | bytes 294920 | tf_op jit(solution)/shard_map/ppermute | solution.py:22
  6.2 11.2 %collective-permute-start.4 = (bf16[192,256]{1,0:T(8,128)(2,1)}, bf16[192,256]{1,0:T(8,128)(2,1)S(1)}, u32[]{:S(2)}, u32[]{:S(2)}) collective-permute-start(bf16[192,256]{1,0:T(8,128)(2,1)} %get-tuple-element.27), channel_id=1, source_target_pairs={{0,4},{1,5},{2,6},{3,7},{4,0},{5,1},{6,2},{7,3},{8,12},{9,13},{10,... | collective-permute-start | bytes 294920 | tf_op jit(solution)/shard_map/ppermute | solution.py:22
  10.7 6.7 %collective-permute-start.1 = (bf16[192,256]{1,0:T(8,128)(2,1)S(1)}, bf16[192,256]{1,0:T(8,128)(2,1)S(1)}, u32[]{:S(2)}, u32[]{:S(2)}) collective-permute-start(bf16[192,256]{1,0:T(8,128)(2,1)S(1)} %collective-permute-done.refs_0_), channel_id=1, source_target_pairs={{0,8},{8,0},{16,24},{24,16},{1,9},{9,1},{17,25},{25,17},{2,10},{10... | collective-permute-start | bytes 294920 | tf_op jit(solution)/shard_map/ppermute | solution.py:27
  13.6 4.6 %collective-permute-start.2 = (bf16[192,256]{1,0:T(8,128)(2,1)S(1)}, bf16[192,256]{1,0:T(8,128)(2,1)S(1)}, u32[]{:S(2)}, u32[]{:S(2)}) collective-permute-start(bf16[192,256]{1,0:T(8,128)(2,1)S(1)} %collective-permute-done.refs_0_), channel_id=1, source_target_pairs={{0,16},{8,24},{16,0},{24,8},{1,17},{9,25},{17,1},{25,9},{2,18},{10... | collective-permute-start | bytes 294920 | tf_op jit(solution)/shard_map/ppermute | solution.py:27
  13.6 6.9 %collective-permute-start.8 = (bf16[256,256]{1,0:T(8,128)(2,1)}, bf16[256,256]{1,0:T(8,128)(2,1)S(1)}, u32[]{:S(2)}, u32[]{:S(2)}) collective-permute-start(bf16[256,256]{1,0:T(8,128)(2,1)} %get-tuple-element.30), channel_id=1, source_target_pairs={{0,4},{1,5},{2,6},{3,7},{4,0},{5,1},{6,2},{7,3},{8,12},{9,13},{10,... | collective-permute-start | bytes 393224 | tf_op jit(solution)/shard_map/ppermute | solution.py:22
  18.2 4.6 %collective-permute-start.6 = (bf16[192,256]{1,0:T(8,128)(2,1)S(1)}, bf16[192,256]{1,0:T(8,128)(2,1)S(1)}, u32[]{:S(2)}, u32[]{:S(2)}) collective-permute-start(bf16[192,256]{1,0:T(8,128)(2,1)S(1)} %collective-permute-done.4.refs_4_), channel_id=1, source_target_pairs={{0,16},{8,24},{16,0},{24,8},{1,17},{9,25},{17,1},{25,9},{2,18},{10... | collective-permute-start | bytes 294920 | tf_op jit(solution)/shard_map/ppermute | solution.py:27
  19.0 4.6 %collective-permute-start.5 = (bf16[192,256]{1,0:T(8,128)(2,1)S(1)}, bf16[192,256]{1,0:T(8,128)(2,1)S(1)}, u32[]{:S(2)}, u32[]{:S(2)}) collective-permute-start(bf16[192,256]{1,0:T(8,128)(2,1)S(1)} %collective-permute-done.4.refs_4_), channel_id=1, source_target_pairs={{0,8},{8,0},{16,24},{24,16},{1,9},{9,1},{17,25},{25,17},{2,10},{10... | collective-permute-start | bytes 294920 | tf_op jit(solution)/shard_map/ppermute | solution.py:27
  19.5 4.6 %collective-permute-start.3 = (bf16[192,256]{1,0:T(8,128)(2,1)S(1)}, bf16[192,256]{1,0:T(8,128)(2,1)S(1)}, u32[]{:S(2)}, u32[]{:S(2)}) collective-permute-start(bf16[192,256]{1,0:T(8,128)(2,1)S(1)} %collective-permute-done.1.refs_1_), channel_id=1, source_target_pairs={{0,16},{8,24},{16,0},{24,8},{1,17},{9,25},{17,1},{25,9},{2,18},{10... | collective-permute-start | bytes 294920 | tf_op jit(solution)/shard_map/ppermute | solution.py:27
  24.1 6.6 %collective-permute-start.9 = (bf16[256,256]{1,0:T(8,128)(2,1)S(1)}, bf16[256,256]{1,0:T(8,128)(2,1)S(1)}, u32[]{:S(2)}, u32[]{:S(2)}) collective-permute-start(bf16[256,256]{1,0:T(8,128)(2,1)S(1)} %collective-permute-done.8.refs_8_), channel_id=1, source_target_pairs={{0,8},{8,0},{16,24},{24,16},{1,9},{9,1},{17,25},{25,17},{2,10},{10... | collective-permute-start | bytes 393224 | tf_op jit(solution)/shard_map/ppermute | solution.py:27
  25.6 9.8 %collective-permute-start.10 = (bf16[256,256]{1,0:T(8,128)(2,1)S(1)}, bf16[256,256]{1,0:T(8,128)(2,1)S(1)}, u32[]{:S(2)}, u32[]{:S(2)}) collective-permute-start(bf16[256,256]{1,0:T(8,128)(2,1)S(1)} %collective-permute-done.8.refs_8_), channel_id=1, source_target_pairs={{0,16},{8,24},{16,0},{24,8},{1,17},{9,25},{17,1},{25,9},{2,18},{10... | collective-permute-start | bytes 393224 | tf_op jit(solution)/shard_map/ppermute | solution.py:27
  26.9 6.9 %collective-permute-start.12 = (bf16[192,256]{1,0:T(8,128)(2,1)}, bf16[192,256]{1,0:T(8,128)(2,1)S(1)}, u32[]{:S(2)}, u32[]{:S(2)}) collective-permute-start(bf16[192,256]{1,0:T(8,128)(2,1)} %get-tuple-element.35), channel_id=1, source_target_pairs={{0,4},{1,5},{2,6},{3,7},{4,0},{5,1},{6,2},{7,3},{8,12},{9,13},{10,... | collective-permute-start | bytes 294920 | tf_op jit(solution)/shard_map/ppermute | solution.py:22
  30.2 5.3 %collective-permute-start.7 = (bf16[192,256]{1,0:T(8,128)(2,1)S(1)}, bf16[192,256]{1,0:T(8,128)(2,1)S(1)}, u32[]{:S(2)}, u32[]{:S(2)}) collective-permute-start(bf16[192,256]{1,0:T(8,128)(2,1)S(1)} %collective-permute-done.6.refs_6_), channel_id=1, source_target_pairs={{0,8},{8,0},{16,24},{24,16},{1,9},{9,1},{17,25},{25,17},{2,10},{10... | collective-permute-start | bytes 294920 | tf_op jit(solution)/shard_map/ppermute | solution.py:27
  30.7 10.4 %collective-permute-start.11 = (bf16[256,256]{1,0:T(8,128)(2,1)S(1)}, bf16[256,256]{1,0:T(8,128)(2,1)S(1)}, u32[]{:S(2)}, u32[]{:S(2)}) collective-permute-start(bf16[256,256]{1,0:T(8,128)(2,1)S(1)} %collective-permute-done.9.refs_9_), channel_id=1, source_target_pairs={{0,16},{8,24},{16,0},{24,8},{1,17},{9,25},{17,1},{25,9},{2,18},{10... | collective-permute-start | bytes 393224 | tf_op jit(solution)/shard_map/ppermute | solution.py:27
  31.2 5.8 %collective-permute-start.16 = (bf16[208,256]{1,0:T(8,128)(2,1)}, bf16[208,256]{1,0:T(8,128)(2,1)S(1)}, u32[]{:S(2)}, u32[]{:S(2)}) collective-permute-start(bf16[208,256]{1,0:T(8,128)(2,1)} %get-tuple-element.38), channel_id=1, source_target_pairs={{0,4},{1,5},{2,6},{3,7},{4,0},{5,1},{6,2},{7,3},{8,12},{9,13},{10,... | collective-permute-start | bytes 319496 | tf_op jit(solution)/shard_map/ppermute | solution.py:22
  35.5 5.6 %collective-permute-start.13 = (bf16[192,256]{1,0:T(8,128)(2,1)S(1)}, bf16[192,256]{1,0:T(8,128)(2,1)S(1)}, u32[]{:S(2)}, u32[]{:S(2)}) collective-permute-start(bf16[192,256]{1,0:T(8,128)(2,1)S(1)} %collective-permute-done.12.refs_0_), channel_id=1, source_target_pairs={{0,8},{8,0},{16,24},{24,16},{1,9},{9,1},{17,25},{25,17},{2,10},{10... | collective-permute-start | bytes 294920 | tf_op jit(solution)/shard_map/ppermute | solution.py:27
  36.2 4.9 %collective-permute-start.14 = (bf16[192,256]{1,0:T(8,128)(2,1)S(1)}, bf16[192,256]{1,0:T(8,128)(2,1)S(1)}, u32[]{:S(2)}, u32[]{:S(2)}) collective-permute-start(bf16[192,256]{1,0:T(8,128)(2,1)S(1)} %collective-permute-done.12.refs_0_), channel_id=1, source_target_pairs={{0,16},{8,24},{16,0},{24,8},{1,17},{9,25},{17,1},{25,9},{2,18},{10... | collective-permute-start | bytes 294920 | tf_op jit(solution)/shard_map/ppermute | solution.py:27
  41.7 4.8 %collective-permute-start.17 = (bf16[208,256]{1,0:T(8,128)(2,1)S(1)}, bf16[208,256]{1,0:T(8,128)(2,1)S(1)}, u32[]{:S(2)}, u32[]{:S(2)}) collective-permute-start(bf16[208,256]{1,0:T(8,128)(2,1)S(1)} %collective-permute-done.16.refs_4_), channel_id=1, source_target_pairs={{0,8},{8,0},{16,24},{24,16},{1,9},{9,1},{17,25},{25,17},{2,10},{10... | collective-permute-start | bytes 319496 | tf_op jit(solution)/shard_map/ppermute | solution.py:27
  44.1 6.2 %collective-permute-start.15 = (bf16[192,256]{1,0:T(8,128)(2,1)S(1)}, bf16[192,256]{1,0:T(8,128)(2,1)S(1)}, u32[]{:S(2)}, u32[]{:S(2)}) collective-permute-start(bf16[192,256]{1,0:T(8,128)(2,1)S(1)} %collective-permute-done.14.refs_2_), channel_id=1, source_target_pairs={{0,8},{8,0},{16,24},{24,16},{1,9},{9,1},{17,25},{25,17},{2,10},{10... | collective-permute-start | bytes 294920 | tf_op jit(solution)/shard_map/ppermute | solution.py:27
  45.2 5.8 %collective-permute-start.18 = (bf16[208,256]{1,0:T(8,128)(2,1)S(1)}, bf16[208,256]{1,0:T(8,128)(2,1)S(1)}, u32[]{:S(2)}, u32[]{:S(2)}) collective-permute-start(bf16[208,256]{1,0:T(8,128)(2,1)S(1)} %collective-permute-done.16.refs_4_), channel_id=1, source_target_pairs={{0,16},{8,24},{16,0},{24,8},{1,17},{9,25},{17,1},{25,9},{2,18},{10... | collective-permute-start | bytes 319496 | tf_op jit(solution)/shard_map/ppermute | solution.py:27
  46.5 6.7 %collective-permute-start.19 = (bf16[208,256]{1,0:T(8,128)(2,1)S(1)}, bf16[208,256]{1,0:T(8,128)(2,1)S(1)}, u32[]{:S(2)}, u32[]{:S(2)}) collective-permute-start(bf16[208,256]{1,0:T(8,128)(2,1)S(1)} %collective-permute-done.17.refs_5_), channel_id=1, source_target_pairs={{0,16},{8,24},{16,0},{24,8},{1,17},{9,25},{17,1},{25,9},{2,18},{10... | collective-permute-start | bytes 319496 | tf_op jit(solution)/shard_map/ppermute | solution.py:27
  54.2 8.3 %collective-permute-start.24 = (bf16[256,512]{1,0:T(8,128)(2,1)S(1)}, bf16[256,512]{1,0:T(8,128)(2,1)S(1)}, u32[]{:S(2)}, u32[]{:S(2)}) collective-permute-start(bf16[256,512]{1,0:T(8,128)(2,1)S(1)} %get-tuple-element.48), channel_id=1, source_target_pairs={{0,16},{8,24},{16,0},{24,8},{1,17},{9,25},{17,1},{25,9},{2,18},{10... | collective-permute-start | bytes 786440 | tf_op jit(solution)/shard_map/ppermute | solution.py:27
  54.3 9.4 %collective-permute-start.21 = (bf16[256,512]{1,0:T(8,128)(2,1)S(1)}, bf16[256,512]{1,0:T(8,128)(2,1)S(1)}, u32[]{:S(2)}, u32[]{:S(2)}) collective-permute-start(bf16[256,512]{1,0:T(8,128)(2,1)S(1)} %get-tuple-element.45), channel_id=1, source_target_pairs={{0,8},{8,0},{16,24},{24,16},{1,9},{9,1},{17,25},{25,17},{2,10},{10... | collective-permute-start | bytes 786440 | tf_op jit(solution)/shard_map/ppermute | solution.py:27
  57.4 7.1 %collective-permute-start.20 = (bf16[256,512]{1,0:T(8,128)(2,1)S(1)}, bf16[256,512]{1,0:T(8,128)(2,1)S(1)}, u32[]{:S(2)}, u32[]{:S(2)}) collective-permute-start(bf16[256,512]{1,0:T(8,128)(2,1)S(1)} %get-tuple-element.43), channel_id=1, source_target_pairs={{0,8},{8,0},{16,24},{24,16},{1,9},{9,1},{17,25},{25,17},{2,10},{10... | collective-permute-start | bytes 786440 | tf_op jit(solution)/shard_map/ppermute | solution.py:27
  58.4 6.9 %collective-permute-start.23 = (bf16[256,512]{1,0:T(8,128)(2,1)S(1)}, bf16[256,512]{1,0:T(8,128)(2,1)S(1)}, u32[]{:S(2)}, u32[]{:S(2)}) collective-permute-start(bf16[256,512]{1,0:T(8,128)(2,1)S(1)} %get-tuple-element.46), channel_id=1, source_target_pairs={{0,16},{8,24},{16,0},{24,8},{1,17},{9,25},{17,1},{25,9},{2,18},{10... | collective-permute-start | bytes 786440 | tf_op jit(solution)/shard_map/ppermute | solution.py:27
  62.6 6.4 %collective-permute-start.25 = (bf16[256,512]{1,0:T(8,128)(2,1)S(1)}, bf16[256,512]{1,0:T(8,128)(2,1)S(1)}, u32[]{:S(2)}, u32[]{:S(2)}) collective-permute-start(bf16[256,512]{1,0:T(8,128)(2,1)S(1)} %add_convert_fusion), channel_id=1, source_target_pairs={{0,8},{8,0},{16,24},{24,16},{1,9},{9,1},{17,25},{25,17},{2,10},{10... | collective-permute-start | bytes 786440 | tf_op jit(solution)/shard_map/ppermute | solution.py:27
  63.8 6.4 %collective-permute-start.22 = (bf16[256,512]{1,0:T(8,128)(2,1)S(1)}, bf16[256,512]{1,0:T(8,128)(2,1)S(1)}, u32[]{:S(2)}, u32[]{:S(2)}) collective-permute-start(bf16[256,512]{1,0:T(8,128)(2,1)S(1)} %add_convert_fusion.1), channel_id=1, source_target_pairs={{0,16},{8,24},{16,0},{24,8},{1,17},{9,25},{17,1},{25,9},{2,18},{10... | collective-permute-start | bytes 786440 | tf_op jit(solution)/shard_map/ppermute | solution.py:27

commit v3 on v0

v3 whole, which is shorter than its diff:
```python
import functools

import jax
import jax.numpy as jnp
from jax import lax
from jax.experimental import pallas as pl
from jax.experimental.pallas import tpu as pltpu
from jax.sharding import PartitionSpec as P

TILE = 256
EXTRA = 16
VMEM = 24 * 1024 * 1024
PACK_VMEM = 60 * 1024 * 1024
SMEM_SPEC = pl.BlockSpec(memory_space=pltpu.SMEM)
VMEM_SPEC = pl.BlockSpec(memory_space=pltpu.VMEM)
BF16 = jnp.bfloat16
F32 = jnp.float32


def shifted(value, axis, steps):
    count = lax.axis_size(axis)
    pairs = [(source, (source + steps) % count) for source in range(count)]
    return lax.ppermute(value, axis, pairs)


def swapped(value, flip):
    count = lax.axis_size("dp")
    return lax.ppermute(value, "dp", [(source, source ^ flip) for source in range(count)])


def block(index):
    return pl.ds(index * TILE, TILE)


def cost(flops, bytes_accessed):
    return pl.CostEstimate(flops=flops, bytes_accessed=bytes_accessed, transcendentals=0)


def below(tiles):
    return [(i, j) for j in range(tiles) for i in range(j + 1, tiles)]


def pick_kernel(me_ref, *refs):
    count = len(refs) // 2
    for source, target in zip(refs[:count], refs[count:]):
        target[...] = source[0, 0]


def pick(me, grads, groups, wanted, name):
    width = grads.shape[-1]
    strip, half = width // groups, width // 2

    def index_map(flip, h):
        return lambda step, me: (0, 0, jnp.bitwise_xor(me[0], flip), h)

    return pl.pallas_call(
        pick_kernel,
        grid_spec=pltpu.PrefetchScalarGridSpec(
            num_scalar_prefetch=1,
            grid=(1,),
            in_specs=[pl.BlockSpec((1, 1, strip, half), index_map(flip, h)) for flip, h in wanted],
            out_specs=[pl.BlockSpec((strip, half), lambda step, me: (0, 0))] * len(wanted),
        ),
        out_shape=[jax.ShapeDtypeStruct((strip, half), BF16)] * len(wanted),
        compiler_params=pltpu.CompilerParams(vmem_limit_bytes=PACK_VMEM),
        name=name,
    )(me, *[grads] * len(wanted))


def fold_kernel(tiles, me_ref, *refs):
    rights, out = refs[:tiles], refs[-1]
    strip = rights[0].shape[1]
    places = [(pl.ds(k // tiles * strip, strip), block(k % tiles)) for k in range(tiles * tiles // 2)]
    blocks = below(tiles)
    for (i, j), at in zip(blocks, places):
        out[at] = rights[i][0, :, block(j)]
    row = lax.broadcasted_iota(jnp.int32, (strip, TILE), 0) + me_ref[0] * strip
    column = lax.broadcasted_iota(jnp.int32, (strip, TILE), 1)
    for pair, at in enumerate(places[len(blocks) :]):
        even, odd = 2 * pair, 2 * pair + 1
        out[at] = jnp.where(row >= column, rights[even][0, :, block(even)], rights[odd][0, :, block(odd)])


def fold(me, right, groups):
    width = right.shape[-1]
    strip = TILE // groups
    tiles = width // TILE

    def index_map(i):
        return lambda step, me: (0, i * groups + me[0], 0)

    return pl.pallas_call(
        functools.partial(fold_kernel, tiles),
        grid_spec=pltpu.PrefetchScalarGridSpec(
            num_scalar_prefetch=1,
            grid=(1,),
            in_specs=[pl.BlockSpec((1, strip, width), index_map(i)) for i in range(tiles)],
            out_specs=pl.BlockSpec((tiles // 2 * strip, width), lambda step, me: (0, 0)),
        ),
        out_shape=jax.ShapeDtypeStruct((tiles // 2 * strip, width), BF16),
        compiler_params=pltpu.CompilerParams(vmem_limit_bytes=PACK_VMEM),
        name="fold_right",
    )(me, *[right] * tiles)


def left_strip_kernel(tiles, me_ref, left_ref, *refs):
    corners, out = refs[:tiles], refs[-1]
    strip = left_ref.shape[1]
    out[pl.ds(0, strip), :] = left_ref[0]
    on_diag = lax.broadcasted_iota(jnp.int32, (TILE, TILE), 0) == lax.broadcasted_iota(jnp.int32, (TILE, TILE), 1)
    lines = [
        jnp.sum(jnp.where(on_diag, corner[0].astype(F32), 0.0), axis=0, keepdims=True) for corner in corners
    ]
    line = jnp.concatenate(lines, axis=1)
    out[pl.ds(strip, EXTRA), :] = jnp.broadcast_to(line, (EXTRA, line.shape[1])).astype(BF16)


def left_strip(me, left, right, groups):
    width = left.shape[-1]
    strip = width // groups
    tiles = width // TILE

    def corner_map(i):
        return lambda step, me: (0, i, i)

    return pl.pallas_call(
        functools.partial(left_strip_kernel, tiles),
        grid_spec=pltpu.PrefetchScalarGridSpec(
            num_scalar_prefetch=1,
            grid=(1,),
            in_specs=[pl.BlockSpec((1, strip, width), lambda step, me: (0, me[0], 0))]
            + [pl.BlockSpec((1, TILE, TILE), corner_map(i)) for i in range(tiles)],
            out_specs=pl.BlockSpec((strip + EXTRA, width), lambda step, me: (0, 0)),
        ),
        out_shape=jax.ShapeDtypeStruct((strip + EXTRA, width), BF16),
        compiler_params=pltpu.CompilerParams(vmem_limit_bytes=PACK_VMEM),
        name="left_strip",
    )(me, left, *[right] * tiles)


def payload_kernel(h, groups, me_ref, rows_ref, cols_ref, folded_ref, own_ref, *refs):
    terms, out = refs[:-1], refs[-1]
    strip, half = own_ref.shape
    total = own_ref[...].astype(F32)
    for term in terms:
        total = total + term[...].astype(F32)
    column = lax.broadcasted_iota(jnp.int32, (strip, half), 1) + h * half
    row = lax.broadcasted_iota(jnp.int32, (strip, half), 0) + me_ref[0] * strip
    keep = (row < rows_ref[0]) & (column < cols_ref[0])
    out[pl.ds(0, strip), :] = jnp.where(keep, total, 0.0).astype(BF16)
    out[pl.ds(strip, out.shape[0] - strip), :] = folded_ref[:, pl.ds(h * half, half)]


def payload(me, rows_valid, cols_valid, folded, own, terms, h, groups):
    strip, half = own.shape
    return pl.pallas_call(
        functools.partial(payload_kernel, h, groups),
        in_specs=[SMEM_SPEC] * 3 + [VMEM_SPEC] * (2 + len(terms)),
        out_specs=VMEM_SPEC,
        out_shape=jax.ShapeDtypeStruct((strip + folded.shape[0], half), BF16),
        compiler_params=pltpu.CompilerParams(vmem_limit_bytes=VMEM),
        cost_estimate=cost(8 * strip * half, 8 * strip * half),
        name="payload",
    )(me, rows_valid, cols_valid, folded, own, *terms)


def update_kernel(groups, me_ref, rows_ref, cols_ref, left_ref, *refs):
    pieces, (out, masked, right, folded) = refs[: 2 * groups], refs[2 * groups :]
    me = me_ref[0]
    width = masked.shape[0]
    tiles = width // TILE
    strip, part, half = width // groups, TILE // groups, width // 2
    blocks = below(tiles)
    for flip in range(groups):
        other = jnp.bitwise_xor(me, flip)
        rows = pl.ds(pl.multiple_of(other * strip, strip), strip)
        for h in range(2):
            piece = pieces[2 * flip + h]
            masked[rows, pl.ds(h * half, half)] = piece[pl.ds(0, strip), :]
            for k in range(tiles * tiles // 2):
                side = k % tiles * TILE - h * half
                if side < 0 or side >= half:
                    continue
                value = piece[pl.ds(strip + k // tiles * part, part), pl.ds(side, TILE)]
                if k < len(blocks):
                    i, j = blocks[k]
                    right[pl.ds(pl.multiple_of(i * TILE + other * part, part), part), block(j)] = value
                else:
                    at = (k - len(blocks)) * TILE + other * part
                    folded[pl.ds(pl.multiple_of(at, part), part), :] = value
    row = lax.broadcasted_iota(jnp.int32, (TILE, TILE), 0)
    column = lax.broadcasted_iota(jnp.int32, (TILE, TILE), 1)
    for i in range(tiles):
        value = folded[block(i // 2), :].astype(F32)
        keep = row >= column if i % 2 == 0 else row < column
        value = jnp.where(keep, value, value.T)
        if i % 2:
            line = left_ref[pl.ds(strip, EXTRA), block(i)].astype(F32)[:1]
            value = jnp.where(row == column, jnp.broadcast_to(line, (TILE, TILE)), value)
        right[block(i), block(i)] = value.astype(BF16)
        for j in range(i):
            right[block(j), block(i)] = right[block(i), block(j)].T
    mixed = jnp.dot(left_ref[pl.ds(0, strip), :], masked[...], preferred_element_type=F32).astype(BF16)
    value = jnp.dot(mixed, right[...], preferred_element_type=F32)
    column = lax.broadcasted_iota(jnp.int32, (strip, width), 1)
    row = lax.broadcasted_iota(jnp.int32, (strip, width), 0) + me * strip
    out[0] = jnp.where((row < rows_ref[0]) & (column < cols_ref[0]), value, 0.0).astype(BF16)


def update(me, rows_valid, cols_valid, left, pieces, groups):
    width = left.shape[-1]
    strip = width // groups
    return pl.pallas_call(
        functools.partial(update_kernel, groups),
        in_specs=[SMEM_SPEC] * 3 + [VMEM_SPEC] * (1 + 2 * groups),
        out_specs=VMEM_SPEC,
        out_shape=jax.ShapeDtypeStruct((1, strip, width), BF16),
        scratch_shapes=[
            pltpu.VMEM((width, width), BF16),
            pltpu.VMEM((width, width), BF16),
            pltpu.VMEM((width // 2, TILE), BF16),
        ],
        compiler_params=pltpu.CompilerParams(vmem_limit_bytes=VMEM),
        cost_estimate=cost(4 * strip * width**2, 8 * width**2),
        name="update",
    )(me, rows_valid, cols_valid, left, *[half for piece in pieces for half in piece])


def added(*terms):
    return functools.reduce(lambda a, b: a + b, [term.astype(F32) for term in terms])


def on_device(grads, left_roots, right_roots, rows_valid, cols_valid):
    groups = lax.axis_size("dp")
    me = lax.axis_index("dp").astype(jnp.int32).reshape(1)
    offset = lax.axis_size("shard") // 2

    if groups == 4:
        far_0, far_1, near_0, near_1 = pick(me, grads, groups, [(3, 0), (3, 1), (1, 0), (2, 1)], "pick_sent")
        far_0, far_1 = swapped(far_0, 1), swapped(far_1, 2)
        folded = shifted(fold(me, right_roots, groups), "shard", offset)
        near_0, near_1 = swapped(near_0, 1), swapped(near_1, 2)
        left = shifted(left_strip(me, left_roots, right_roots, groups), "shard", offset)
        via_0, via_1, own_0, own_1 = pick(me, grads, groups, [(2, 0), (1, 1), (0, 0), (0, 1)], "pick_kept")
        via_0 = swapped(added(via_0, far_0).astype(BF16), 2)
        via_1 = swapped(added(via_1, far_1).astype(BF16), 1)
        mine_0 = payload(me, rows_valid, cols_valid, folded, own_0, [near_0, via_0], 0, groups)
        mine_1 = payload(me, rows_valid, cols_valid, folded, own_1, [near_1, via_1], 1, groups)
        up_0, side_1 = swapped(mine_0, 2), swapped(mine_1, 1)
        side_0, up_1 = swapped(mine_0, 1), swapped(mine_1, 2)
        pieces = [(mine_0, mine_1), (side_0, side_1), (up_0, up_1), (swapped(up_0, 1), swapped(side_1, 2))]
    else:
        folded = shifted(fold(me, right_roots, groups), "shard", offset)
        left = shifted(left_strip(me, left_roots, right_roots, groups), "shard", offset)
        mine = []
        for h in range(2):
            terms = pick(me, grads, groups, [(flip, h) for flip in range(groups)], "pick_all")
            got = [swapped(terms[flip], flip) for flip in range(1, groups)]
            mine.append(payload(me, rows_valid, cols_valid, folded, terms[0], got, h, groups))
        pieces = [mine] + [[swapped(part, flip) for part in mine] for flip in range(1, groups)]
    return update(me, rows_valid, cols_valid, left, pieces, groups)


def solution(mesh):
    placed = (
        P("dp", "shard", None, None),
        P("shard", None, None),
        P("shard", None, None),
        P("shard"),
        P("shard"),
    )
    return jax.shard_map(
        on_device, mesh=mesh, in_specs=placed, out_specs=P("shard", "dp", None), check_vma=False
    )
```

time: 247 us -> 58.4 us (0.24)
  waiting for transfers between devices: 216 us -> 23.6 us
  starting transfers between devices: 4.11 us -> 19.1 us
  between operations: 14.7 us -> 1.35 us
  Pallas kernels: 0 us -> 11 us
  local copies, waits for them, and re-layouts: 6.44 us -> 0.96 us
  matrix products: 4.65 us -> 0 us
    ppermute x2, waiting for transfers between devices: 179 us -> 17.7 us  [shifted(): return lax.ppermute(value, axis, pairs)]
    reduce_scatter x2 -> x0, waiting for transfers between devices: 36.5 us -> none  [the longest x1 36.5 us: precondition(): lax.psum_scatter(jnp.einsum('bsi,bsj->ibj', own_rows, half, preferred_ele...]
    ppermute x0 -> x12, starting transfers between devices: none -> 14 us  [swapped(): lax.ppermute(value, 'dp', [(source, source ^ flip) for source in range(co...]
    pallas_call x0 -> x7, Pallas kernels: none -> 11 us  [the longest x2 4.38 us: pick(): pl.pallas_call(pick_kernel, grid_spec=pltpu.PrefetchScalarGridSpec(num_sc...]
    ppermute x0 -> x12, waiting for transfers between devices: none -> 5.83 us  [swapped(): lax.ppermute(value, 'dp', [(source, source ^ flip) for source in range(co...]
    dot_general x1 -> x0, matrix products: 4.65 us -> none  [precondition(): jnp.einsum('bsi,bsj->ibj', own_rows, half, preferred_element_type=jnp.flo...]
    unnamed x3 -> x8, local copies, waits for them, and re-layouts: 5.44 us -> 0.96 us
  transfers between devices with their start and end apart: 4 -> 14, of which waited for: 3 -> 5; matrix products, arithmetic and copies ran while one was open for 0% -> 4% of each run, Pallas kernels for 0% -> 11%
where the time goes in v3:
time: 58.4 us; the launch traced here: 58.1 us
  waiting for transfers between devices  23.6 us (40%)
  starting transfers between devices  19.1 us (33%)
  Pallas kernels  11 us (19%)
  other arithmetic  2.07 us (4%)
  between operations  1.35 us (2%)
  local copies, waits for them, and re-layouts  0.96 us (2%)
    ppermute x2, waiting for transfers between devices, shifted(): return lax.ppermute(value, axis, pairs)  17.7 us
    ppermute x12, starting transfers between devices, swapped(): lax.ppermute(value, 'dp', [(source, source ^ flip) for source in range(co...  14 us
    ppermute x12, waiting for transfers between devices, swapped(): lax.ppermute(value, 'dp', [(source, source ^ flip) for source in range(co...  5.83 us
    ppermute x2, starting transfers between devices, shifted(): return lax.ppermute(value, axis, pairs)  5.18 us
    pallas_call x2, Pallas kernels, pick(): pl.pallas_call(pick_kernel, grid_spec=pltpu.PrefetchScalarGridSpec(num_sc...  4.38 us
    pallas_call x1, Pallas kernels, update(): pl.pallas_call(functools.partial(update_kernel, groups), in_specs=[SMEM_S...  2.31 us
    pallas_call x1, Pallas kernels, left_strip(): pl.pallas_call(functools.partial(left_strip_kernel, tiles), grid_spec=plt...  2.17 us
    pallas_call x1, Pallas kernels, fold(): pl.pallas_call(functools.partial(fold_kernel, tiles), grid_spec=pltpu.Pre...  1.82 us
  transfers between devices with their start and end apart: 14, of which 5 were waited for; matrix products, arithmetic and copies ran while one was open for 4% of the time, Pallas kernels for 11%

profile of v3, /device:TPU:0, one launch (start us, length us, event | category | flops | bytes accessed | tf_op | source)
XLA Modules:
  0.0 58.1 jit_solution(836944937762105146)
XLA Ops:
  0.0 2.2 %pick_sent.1 = (bf16[256,512]{1,0:T(8,128)(2,1)}, bf16[256,512]{1,0:T(8,128)(2,1)}, bf16[256,512]{1,0:T(8,128)(2,1)}, bf16[256,512]{1,0:T(8,128)(2,1)}) custom-call(s32[1]{0:T(128)} %bitcast.me_ref, bf16[1,1,1024,1024]{3,2,1,0:T(8,128)(2,1)} %refs_3_.7, bf16[1,1,1024,1024]{3,2,1,0:T(8,128)(2,1)} %refs_3_.7, bf16[1,1,1024,1024]{3,2,1,0:T(8,128)(2,1)} %refs_3_.7, ...), custom_call_target="tpu_custom_call" | custom-call | tf_op jit(solution)/shard_map/pick_sent/pallas_call | solution.py:56
  2.2 3.0 %collective-permute-start.6 = (bf16[256,512]{1,0:T(8,128)(2,1)}, bf16[256,512]{1,0:T(8,128)(2,1)S(1)}, u32[]{:S(2)}, u32[]{:S(2)}) collective-permute-start(bf16[256,512]{1,0:T(8,128)(2,1)} %get-tuple-element.20), channel_id=1, source_target_pairs={{0,16},{8,24},{16,0},{24,8},{1,17},{9,25},{17,1},{25,9},{2,18},{10... | collective-permute-start | bytes 786440 | tf_op jit(solution)/shard_map/ppermute | solution.py:28
  5.1 1.5 %collective-permute-start.3 = (bf16[256,512]{1,0:T(8,128)(2,1)}, bf16[256,512]{1,0:T(8,128)(2,1)S(1)}, u32[]{:S(2)}, u32[]{:S(2)}) collective-permute-start(bf16[256,512]{1,0:T(8,128)(2,1)} %get-tuple-element.16), channel_id=1, source_target_pairs={{0,8},{8,0},{16,24},{24,16},{1,9},{9,1},{17,25},{25,17},{2,10},{10... | collective-permute-start | bytes 786440 | tf_op jit(solution)/shard_map/ppermute | solution.py:28
  6.6 1.8 %fold_right.1 = bf16[128,1024]{1,0:T(8,128)(2,1)} custom-call(s32[1]{0:T(128)} %bitcast.me_ref, bf16[1,1024,1024]{2,1,0:T(8,128)(2,1)} %refs_3_.5, bf16[1,1024,1024]{2,1,0:T(8,128)(2,1)} %refs_3_.5, bf16[1,1024,1024]{2,1,0:T(8,128)(2,1)} %refs_3_.5, bf16[1,1024,1024]{2,1,0:T(8,128)(2,1)} %refs_3_.5), custom_call_target="tpu_custom_call" | custom-call | tf_op jit(solution)/shard_map/fold_right/pallas_call | solution.py:92
  8.5 2.6 %collective-permute-start.1 = (bf16[128,1024]{1,0:T(8,128)(2,1)}, bf16[128,1024]{1,0:T(8,128)(2,1)S(1)}, u32[]{:S(2)}, u32[]{:S(2)}) collective-permute-start(bf16[128,1024]{1,0:T(8,128)(2,1)} %fold_right.1), channel_id=1, source_target_pairs={{0,4},{1,5},{2,6},{3,7},{4,0},{5,1},{6,2},{7,3},{8,12},{9,13},{10,... | collective-permute-start | bytes 786440 | tf_op jit(solution)/shard_map/ppermute | solution.py:23
  11.0 0.5 collective-permute-start.2
  11.6 0.5 collective-permute-start.5
  12.1 2.2 %pick_kept.1 = (bf16[256,512]{1,0:T(8,128)(2,1)}, bf16[256,512]{1,0:T(8,128)(2,1)}, bf16[256,512]{1,0:T(8,128)(2,1)}, bf16[256,512]{1,0:T(8,128)(2,1)}) custom-call(s32[1]{0:T(128)} %bitcast.me_ref, bf16[1,1,1024,1024]{3,2,1,0:T(8,128)(2,1)} %refs_3_.7, bf16[1,1,1024,1024]{3,2,1,0:T(8,128)(2,1)} %refs_3_.7, bf16[1,1,1024,1024]{3,2,1,0:T(8,128)(2,1)} %refs_3_.7, ...), custom_call_target="tpu_custom_call" | custom-call | tf_op jit(solution)/shard_map/pick_kept/pallas_call | solution.py:56
  14.3 0.0 collective-permute-done.6
  14.3 1.1 %add_convert_fusion = bf16[256,512]{1,0:T(8,128)(2,1)S(1)} fusion(bf16[256,512]{1,0:T(8,128)(2,1)S(1)} %collective-permute-done.6, bf16[256,512]{1,0:T(8,128)(2,1)} %get-tuple-element.19), kind=kLoop, calls=%fused_computation | loop fusion | flops 524288 | bytes 786432 | tf_op jit(solution)/shard_map/convert_element_type | solution.py:246
  15.4 1.6 %collective-permute-start.7 = (bf16[256,512]{1,0:T(8,128)(2,1)S(1)}, bf16[256,512]{1,0:T(8,128)(2,1)S(1)}, u32[]{:S(2)}, u32[]{:S(2)}) collective-permute-start(bf16[256,512]{1,0:T(8,128)(2,1)S(1)} %add_convert_fusion), channel_id=1, source_target_pairs={{0,8},{8,0},{16,24},{24,16},{1,9},{9,1},{17,25},{25,17},{2,10},{10... | collective-permute-start | bytes 786440 | tf_op jit(solution)/shard_map/ppermute | solution.py:28
  16.9 0.0 collective-permute-done.3
  16.9 1.0 %add_convert_fusion.1 = bf16[256,512]{1,0:T(8,128)(2,1)S(1)} fusion(bf16[256,512]{1,0:T(8,128)(2,1)S(1)} %collective-permute-done.3, bf16[256,512]{1,0:T(8,128)(2,1)} %get-tuple-element.15), kind=kLoop, calls=%fused_computation.1 | loop fusion | flops 524288 | bytes 786432 | tf_op jit(solution)/shard_map/convert_element_type | solution.py:245
  17.9 1.6 %collective-permute-start.4 = (bf16[256,512]{1,0:T(8,128)(2,1)S(1)}, bf16[256,512]{1,0:T(8,128)(2,1)S(1)}, u32[]{:S(2)}, u32[]{:S(2)}) collective-permute-start(bf16[256,512]{1,0:T(8,128)(2,1)S(1)} %add_convert_fusion.1), channel_id=1, source_target_pairs={{0,16},{8,24},{16,0},{24,8},{1,17},{9,25},{17,1},{25,9},{2,18},{10... | collective-permute-start | bytes 786440 | tf_op jit(solution)/shard_map/ppermute | solution.py:28
  20.8 1.8 %collective-permute-done.1.folded_ref = bf16[128,1024]{1,0:T(8,128)(2,1)S(1)} collective-permute-done((bf16[128,1024]{1,0:T(8,128)(2,1)}, bf16[128,1024]{1,0:T(8,128)(2,1)S(1)}, u32[]{:S(2)}, u32[]{:S(2)}) %collective-permute-start.1) | collective-permute-done | bytes 262176 | tf_op jit(solution)/shard_map/ppermute | solution.py:23
  22.7 0.0 collective-permute-done.5.refs_0_
  22.7 1.7 %collective-permute-done.7.refs_1_ = bf16[256,512]{1,0:T(8,128)(2,1)S(1)} collective-permute-done((bf16[256,512]{1,0:T(8,128)(2,1)S(1)}, bf16[256,512]{1,0:T(8,128)(2,1)S(1)}, u32[]{:S(2)}, u32[]{:S(2)}) %collective-permute-start.7) | collective-permute-done | bytes 262176 | tf_op jit(solution)/shard_map/ppermute | solution.py:28
  24.4 0.9 %copy-done.1 = bf16[256,512]{1,0:T(8,128)(2,1)S(1)} copy-done((bf16[256,512]{1,0:T(8,128)(2,1)S(1)}, bf16[256,512]{1,0:T(8,128)(2,1)}, u32[]{:S(2)}) %copy-start.1) | copy-done | bytes 262168
  25.3 0.1 payload.3.refs_1_
  25.5 1.6 %collective-permute-start.9 = (bf16[384,512]{1,0:T(8,128)(2,1)S(1)}, bf16[384,512]{1,0:T(8,128)(2,1)S(1)}, u32[]{:S(2)}, u32[]{:S(2)}) collective-permute-start(bf16[384,512]{1,0:T(8,128)(2,1)S(1)} %payload.3.refs_1_), channel_id=1, source_target_pairs={{0,8},{8,0},{16,24},{24,16},{1,9},{9,1},{17,25},{25,17},{2,10},{10... | collective-permute-start | bytes 1179656 | tf_op jit(solution)/shard_map/ppermute | solution.py:28
  27.0 0.1 payload.2.refs_0_
  27.2 0.6 collective-permute-start.10
  27.8 2.2 %left_strip.1 = bf16[272,1024]{1,0:T(8,128)(2,1)} custom-call(s32[1]{0:T(128)} %bitcast.me_ref, bf16[1,1024,1024]{2,1,0:T(8,128)(2,1)} %left_ref.1, bf16[1,1024,1024]{2,1,0:T(8,128)(2,1)} %refs_3_.5, bf16[1,1024,1024]{2,1,0:T(8,128)(2,1)} %refs_3_.5, bf16[1,1024,1024]{2,1,0:T(8,128)(2,1)} %refs_3_.5, bf16[1,1024,1024]{2,1,0:T(8,128)(2,1)} %refs_3_.5), custom_call_target="tpu_custom_call" | custom-call | tf_op jit(solution)/shard_map/left_strip/pallas_call | solution.py:126
  29.9 2.6 %collective-permute-start = (bf16[272,1024]{1,0:T(8,128)(2,1)}, bf16[272,1024]{1,0:T(8,128)(2,1)S(1)}, u32[]{:S(2)}, u32[]{:S(2)}) collective-permute-start(bf16[272,1024]{1,0:T(8,128)(2,1)} %left_strip.1), channel_id=1, source_target_pairs={{0,4},{1,5},{2,6},{3,7},{4,0},{5,1},{6,2},{7,3},{8,12},{9,13},{10,... | collective-permute-start | bytes 1671176 | tf_op jit(solution)/shard_map/ppermute | solution.py:23
  32.5 1.5 %collective-permute-start.11 = (bf16[384,512]{1,0:T(8,128)(2,1)S(1)}, bf16[384,512]{1,0:T(8,128)(2,1)S(1)}, u32[]{:S(2)}, u32[]{:S(2)}) collective-permute-start(bf16[384,512]{1,0:T(8,128)(2,1)S(1)} %payload.3.refs_1_), channel_id=1, source_target_pairs={{0,16},{8,24},{16,0},{24,8},{1,17},{9,25},{17,1},{25,9},{2,18},{10... | collective-permute-start | bytes 1179656 | tf_op jit(solution)/shard_map/ppermute | solution.py:28
  34.0 0.5 collective-permute-start.8
  34.6 1.7 %collective-permute-done.9.refs_3_ = bf16[384,512]{1,0:T(8,128)(2,1)S(1)} collective-permute-done((bf16[384,512]{1,0:T(8,128)(2,1)S(1)}, bf16[384,512]{1,0:T(8,128)(2,1)S(1)}, u32[]{:S(2)}, u32[]{:S(2)}) %collective-permute-start.9) | collective-permute-done | bytes 393248 | tf_op jit(solution)/shard_map/ppermute | solution.py:28
  36.3 0.6 %collective-permute-start.13 = (bf16[384,512]{1,0:T(8,128)(2,1)S(1)}, bf16[384,512]{1,0:T(8,128)(2,1)S(1)}, u32[]{:S(2)}, u32[]{:S(2)}) collective-permute-start(bf16[384,512]{1,0:T(8,128)(2,1)S(1)} %collective-permute-done.9.refs_3_), channel_id=1, source_target_pairs={{0,16},{8,24},{16,0},{24,8},{1,17},{9,25},{17,1},{25,9},{2,18},{10... | collective-permute-start | bytes 1179656 | tf_op jit(solution)/shard_map/ppermute | solution.py:28
  36.9 2.4 %collective-permute-done.10.refs_4_ = bf16[384,512]{1,0:T(8,128)(2,1)S(1)} collective-permute-done((bf16[384,512]{1,0:T(8,128)(2,1)S(1)}, bf16[384,512]{1,0:T(8,128)(2,1)S(1)}, u32[]{:S(2)}, u32[]{:S(2)}) %collective-permute-start.10) | collective-permute-done | bytes 393248 | tf_op jit(solution)/shard_map/ppermute | solution.py:28
  39.3 0.5 collective-permute-start.12
  39.8 15.9 %collective-permute-done.left_ref = bf16[272,1024]{1,0:T(8,128)(2,1)S(1)} collective-permute-done((bf16[272,1024]{1,0:T(8,128)(2,1)}, bf16[272,1024]{1,0:T(8,128)(2,1)S(1)}, u32[]{:S(2)}, u32[]{:S(2)}) %collective-permute-start) | collective-permute-done | bytes 557088 | tf_op jit(solution)/shard_map/ppermute | solution.py:23
  55.7 2.3 %update.1 = bf16[1,256,1024]{2,1,0:T(8,128)(2,1)} custom-call(s32[1]{0:T(128)} %bitcast.me_ref, s32[1]{0:T(128)S(6)} %copy.6.rows_ref, s32[1]{0:T(128)S(6)} %copy.7.cols_ref, bf16[272,1024]{1,0:T(8,128)(2,1)S(1)} %collective-permute-done.left_ref, bf16[384,512]{1,0:T(8,128)(2,1)S(1)} %payload.2.refs_0_, bf16[384,512]{1,0:T(8,128)(2,1)S(1)} %payload.3.refs_1_, ...), custom_call_target="tpu_custom_call" | custom-call | flops 1073741824 | bytes 8388608 | tf_op jit(solution)/shard_map/update/pallas_call | solution.py:213
  (13 shorter events, 0.0 us)
Async XLA Ops:
  2.2 12.1 %collective-permute-start.6 = (bf16[256,512]{1,0:T(8,128)(2,1)}, bf16[256,512]{1,0:T(8,128)(2,1)S(1)}, u32[]{:S(2)}, u32[]{:S(2)}) collective-permute-start(bf16[256,512]{1,0:T(8,128)(2,1)} %get-tuple-element.20), channel_id=1, source_target_pairs={{0,16},{8,24},{16,0},{24,8},{1,17},{9,25},{17,1},{25,9},{2,18},{10... | collective-permute-start | bytes 786440 | tf_op jit(solution)/shard_map/ppermute | solution.py:28
  5.1 5.9 %copy-start.2 = (bf16[256,512]{1,0:T(8,128)(2,1)S(1)}, bf16[256,512]{1,0:T(8,128)(2,1)}, u32[]{:S(2)}) copy-start(bf16[256,512]{1,0:T(8,128)(2,1)} %get-tuple-element.14) | copy-start | bytes 786436
  5.1 6.4 %copy-start.3 = (bf16[256,512]{1,0:T(8,128)(2,1)S(1)}, bf16[256,512]{1,0:T(8,128)(2,1)}, u32[]{:S(2)}) copy-start(bf16[256,512]{1,0:T(8,128)(2,1)} %get-tuple-element.18) | copy-start | bytes 786436
  5.1 11.8 %collective-permute-start.3 = (bf16[256,512]{1,0:T(8,128)(2,1)}, bf16[256,512]{1,0:T(8,128)(2,1)S(1)}, u32[]{:S(2)}, u32[]{:S(2)}) collective-permute-start(bf16[256,512]{1,0:T(8,128)(2,1)} %get-tuple-element.16), channel_id=1, source_target_pairs={{0,8},{8,0},{16,24},{24,16},{1,9},{9,1},{17,25},{25,17},{2,10},{10... | collective-permute-start | bytes 786440 | tf_op jit(solution)/shard_map/ppermute | solution.py:28
  8.5 14.2 %collective-permute-start.1 = (bf16[128,1024]{1,0:T(8,128)(2,1)}, bf16[128,1024]{1,0:T(8,128)(2,1)S(1)}, u32[]{:S(2)}, u32[]{:S(2)}) collective-permute-start(bf16[128,1024]{1,0:T(8,128)(2,1)} %fold_right.1), channel_id=1, source_target_pairs={{0,4},{1,5},{2,6},{3,7},{4,0},{5,1},{6,2},{7,3},{8,12},{9,13},{10,... | collective-permute-start | bytes 786440 | tf_op jit(solution)/shard_map/ppermute | solution.py:23
  11.0 16.0 %collective-permute-start.2 = (bf16[256,512]{1,0:T(8,128)(2,1)S(1)}, bf16[256,512]{1,0:T(8,128)(2,1)S(1)}, u32[]{:S(2)}, u32[]{:S(2)}) collective-permute-start(bf16[256,512]{1,0:T(8,128)(2,1)S(1)} %copy-done.2), channel_id=1, source_target_pairs={{0,8},{8,0},{16,24},{24,16},{1,9},{9,1},{17,25},{25,17},{2,10},{10... | collective-permute-start | bytes 786440 | tf_op jit(solution)/shard_map/ppermute | solution.py:28
  11.6 11.1 %collective-permute-start.5 = (bf16[256,512]{1,0:T(8,128)(2,1)S(1)}, bf16[256,512]{1,0:T(8,128)(2,1)S(1)}, u32[]{:S(2)}, u32[]{:S(2)}) collective-permute-start(bf16[256,512]{1,0:T(8,128)(2,1)S(1)} %copy-done.3), channel_id=1, source_target_pairs={{0,16},{8,24},{16,0},{24,8},{1,17},{9,25},{17,1},{25,9},{2,18},{10... | collective-permute-start | bytes 786440 | tf_op jit(solution)/shard_map/ppermute | solution.py:28
  14.3 12.7 %copy-start = (bf16[256,512]{1,0:T(8,128)(2,1)S(1)}, bf16[256,512]{1,0:T(8,128)(2,1)}, u32[]{:S(2)}) copy-start(bf16[256,512]{1,0:T(8,128)(2,1)} %get-tuple-element.13.own_ref) | copy-start | bytes 786436
  15.4 9.0 %collective-permute-start.7 = (bf16[256,512]{1,0:T(8,128)(2,1)S(1)}, bf16[256,512]{1,0:T(8,128)(2,1)S(1)}, u32[]{:S(2)}, u32[]{:S(2)}) collective-permute-start(bf16[256,512]{1,0:T(8,128)(2,1)S(1)} %add_convert_fusion), channel_id=1, source_target_pairs={{0,8},{8,0},{16,24},{24,16},{1,9},{9,1},{17,25},{25,17},{2,10},{10... | collective-permute-start | bytes 786440 | tf_op jit(solution)/shard_map/ppermute | solution.py:28
  17.9 9.1 %collective-permute-start.4 = (bf16[256,512]{1,0:T(8,128)(2,1)S(1)}, bf16[256,512]{1,0:T(8,128)(2,1)S(1)}, u32[]{:S(2)}, u32[]{:S(2)}) collective-permute-start(bf16[256,512]{1,0:T(8,128)(2,1)S(1)} %add_convert_fusion.1), channel_id=1, source_target_pairs={{0,16},{8,24},{16,0},{24,8},{1,17},{9,25},{17,1},{25,9},{2,18},{10... | collective-permute-start | bytes 786440 | tf_op jit(solution)/shard_map/ppermute | solution.py:28
  24.4 1.0 %copy-start.1 = (bf16[256,512]{1,0:T(8,128)(2,1)S(1)}, bf16[256,512]{1,0:T(8,128)(2,1)}, u32[]{:S(2)}) copy-start(bf16[256,512]{1,0:T(8,128)(2,1)} %get-tuple-element.17.own_ref) | copy-start | bytes 786436
  25.5 10.8 %collective-permute-start.9 = (bf16[384,512]{1,0:T(8,128)(2,1)S(1)}, bf16[384,512]{1,0:T(8,128)(2,1)S(1)}, u32[]{:S(2)}, u32[]{:S(2)}) collective-permute-start(bf16[384,512]{1,0:T(8,128)(2,1)S(1)} %payload.3.refs_1_), channel_id=1, source_target_pairs={{0,8},{8,0},{16,24},{24,16},{1,9},{9,1},{17,25},{25,17},{2,10},{10... | collective-permute-start | bytes 1179656 | tf_op jit(solution)/shard_map/ppermute | solution.py:28
  27.2 12.1 %collective-permute-start.10 = (bf16[384,512]{1,0:T(8,128)(2,1)S(1)}, bf16[384,512]{1,0:T(8,128)(2,1)S(1)}, u32[]{:S(2)}, u32[]{:S(2)}) collective-permute-start(bf16[384,512]{1,0:T(8,128)(2,1)S(1)} %payload.2.refs_0_), channel_id=1, source_target_pairs={{0,16},{8,24},{16,0},{24,8},{1,17},{9,25},{17,1},{25,9},{2,18},{10... | collective-permute-start | bytes 1179656 | tf_op jit(solution)/shard_map/ppermute | solution.py:28
  29.9 25.8 %collective-permute-start = (bf16[272,1024]{1,0:T(8,128)(2,1)}, bf16[272,1024]{1,0:T(8,128)(2,1)S(1)}, u32[]{:S(2)}, u32[]{:S(2)}) collective-permute-start(bf16[272,1024]{1,0:T(8,128)(2,1)} %left_strip.1), channel_id=1, source_target_pairs={{0,4},{1,5},{2,6},{3,7},{4,0},{5,1},{6,2},{7,3},{8,12},{9,13},{10,... | collective-permute-start | bytes 1671176 | tf_op jit(solution)/shard_map/ppermute | solution.py:23
  32.5 23.2 %collective-permute-start.11 = (bf16[384,512]{1,0:T(8,128)(2,1)S(1)}, bf16[384,512]{1,0:T(8,128)(2,1)S(1)}, u32[]{:S(2)}, u32[]{:S(2)}) collective-permute-start(bf16[384,512]{1,0:T(8,128)(2,1)S(1)} %payload.3.refs_1_), channel_id=1, source_target_pairs={{0,16},{8,24},{16,0},{24,8},{1,17},{9,25},{17,1},{25,9},{2,18},{10... | collective-permute-start | bytes 1179656 | tf_op jit(solution)/shard_map/ppermute | solution.py:28
  34.0 21.7 %collective-permute-start.8 = (bf16[384,512]{1,0:T(8,128)(2,1)S(1)}, bf16[384,512]{1,0:T(8,128)(2,1)S(1)}, u32[]{:S(2)}, u32[]{:S(2)}) collective-permute-start(bf16[384,512]{1,0:T(8,128)(2,1)S(1)} %payload.2.refs_0_), channel_id=1, source_target_pairs={{0,8},{8,0},{16,24},{24,16},{1,9},{9,1},{17,25},{25,17},{2,10},{10... | collective-permute-start | bytes 1179656 | tf_op jit(solution)/shard_map/ppermute | solution.py:28
  36.3 19.4 %collective-permute-start.13 = (bf16[384,512]{1,0:T(8,128)(2,1)S(1)}, bf16[384,512]{1,0:T(8,128)(2,1)S(1)}, u32[]{:S(2)}, u32[]{:S(2)}) collective-permute-start(bf16[384,512]{1,0:T(8,128)(2,1)S(1)} %collective-permute-done.9.refs_3_), channel_id=1, source_target_pairs={{0,16},{8,24},{16,0},{24,8},{1,17},{9,25},{17,1},{25,9},{2,18},{10... | collective-permute-start | bytes 1179656 | tf_op jit(solution)/shard_map/ppermute | solution.py:28
  39.3 16.4 %collective-permute-start.12 = (bf16[384,512]{1,0:T(8,128)(2,1)S(1)}, bf16[384,512]{1,0:T(8,128)(2,1)S(1)}, u32[]{:S(2)}, u32[]{:S(2)}) collective-permute-start(bf16[384,512]{1,0:T(8,128)(2,1)S(1)} %collective-permute-done.10.refs_4_), channel_id=1, source_target_pairs={{0,8},{8,0},{16,24},{24,16},{1,9},{9,1},{17,25},{25,17},{2,10},{10... | collective-permute-start | bytes 1179656 | tf_op jit(solution)/shard_map/ppermute | solution.py:28

commit v4 on v0

v4 whole, which is shorter than its diff:
```python
import functools

import jax
import jax.numpy as jnp
from jax import lax
from jax.experimental import pallas as pl
from jax.experimental.pallas import tpu as pltpu
from jax.sharding import PartitionSpec as P

TILE = 256
EXTRA = 16
VMEM = 24 * 1024 * 1024
SMEM_SPEC = pl.BlockSpec(memory_space=pltpu.SMEM)
VMEM_SPEC = pl.BlockSpec(memory_space=pltpu.VMEM)
HBM_SPEC = pl.BlockSpec(memory_space=pltpu.HBM)
BF16 = jnp.bfloat16
F32 = jnp.float32


def shifted(value, axis, steps):
    count = lax.axis_size(axis)
    pairs = [(source, (source + steps) % count) for source in range(count)]
    return lax.ppermute(value, axis, pairs)


def swapped(value, flip):
    count = lax.axis_size("dp")
    return lax.ppermute(value, "dp", [(source, source ^ flip) for source in range(count)])


def after(value, *earlier):
    return lax.optimization_barrier((value, *earlier))[0]


def block(index):
    return pl.ds(index * TILE, TILE)


def strip_of(index, size):
    return pl.ds(pl.multiple_of(index * size, size), size)


def cost(flops, bytes_accessed):
    return pl.CostEstimate(flops=flops, bytes_accessed=bytes_accessed, transcendentals=0)


def below(tiles):
    return [(i, j) for j in range(tiles) for i in range(j + 1, tiles)]


def pick_copies(wanted, me, grad_ref, outs, sems):
    copies = []
    for parts, out in zip(wanted, outs):
        half, strip = out.shape[0] // len(parts), out.shape[1]
        for part, (flip, h) in enumerate(parts):
            source = grad_ref.at[0, 0, pl.ds(h * half, half), strip_of(jnp.bitwise_xor(me, flip), strip)]
            copies.append(
                pltpu.make_async_copy(source, out.at[pl.ds(part * half, half), :], sems.at[len(copies)])
            )
    return copies


def picked_shapes(wanted, width, groups):
    return [pltpu.VMEM((len(parts) * (width // 2), width // groups), BF16) for parts in wanted]


def pick_kernel(wanted, me_ref, grad_ref, *refs):
    copies = pick_copies(wanted, me_ref[0], grad_ref, refs[:-1], refs[-1])
    for copy in copies:
        copy.start()
    for copy in copies:
        copy.wait()


def pick(me, grads, groups, wanted):
    return pl.pallas_call(
        functools.partial(pick_kernel, wanted),
        in_specs=[SMEM_SPEC, HBM_SPEC],
        out_specs=[VMEM_SPEC] * len(wanted),
        out_shape=picked_shapes(wanted, grads.shape[-1], groups),
        scratch_shapes=[pltpu.SemaphoreType.DMA((sum(len(parts) for parts in wanted),))],
        compiler_params=pltpu.CompilerParams(vmem_limit_bytes=VMEM),
        name="pick_kept",
    )(me, grads)


def fold_copies(me, root_ref, strips, odd_corners, sems):
    tiles, strip, _ = strips.shape
    return [
        pltpu.make_async_copy(
            root_ref.at[0, pl.ds(pl.multiple_of(i * TILE + me * strip, strip), strip), :], strips.at[i], sems.at[i]
        )
        for i in range(tiles)
    ] + [
        pltpu.make_async_copy(
            root_ref.at[0, block(2 * pair + 1), block(2 * pair + 1)], odd_corners.at[pair], sems.at[tiles + pair]
        )
        for pair in range(tiles // 2)
    ]


def fold(me, strips, odd_corners, out):
    tiles, strip, _ = strips.shape
    blocks = below(tiles)
    for k, (i, j) in enumerate(blocks):
        out[pl.ds(k * strip, strip), :] = strips[i, :, block(j)]
    row = lax.broadcasted_iota(jnp.int32, (strip, TILE), 0) + me * strip
    column = lax.broadcasted_iota(jnp.int32, (strip, TILE), 1)
    on_diag = lax.broadcasted_iota(jnp.int32, (TILE, TILE), 0) == lax.broadcasted_iota(jnp.int32, (TILE, TILE), 1)
    lines = []
    for pair in range(tiles // 2):
        even, odd = 2 * pair, 2 * pair + 1
        out[pl.ds((len(blocks) + pair) * strip, strip), :] = jnp.where(
            row >= column, strips[even, :, block(even)], strips[odd, :, block(odd)]
        )
        corner = odd_corners[pair].astype(F32)
        lines.append(jnp.sum(jnp.where(on_diag, corner, 0.0), axis=0, keepdims=True))
    lines.append(jnp.zeros((EXTRA - len(lines), TILE), F32))
    out[pl.ds(tiles * tiles // 2 * strip, EXTRA), :] = jnp.concatenate(lines, axis=0).astype(BF16)


def messages_kernel(wanted, me_ref, grad_ref, left_ref, right_ref, *refs):
    outs, (left, right, strips, odd_corners, pick_sems, fold_sems) = refs[: len(wanted)], refs[len(wanted) :]
    me = me_ref[0]
    copies = pick_copies(wanted, me, grad_ref, outs, pick_sems)
    roots = [
        fold_copies(me, root, strips.at[index], odd_corners.at[index], fold_sems.at[index])
        for index, root in enumerate((left_ref, right_ref))
    ]
    for copy in roots[0] + roots[1] + copies:
        copy.start()
    for index, out in enumerate((left, right)):
        for copy in roots[index]:
            copy.wait()
        fold(me, strips.at[index], odd_corners.at[index], out)
    for copy in copies:
        copy.wait()


def messages(me, grads, left, right, groups, wanted):
    width = grads.shape[-1]
    strip, tiles = TILE // groups, width // TILE
    count = sum(len(parts) for parts in wanted)
    folded = pltpu.VMEM((tiles * tiles // 2 * strip + EXTRA, TILE), BF16)
    return pl.pallas_call(
        functools.partial(messages_kernel, wanted),
        in_specs=[SMEM_SPEC] + [HBM_SPEC] * 3,
        out_specs=[VMEM_SPEC] * (len(wanted) + 2),
        out_shape=picked_shapes(wanted, width, groups) + [folded] * 2,
        scratch_shapes=[
            pltpu.VMEM((2, tiles, strip, width), BF16),
            pltpu.VMEM((2, tiles // 2, TILE, TILE), BF16),
            pltpu.SemaphoreType.DMA((max(count, 1),)),
            pltpu.SemaphoreType.DMA((2, tiles + tiles // 2)),
        ],
        compiler_params=pltpu.CompilerParams(vmem_limit_bytes=VMEM),
        name="messages",
    )(me, grads, left, right)


def unfold(pieces, me, root, folded):
    tiles = root.shape[0] // TILE
    strip = TILE // len(pieces)
    blocks = below(tiles)
    for flip, piece in enumerate(pieces):
        other = jnp.bitwise_xor(me, flip)
        for k in range(tiles * tiles // 2):
            value = piece[pl.ds(k * strip, strip), :]
            if k < len(blocks):
                i, j = blocks[k]
                root[pl.ds(pl.multiple_of(i * TILE + other * strip, strip), strip), block(j)] = value
            else:
                at = (k - len(blocks)) * TILE + other * strip
                folded[pl.ds(pl.multiple_of(at, strip), strip), :] = value
    row = lax.broadcasted_iota(jnp.int32, (TILE, TILE), 0)
    column = lax.broadcasted_iota(jnp.int32, (TILE, TILE), 1)
    lines = pieces[0][pl.ds(tiles * tiles // 2 * strip, EXTRA), :].astype(F32)
    for i in range(tiles):
        value = folded[block(i // 2), :].astype(F32)
        value = jnp.where(row >= column if i % 2 == 0 else row < column, value, value.T)
        if i % 2:
            line = jnp.broadcast_to(lines[i // 2 : i // 2 + 1, :], (TILE, TILE))
            value = jnp.where(row == column, line, value)
        root[block(i), block(i)] = value.astype(BF16)
        for j in range(i):
            root[block(j), block(i)] = root[block(i), block(j)].T


def columns_kernel(groups, split, me_ref, rows_ref, cols_ref, *refs):
    count = sum(split)
    pieces, terms, outs = refs[:groups], refs[groups : groups + count], refs[groups + count : 2 * groups + count]
    left, folded, masked, mixed = refs[2 * groups + count :]
    me = me_ref[0]
    width, strip = masked.shape
    unfold(pieces, me, left, folded)
    part = width // len(split)
    column = lax.broadcasted_iota(jnp.int32, (part, strip), 1) + me * strip
    row = lax.broadcasted_iota(jnp.int32, (part, strip), 0)
    for index, number in enumerate(split):
        used, terms = terms[:number], terms[number:]
        total = functools.reduce(lambda a, b: a + b, [term[pl.ds(0, part), :].astype(F32) for term in used])
        keep = (row + index * part < rows_ref[0]) & (column < cols_ref[0])
        masked[pl.ds(index * part, part), :] = jnp.where(keep, total, 0.0).astype(BF16)
    mixed[...] = jnp.dot(left[...], masked[...], preferred_element_type=F32).astype(BF16)
    for flip, out in enumerate(outs):
        out[...] = mixed[strip_of(jnp.bitwise_xor(me, flip), strip), :]


def left_columns(me, rows_valid, cols_valid, pieces, terms, width):
    groups = len(pieces)
    strip = width // groups
    flat = [term for part in terms for term in part]
    return pl.pallas_call(
        functools.partial(columns_kernel, groups, [len(part) for part in terms]),
        in_specs=[SMEM_SPEC] * 3 + [VMEM_SPEC] * (groups + len(flat)),
        out_specs=[VMEM_SPEC] * groups,
        out_shape=[pltpu.VMEM((strip, strip), BF16)] * groups,
        scratch_shapes=[
            pltpu.VMEM((width, width), BF16),
            pltpu.VMEM((width // 2, TILE), BF16),
            pltpu.VMEM((width, strip), BF16),
            pltpu.VMEM((width, strip), BF16),
        ],
        compiler_params=pltpu.CompilerParams(vmem_limit_bytes=VMEM),
        cost_estimate=cost(2 * strip * width**2, 4 * width**2),
        name="left_columns",
    )(me, rows_valid, cols_valid, *pieces, *flat)


def rows_kernel(groups, me_ref, rows_ref, cols_ref, *refs):
    pieces, strips, (out, right, folded) = refs[:groups], refs[groups : 2 * groups], refs[2 * groups :]
    me = me_ref[0]
    width = right.shape[0]
    strip = width // groups
    unfold(pieces, me, right, folded)
    value = functools.reduce(
        lambda a, b: a + b,
        [
            jnp.dot(
                part[...], right[strip_of(jnp.bitwise_xor(me, flip), strip), :], preferred_element_type=F32
            )
            for flip, part in enumerate(strips)
        ],
    )
    column = lax.broadcasted_iota(jnp.int32, (strip, width), 1)
    row = lax.broadcasted_iota(jnp.int32, (strip, width), 0) + me * strip
    out[0] = jnp.where((row < rows_ref[0]) & (column < cols_ref[0]), value, 0.0).astype(BF16)


def update_rows(me, rows_valid, cols_valid, pieces, strips, width):
    groups = len(pieces)
    strip = width // groups
    return pl.pallas_call(
        functools.partial(rows_kernel, groups),
        in_specs=[SMEM_SPEC] * 3 + [VMEM_SPEC] * (2 * groups),
        out_specs=VMEM_SPEC,
        out_shape=jax.ShapeDtypeStruct((1, strip, width), BF16),
        scratch_shapes=[pltpu.VMEM((width, width), BF16), pltpu.VMEM((width // 2, TILE), BF16)],
        compiler_params=pltpu.CompilerParams(vmem_limit_bytes=VMEM),
        cost_estimate=cost(2 * strip * width**2, 4 * width**2),
        name="update_rows",
    )(me, rows_valid, cols_valid, *pieces, *strips)


def added(*terms):
    return functools.reduce(lambda a, b: a + b, [term.astype(F32) for term in terms])


def on_device(grads, left_roots, right_roots, rows_valid, cols_valid):
    groups = lax.axis_size("dp")
    me = lax.axis_index("dp").astype(jnp.int32).reshape(1)
    offset = lax.axis_size("shard") // 2
    width = grads.shape[-1]
    half, strip = width // 2, width // groups
    plain = grads
    grads, left_roots, right_roots = (
        pltpu.with_memory_space_constraint(array, pltpu.HBM) for array in (grads, left_roots, right_roots)
    )

    if groups == 4:
        sent_0, sent_1, left, right = messages(
            me, grads, left_roots, right_roots, groups, [[(1, 0), (3, 0)], [(2, 1), (3, 1)]]
        )
        sent_0, sent_1 = swapped(sent_0, 1), swapped(sent_1, 2)
        left, right = shifted((left, right), "shard", offset)
        kept = pick(me, grads, groups, [[(2, 0)], [(1, 1)], [(0, 0)], [(0, 1)]])
        via_0, via_1 = added(kept[0], sent_0[half:]).astype(BF16), added(kept[1], sent_1[half:]).astype(BF16)
        left = after(left, via_0, via_1)
        via_0, via_1 = swapped(via_0, 2), swapped(via_1, 1)
        lefts = [left, swapped(left, 1), swapped(left, 2)]
        lefts.append(swapped(lefts[1], 2))
        strips = left_columns(
            me, rows_valid, cols_valid, lefts, [[kept[2], sent_0, via_0], [kept[3], sent_1, via_1]], width
        )
        right = after(right, via_0, via_1)
        rights = [right, swapped(right, 1), swapped(right, 2)]
        rights.append(swapped(after(rights[2], strips[0]), 1))
    else:
        left, right = messages(me, grads, left_roots, right_roots, groups, [])
        left, right = shifted((left, right), "shard", offset)
        parts = [
            lax.dynamic_slice_in_dim(plain[0, 0], jnp.bitwise_xor(me[0], flip) * strip, strip, 1)
            for flip in range(groups)
        ]
        terms = [parts[:1] + [swapped(parts[flip], flip) for flip in range(1, groups)]]
        lefts = [left] + [swapped(left, flip) for flip in range(1, groups)]
        strips = left_columns(me, rows_valid, cols_valid, lefts, terms, width)
        rights = [right] + [swapped(right, flip) for flip in range(1, groups)]
    strips = [strips[0]] + [swapped(strips[flip], flip) for flip in range(1, groups)]
    return update_rows(me, rows_valid, cols_valid, rights, strips, width)


def solution(mesh):
    placed = (
        P("dp", "shard", None, None),
        P("shard", None, None),
        P("shard", None, None),
        P("shard"),
        P("shard"),
    )
    return jax.shard_map(
        on_device, mesh=mesh, in_specs=placed, out_specs=P("shard", "dp", None), check_vma=False
    )
```

time: 247 us -> 62.1 us (0.25)
  the two profiles are of different devices: /device:TPU:0 before, /device:TPU:14 now
where the time goes in v4:
time: 62.1 us; the launch traced here: 61.9 us
  waiting for transfers between devices  33.8 us (54%)
  starting transfers between devices  20.4 us (33%)
  Pallas kernels  6.18 us (10%)
  between operations  1.35 us (2%)
    ppermute x13, waiting for transfers between devices, swapped(): lax.ppermute(value, 'dp', [(source, source ^ flip) for source in range(co...  31.2 us
    ppermute x13, starting transfers between devices, swapped(): lax.ppermute(value, 'dp', [(source, source ^ flip) for source in range(co...  14.4 us
    ppermute x2, starting transfers between devices, shifted(): return lax.ppermute(value, axis, pairs)  5.97 us
    ppermute x2, waiting for transfers between devices, shifted(): return lax.ppermute(value, axis, pairs)  2.59 us
    pallas_call x1, Pallas kernels, update_rows(): pl.pallas_call(functools.partial(rows_kernel, groups), in_specs=[SMEM_SPE...  1.99 us
    pallas_call x1, Pallas kernels, messages(): pl.pallas_call(functools.partial(messages_kernel, wanted), in_specs=[SMEM...  1.92 us
  transfers between devices with their start and end apart: 15, of which 11 were waited for; matrix products, arithmetic and copies ran while one was open for 0% of the time, Pallas kernels for 4%

profile of v4, /device:TPU:14, one launch (start us, length us, event | category | flops | bytes accessed | tf_op | source)
XLA Modules:
  0.0 61.9 jit_solution(15024463521233492057)
XLA Ops:
  0.0 1.9 %messages.1 = (bf16[1024,256]{1,0:T(8,128)(2,1)S(1)}, bf16[1024,256]{1,0:T(8,128)(2,1)S(1)}, bf16[528,256]{1,0:T(8,128)(2,1)S(1)}, bf16[528,256]{1,0:T(8,128)(2,1)S(1)}) custom-call(s32[1]{0:T(128)} %bitcast.me_ref, bf16[1,1,1024,1024]{3,2,1,0:T(8,128)(2,1)} %grad_ref.3, bf16[1,1024,1024]{2,1,0:T(8,128)(2,1)} %left_ref.1, bf16[1,1024,1024]{2,1,0:T(8,128)(2,1)} %right_ref.1), custom_call_target="tpu_custom_call" | custom-call | tf_op jit(solution)/shard_map/messages/pallas_call | solution.py:145
  1.9 0.6 collective-permute-start.3
  2.5 0.5 collective-permute-start.1
  3.0 2.6 %collective-permute-start.7 = (bf16[528,256]{1,0:T(8,128)(2,1)S(1)}, bf16[528,256]{1,0:T(8,128)(2,1)S(1)}, u32[]{:S(2)}, u32[]{:S(2)}) collective-permute-start(bf16[528,256]{1,0:T(8,128)(2,1)S(1)} %get-tuple-element.26), channel_id=1, source_target_pairs={{0,4},{1,5},{2,6},{3,7},{4,0},{5,1},{6,2},{7,3},{8,12},{9,13},{10,... | collective-permute-start | bytes 811016 | tf_op jit(solution)/shard_map/ppermute | solution.py:23
  5.6 1.2 %pick_kept.1 = (bf16[512,256]{1,0:T(8,128)(2,1)S(1)}, bf16[512,256]{1,0:T(8,128)(2,1)S(1)}, bf16[512,256]{1,0:T(8,128)(2,1)S(1)}, bf16[512,256]{1,0:T(8,128)(2,1)S(1)}) custom-call(s32[1]{0:T(128)} %bitcast.me_ref, bf16[1,1,1024,1024]{3,2,1,0:T(8,128)(2,1)} %grad_ref.3), custom_call_target="tpu_custom_call" | custom-call | tf_op jit(solution)/shard_map/pick_kept/pallas_call | solution.py:76
  6.9 8.8 %collective-permute-done.3.refs_8_ = bf16[1024,256]{1,0:T(8,128)(2,1)S(1)} collective-permute-done((bf16[1024,256]{1,0:T(8,128)(2,1)S(1)}, bf16[1024,256]{1,0:T(8,128)(2,1)S(1)}, u32[]{:S(2)}, u32[]{:S(2)}) %collective-permute-start.3) | collective-permute-done | bytes 524320 | tf_op jit(solution)/shard_map/ppermute | solution.py:28
  15.7 0.1 add_convert_fusion
  15.7 0.1 collective-permute-done.1.refs_5_
  15.9 0.1 add_convert_fusion.1
  16.0 0.5 collective-permute-done.7.refs_0_
  16.5 1.5 %collective-permute-start.8 = (bf16[528,256]{1,0:T(8,128)(2,1)S(1)}, bf16[528,256]{1,0:T(8,128)(2,1)S(1)}, u32[]{:S(2)}, u32[]{:S(2)}) collective-permute-start(bf16[528,256]{1,0:T(8,128)(2,1)S(1)} %collective-permute-done.7.refs_0_), channel_id=1, source_target_pairs={{0,8},{8,0},{16,24},{24,16},{1,9},{9,1},{17,25},{25,17},{2,10},{10... | collective-permute-start | bytes 811016 | tf_op jit(solution)/shard_map/ppermute | solution.py:28
  18.0 3.4 %collective-permute-start = (bf16[528,256]{1,0:T(8,128)(2,1)S(1)}, bf16[528,256]{1,0:T(8,128)(2,1)S(1)}, u32[]{:S(2)}, u32[]{:S(2)}) collective-permute-start(bf16[528,256]{1,0:T(8,128)(2,1)S(1)} %get-tuple-element.20), channel_id=1, source_target_pairs={{0,4},{1,5},{2,6},{3,7},{4,0},{5,1},{6,2},{7,3},{8,12},{9,13},{10,... | collective-permute-start | bytes 811016 | tf_op jit(solution)/shard_map/ppermute | solution.py:23
  21.4 1.5 %collective-permute-start.2 = (bf16[512,256]{1,0:T(8,128)(2,1)S(1)}, bf16[512,256]{1,0:T(8,128)(2,1)S(1)}, u32[]{:S(2)}, u32[]{:S(2)}) collective-permute-start(bf16[512,256]{1,0:T(8,128)(2,1)S(1)} %add_convert_fusion.1), channel_id=1, source_target_pairs={{0,16},{8,24},{16,0},{24,8},{1,17},{9,25},{17,1},{25,9},{2,18},{10... | collective-permute-start | bytes 786440 | tf_op jit(solution)/shard_map/ppermute | solution.py:28
  22.9 0.5 collective-permute-start.4
  23.4 0.5 collective-permute-start.9
  23.9 1.1 %collective-permute-done.8.refs_1_ = bf16[528,256]{1,0:T(8,128)(2,1)S(1)} collective-permute-done((bf16[528,256]{1,0:T(8,128)(2,1)S(1)}, bf16[528,256]{1,0:T(8,128)(2,1)S(1)}, u32[]{:S(2)}, u32[]{:S(2)}) %collective-permute-start.8) | collective-permute-done | bytes 270368 | tf_op jit(solution)/shard_map/ppermute | solution.py:28
  25.1 2.3 %collective-permute-start.10 = (bf16[528,256]{1,0:T(8,128)(2,1)S(1)}, bf16[528,256]{1,0:T(8,128)(2,1)S(1)}, u32[]{:S(2)}, u32[]{:S(2)}) collective-permute-start(bf16[528,256]{1,0:T(8,128)(2,1)S(1)} %collective-permute-done.8.refs_1_), channel_id=1, source_target_pairs={{0,16},{8,24},{16,0},{24,8},{1,17},{9,25},{17,1},{25,9},{2,18},{10... | collective-permute-start | bytes 811016 | tf_op jit(solution)/shard_map/ppermute | solution.py:28
  27.3 2.1 %collective-permute-done.refs_0_ = bf16[528,256]{1,0:T(8,128)(2,1)S(1)} collective-permute-done((bf16[528,256]{1,0:T(8,128)(2,1)S(1)}, bf16[528,256]{1,0:T(8,128)(2,1)S(1)}, u32[]{:S(2)}, u32[]{:S(2)}) %collective-permute-start) | collective-permute-done | bytes 270368 | tf_op jit(solution)/shard_map/ppermute | solution.py:23
  29.4 1.2 %collective-permute-done.2.refs_6_ = bf16[512,256]{1,0:T(8,128)(2,1)S(1)} collective-permute-done((bf16[512,256]{1,0:T(8,128)(2,1)S(1)}, bf16[512,256]{1,0:T(8,128)(2,1)S(1)}, u32[]{:S(2)}, u32[]{:S(2)}) %collective-permute-start.2) | collective-permute-done | bytes 262176 | tf_op jit(solution)/shard_map/ppermute | solution.py:28
  30.6 1.5 %collective-permute-start.6 = (bf16[528,256]{1,0:T(8,128)(2,1)S(1)}, bf16[528,256]{1,0:T(8,128)(2,1)S(1)}, u32[]{:S(2)}, u32[]{:S(2)}) collective-permute-start(bf16[528,256]{1,0:T(8,128)(2,1)S(1)} %collective-permute-done.refs_0_), channel_id=1, source_target_pairs={{0,16},{8,24},{16,0},{24,8},{1,17},{9,25},{17,1},{25,9},{2,18},{10... | collective-permute-start | bytes 811016 | tf_op jit(solution)/shard_map/ppermute | solution.py:28
  33.4 1.5 %collective-permute-start.5 = (bf16[528,256]{1,0:T(8,128)(2,1)S(1)}, bf16[528,256]{1,0:T(8,128)(2,1)S(1)}, u32[]{:S(2)}, u32[]{:S(2)}) collective-permute-start(bf16[528,256]{1,0:T(8,128)(2,1)S(1)} %collective-permute-done.refs_0_), channel_id=1, source_target_pairs={{0,8},{8,0},{16,24},{24,16},{1,9},{9,1},{17,25},{25,17},{2,10},{10... | collective-permute-start | bytes 811016 | tf_op jit(solution)/shard_map/ppermute | solution.py:28
  34.9 1.5 %collective-permute-done.9.refs_2_ = bf16[528,256]{1,0:T(8,128)(2,1)S(1)} collective-permute-done((bf16[528,256]{1,0:T(8,128)(2,1)S(1)}, bf16[528,256]{1,0:T(8,128)(2,1)S(1)}, u32[]{:S(2)}, u32[]{:S(2)}) %collective-permute-start.9) | collective-permute-done | bytes 270368 | tf_op jit(solution)/shard_map/ppermute | solution.py:28
  36.4 5.8 %collective-permute-done.10.refs_3_ = bf16[528,256]{1,0:T(8,128)(2,1)S(1)} collective-permute-done((bf16[528,256]{1,0:T(8,128)(2,1)S(1)}, bf16[528,256]{1,0:T(8,128)(2,1)S(1)}, u32[]{:S(2)}, u32[]{:S(2)}) %collective-permute-start.10) | collective-permute-done | bytes 270368 | tf_op jit(solution)/shard_map/ppermute | solution.py:28
  42.2 1.0 %left_columns.1 = (bf16[256,256]{1,0:T(8,128)(2,1)S(1)}, bf16[256,256]{1,0:T(8,128)(2,1)S(1)}, bf16[256,256]{1,0:T(8,128)(2,1)S(1)}, bf16[256,256]{1,0:T(8,128)(2,1)S(1)}) custom-call(s32[1]{0:T(128)} %bitcast.me_ref, s32[1]{0:T(128)S(6)} %copy.6.rows_ref, s32[1]{0:T(128)S(6)} %copy.7.cols_ref, bf16[528,256]{1,0:T(8,128)(2,1)S(1)} %collective-permute-done.7.refs_0_, ...), custom_call_target="tpu_custom_call" | custom-call | flops 536870912 | bytes 4194304 | tf_op jit(solution)/shard_map/left_columns/pallas_call | solution.py:213
  43.2 3.2 %collective-permute-done.6.refs_2_ = bf16[528,256]{1,0:T(8,128)(2,1)S(1)} collective-permute-done((bf16[528,256]{1,0:T(8,128)(2,1)S(1)}, bf16[528,256]{1,0:T(8,128)(2,1)S(1)}, u32[]{:S(2)}, u32[]{:S(2)}) %collective-permute-start.6) | collective-permute-done | bytes 270368 | tf_op jit(solution)/shard_map/ppermute | solution.py:28
  46.4 0.5 collective-permute-start.11
  46.9 1.5 %collective-permute-start.12 = (bf16[256,256]{1,0:T(8,128)(2,1)S(1)}, bf16[256,256]{1,0:T(8,128)(2,1)S(1)}, u32[]{:S(2)}, u32[]{:S(2)}) collective-permute-start(bf16[256,256]{1,0:T(8,128)(2,1)S(1)} %get-tuple-element.32), channel_id=1, source_target_pairs={{0,8},{8,0},{16,24},{24,16},{1,9},{9,1},{17,25},{25,17},{2,10},{10... | collective-permute-start | bytes 393224 | tf_op jit(solution)/shard_map/ppermute | solution.py:28
  48.4 1.5 %collective-permute-start.13 = (bf16[256,256]{1,0:T(8,128)(2,1)S(1)}, bf16[256,256]{1,0:T(8,128)(2,1)S(1)}, u32[]{:S(2)}, u32[]{:S(2)}) collective-permute-start(bf16[256,256]{1,0:T(8,128)(2,1)S(1)} %get-tuple-element.33), channel_id=1, source_target_pairs={{0,16},{8,24},{16,0},{24,8},{1,17},{9,25},{17,1},{25,9},{2,18},{10... | collective-permute-start | bytes 393224 | tf_op jit(solution)/shard_map/ppermute | solution.py:28
  50.0 0.5 collective-permute-start.14
  50.4 7.1 %collective-permute-done.12.refs_5_ = bf16[256,256]{1,0:T(8,128)(2,1)S(1)} collective-permute-done((bf16[256,256]{1,0:T(8,128)(2,1)S(1)}, bf16[256,256]{1,0:T(8,128)(2,1)S(1)}, u32[]{:S(2)}, u32[]{:S(2)}) %collective-permute-start.12) | collective-permute-done | bytes 131104 | tf_op jit(solution)/shard_map/ppermute | solution.py:28
  57.5 2.4 %collective-permute-done.14.refs_7_ = bf16[256,256]{1,0:T(8,128)(2,1)S(1)} collective-permute-done((bf16[256,256]{1,0:T(8,128)(2,1)S(1)}, bf16[256,256]{1,0:T(8,128)(2,1)S(1)}, u32[]{:S(2)}, u32[]{:S(2)}) %collective-permute-start.14) | collective-permute-done | bytes 131104 | tf_op jit(solution)/shard_map/ppermute | solution.py:28
  59.9 2.0 %update_rows.1 = bf16[1,256,1024]{2,1,0:T(8,128)(2,1)} custom-call(s32[1]{0:T(128)} %bitcast.me_ref, s32[1]{0:T(128)S(6)} %copy.6.rows_ref, s32[1]{0:T(128)S(6)} %copy.7.cols_ref, bf16[528,256]{1,0:T(8,128)(2,1)S(1)} %collective-permute-done.refs_0_, bf16[528,256]{1,0:T(8,128)(2,1)S(1)} %collective-permute-done.5.refs_1_, ...), custom_call_target="tpu_custom_call" | custom-call | flops 536870912 | bytes 4194304 | tf_op jit(solution)/shard_map/update_rows/pallas_call | solution.py:253
  (4 shorter events, 0.0 us)
Async XLA Ops:
  1.9 13.7 %collective-permute-start.3 = (bf16[1024,256]{1,0:T(8,128)(2,1)S(1)}, bf16[1024,256]{1,0:T(8,128)(2,1)S(1)}, u32[]{:S(2)}, u32[]{:S(2)}) collective-permute-start(bf16[1024,256]{1,0:T(8,128)(2,1)S(1)} %get-tuple-element.24), channel_id=1, source_target_pairs={{0,16},{8,24},{16,0},{24,8},{1,17},{9,25},{17,1},{25,9},{2,18},{10... | collective-permute-start | bytes 1572872 | tf_op jit(solution)/shard_map/ppermute | solution.py:28
  2.5 13.4 %collective-permute-start.1 = (bf16[1024,256]{1,0:T(8,128)(2,1)S(1)}, bf16[1024,256]{1,0:T(8,128)(2,1)S(1)}, u32[]{:S(2)}, u32[]{:S(2)}) collective-permute-start(bf16[1024,256]{1,0:T(8,128)(2,1)S(1)} %get-tuple-element.22), channel_id=1, source_target_pairs={{0,8},{8,0},{16,24},{24,16},{1,9},{9,1},{17,25},{25,17},{2,10},{10... | collective-permute-start | bytes 1572872 | tf_op jit(solution)/shard_map/ppermute | solution.py:28
  3.0 13.4 %collective-permute-start.7 = (bf16[528,256]{1,0:T(8,128)(2,1)S(1)}, bf16[528,256]{1,0:T(8,128)(2,1)S(1)}, u32[]{:S(2)}, u32[]{:S(2)}) collective-permute-start(bf16[528,256]{1,0:T(8,128)(2,1)S(1)} %get-tuple-element.26), channel_id=1, source_target_pairs={{0,4},{1,5},{2,6},{3,7},{4,0},{5,1},{6,2},{7,3},{8,12},{9,13},{10,... | collective-permute-start | bytes 811016 | tf_op jit(solution)/shard_map/ppermute | solution.py:23
  16.5 8.6 %collective-permute-start.8 = (bf16[528,256]{1,0:T(8,128)(2,1)S(1)}, bf16[528,256]{1,0:T(8,128)(2,1)S(1)}, u32[]{:S(2)}, u32[]{:S(2)}) collective-permute-start(bf16[528,256]{1,0:T(8,128)(2,1)S(1)} %collective-permute-done.7.refs_0_), channel_id=1, source_target_pairs={{0,8},{8,0},{16,24},{24,16},{1,9},{9,1},{17,25},{25,17},{2,10},{10... | collective-permute-start | bytes 811016 | tf_op jit(solution)/shard_map/ppermute | solution.py:28
  18.0 11.4 %collective-permute-start = (bf16[528,256]{1,0:T(8,128)(2,1)S(1)}, bf16[528,256]{1,0:T(8,128)(2,1)S(1)}, u32[]{:S(2)}, u32[]{:S(2)}) collective-permute-start(bf16[528,256]{1,0:T(8,128)(2,1)S(1)} %get-tuple-element.20), channel_id=1, source_target_pairs={{0,4},{1,5},{2,6},{3,7},{4,0},{5,1},{6,2},{7,3},{8,12},{9,13},{10,... | collective-permute-start | bytes 811016 | tf_op jit(solution)/shard_map/ppermute | solution.py:23
  21.4 9.2 %collective-permute-start.2 = (bf16[512,256]{1,0:T(8,128)(2,1)S(1)}, bf16[512,256]{1,0:T(8,128)(2,1)S(1)}, u32[]{:S(2)}, u32[]{:S(2)}) collective-permute-start(bf16[512,256]{1,0:T(8,128)(2,1)S(1)} %add_convert_fusion.1), channel_id=1, source_target_pairs={{0,16},{8,24},{16,0},{24,8},{1,17},{9,25},{17,1},{25,9},{2,18},{10... | collective-permute-start | bytes 786440 | tf_op jit(solution)/shard_map/ppermute | solution.py:28
  22.9 7.7 %collective-permute-start.4 = (bf16[512,256]{1,0:T(8,128)(2,1)S(1)}, bf16[512,256]{1,0:T(8,128)(2,1)S(1)}, u32[]{:S(2)}, u32[]{:S(2)}) collective-permute-start(bf16[512,256]{1,0:T(8,128)(2,1)S(1)} %add_convert_fusion), channel_id=1, source_target_pairs={{0,8},{8,0},{16,24},{24,16},{1,9},{9,1},{17,25},{25,17},{2,10},{10... | collective-permute-start | bytes 786440 | tf_op jit(solution)/shard_map/ppermute | solution.py:28
  23.4 13.0 %collective-permute-start.9 = (bf16[528,256]{1,0:T(8,128)(2,1)S(1)}, bf16[528,256]{1,0:T(8,128)(2,1)S(1)}, u32[]{:S(2)}, u32[]{:S(2)}) collective-permute-start(bf16[528,256]{1,0:T(8,128)(2,1)S(1)} %collective-permute-done.7.refs_0_), channel_id=1, source_target_pairs={{0,16},{8,24},{16,0},{24,8},{1,17},{9,25},{17,1},{25,9},{2,18},{10... | collective-permute-start | bytes 811016 | tf_op jit(solution)/shard_map/ppermute | solution.py:28
  25.1 17.1 %collective-permute-start.10 = (bf16[528,256]{1,0:T(8,128)(2,1)S(1)}, bf16[528,256]{1,0:T(8,128)(2,1)S(1)}, u32[]{:S(2)}, u32[]{:S(2)}) collective-permute-start(bf16[528,256]{1,0:T(8,128)(2,1)S(1)} %collective-permute-done.8.refs_1_), channel_id=1, source_target_pairs={{0,16},{8,24},{16,0},{24,8},{1,17},{9,25},{17,1},{25,9},{2,18},{10... | collective-permute-start | bytes 811016 | tf_op jit(solution)/shard_map/ppermute | solution.py:28
  30.6 15.8 %collective-permute-start.6 = (bf16[528,256]{1,0:T(8,128)(2,1)S(1)}, bf16[528,256]{1,0:T(8,128)(2,1)S(1)}, u32[]{:S(2)}, u32[]{:S(2)}) collective-permute-start(bf16[528,256]{1,0:T(8,128)(2,1)S(1)} %collective-permute-done.refs_0_), channel_id=1, source_target_pairs={{0,16},{8,24},{16,0},{24,8},{1,17},{9,25},{17,1},{25,9},{2,18},{10... | collective-permute-start | bytes 811016 | tf_op jit(solution)/shard_map/ppermute | solution.py:28
  33.4 17.0 %collective-permute-start.5 = (bf16[528,256]{1,0:T(8,128)(2,1)S(1)}, bf16[528,256]{1,0:T(8,128)(2,1)S(1)}, u32[]{:S(2)}, u32[]{:S(2)}) collective-permute-start(bf16[528,256]{1,0:T(8,128)(2,1)S(1)} %collective-permute-done.refs_0_), channel_id=1, source_target_pairs={{0,8},{8,0},{16,24},{24,16},{1,9},{9,1},{17,25},{25,17},{2,10},{10... | collective-permute-start | bytes 811016 | tf_op jit(solution)/shard_map/ppermute | solution.py:28
  46.4 13.5 %collective-permute-start.11 = (bf16[528,256]{1,0:T(8,128)(2,1)S(1)}, bf16[528,256]{1,0:T(8,128)(2,1)S(1)}, u32[]{:S(2)}, u32[]{:S(2)}) collective-permute-start(bf16[528,256]{1,0:T(8,128)(2,1)S(1)} %collective-permute-done.6.refs_2_), channel_id=1, source_target_pairs={{0,8},{8,0},{16,24},{24,16},{1,9},{9,1},{17,25},{25,17},{2,10},{10... | collective-permute-start | bytes 811016 | tf_op jit(solution)/shard_map/ppermute | solution.py:28
  46.9 10.6 %collective-permute-start.12 = (bf16[256,256]{1,0:T(8,128)(2,1)S(1)}, bf16[256,256]{1,0:T(8,128)(2,1)S(1)}, u32[]{:S(2)}, u32[]{:S(2)}) collective-permute-start(bf16[256,256]{1,0:T(8,128)(2,1)S(1)} %get-tuple-element.32), channel_id=1, source_target_pairs={{0,8},{8,0},{16,24},{24,16},{1,9},{9,1},{17,25},{25,17},{2,10},{10... | collective-permute-start | bytes 393224 | tf_op jit(solution)/shard_map/ppermute | solution.py:28
  48.4 9.1 %collective-permute-start.13 = (bf16[256,256]{1,0:T(8,128)(2,1)S(1)}, bf16[256,256]{1,0:T(8,128)(2,1)S(1)}, u32[]{:S(2)}, u32[]{:S(2)}) collective-permute-start(bf16[256,256]{1,0:T(8,128)(2,1)S(1)} %get-tuple-element.33), channel_id=1, source_target_pairs={{0,16},{8,24},{16,0},{24,8},{1,17},{9,25},{17,1},{25,9},{2,18},{10... | collective-permute-start | bytes 393224 | tf_op jit(solution)/shard_map/ppermute | solution.py:28
  50.0 9.9 %collective-permute-start.14 = (bf16[256,256]{1,0:T(8,128)(2,1)S(1)}, bf16[256,256]{1,0:T(8,128)(2,1)S(1)}, u32[]{:S(2)}, u32[]{:S(2)}) collective-permute-start(bf16[256,256]{1,0:T(8,128)(2,1)S(1)} %get-tuple-element.34), channel_id=1, source_target_pairs={{0,24},{8,16},{16,8},{24,0},{1,25},{9,17},{17,9},{25,1},{2,26},{10... | collective-permute-start | bytes 393224 | tf_op jit(solution)/shard_map/ppermute | solution.py:28

commit v5 on v4

--- a/solution.py
+++ b/solution.py
@@ -17,15 +17,16 @@
 F32 = jnp.float32
 
 
-def shifted(value, axis, steps):
-    count = lax.axis_size(axis)
-    pairs = [(source, (source + steps) % count) for source in range(count)]
-    return lax.ppermute(value, axis, pairs)
-
-
-def swapped(value, flip):
+def shifted(value, name):
+    count = lax.axis_size("shard")
+    with jax.named_scope(name):
+        return lax.ppermute(value, "shard", [(source, (source + count // 2) % count) for source in range(count)])
+
+
+def swapped(value, flip, name):
     count = lax.axis_size("dp")
-    return lax.ppermute(value, "dp", [(source, source ^ flip) for source in range(count)])
+    with jax.named_scope(name):
+        return lax.ppermute(value, "dp", [(source, source ^ flip) for source in range(count)])
 
 
 def after(value, *earlier):
@@ -162,10 +163,12 @@
     tiles = root.shape[0] // TILE
     strip = TILE // len(pieces)
     blocks = below(tiles)
-    for flip, piece in enumerate(pieces):
+    whole = tiles * tiles // 2
+    for flip, parts in enumerate(pieces):
         other = jnp.bitwise_xor(me, flip)
-        for k in range(tiles * tiles // 2):
-            value = piece[pl.ds(k * strip, strip), :]
+        each = whole // len(parts)
+        for k in range(whole):
+            value = parts[k // each][pl.ds(k % each * strip, strip), :]
             if k < len(blocks):
                 i, j = blocks[k]
                 root[pl.ds(pl.multiple_of(i * TILE + other * strip, strip), strip), block(j)] = value
@@ -174,7 +177,7 @@
                 folded[pl.ds(pl.multiple_of(at, strip), strip), :] = value
     row = lax.broadcasted_iota(jnp.int32, (TILE, TILE), 0)
     column = lax.broadcasted_iota(jnp.int32, (TILE, TILE), 1)
-    lines = pieces[0][pl.ds(tiles * tiles // 2 * strip, EXTRA), :].astype(F32)
+    lines = pieces[0][0][pl.ds(whole * strip, EXTRA), :].astype(F32)
     for i in range(tiles):
         value = folded[block(i // 2), :].astype(F32)
         value = jnp.where(row >= column if i % 2 == 0 else row < column, value, value.T)
@@ -186,18 +189,25 @@
             root[block(j), block(i)] = root[block(i), block(j)].T
 
 
-def columns_kernel(groups, split, me_ref, rows_ref, cols_ref, *refs):
-    count = sum(split)
-    pieces, terms, outs = refs[:groups], refs[groups : groups + count], refs[groups + count : 2 * groups + count]
-    left, folded, masked, mixed = refs[2 * groups + count :]
+def dealt(refs, counts):
+    lists = []
+    for count in counts:
+        lists.append(refs[:count])
+        refs = refs[count:]
+    return lists, refs
+
+
+def columns_kernel(groups, held, split, me_ref, rows_ref, cols_ref, *refs):
+    pieces, refs = dealt(refs, held)
+    terms, refs = dealt(refs, split)
+    outs, (left, folded, masked, mixed) = refs[:groups], refs[groups:]
     me = me_ref[0]
     width, strip = masked.shape
     unfold(pieces, me, left, folded)
-    part = width // len(split)
+    part = width // len(terms)
     column = lax.broadcasted_iota(jnp.int32, (part, strip), 1) + me * strip
     row = lax.broadcasted_iota(jnp.int32, (part, strip), 0)
-    for index, number in enumerate(split):
-        used, terms = terms[:number], terms[number:]
+    for index, used in enumerate(terms):
         total = functools.reduce(lambda a, b: a + b, [term[pl.ds(0, part), :].astype(F32) for term in used])
         keep = (row + index * part < rows_ref[0]) & (column < cols_ref[0])
         masked[pl.ds(index * part, part), :] = jnp.where(keep, total, 0.0).astype(BF16)
@@ -209,10 +219,10 @@
 def left_columns(me, rows_valid, cols_valid, pieces, terms, width):
     groups = len(pieces)
     strip = width // groups
-    flat = [term for part in terms for term in part]
+    flat = [array for part in (*pieces, *terms) for array in part]
     return pl.pallas_call(
-        functools.partial(columns_kernel, groups, [len(part) for part in terms]),
-        in_specs=[SMEM_SPEC] * 3 + [VMEM_SPEC] * (groups + len(flat)),
+        functools.partial(columns_kernel, groups, [len(part) for part in pieces], [len(part) for part in terms]),
+        in_specs=[SMEM_SPEC] * 3 + [VMEM_SPEC] * len(flat),
         out_specs=[VMEM_SPEC] * groups,
         out_shape=[pltpu.VMEM((strip, strip), BF16)] * groups,
         scratch_shapes=[
@@ -224,24 +234,25 @@
         compiler_params=pltpu.CompilerParams(vmem_limit_bytes=VMEM),
         cost_estimate=cost(2 * strip * width**2, 4 * width**2),
         name="left_columns",
-    )(me, rows_valid, cols_valid, *pieces, *flat)
-
-
-def rows_kernel(groups, me_ref, rows_ref, cols_ref, *refs):
-    pieces, strips, (out, right, folded) = refs[:groups], refs[groups : 2 * groups], refs[2 * groups :]
+    )(me, rows_valid, cols_valid, *flat)
+
+
+def rows_kernel(groups, held, me_ref, rows_ref, cols_ref, *refs):
+    pieces, refs = dealt(refs, held)
+    strips, (out, right, folded, mixed) = refs[:groups], refs[groups:]
     me = me_ref[0]
     width = right.shape[0]
     strip = width // groups
     unfold(pieces, me, right, folded)
-    value = functools.reduce(
-        lambda a, b: a + b,
-        [
-            jnp.dot(
-                part[...], right[strip_of(jnp.bitwise_xor(me, flip), strip), :], preferred_element_type=F32
-            )
-            for flip, part in enumerate(strips)
-        ],
-    )
+    if strip % 128 == 0:
+        for flip, part in enumerate(strips):
+            mixed[:, strip_of(jnp.bitwise_xor(me, flip), strip)] = part[...]
+        value = jnp.dot(mixed[...], right[...], preferred_element_type=F32)
+    else:
+        value = 0.0
+        for flip, part in enumerate(strips):
+            rows = right[strip_of(jnp.bitwise_xor(me, flip), strip), :]
+            value += jnp.dot(part[...], rows, preferred_element_type=F32)
     column = lax.broadcasted_iota(jnp.int32, (strip, width), 1)
     row = lax.broadcasted_iota(jnp.int32, (strip, width), 0) + me * strip
     out[0] = jnp.where((row < rows_ref[0]) & (column < cols_ref[0]), value, 0.0).astype(BF16)
@@ -250,16 +261,21 @@
 def update_rows(me, rows_valid, cols_valid, pieces, strips, width):
     groups = len(pieces)
     strip = width // groups
+    flat = [array for part in pieces for array in part]
     return pl.pallas_call(
-        functools.partial(rows_kernel, groups),
-        in_specs=[SMEM_SPEC] * 3 + [VMEM_SPEC] * (2 * groups),
+        functools.partial(rows_kernel, groups, [len(part) for part in pieces]),
+        in_specs=[SMEM_SPEC] * 3 + [VMEM_SPEC] * (len(flat) + groups),
         out_specs=VMEM_SPEC,
         out_shape=jax.ShapeDtypeStruct((1, strip, width), BF16),
-        scratch_shapes=[pltpu.VMEM((width, width), BF16), pltpu.VMEM((width // 2, TILE), BF16)],
+        scratch_shapes=[
+            pltpu.VMEM((width, width), BF16),
+            pltpu.VMEM((width // 2, TILE), BF16),
+            pltpu.VMEM((strip, width), BF16),
+        ],
         compiler_params=pltpu.CompilerParams(vmem_limit_bytes=VMEM),
         cost_estimate=cost(2 * strip * width**2, 4 * width**2),
         name="update_rows",
-    )(me, rows_valid, cols_valid, *pieces, *strips)
+    )(me, rows_valid, cols_valid, *flat, *strips)
 
 
 def added(*terms):
@@ -269,7 +285,6 @@
 def on_device(grads, left_roots, right_roots, rows_valid, cols_valid):
     groups = lax.axis_size("dp")
     me = lax.axis_index("dp").astype(jnp.int32).reshape(1)
-    offset = lax.axis_size("shard") // 2
     width = grads.shape[-1]
     half, strip = width // 2, width // groups
     plain = grads
@@ -278,35 +293,49 @@
     )
 
     if groups == 4:
-        sent_0, sent_1, left, right = messages(
-            me, grads, left_roots, right_roots, groups, [[(1, 0), (3, 0)], [(2, 1), (3, 1)]]
-        )
-        sent_0, sent_1 = swapped(sent_0, 1), swapped(sent_1, 2)
-        left, right = shifted((left, right), "shard", offset)
+        far_0, far_1, near_0, near_1, left, right = messages(
+            me, grads, left_roots, right_roots, groups, [[(3, 0)], [(3, 1)], [(1, 0)], [(2, 1)]]
+        )
+        far_0, far_1 = swapped(far_0, 1, "far_0"), swapped(far_1, 2, "far_1")
+        near_0, near_1 = swapped(near_0, 1, "near_0"), swapped(near_1, 2, "near_1")
+        left, right = shifted(left, "left"), shifted(right, "right")
         kept = pick(me, grads, groups, [[(2, 0)], [(1, 1)], [(0, 0)], [(0, 1)]])
-        via_0, via_1 = added(kept[0], sent_0[half:]).astype(BF16), added(kept[1], sent_1[half:]).astype(BF16)
-        left = after(left, via_0, via_1)
-        via_0, via_1 = swapped(via_0, 2), swapped(via_1, 1)
-        lefts = [left, swapped(left, 1), swapped(left, 2)]
-        lefts.append(swapped(lefts[1], 2))
+        via_0, via_1 = added(kept[0], far_0).astype(BF16), added(kept[1], far_1).astype(BF16)
+        left = after(left, via_0, via_1, near_0, near_1)
+        via_0, via_1 = swapped(via_0, 2, "via_0"), swapped(via_1, 1, "via_1")
+        left_1, left_2 = swapped(left, 1, "left_1"), swapped(left, 2, "left_2")
+        cut = (left.shape[0] - EXTRA) // 2
+        left_3 = [
+            swapped(left_1[:cut], 2, "left_3a"),
+            swapped(left_2[cut : 2 * cut], 1, "left_3b"),
+        ]
         strips = left_columns(
-            me, rows_valid, cols_valid, lefts, [[kept[2], sent_0, via_0], [kept[3], sent_1, via_1]], width
+            me,
+            rows_valid,
+            cols_valid,
+            [[left], [left_1], [left_2], left_3],
+            [[kept[2], near_0, via_0], [kept[3], near_1, via_1]],
+            width,
         )
         right = after(right, via_0, via_1)
-        rights = [right, swapped(right, 1), swapped(right, 2)]
-        rights.append(swapped(after(rights[2], strips[0]), 1))
+        right_1, right_2 = swapped(right, 1, "right_1"), swapped(right, 2, "right_2")
+        right_3 = [
+            swapped(after(right_1[:cut], strips[0]), 2, "right_3a"),
+            swapped(after(right_2[cut : 2 * cut], strips[0]), 1, "right_3b"),
+        ]
+        rights = [[right], [right_1], [right_2], right_3]
     else:
         left, right = messages(me, grads, left_roots, right_roots, groups, [])
-        left, right = shifted((left, right), "shard", offset)
+        left, right = shifted(left, "left"), shifted(right, "right")
         parts = [
             lax.dynamic_slice_in_dim(plain[0, 0], jnp.bitwise_xor(me[0], flip) * strip, strip, 1)
             for flip in range(groups)
         ]
-        terms = [parts[:1] + [swapped(parts[flip], flip) for flip in range(1, groups)]]
-        lefts = [left] + [swapped(left, flip) for flip in range(1, groups)]
+        terms = [parts[:1] + [swapped(parts[flip], flip, "grad") for flip in range(1, groups)]]
+        lefts = [[left]] + [[swapped(left, flip, "left")] for flip in range(1, groups)]
         strips = left_columns(me, rows_valid, cols_valid, lefts, terms, width)
-        rights = [right] + [swapped(right, flip) for flip in range(1, groups)]
-    strips = [strips[0]] + [swapped(strips[flip], flip) for flip in range(1, groups)]
+        rights = [[right]] + [[swapped(right, flip, "right")] for flip in range(1, groups)]
+    strips = [strips[0]] + [swapped(strips[flip], flip, "strip_%d" % flip) for flip in range(1, groups)]
     return update_rows(me, rows_valid, cols_valid, rights, strips, width)
 
 

time: 62.1 us -> 58.7 us (0.945)
  the two profiles are of different devices: /device:TPU:14 before, /device:TPU:0 now
where the time goes in v5:
time: 58.7 us; the launch traced here: 58.6 us
  starting transfers between devices  27 us (46%)
  waiting for transfers between devices  24.1 us (41%)
  Pallas kernels  5.96 us (10%)
  between operations  1.38 us (2%)
    ppermute x17, starting transfers between devices, swapped(): lax.ppermute(value, 'dp', [(source, source ^ flip) for source in range(co...  20.8 us
    ppermute x17, waiting for transfers between devices, swapped(): lax.ppermute(value, 'dp', [(source, source ^ flip) for source in range(co...  14 us
    ppermute x2, waiting for transfers between devices, shifted(): lax.ppermute(value, 'shard', [(source, (source + count // 2) % count) for...  10 us
    ppermute x2, starting transfers between devices, shifted(): lax.ppermute(value, 'shard', [(source, (source + count // 2) % count) for...  6.2 us
    pallas_call x1, Pallas kernels, messages(): pl.pallas_call(functools.partial(messages_kernel, wanted), in_specs=[SMEM...  1.92 us
    pallas_call x1, Pallas kernels, update_rows(): pl.pallas_call(functools.partial(rows_kernel, groups, [len(part) for part...  1.77 us
    pallas_call x1, Pallas kernels, pick(): pl.pallas_call(functools.partial(pick_kernel, wanted), in_specs=[SMEM_SPE...  1.23 us
  transfers between devices with their start and end apart: 19, of which 11 were waited for; matrix products, arithmetic and copies ran while one was open for 0% of the time, Pallas kernels for 4%

profile of v5, /device:TPU:0, one launch (start us, length us, event | category | flops | bytes accessed | tf_op | source)
XLA Modules:
  0.0 58.6 jit_solution(14802187863826105763)
XLA Ops:
  0.0 1.9 %messages.1 = (bf16[512,256]{1,0:T(8,128)(2,1)S(1)}, bf16[512,256]{1,0:T(8,128)(2,1)S(1)}, bf16[512,256]{1,0:T(8,128)(2,1)S(1)}, bf16[512,256]{1,0:T(8,128)(2,1)...) custom-call(s32[1]{0:T(128)} %bitcast.me_ref, bf16[1,1,1024,1024]{3,2,1,0:T(8,128)(2,1)} %grad_ref.3, ...), custom_call_target="tpu_custom_call" | custom-call | tf_op jit(solution)/shard_map/messages/pallas_call | solution.py:146
  1.9 3.0 %collective-permute-start.1 = (bf16[512,256]{1,0:T(8,128)(2,1)S(1)}, bf16[512,256]{1,0:T(8,128)(2,1)S(1)}, u32[]{:S(2)}, u32[]{:S(2)}) collective-permute-start(bf16[512,256]{1,0:T(8,128)(2,1)S(1)} %get-tuple-element.25), channel_id=1, source_target_pairs={{0,8},{8,0},{16,24},{24,16},{1,9},{9,1},{17,25},{25,17},{2,10},{10... | collective-permute-start | bytes 786440 | tf_op jit(solution)/shard_map/far_0/ppermute | solution.py:29
  4.9 1.5 %collective-permute-start.3 = (bf16[512,256]{1,0:T(8,128)(2,1)S(1)}, bf16[512,256]{1,0:T(8,128)(2,1)S(1)}, u32[]{:S(2)}, u32[]{:S(2)}) collective-permute-start(bf16[512,256]{1,0:T(8,128)(2,1)S(1)} %get-tuple-element.27), channel_id=1, source_target_pairs={{0,16},{8,24},{16,0},{24,8},{1,17},{9,25},{17,1},{25,9},{2,18},{10... | collective-permute-start | bytes 786440 | tf_op jit(solution)/shard_map/far_1/ppermute | solution.py:29
  6.5 0.5 collective-permute-start.8
  7.0 3.0 %collective-permute-start.7 = (bf16[528,256]{1,0:T(8,128)(2,1)S(1)}, bf16[528,256]{1,0:T(8,128)(2,1)S(1)}, u32[]{:S(2)}, u32[]{:S(2)}) collective-permute-start(bf16[528,256]{1,0:T(8,128)(2,1)S(1)} %get-tuple-element.29), channel_id=1, source_target_pairs={{0,4},{1,5},{2,6},{3,7},{4,0},{5,1},{6,2},{7,3},{8,12},{9,13},{10,... | collective-permute-start | bytes 811016 | tf_op jit(solution)/shard_map/left/ppermute | solution.py:23
  10.1 1.2 %pick_kept.1 = (bf16[512,256]{1,0:T(8,128)(2,1)S(1)}, bf16[512,256]{1,0:T(8,128)(2,1)S(1)}, bf16[512,256]{1,0:T(8,128)(2,1)S(1)}, bf16[512,256]{1,0:T(8,128)(2,1)S(1)}) custom-call(s32[1]{0:T(128)} %bitcast.me_ref, bf16[1,1,1024,1024]{3,2,1,0:T(8,128)(2,1)} %grad_ref.3), custom_call_target="tpu_custom_call" | custom-call | tf_op jit(solution)/shard_map/pick_kept/pallas_call | solution.py:77
  11.3 0.7 %collective-permute-done.1 = bf16[512,256]{1,0:T(8,128)(2,1)S(1)} collective-permute-done((bf16[512,256]{1,0:T(8,128)(2,1)S(1)}, bf16[512,256]{1,0:T(8,128)(2,1)S(1)}, u32[]{:S(2)}, u32[]{:S(2)}) %collective-permute-start.1) | collective-permute-done | bytes 262176 | tf_op jit(solution)/shard_map/far_0/ppermute | solution.py:29
  12.1 3.2 %collective-permute-start = (bf16[528,256]{1,0:T(8,128)(2,1)S(1)}, bf16[528,256]{1,0:T(8,128)(2,1)S(1)}, u32[]{:S(2)}, u32[]{:S(2)}) collective-permute-start(bf16[528,256]{1,0:T(8,128)(2,1)S(1)} %get-tuple-element.23), channel_id=1, source_target_pairs={{0,4},{1,5},{2,6},{3,7},{4,0},{5,1},{6,2},{7,3},{8,12},{9,13},{10,... | collective-permute-start | bytes 811016 | tf_op jit(solution)/shard_map/right/ppermute | solution.py:23
  15.3 1.6 %collective-permute-start.2 = (bf16[512,256]{1,0:T(8,128)(2,1)S(1)}, bf16[512,256]{1,0:T(8,128)(2,1)S(1)}, u32[]{:S(2)}, u32[]{:S(2)}) collective-permute-start(bf16[512,256]{1,0:T(8,128)(2,1)S(1)} %add_convert_fusion.1), channel_id=1, source_target_pairs={{0,16},{8,24},{16,0},{24,8},{1,17},{9,25},{17,1},{25,9},{2,18},{10... | collective-permute-start | bytes 786440 | tf_op jit(solution)/shard_map/via_0/ppermute | solution.py:29
  17.0 1.6 %collective-permute-start.4 = (bf16[512,256]{1,0:T(8,128)(2,1)S(1)}, bf16[512,256]{1,0:T(8,128)(2,1)S(1)}, u32[]{:S(2)}, u32[]{:S(2)}) collective-permute-start(bf16[512,256]{1,0:T(8,128)(2,1)S(1)} %add_convert_fusion), channel_id=1, source_target_pairs={{0,8},{8,0},{16,24},{24,16},{1,9},{9,1},{17,25},{25,17},{2,10},{10... | collective-permute-start | bytes 786440 | tf_op jit(solution)/shard_map/via_1/ppermute | solution.py:29
  18.6 1.2 %collective-permute-done.9.refs_9_ = bf16[512,256]{1,0:T(8,128)(2,1)S(1)} collective-permute-done((bf16[512,256]{1,0:T(8,128)(2,1)S(1)}, bf16[512,256]{1,0:T(8,128)(2,1)S(1)}, u32[]{:S(2)}, u32[]{:S(2)}) %collective-permute-start.9) | collective-permute-done | bytes 262176 | tf_op jit(solution)/shard_map/near_1/ppermute | solution.py:29
  19.8 8.5 %collective-permute-done.7.refs_0_ = bf16[528,256]{1,0:T(8,128)(2,1)S(1)} collective-permute-done((bf16[528,256]{1,0:T(8,128)(2,1)S(1)}, bf16[528,256]{1,0:T(8,128)(2,1)S(1)}, u32[]{:S(2)}, u32[]{:S(2)}) %collective-permute-start.7) | collective-permute-done | bytes 270368 | tf_op jit(solution)/shard_map/left/ppermute | solution.py:23
  28.3 1.5 %collective-permute-start.10 = (bf16[528,256]{1,0:T(8,128)(2,1)S(1)}, bf16[528,256]{1,0:T(8,128)(2,1)S(1)}, u32[]{:S(2)}, u32[]{:S(2)}) collective-permute-start(bf16[528,256]{1,0:T(8,128)(2,1)S(1)} %collective-permute-done.7.refs_0_), channel_id=1, source_target_pairs={{0,8},{8,0},{16,24},{24,16},{1,9},{9,1},{17,25},{25,17},{2,10},{10... | collective-permute-start | bytes 811016 | tf_op jit(solution)/shard_map/left_1/ppermute | solution.py:29
  29.7 1.5 %collective-permute-start.11 = (bf16[528,256]{1,0:T(8,128)(2,1)S(1)}, bf16[528,256]{1,0:T(8,128)(2,1)S(1)}, u32[]{:S(2)}, u32[]{:S(2)}) collective-permute-start(bf16[528,256]{1,0:T(8,128)(2,1)S(1)} %collective-permute-done.7.refs_0_), channel_id=1, source_target_pairs={{0,16},{8,24},{16,0},{24,8},{1,17},{9,25},{17,1},{25,9},{2,18},{10... | collective-permute-start | bytes 811016 | tf_op jit(solution)/shard_map/left_2/ppermute | solution.py:29
  31.3 1.6 %collective-permute-done.refs_0_ = bf16[528,256]{1,0:T(8,128)(2,1)S(1)} collective-permute-done((bf16[528,256]{1,0:T(8,128)(2,1)S(1)}, bf16[528,256]{1,0:T(8,128)(2,1)S(1)}, u32[]{:S(2)}, u32[]{:S(2)}) %collective-permute-start) | collective-permute-done | bytes 270368 | tf_op jit(solution)/shard_map/right/ppermute | solution.py:23
  32.8 1.6 %collective-permute-start.6 = (bf16[528,256]{1,0:T(8,128)(2,1)S(1)}, bf16[528,256]{1,0:T(8,128)(2,1)S(1)}, u32[]{:S(2)}, u32[]{:S(2)}) collective-permute-start(bf16[528,256]{1,0:T(8,128)(2,1)S(1)} %collective-permute-done.refs_0_), channel_id=1, source_target_pairs={{0,16},{8,24},{16,0},{24,8},{1,17},{9,25},{17,1},{25,9},{2,18},{10... | collective-permute-start | bytes 811016 | tf_op jit(solution)/shard_map/right_2/ppermute | solution.py:29
  34.4 1.5 %collective-permute-start.5 = (bf16[528,256]{1,0:T(8,128)(2,1)S(1)}, bf16[528,256]{1,0:T(8,128)(2,1)S(1)}, u32[]{:S(2)}, u32[]{:S(2)}) collective-permute-start(bf16[528,256]{1,0:T(8,128)(2,1)S(1)} %collective-permute-done.refs_0_), channel_id=1, source_target_pairs={{0,8},{8,0},{16,24},{24,16},{1,9},{9,1},{17,25},{25,17},{2,10},{10... | collective-permute-start | bytes 811016 | tf_op jit(solution)/shard_map/right_1/ppermute | solution.py:29
  35.9 0.6 collective-permute-start.12
  36.5 1.6 %collective-permute-done.11.refs_2_ = bf16[528,256]{1,0:T(8,128)(2,1)S(1)} collective-permute-done((bf16[528,256]{1,0:T(8,128)(2,1)S(1)}, bf16[528,256]{1,0:T(8,128)(2,1)S(1)}, u32[]{:S(2)}, u32[]{:S(2)}) %collective-permute-start.11) | collective-permute-done | bytes 270368 | tf_op jit(solution)/shard_map/left_2/ppermute | solution.py:29
  39.5 5.3 %collective-permute-done.12.refs_3_ = bf16[256,256]{1,0:T(8,128)(2,1)S(1)} collective-permute-done((bf16[256,256]{1,0:T(8,128)(2,1)S(1)}, bf16[256,256]{1,0:T(8,128)(2,1)S(1)}, u32[]{:S(2)}, u32[]{:S(2)}) %collective-permute-start.12) | collective-permute-done | bytes 131104 | tf_op jit(solution)/shard_map/left_3a/ppermute | solution.py:29
  44.8 1.0 %left_columns.1 = (bf16[256,256]{1,0:T(8,128)(2,1)S(1)}, bf16[256,256]{1,0:T(8,128)(2,1)S(1)}, bf16[256,256]{1,0:T(8,128)(2,1)S(1)}, bf16[256,256]{1,0:T(8,128)(2,1)S(1)}) custom-call(s32[1]{0:T(128)} %bitcast.me_ref, s32[1]{0:T(128)S(6)} %copy.6.rows_ref, s32[1]{0:T(128)S(6)} %copy.7.cols_ref, bf16[528,256]{1,0:T(8,128)(2,1)S(1)} %collective-permute-done.7.refs_0_, ...), custom_call_target="tpu_custom_call" | custom-call | flops 536870912 | bytes 4194304 | tf_op jit(solution)/shard_map/left_columns/pallas_call | solution.py:223
  45.9 1.0 %collective-permute-start.16 = (bf16[256,256]{1,0:T(8,128)(2,1)S(1)}, bf16[256,256]{1,0:T(8,128)(2,1)S(1)}, u32[]{:S(2)}, u32[]{:S(2)}) collective-permute-start(bf16[256,256]{1,0:T(8,128)(2,1)S(1)} %get-tuple-element.38), channel_id=1, source_target_pairs={{0,8},{8,0},{16,24},{24,16},{1,9},{9,1},{17,25},{25,17},{2,10},{10... | collective-permute-start | bytes 393224 | tf_op jit(solution)/shard_map/strip_1/ppermute | solution.py:29
  46.9 1.1 %collective-permute-start.17 = (bf16[256,256]{1,0:T(8,128)(2,1)S(1)}, bf16[256,256]{1,0:T(8,128)(2,1)S(1)}, u32[]{:S(2)}, u32[]{:S(2)}) collective-permute-start(bf16[256,256]{1,0:T(8,128)(2,1)S(1)} %get-tuple-element.39), channel_id=1, source_target_pairs={{0,16},{8,24},{16,0},{24,8},{1,17},{9,25},{17,1},{25,9},{2,18},{10... | collective-permute-start | bytes 393224 | tf_op jit(solution)/shard_map/strip_2/ppermute | solution.py:29
  48.0 1.4 %collective-permute-start.18 = (bf16[256,256]{1,0:T(8,128)(2,1)S(1)}, bf16[256,256]{1,0:T(8,128)(2,1)S(1)}, u32[]{:S(2)}, u32[]{:S(2)}) collective-permute-start(bf16[256,256]{1,0:T(8,128)(2,1)S(1)} %get-tuple-element.40), channel_id=1, source_target_pairs={{0,24},{8,16},{16,8},{24,0},{1,25},{9,17},{17,9},{25,1},{2,26},{10... | collective-permute-start | bytes 393224 | tf_op jit(solution)/shard_map/strip_3/ppermute | solution.py:29
  49.4 1.0 %collective-permute-start.15 = (bf16[256,256]{1,0:T(8,128)(2,1)S(1)}, bf16[256,256]{1,0:T(8,128)(2,1)S(1)}, u32[]{:S(2)}, u32[]{:S(2)}) collective-permute-start(bf16[256,256]{1,0:T(8,128)(2,1)S(1)} %slice.19), channel_id=1, source_target_pairs={{0,8},{8,0},{16,24},{24,16},{1,9},{9,1},{17,25},{25,17},{2,10},{10... | collective-permute-start | bytes 393224 | tf_op jit(solution)/shard_map/right_3b/ppermute | solution.py:29
  50.5 1.2 %collective-permute-start.14 = (bf16[256,256]{1,0:T(8,128)(2,1)S(1)}, bf16[256,256]{1,0:T(8,128)(2,1)S(1)}, u32[]{:S(2)}, u32[]{:S(2)}) collective-permute-start(bf16[256,256]{1,0:T(8,128)(2,1)S(1)} %slice.16), channel_id=1, source_target_pairs={{0,16},{8,24},{16,0},{24,8},{1,17},{9,25},{17,1},{25,9},{2,18},{10... | collective-permute-start | bytes 393224 | tf_op jit(solution)/shard_map/right_3a/ppermute | solution.py:29
  51.6 0.6 %collective-permute-done.16.refs_6_ = bf16[256,256]{1,0:T(8,128)(2,1)S(1)} collective-permute-done((bf16[256,256]{1,0:T(8,128)(2,1)S(1)}, bf16[256,256]{1,0:T(8,128)(2,1)S(1)}, u32[]{:S(2)}, u32[]{:S(2)}) %collective-permute-start.16) | collective-permute-done | bytes 131104 | tf_op jit(solution)/shard_map/strip_1/ppermute | solution.py:29
  52.3 2.5 %collective-permute-done.17.refs_7_ = bf16[256,256]{1,0:T(8,128)(2,1)S(1)} collective-permute-done((bf16[256,256]{1,0:T(8,128)(2,1)S(1)}, bf16[256,256]{1,0:T(8,128)(2,1)S(1)}, u32[]{:S(2)}, u32[]{:S(2)}) %collective-permute-start.17) | collective-permute-done | bytes 131104 | tf_op jit(solution)/shard_map/strip_2/ppermute | solution.py:29
  54.7 0.7 %collective-permute-done.18.refs_8_ = bf16[256,256]{1,0:T(8,128)(2,1)S(1)} collective-permute-done((bf16[256,256]{1,0:T(8,128)(2,1)S(1)}, bf16[256,256]{1,0:T(8,128)(2,1)S(1)}, u32[]{:S(2)}, u32[]{:S(2)}) %collective-permute-start.18) | collective-permute-done | bytes 131104 | tf_op jit(solution)/shard_map/strip_3/ppermute | solution.py:29
  55.5 0.3 collective-permute-done.15.refs_4_
  55.8 1.0 %collective-permute-done.14.refs_3_ = bf16[256,256]{1,0:T(8,128)(2,1)S(1)} collective-permute-done((bf16[256,256]{1,0:T(8,128)(2,1)S(1)}, bf16[256,256]{1,0:T(8,128)(2,1)S(1)}, u32[]{:S(2)}, u32[]{:S(2)}) %collective-permute-start.14) | collective-permute-done | bytes 131104 | tf_op jit(solution)/shard_map/right_3a/ppermute | solution.py:29
  56.8 1.8 %update_rows.1 = bf16[1,256,1024]{2,1,0:T(8,128)(2,1)} custom-call(s32[1]{0:T(128)} %bitcast.me_ref, s32[1]{0:T(128)S(6)} %copy.6.rows_ref, s32[1]{0:T(128)S(6)} %copy.7.cols_ref, bf16[528,256]{1,0:T(8,128)(2,1)S(1)} %collective-permute-done.refs_0_, bf16[528,256]{1,0:T(8,128)(2,1)S(1)} %collective-permute-done.5.refs_1_, ...), custom_call_target="tpu_custom_call" | custom-call | flops 536870912 | bytes 4194304 | tf_op jit(solution)/shard_map/update_rows/pallas_call | solution.py:265
  (16 shorter events, 0.3 us)
Async XLA Ops:
  1.9 10.1 %collective-permute-start.1 = (bf16[512,256]{1,0:T(8,128)(2,1)S(1)}, bf16[512,256]{1,0:T(8,128)(2,1)S(1)}, u32[]{:S(2)}, u32[]{:S(2)}) collective-permute-start(bf16[512,256]{1,0:T(8,128)(2,1)S(1)} %get-tuple-element.25), channel_id=1, source_target_pairs={{0,8},{8,0},{16,24},{24,16},{1,9},{9,1},{17,25},{25,17},{2,10},{10... | collective-permute-start | bytes 786440 | tf_op jit(solution)/shard_map/far_0/ppermute | solution.py:29
  4.9 10.4 %collective-permute-start.3 = (bf16[512,256]{1,0:T(8,128)(2,1)S(1)}, bf16[512,256]{1,0:T(8,128)(2,1)S(1)}, u32[]{:S(2)}, u32[]{:S(2)}) collective-permute-start(bf16[512,256]{1,0:T(8,128)(2,1)S(1)} %get-tuple-element.27), channel_id=1, source_target_pairs={{0,16},{8,24},{16,0},{24,8},{1,17},{9,25},{17,1},{25,9},{2,18},{10... | collective-permute-start | bytes 786440 | tf_op jit(solution)/shard_map/far_1/ppermute | solution.py:29
  6.5 10.5 %collective-permute-start.8 = (bf16[512,256]{1,0:T(8,128)(2,1)S(1)}, bf16[512,256]{1,0:T(8,128)(2,1)S(1)}, u32[]{:S(2)}, u32[]{:S(2)}) collective-permute-start(bf16[512,256]{1,0:T(8,128)(2,1)S(1)} %get-tuple-element.30), channel_id=1, source_target_pairs={{0,8},{8,0},{16,24},{24,16},{1,9},{9,1},{17,25},{25,17},{2,10},{10... | collective-permute-start | bytes 786440 | tf_op jit(solution)/shard_map/near_0/ppermute | solution.py:29
  7.0 12.8 %collective-permute-start.9 = (bf16[512,256]{1,0:T(8,128)(2,1)S(1)}, bf16[512,256]{1,0:T(8,128)(2,1)S(1)}, u32[]{:S(2)}, u32[]{:S(2)}) collective-permute-start(bf16[512,256]{1,0:T(8,128)(2,1)S(1)} %get-tuple-element.31), channel_id=1, source_target_pairs={{0,16},{8,24},{16,0},{24,8},{1,17},{9,25},{17,1},{25,9},{2,18},{10... | collective-permute-start | bytes 786440 | tf_op jit(solution)/shard_map/near_1/ppermute | solution.py:29
  7.0 21.2 %collective-permute-start.7 = (bf16[528,256]{1,0:T(8,128)(2,1)S(1)}, bf16[528,256]{1,0:T(8,128)(2,1)S(1)}, u32[]{:S(2)}, u32[]{:S(2)}) collective-permute-start(bf16[528,256]{1,0:T(8,128)(2,1)S(1)} %get-tuple-element.29), channel_id=1, source_target_pairs={{0,4},{1,5},{2,6},{3,7},{4,0},{5,1},{6,2},{7,3},{8,12},{9,13},{10,... | collective-permute-start | bytes 811016 | tf_op jit(solution)/shard_map/left/ppermute | solution.py:23
  12.1 20.8 %collective-permute-start = (bf16[528,256]{1,0:T(8,128)(2,1)S(1)}, bf16[528,256]{1,0:T(8,128)(2,1)S(1)}, u32[]{:S(2)}, u32[]{:S(2)}) collective-permute-start(bf16[528,256]{1,0:T(8,128)(2,1)S(1)} %get-tuple-element.23), channel_id=1, source_target_pairs={{0,4},{1,5},{2,6},{3,7},{4,0},{5,1},{6,2},{7,3},{8,12},{9,13},{10,... | collective-permute-start | bytes 811016 | tf_op jit(solution)/shard_map/right/ppermute | solution.py:23
  15.3 17.5 %collective-permute-start.2 = (bf16[512,256]{1,0:T(8,128)(2,1)S(1)}, bf16[512,256]{1,0:T(8,128)(2,1)S(1)}, u32[]{:S(2)}, u32[]{:S(2)}) collective-permute-start(bf16[512,256]{1,0:T(8,128)(2,1)S(1)} %add_convert_fusion.1), channel_id=1, source_target_pairs={{0,16},{8,24},{16,0},{24,8},{1,17},{9,25},{17,1},{25,9},{2,18},{10... | collective-permute-start | bytes 786440 | tf_op jit(solution)/shard_map/via_0/ppermute | solution.py:29
  17.0 15.8 %collective-permute-start.4 = (bf16[512,256]{1,0:T(8,128)(2,1)S(1)}, bf16[512,256]{1,0:T(8,128)(2,1)S(1)}, u32[]{:S(2)}, u32[]{:S(2)}) collective-permute-start(bf16[512,256]{1,0:T(8,128)(2,1)S(1)} %add_convert_fusion), channel_id=1, source_target_pairs={{0,8},{8,0},{16,24},{24,16},{1,9},{9,1},{17,25},{25,17},{2,10},{10... | collective-permute-start | bytes 786440 | tf_op jit(solution)/shard_map/via_1/ppermute | solution.py:29
  28.3 7.6 %collective-permute-start.10 = (bf16[528,256]{1,0:T(8,128)(2,1)S(1)}, bf16[528,256]{1,0:T(8,128)(2,1)S(1)}, u32[]{:S(2)}, u32[]{:S(2)}) collective-permute-start(bf16[528,256]{1,0:T(8,128)(2,1)S(1)} %collective-permute-done.7.refs_0_), channel_id=1, source_target_pairs={{0,8},{8,0},{16,24},{24,16},{1,9},{9,1},{17,25},{25,17},{2,10},{10... | collective-permute-start | bytes 811016 | tf_op jit(solution)/shard_map/left_1/ppermute | solution.py:29
  29.7 8.4 %collective-permute-start.11 = (bf16[528,256]{1,0:T(8,128)(2,1)S(1)}, bf16[528,256]{1,0:T(8,128)(2,1)S(1)}, u32[]{:S(2)}, u32[]{:S(2)}) collective-permute-start(bf16[528,256]{1,0:T(8,128)(2,1)S(1)} %collective-permute-done.7.refs_0_), channel_id=1, source_target_pairs={{0,16},{8,24},{16,0},{24,8},{1,17},{9,25},{17,1},{25,9},{2,18},{10... | collective-permute-start | bytes 811016 | tf_op jit(solution)/shard_map/left_2/ppermute | solution.py:29
  32.8 16.6 %collective-permute-start.6 = (bf16[528,256]{1,0:T(8,128)(2,1)S(1)}, bf16[528,256]{1,0:T(8,128)(2,1)S(1)}, u32[]{:S(2)}, u32[]{:S(2)}) collective-permute-start(bf16[528,256]{1,0:T(8,128)(2,1)S(1)} %collective-permute-done.refs_0_), channel_id=1, source_target_pairs={{0,16},{8,24},{16,0},{24,8},{1,17},{9,25},{17,1},{25,9},{2,18},{10... | collective-permute-start | bytes 811016 | tf_op jit(solution)/shard_map/right_2/ppermute | solution.py:29
  34.4 16.0 %collective-permute-start.5 = (bf16[528,256]{1,0:T(8,128)(2,1)S(1)}, bf16[528,256]{1,0:T(8,128)(2,1)S(1)}, u32[]{:S(2)}, u32[]{:S(2)}) collective-permute-start(bf16[528,256]{1,0:T(8,128)(2,1)S(1)} %collective-permute-done.refs_0_), channel_id=1, source_target_pairs={{0,8},{8,0},{16,24},{24,16},{1,9},{9,1},{17,25},{25,17},{2,10},{10... | collective-permute-start | bytes 811016 | tf_op jit(solution)/shard_map/right_1/ppermute | solution.py:29
  35.9 8.9 %collective-permute-start.12 = (bf16[256,256]{1,0:T(8,128)(2,1)S(1)}, bf16[256,256]{1,0:T(8,128)(2,1)S(1)}, u32[]{:S(2)}, u32[]{:S(2)}) collective-permute-start(bf16[256,256]{1,0:T(8,128)(2,1)S(1)} %slice.17), channel_id=1, source_target_pairs={{0,16},{8,24},{16,0},{24,8},{1,17},{9,25},{17,1},{25,9},{2,18},{10... | collective-permute-start | bytes 393224 | tf_op jit(solution)/shard_map/left_3a/ppermute | solution.py:29
  38.1 6.7 %collective-permute-start.13 = (bf16[256,256]{1,0:T(8,128)(2,1)S(1)}, bf16[256,256]{1,0:T(8,128)(2,1)S(1)}, u32[]{:S(2)}, u32[]{:S(2)}) collective-permute-start(bf16[256,256]{1,0:T(8,128)(2,1)S(1)} %slice.18), channel_id=1, source_target_pairs={{0,8},{8,0},{16,24},{24,16},{1,9},{9,1},{17,25},{25,17},{2,10},{10... | collective-permute-start | bytes 393224 | tf_op jit(solution)/shard_map/left_3b/ppermute | solution.py:29
  45.9 6.4 %collective-permute-start.16 = (bf16[256,256]{1,0:T(8,128)(2,1)S(1)}, bf16[256,256]{1,0:T(8,128)(2,1)S(1)}, u32[]{:S(2)}, u32[]{:S(2)}) collective-permute-start(bf16[256,256]{1,0:T(8,128)(2,1)S(1)} %get-tuple-element.38), channel_id=1, source_target_pairs={{0,8},{8,0},{16,24},{24,16},{1,9},{9,1},{17,25},{25,17},{2,10},{10... | collective-permute-start | bytes 393224 | tf_op jit(solution)/shard_map/strip_1/ppermute | solution.py:29
  46.9 7.9 %collective-permute-start.17 = (bf16[256,256]{1,0:T(8,128)(2,1)S(1)}, bf16[256,256]{1,0:T(8,128)(2,1)S(1)}, u32[]{:S(2)}, u32[]{:S(2)}) collective-permute-start(bf16[256,256]{1,0:T(8,128)(2,1)S(1)} %get-tuple-element.39), channel_id=1, source_target_pairs={{0,16},{8,24},{16,0},{24,8},{1,17},{9,25},{17,1},{25,9},{2,18},{10... | collective-permute-start | bytes 393224 | tf_op jit(solution)/shard_map/strip_2/ppermute | solution.py:29
  48.0 7.5 %collective-permute-start.18 = (bf16[256,256]{1,0:T(8,128)(2,1)S(1)}, bf16[256,256]{1,0:T(8,128)(2,1)S(1)}, u32[]{:S(2)}, u32[]{:S(2)}) collective-permute-start(bf16[256,256]{1,0:T(8,128)(2,1)S(1)} %get-tuple-element.40), channel_id=1, source_target_pairs={{0,24},{8,16},{16,8},{24,0},{1,25},{9,17},{17,9},{25,1},{2,26},{10... | collective-permute-start | bytes 393224 | tf_op jit(solution)/shard_map/strip_3/ppermute | solution.py:29
  49.4 6.4 %collective-permute-start.15 = (bf16[256,256]{1,0:T(8,128)(2,1)S(1)}, bf16[256,256]{1,0:T(8,128)(2,1)S(1)}, u32[]{:S(2)}, u32[]{:S(2)}) collective-permute-start(bf16[256,256]{1,0:T(8,128)(2,1)S(1)} %slice.19), channel_id=1, source_target_pairs={{0,8},{8,0},{16,24},{24,16},{1,9},{9,1},{17,25},{25,17},{2,10},{10... | collective-permute-start | bytes 393224 | tf_op jit(solution)/shard_map/right_3b/ppermute | solution.py:29
  50.5 6.3 %collective-permute-start.14 = (bf16[256,256]{1,0:T(8,128)(2,1)S(1)}, bf16[256,256]{1,0:T(8,128)(2,1)S(1)}, u32[]{:S(2)}, u32[]{:S(2)}) collective-permute-start(bf16[256,256]{1,0:T(8,128)(2,1)S(1)} %slice.16), channel_id=1, source_target_pairs={{0,16},{8,24},{16,0},{24,8},{1,17},{9,25},{17,1},{25,9},{2,18},{10... | collective-permute-start | bytes 393224 | tf_op jit(solution)/shard_map/right_3a/ppermute | solution.py:29

commit v6 on v5

--- a/solution.py
+++ b/solution.py
@@ -85,55 +85,67 @@
     )(me, grads)
 
 
-def fold_copies(me, root_ref, strips, odd_corners, sems):
+def strip_copies(me, root_ref, strips, sems):
     tiles, strip, _ = strips.shape
     return [
         pltpu.make_async_copy(
             root_ref.at[0, pl.ds(pl.multiple_of(i * TILE + me * strip, strip), strip), :], strips.at[i], sems.at[i]
         )
         for i in range(tiles)
-    ] + [
-        pltpu.make_async_copy(
-            root_ref.at[0, block(2 * pair + 1), block(2 * pair + 1)], odd_corners.at[pair], sems.at[tiles + pair]
-        )
-        for pair in range(tiles // 2)
     ]
 
 
-def fold(me, strips, odd_corners, out):
+def corner_copies(root_ref, corners, sems):
+    return [
+        pltpu.make_async_copy(root_ref.at[0, block(i), block(i)], corners.at[i], sems.at[i])
+        for i in range(corners.shape[0])
+    ]
+
+
+def fold_below(strips, out):
     tiles, strip, _ = strips.shape
-    blocks = below(tiles)
-    for k, (i, j) in enumerate(blocks):
+    for k, (i, j) in enumerate(below(tiles)):
         out[pl.ds(k * strip, strip), :] = strips[i, :, block(j)]
-    row = lax.broadcasted_iota(jnp.int32, (strip, TILE), 0) + me * strip
+
+
+def fold_corners(corners, start, strip, out, base):
+    tiles = corners.shape[0]
+    row = lax.broadcasted_iota(jnp.int32, (strip, TILE), 0) + start
     column = lax.broadcasted_iota(jnp.int32, (strip, TILE), 1)
     on_diag = lax.broadcasted_iota(jnp.int32, (TILE, TILE), 0) == lax.broadcasted_iota(jnp.int32, (TILE, TILE), 1)
+    rows = pl.ds(pl.multiple_of(start, strip), strip) if strip < TILE else pl.ds(0, TILE)
     lines = []
     for pair in range(tiles // 2):
         even, odd = 2 * pair, 2 * pair + 1
-        out[pl.ds((len(blocks) + pair) * strip, strip), :] = jnp.where(
-            row >= column, strips[even, :, block(even)], strips[odd, :, block(odd)]
+        out[pl.ds(base + pair * strip, strip), :] = jnp.where(
+            row >= column, corners[even, rows, :], corners[odd, rows, :]
         )
-        corner = odd_corners[pair].astype(F32)
-        lines.append(jnp.sum(jnp.where(on_diag, corner, 0.0), axis=0, keepdims=True))
+        lines.append(jnp.sum(jnp.where(on_diag, corners[odd].astype(F32), 0.0), axis=0, keepdims=True))
     lines.append(jnp.zeros((EXTRA - len(lines), TILE), F32))
-    out[pl.ds(tiles * tiles // 2 * strip, EXTRA), :] = jnp.concatenate(lines, axis=0).astype(BF16)
+    out[pl.ds(base + tiles // 2 * strip, EXTRA), :] = jnp.concatenate(lines, axis=0).astype(BF16)
 
 
 def messages_kernel(wanted, me_ref, grad_ref, left_ref, right_ref, *refs):
-    outs, (left, right, strips, odd_corners, pick_sems, fold_sems) = refs[: len(wanted)], refs[len(wanted) :]
+    outs, (left, right, right_corners, strips, corners, pick_sems, strip_sems, corner_sems) = (
+        refs[: len(wanted)],
+        refs[len(wanted) :],
+    )
     me = me_ref[0]
+    tiles, strip = strips.shape[1:3]
     copies = pick_copies(wanted, me, grad_ref, outs, pick_sems)
-    roots = [
-        fold_copies(me, root, strips.at[index], odd_corners.at[index], fold_sems.at[index])
+    rooted = [
+        strip_copies(me, root, strips.at[index], strip_sems.at[index])
+        + corner_copies(root, corners.at[index], corner_sems.at[index])
         for index, root in enumerate((left_ref, right_ref))
     ]
-    for copy in roots[0] + roots[1] + copies:
+    for copy in copies + rooted[0] + rooted[1]:
         copy.start()
-    for index, out in enumerate((left, right)):
-        for copy in roots[index]:
-            copy.wait()
-        fold(me, strips.at[index], odd_corners.at[index], out)
+    for copy in rooted[0] + rooted[1]:
+        copy.wait()
+    fold_below(strips.at[0], left)
+    fold_corners(corners.at[0], me * strip, strip, left, len(below(tiles)) * strip)
+    fold_below(strips.at[1], right)
+    fold_corners(corners.at[1], 0, TILE, right_corners, 0)
     for copy in copies:
         copy.wait()
 
@@ -142,51 +154,74 @@
     width = grads.shape[-1]
     strip, tiles = TILE // groups, width // TILE
     count = sum(len(parts) for parts in wanted)
-    folded = pltpu.VMEM((tiles * tiles // 2 * strip + EXTRA, TILE), BF16)
+    low = len(below(tiles)) * strip
     return pl.pallas_call(
         functools.partial(messages_kernel, wanted),
         in_specs=[SMEM_SPEC] + [HBM_SPEC] * 3,
-        out_specs=[VMEM_SPEC] * (len(wanted) + 2),
-        out_shape=picked_shapes(wanted, width, groups) + [folded] * 2,
+        out_specs=[VMEM_SPEC] * (len(wanted) + 3),
+        out_shape=picked_shapes(wanted, width, groups)
+        + [
+            pltpu.VMEM((low + tiles // 2 * strip + EXTRA, TILE), BF16),
+            pltpu.VMEM((low, TILE), BF16),
+            pltpu.VMEM((tiles // 2 * TILE + EXTRA, TILE), BF16),
+        ],
         scratch_shapes=[
             pltpu.VMEM((2, tiles, strip, width), BF16),
-            pltpu.VMEM((2, tiles // 2, TILE, TILE), BF16),
+            pltpu.VMEM((2, tiles, TILE, TILE), BF16),
             pltpu.SemaphoreType.DMA((max(count, 1),)),
-            pltpu.SemaphoreType.DMA((2, tiles + tiles // 2)),
+            pltpu.SemaphoreType.DMA((2, tiles)),
+            pltpu.SemaphoreType.DMA((2, tiles)),
         ],
         compiler_params=pltpu.CompilerParams(vmem_limit_bytes=VMEM),
         name="messages",
     )(me, grads, left, right)
 
 
-def unfold(pieces, me, root, folded):
+def unfold_below(pieces, me, root):
     tiles = root.shape[0] // TILE
     strip = TILE // len(pieces)
     blocks = below(tiles)
-    whole = tiles * tiles // 2
     for flip, parts in enumerate(pieces):
         other = jnp.bitwise_xor(me, flip)
-        each = whole // len(parts)
-        for k in range(whole):
-            value = parts[k // each][pl.ds(k % each * strip, strip), :]
-            if k < len(blocks):
-                i, j = blocks[k]
-                root[pl.ds(pl.multiple_of(i * TILE + other * strip, strip), strip), block(j)] = value
-            else:
-                at = (k - len(blocks)) * TILE + other * strip
-                folded[pl.ds(pl.multiple_of(at, strip), strip), :] = value
+        for k, (i, j) in enumerate(blocks):
+            part, row = 0, k * strip
+            while row >= parts[part].shape[0]:
+                row -= parts[part].shape[0]
+                part += 1
+            at = pl.ds(pl.multiple_of(i * TILE + other * strip, strip), strip)
+            root[at, block(j)] = parts[part][pl.ds(row, strip), :]
+    for i, j in blocks:
+        root[block(j), block(i)] = root[block(i), block(j)].T
+
+
+def unfold_corners(folded, lines, root):
     row = lax.broadcasted_iota(jnp.int32, (TILE, TILE), 0)
     column = lax.broadcasted_iota(jnp.int32, (TILE, TILE), 1)
-    lines = pieces[0][0][pl.ds(whole * strip, EXTRA), :].astype(F32)
-    for i in range(tiles):
+    lines = lines.astype(F32)
+    for i in range(root.shape[0] // TILE):
         value = folded[block(i // 2), :].astype(F32)
         value = jnp.where(row >= column if i % 2 == 0 else row < column, value, value.T)
         if i % 2:
             line = jnp.broadcast_to(lines[i // 2 : i // 2 + 1, :], (TILE, TILE))
             value = jnp.where(row == column, line, value)
         root[block(i), block(i)] = value.astype(BF16)
-        for j in range(i):
-            root[block(j), block(i)] = root[block(i), block(j)].T
+
+
+def unfold(pieces, me, root, folded):
+    tiles = root.shape[0] // TILE
+    strip = TILE // len(pieces)
+    unfold_below(pieces, me, root)
+    base = len(below(tiles)) * strip
+    for flip, parts in enumerate(pieces):
+        other = jnp.bitwise_xor(me, flip)
+        for pair in range(tiles // 2):
+            part, row = 0, base + pair * strip
+            while row >= parts[part].shape[0]:
+                row -= parts[part].shape[0]
+                part += 1
+            at = pl.ds(pl.multiple_of(pair * TILE + other * strip, strip), strip)
+            folded[at, :] = parts[part][pl.ds(row, strip), :]
+    unfold_corners(folded, pieces[0][0][pl.ds(base + tiles // 2 * strip, EXTRA), :], root)
 
 
 def dealt(refs, counts):
@@ -237,13 +272,14 @@
     )(me, rows_valid, cols_valid, *flat)
 
 
-def rows_kernel(groups, held, me_ref, rows_ref, cols_ref, *refs):
+def rows_kernel(groups, held, me_ref, rows_ref, cols_ref, corners_ref, *refs):
     pieces, refs = dealt(refs, held)
-    strips, (out, right, folded, mixed) = refs[:groups], refs[groups:]
+    strips, (out, right, mixed) = refs[:groups], refs[groups:]
     me = me_ref[0]
     width = right.shape[0]
     strip = width // groups
-    unfold(pieces, me, right, folded)
+    unfold_below(pieces, me, right)
+    unfold_corners(corners_ref, corners_ref[pl.ds(width // 2, EXTRA), :], right)
     if strip % 128 == 0:
         for flip, part in enumerate(strips):
             mixed[:, strip_of(jnp.bitwise_xor(me, flip), strip)] = part[...]
@@ -258,24 +294,23 @@
     out[0] = jnp.where((row < rows_ref[0]) & (column < cols_ref[0]), value, 0.0).astype(BF16)
 
 
-def update_rows(me, rows_valid, cols_valid, pieces, strips, width):
+def update_rows(me, rows_valid, cols_valid, corners, pieces, strips, width):
     groups = len(pieces)
     strip = width // groups
     flat = [array for part in pieces for array in part]
     return pl.pallas_call(
         functools.partial(rows_kernel, groups, [len(part) for part in pieces]),
-        in_specs=[SMEM_SPEC] * 3 + [VMEM_SPEC] * (len(flat) + groups),
+        in_specs=[SMEM_SPEC] * 3 + [VMEM_SPEC] * (1 + len(flat) + groups),
         out_specs=VMEM_SPEC,
         out_shape=jax.ShapeDtypeStruct((1, strip, width), BF16),
         scratch_shapes=[
             pltpu.VMEM((width, width), BF16),
-            pltpu.VMEM((width // 2, TILE), BF16),
             pltpu.VMEM((strip, width), BF16),
         ],
         compiler_params=pltpu.CompilerParams(vmem_limit_bytes=VMEM),
         cost_estimate=cost(2 * strip * width**2, 4 * width**2),
         name="update_rows",
-    )(me, rows_valid, cols_valid, *flat, *strips)
+    )(me, rows_valid, cols_valid, corners, *flat, *strips)
 
 
 def added(*terms):
@@ -293,22 +328,23 @@
     )
 
     if groups == 4:
-        far_0, far_1, near_0, near_1, left, right = messages(
+        far_0, far_1, near_0, near_1, left, right, corners = messages(
             me, grads, left_roots, right_roots, groups, [[(3, 0)], [(3, 1)], [(1, 0)], [(2, 1)]]
         )
         far_0, far_1 = swapped(far_0, 1, "far_0"), swapped(far_1, 2, "far_1")
         near_0, near_1 = swapped(near_0, 1, "near_0"), swapped(near_1, 2, "near_1")
-        left, right = shifted(left, "left"), shifted(right, "right")
+        left = shifted(left, "left")
         kept = pick(me, grads, groups, [[(2, 0)], [(1, 1)], [(0, 0)], [(0, 1)]])
         via_0, via_1 = added(kept[0], far_0).astype(BF16), added(kept[1], far_1).astype(BF16)
+        right = shifted(after(right, left), "right")
         left = after(left, via_0, via_1, near_0, near_1)
         via_0, via_1 = swapped(via_0, 2, "via_0"), swapped(via_1, 1, "via_1")
-        left_1, left_2 = swapped(left, 1, "left_1"), swapped(left, 2, "left_2")
+        left_1, left_2 = swapped(after(left, via_1), 1, "left_1"), swapped(after(left, via_0), 2, "left_2")
         cut = (left.shape[0] - EXTRA) // 2
-        left_3 = [
-            swapped(left_1[:cut], 2, "left_3a"),
-            swapped(left_2[cut : 2 * cut], 1, "left_3b"),
-        ]
+        left_3a, left_3b = left_1[:cut], left_2[cut : 2 * cut]
+        tie_0, tie_1 = left_3a, left_3b = after(left_3a, via_0, via_1), after(left_3b, via_0, via_1)
+        corners = shifted(after(corners, right, tie_0, tie_1), "corners")
+        left_3 = [swapped(left_3a, 2, "left_3a"), swapped(left_3b, 1, "left_3b")]
         strips = left_columns(
             me,
             rows_valid,
@@ -319,14 +355,15 @@
         )
         right = after(right, via_0, via_1)
         right_1, right_2 = swapped(right, 1, "right_1"), swapped(right, 2, "right_2")
+        cut = right.shape[0] // 2
         right_3 = [
-            swapped(after(right_1[:cut], strips[0]), 2, "right_3a"),
-            swapped(after(right_2[cut : 2 * cut], strips[0]), 1, "right_3b"),
+            swapped(after(right_1[:cut], left), 2, "right_3a"),
+            swapped(after(right_2[cut:], left), 1, "right_3b"),
         ]
         rights = [[right], [right_1], [right_2], right_3]
     else:
-        left, right = messages(me, grads, left_roots, right_roots, groups, [])
-        left, right = shifted(left, "left"), shifted(right, "right")
+        left, right, corners = messages(me, grads, left_roots, right_roots, groups, [])
+        left, right, corners = shifted(left, "left"), shifted(right, "right"), shifted(corners, "corners")
         parts = [
             lax.dynamic_slice_in_dim(plain[0, 0], jnp.bitwise_xor(me[0], flip) * strip, strip, 1)
             for flip in range(groups)
@@ -336,7 +373,7 @@
         strips = left_columns(me, rows_valid, cols_valid, lefts, terms, width)
         rights = [[right]] + [[swapped(right, flip, "right")] for flip in range(1, groups)]
     strips = [strips[0]] + [swapped(strips[flip], flip, "strip_%d" % flip) for flip in range(1, groups)]
-    return update_rows(me, rows_valid, cols_valid, rights, strips, width)
+    return update_rows(me, rows_valid, cols_valid, corners, rights, strips, width)
 
 
 def solution(mesh):

time: 58.7 us -> 53.4 us (0.910)
  waiting for transfers between devices: 24.1 us -> 18.4 us
    ppermute x17, waiting for transfers between devices: 14 us -> 7.85 us  [swapped(): lax.ppermute(value, 'dp', [(source, source ^ flip) for source in range(co...]
    ppermute x2 -> x3, starting transfers between devices: 6.2 us -> 4.87 us  [shifted(): lax.ppermute(value, 'shard', [(source, (source + count // 2) % count) for...]
    ppermute x17, starting transfers between devices: 20.8 us -> 22 us  [swapped(): lax.ppermute(value, 'dp', [(source, source ^ flip) for source in range(co...]
    ppermute x2 -> x3, waiting for transfers between devices: 10 us -> 10.5 us  [shifted(): lax.ppermute(value, 'shard', [(source, (source + count // 2) % count) for...]
  transfers between devices with their start and end apart: 19 -> 20, of which waited for: 11 -> 5; matrix products, arithmetic and copies ran while one was open for 0% -> 0% of each run, Pallas kernels for 4% -> 4%
where the time goes in v6:
time: 53.4 us; the launch traced here: 53.2 us
  starting transfers between devices  26.9 us (50%)
  waiting for transfers between devices  18.4 us (34%)
  Pallas kernels  6.33 us (12%)
  between operations  1.4 us (3%)
    ppermute x17, starting transfers between devices, swapped(): lax.ppermute(value, 'dp', [(source, source ^ flip) for source in range(co...  22 us
    ppermute x3, waiting for transfers between devices, shifted(): lax.ppermute(value, 'shard', [(source, (source + count // 2) % count) for...  10.5 us
    ppermute x17, waiting for transfers between devices, swapped(): lax.ppermute(value, 'dp', [(source, source ^ flip) for source in range(co...  7.85 us
    ppermute x3, starting transfers between devices, shifted(): lax.ppermute(value, 'shard', [(source, (source + count // 2) % count) for...  4.87 us
    pallas_call x1, Pallas kernels, messages(): pl.pallas_call(functools.partial(messages_kernel, wanted), in_specs=[SMEM...  2.25 us
    pallas_call x1, Pallas kernels, update_rows(): pl.pallas_call(functools.partial(rows_kernel, groups, [len(part) for part...  1.8 us
    pallas_call x1, Pallas kernels, pick(): pl.pallas_call(functools.partial(pick_kernel, wanted), in_specs=[SMEM_SPE...  1.23 us
  transfers between devices with their start and end apart: 20, of which 5 were waited for; matrix products, arithmetic and copies ran while one was open for 0% of the time, Pallas kernels for 4%

profile of v6, /device:TPU:0, one launch (start us, length us, event | category | flops | bytes accessed | tf_op | source)
XLA Modules:
  0.0 53.2 jit_solution(3112343039007270950)
XLA Ops:
  0.0 2.3 %messages.1 = (bf16[512,256]{1,0:T(8,128)(2,1)S(1)}, bf16[512,256]{1,0:T(8,128)(2,1)S(1)}, bf16[512,256]{1,0:T(8,128)(2,1)S(1)}, bf16[512,256]{1,0:T(8,128)(2,1)...) custom-call(s32[1]{0:T(128)} %bitcast.me_ref, ...), custom_call_target="tpu_custom_call" | custom-call | tf_op jit(solution)/shard_map/messages/pallas_call | solution.py:158
  2.3 3.0 %collective-permute-start.2 = (bf16[512,256]{1,0:T(8,128)(2,1)S(1)}, bf16[512,256]{1,0:T(8,128)(2,1)S(1)}, u32[]{:S(2)}, u32[]{:S(2)}) collective-permute-start(bf16[512,256]{1,0:T(8,128)(2,1)S(1)} %get-tuple-element.35), channel_id=1, source_target_pairs={{0,8},{8,0},{16,24},{24,16},{1,9},{9,1},{17,25},{25,17},{2,10},{10... | collective-permute-start | bytes 786440 | tf_op jit(solution)/shard_map/far_0/ppermute | solution.py:29
  5.3 1.5 %collective-permute-start.3 = (bf16[512,256]{1,0:T(8,128)(2,1)S(1)}, bf16[512,256]{1,0:T(8,128)(2,1)S(1)}, u32[]{:S(2)}, u32[]{:S(2)}) collective-permute-start(bf16[512,256]{1,0:T(8,128)(2,1)S(1)} %get-tuple-element.37), channel_id=1, source_target_pairs={{0,16},{8,24},{16,0},{24,8},{1,17},{9,25},{17,1},{25,9},{2,18},{10... | collective-permute-start | bytes 786440 | tf_op jit(solution)/shard_map/far_1/ppermute | solution.py:29
  6.8 2.6 %collective-permute-start = (bf16[528,256]{1,0:T(8,128)(2,1)S(1)}, bf16[528,256]{1,0:T(8,128)(2,1)S(1)}, u32[]{:S(2)}, u32[]{:S(2)}) collective-permute-start(bf16[528,256]{1,0:T(8,128)(2,1)S(1)} %get-tuple-element.32), channel_id=1, source_target_pairs={{0,4},{1,5},{2,6},{3,7},{4,0},{5,1},{6,2},{7,3},{8,12},{9,13},{10,... | collective-permute-start | bytes 811016 | tf_op jit(solution)/shard_map/left/ppermute | solution.py:23
  9.4 0.5 %collective-permute-start.4 = (bf16[512,256]{1,0:T(8,128)(2,1)S(1)}, bf16[512,256]{1,0:T(8,128)(2,1)S(1)}, u32[]{:S(2)}, u32[]{:S(2)}) collective-permute-start(bf16[512,256]{1,0:T(8,128)(2,1)S(1)} %get-tuple-element.38), channel_id=1, source_target_pairs={{0,8},{8,0},{16,24},{24,16},{1,9},{9,1},{17,25},{25,17},{2,10},{10... | collective-permute-start | bytes 786440 | tf_op jit(solution)/shard_map/near_0/ppermute | solution.py:29
  9.9 0.5 collective-permute-start.5
  10.4 1.2 %pick_kept.1 = (bf16[512,256]{1,0:T(8,128)(2,1)S(1)}, bf16[512,256]{1,0:T(8,128)(2,1)S(1)}, bf16[512,256]{1,0:T(8,128)(2,1)S(1)}, bf16[512,256]{1,0:T(8,128)(2,1)S(1)}) custom-call(s32[1]{0:T(128)} %bitcast.me_ref, bf16[1,1,1024,1024]{3,2,1,0:T(8,128)(2,1)} %grad_ref.3), custom_call_target="tpu_custom_call" | custom-call | tf_op jit(solution)/shard_map/pick_kept/pallas_call | solution.py:77
  11.7 0.5 collective-permute-done.2
  12.1 0.1 add_convert_fusion.1
  12.2 2.4 %collective-permute-start.8 = (bf16[512,256]{1,0:T(8,128)(2,1)S(1)}, bf16[512,256]{1,0:T(8,128)(2,1)S(1)}, u32[]{:S(2)}, u32[]{:S(2)}) collective-permute-start(bf16[512,256]{1,0:T(8,128)(2,1)S(1)} %add_convert_fusion.1), channel_id=1, source_target_pairs={{0,16},{8,24},{16,0},{24,8},{1,17},{9,25},{17,1},{25,9},{2,18},{10... | collective-permute-start | bytes 786440 | tf_op jit(solution)/shard_map/via_0/ppermute | solution.py:29
  14.6 0.1 add_convert_fusion
  14.7 1.6 %collective-permute-start.6 = (bf16[512,256]{1,0:T(8,128)(2,1)S(1)}, bf16[512,256]{1,0:T(8,128)(2,1)S(1)}, u32[]{:S(2)}, u32[]{:S(2)}) collective-permute-start(bf16[512,256]{1,0:T(8,128)(2,1)S(1)} %add_convert_fusion), channel_id=1, source_target_pairs={{0,8},{8,0},{16,24},{24,16},{1,9},{9,1},{17,25},{25,17},{2,10},{10... | collective-permute-start | bytes 786440 | tf_op jit(solution)/shard_map/via_1/ppermute | solution.py:29
  16.3 4.9 %collective-permute-done.refs_0_ = bf16[528,256]{1,0:T(8,128)(2,1)S(1)} collective-permute-done((bf16[528,256]{1,0:T(8,128)(2,1)S(1)}, bf16[528,256]{1,0:T(8,128)(2,1)S(1)}, u32[]{:S(2)}, u32[]{:S(2)}) %collective-permute-start) | collective-permute-done | bytes 270368 | tf_op jit(solution)/shard_map/left/ppermute | solution.py:23
  21.1 0.0 collective-permute-start.1
  21.1 0.0 collective-permute-done.4.refs_6_
  21.2 3.1 %collective-permute-done.8.refs_7_ = bf16[512,256]{1,0:T(8,128)(2,1)S(1)} collective-permute-done((bf16[512,256]{1,0:T(8,128)(2,1)S(1)}, bf16[512,256]{1,0:T(8,128)(2,1)S(1)}, u32[]{:S(2)}, u32[]{:S(2)}) %collective-permute-start.8) | collective-permute-done | bytes 262176 | tf_op jit(solution)/shard_map/via_0/ppermute | solution.py:29
  24.3 1.5 %collective-permute-start.9 = (bf16[528,256]{1,0:T(8,128)(2,1)S(1)}, bf16[528,256]{1,0:T(8,128)(2,1)S(1)}, u32[]{:S(2)}, u32[]{:S(2)}) collective-permute-start(bf16[528,256]{1,0:T(8,128)(2,1)S(1)} %collective-permute-done.refs_0_), channel_id=1, source_target_pairs={{0,16},{8,24},{16,0},{24,8},{1,17},{9,25},{17,1},{25,9},{2,18},{10... | collective-permute-start | bytes 811016 | tf_op jit(solution)/shard_map/left_2/ppermute | solution.py:29
  25.8 0.5 %collective-permute-start.7 = (bf16[528,256]{1,0:T(8,128)(2,1)S(1)}, bf16[528,256]{1,0:T(8,128)(2,1)S(1)}, u32[]{:S(2)}, u32[]{:S(2)}) collective-permute-start(bf16[528,256]{1,0:T(8,128)(2,1)S(1)} %collective-permute-done.refs_0_), channel_id=1, source_target_pairs={{0,8},{8,0},{16,24},{24,16},{1,9},{9,1},{17,25},{25,17},{2,10},{10... | collective-permute-start | bytes 811016 | tf_op jit(solution)/shard_map/left_1/ppermute | solution.py:29
  26.3 5.7 %collective-permute-done.1.refs_0_ = bf16[384,256]{1,0:T(8,128)(2,1)S(1)} collective-permute-done((bf16[384,256]{1,0:T(8,128)(2,1)S(1)}, bf16[384,256]{1,0:T(8,128)(2,1)S(1)}, u32[]{:S(2)}, u32[]{:S(2)}) %collective-permute-start.1) | collective-permute-done | bytes 196640 | tf_op jit(solution)/shard_map/right/ppermute | solution.py:23
  32.0 0.5 collective-permute-start.12
  32.5 0.4 collective-permute-start.11
  33.0 1.7 %collective-permute-start.16 = (bf16[256,256]{1,0:T(8,128)(2,1)S(1)}, bf16[256,256]{1,0:T(8,128)(2,1)S(1)}, u32[]{:S(2)}, u32[]{:S(2)}) collective-permute-start(bf16[256,256]{1,0:T(8,128)(2,1)S(1)} %slice.17), channel_id=1, source_target_pairs={{0,8},{8,0},{16,24},{24,16},{1,9},{9,1},{17,25},{25,17},{2,10},{10... | collective-permute-start | bytes 393224 | tf_op jit(solution)/shard_map/left_3b/ppermute | solution.py:29
  34.6 1.6 %collective-permute-start.15 = (bf16[256,256]{1,0:T(8,128)(2,1)S(1)}, bf16[256,256]{1,0:T(8,128)(2,1)S(1)}, u32[]{:S(2)}, u32[]{:S(2)}) collective-permute-start(bf16[256,256]{1,0:T(8,128)(2,1)S(1)} %slice.16), channel_id=1, source_target_pairs={{0,16},{8,24},{16,0},{24,8},{1,17},{9,25},{17,1},{25,9},{2,18},{10... | collective-permute-start | bytes 393224 | tf_op jit(solution)/shard_map/left_3a/ppermute | solution.py:29
  36.2 2.3 %collective-permute-start.10 = (bf16[528,256]{1,0:T(8,128)(2,1)S(1)}, bf16[528,256]{1,0:T(8,128)(2,1)S(1)}, u32[]{:S(2)}, u32[]{:S(2)}) collective-permute-start(bf16[528,256]{1,0:T(8,128)(2,1)S(1)} %get-tuple-element.45), channel_id=1, source_target_pairs={{0,4},{1,5},{2,6},{3,7},{4,0},{5,1},{6,2},{7,3},{8,12},{9,13},{10,... | collective-permute-start | bytes 811016 | tf_op jit(solution)/shard_map/corners/ppermute | solution.py:23
  38.5 1.6 %collective-permute-start.14 = (bf16[192,256]{1,0:T(8,128)(2,1)S(1)}, bf16[192,256]{1,0:T(8,128)(2,1)S(1)}, u32[]{:S(2)}, u32[]{:S(2)}) collective-permute-start(bf16[192,256]{1,0:T(8,128)(2,1)S(1)} %slice.19), channel_id=1, source_target_pairs={{0,8},{8,0},{16,24},{24,16},{1,9},{9,1},{17,25},{25,17},{2,10},{10... | collective-permute-start | bytes 294920 | tf_op jit(solution)/shard_map/right_3b/ppermute | solution.py:29
  41.4 1.0 %left_columns.1 = (bf16[256,256]{1,0:T(8,128)(2,1)S(1)}, bf16[256,256]{1,0:T(8,128)(2,1)S(1)}, bf16[256,256]{1,0:T(8,128)(2,1)S(1)}, bf16[256,256]{1,0:T(8,128)(2,1)S(1)}) custom-call(s32[1]{0:T(128)} %bitcast.me_ref, s32[1]{0:T(128)S(6)} %copy.6.rows_ref, s32[1]{0:T(128)S(6)} %copy.7.cols_ref, bf16[528,256]{1,0:T(8,128)(2,1)S(1)} %collective-permute-done.refs_0_, ...), custom_call_target="tpu_custom_call" | custom-call | flops 536870912 | bytes 4194304 | tf_op jit(solution)/shard_map/left_columns/pallas_call | solution.py:258
  42.4 0.6 %collective-permute-start.17 = (bf16[256,256]{1,0:T(8,128)(2,1)S(1)}, bf16[256,256]{1,0:T(8,128)(2,1)S(1)}, u32[]{:S(2)}, u32[]{:S(2)}) collective-permute-start(bf16[256,256]{1,0:T(8,128)(2,1)S(1)} %get-tuple-element.52), channel_id=1, source_target_pairs={{0,8},{8,0},{16,24},{24,16},{1,9},{9,1},{17,25},{25,17},{2,10},{10... | collective-permute-start | bytes 393224 | tf_op jit(solution)/shard_map/strip_1/ppermute | solution.py:29
  43.0 1.4 %collective-permute-start.18 = (bf16[256,256]{1,0:T(8,128)(2,1)S(1)}, bf16[256,256]{1,0:T(8,128)(2,1)S(1)}, u32[]{:S(2)}, u32[]{:S(2)}) collective-permute-start(bf16[256,256]{1,0:T(8,128)(2,1)S(1)} %get-tuple-element.53), channel_id=1, source_target_pairs={{0,16},{8,24},{16,0},{24,8},{1,17},{9,25},{17,1},{25,9},{2,18},{10... | collective-permute-start | bytes 393224 | tf_op jit(solution)/shard_map/strip_2/ppermute | solution.py:29
  44.5 1.5 %collective-permute-start.19 = (bf16[256,256]{1,0:T(8,128)(2,1)S(1)}, bf16[256,256]{1,0:T(8,128)(2,1)S(1)}, u32[]{:S(2)}, u32[]{:S(2)}) collective-permute-start(bf16[256,256]{1,0:T(8,128)(2,1)S(1)} %get-tuple-element.54), channel_id=1, source_target_pairs={{0,24},{8,16},{16,8},{24,0},{1,25},{9,17},{17,9},{25,1},{2,26},{10... | collective-permute-start | bytes 393224 | tf_op jit(solution)/shard_map/strip_3/ppermute | solution.py:29
  46.0 1.1 %collective-permute-start.13 = (bf16[192,256]{1,0:T(8,128)(2,1)S(1)}, bf16[192,256]{1,0:T(8,128)(2,1)S(1)}, u32[]{:S(2)}, u32[]{:S(2)}) collective-permute-start(bf16[192,256]{1,0:T(8,128)(2,1)S(1)} %slice.18), channel_id=1, source_target_pairs={{0,16},{8,24},{16,0},{24,8},{1,17},{9,25},{17,1},{25,9},{2,18},{10... | collective-permute-start | bytes 294920 | tf_op jit(solution)/shard_map/right_3a/ppermute | solution.py:29
  47.1 4.2 %collective-permute-done.13.refs_3_ = bf16[192,256]{1,0:T(8,128)(2,1)S(1)} collective-permute-done((bf16[192,256]{1,0:T(8,128)(2,1)S(1)}, bf16[192,256]{1,0:T(8,128)(2,1)S(1)}, u32[]{:S(2)}, u32[]{:S(2)}) %collective-permute-start.13) | collective-permute-done | bytes 98336 | tf_op jit(solution)/shard_map/right_3a/ppermute | solution.py:29
  51.4 1.8 %update_rows.1 = bf16[1,256,1024]{2,1,0:T(8,128)(2,1)} custom-call(s32[1]{0:T(128)} %bitcast.me_ref, s32[1]{0:T(128)S(6)} %copy.6.rows_ref, s32[1]{0:T(128)S(6)} %copy.7.cols_ref, bf16[528,256]{1,0:T(8,128)(2,1)S(1)} %collective-permute-done.10.corners_ref, bf16[384,256]{1,0:T(8,128)(2,1)S(1)} %collective-permute-done.1.refs_0_, ...), custom_call_target="tpu_custom_call" | custom-call | flops 536870912 | bytes 4194304 | tf_op jit(solution)/shard_map/update_rows/pallas_call | solution.py:301
  (18 shorter events, 0.1 us)
Async XLA Ops:
  2.3 9.8 %collective-permute-start.2 = (bf16[512,256]{1,0:T(8,128)(2,1)S(1)}, bf16[512,256]{1,0:T(8,128)(2,1)S(1)}, u32[]{:S(2)}, u32[]{:S(2)}) collective-permute-start(bf16[512,256]{1,0:T(8,128)(2,1)S(1)} %get-tuple-element.35), channel_id=1, source_target_pairs={{0,8},{8,0},{16,24},{24,16},{1,9},{9,1},{17,25},{25,17},{2,10},{10... | collective-permute-start | bytes 786440 | tf_op jit(solution)/shard_map/far_0/ppermute | solution.py:29
  5.3 9.4 %collective-permute-start.3 = (bf16[512,256]{1,0:T(8,128)(2,1)S(1)}, bf16[512,256]{1,0:T(8,128)(2,1)S(1)}, u32[]{:S(2)}, u32[]{:S(2)}) collective-permute-start(bf16[512,256]{1,0:T(8,128)(2,1)S(1)} %get-tuple-element.37), channel_id=1, source_target_pairs={{0,16},{8,24},{16,0},{24,8},{1,17},{9,25},{17,1},{25,9},{2,18},{10... | collective-permute-start | bytes 786440 | tf_op jit(solution)/shard_map/far_1/ppermute | solution.py:29
  6.8 14.4 %collective-permute-start = (bf16[528,256]{1,0:T(8,128)(2,1)S(1)}, bf16[528,256]{1,0:T(8,128)(2,1)S(1)}, u32[]{:S(2)}, u32[]{:S(2)}) collective-permute-start(bf16[528,256]{1,0:T(8,128)(2,1)S(1)} %get-tuple-element.32), channel_id=1, source_target_pairs={{0,4},{1,5},{2,6},{3,7},{4,0},{5,1},{6,2},{7,3},{8,12},{9,13},{10,... | collective-permute-start | bytes 811016 | tf_op jit(solution)/shard_map/left/ppermute | solution.py:23
  9.4 11.8 %collective-permute-start.4 = (bf16[512,256]{1,0:T(8,128)(2,1)S(1)}, bf16[512,256]{1,0:T(8,128)(2,1)S(1)}, u32[]{:S(2)}, u32[]{:S(2)}) collective-permute-start(bf16[512,256]{1,0:T(8,128)(2,1)S(1)} %get-tuple-element.38), channel_id=1, source_target_pairs={{0,8},{8,0},{16,24},{24,16},{1,9},{9,1},{17,25},{25,17},{2,10},{10... | collective-permute-start | bytes 786440 | tf_op jit(solution)/shard_map/near_0/ppermute | solution.py:29
  9.9 11.2 %collective-permute-start.5 = (bf16[512,256]{1,0:T(8,128)(2,1)S(1)}, bf16[512,256]{1,0:T(8,128)(2,1)S(1)}, u32[]{:S(2)}, u32[]{:S(2)}) collective-permute-start(bf16[512,256]{1,0:T(8,128)(2,1)S(1)} %get-tuple-element.39), channel_id=1, source_target_pairs={{0,16},{8,24},{16,0},{24,8},{1,17},{9,25},{17,1},{25,9},{2,18},{10... | collective-permute-start | bytes 786440 | tf_op jit(solution)/shard_map/near_1/ppermute | solution.py:29
  12.2 12.1 %collective-permute-start.8 = (bf16[512,256]{1,0:T(8,128)(2,1)S(1)}, bf16[512,256]{1,0:T(8,128)(2,1)S(1)}, u32[]{:S(2)}, u32[]{:S(2)}) collective-permute-start(bf16[512,256]{1,0:T(8,128)(2,1)S(1)} %add_convert_fusion.1), channel_id=1, source_target_pairs={{0,16},{8,24},{16,0},{24,8},{1,17},{9,25},{17,1},{25,9},{2,18},{10... | collective-permute-start | bytes 786440 | tf_op jit(solution)/shard_map/via_0/ppermute | solution.py:29
  14.7 11.1 %collective-permute-start.6 = (bf16[512,256]{1,0:T(8,128)(2,1)S(1)}, bf16[512,256]{1,0:T(8,128)(2,1)S(1)}, u32[]{:S(2)}, u32[]{:S(2)}) collective-permute-start(bf16[512,256]{1,0:T(8,128)(2,1)S(1)} %add_convert_fusion), channel_id=1, source_target_pairs={{0,8},{8,0},{16,24},{24,16},{1,9},{9,1},{17,25},{25,17},{2,10},{10... | collective-permute-start | bytes 786440 | tf_op jit(solution)/shard_map/via_1/ppermute | solution.py:29
  21.1 10.9 %collective-permute-start.1 = (bf16[384,256]{1,0:T(8,128)(2,1)S(1)}, bf16[384,256]{1,0:T(8,128)(2,1)S(1)}, u32[]{:S(2)}, u32[]{:S(2)}) collective-permute-start(bf16[384,256]{1,0:T(8,128)(2,1)S(1)} %get-tuple-element.33), channel_id=1, source_target_pairs={{0,4},{1,5},{2,6},{3,7},{4,0},{5,1},{6,2},{7,3},{8,12},{9,13},{10,... | collective-permute-start | bytes 589832 | tf_op jit(solution)/shard_map/right/ppermute | solution.py:23
  24.3 8.7 %collective-permute-start.9 = (bf16[528,256]{1,0:T(8,128)(2,1)S(1)}, bf16[528,256]{1,0:T(8,128)(2,1)S(1)}, u32[]{:S(2)}, u32[]{:S(2)}) collective-permute-start(bf16[528,256]{1,0:T(8,128)(2,1)S(1)} %collective-permute-done.refs_0_), channel_id=1, source_target_pairs={{0,16},{8,24},{16,0},{24,8},{1,17},{9,25},{17,1},{25,9},{2,18},{10... | collective-permute-start | bytes 811016 | tf_op jit(solution)/shard_map/left_2/ppermute | solution.py:29
  25.8 8.8 %collective-permute-start.7 = (bf16[528,256]{1,0:T(8,128)(2,1)S(1)}, bf16[528,256]{1,0:T(8,128)(2,1)S(1)}, u32[]{:S(2)}, u32[]{:S(2)}) collective-permute-start(bf16[528,256]{1,0:T(8,128)(2,1)S(1)} %collective-permute-done.refs_0_), channel_id=1, source_target_pairs={{0,8},{8,0},{16,24},{24,16},{1,9},{9,1},{17,25},{25,17},{2,10},{10... | collective-permute-start | bytes 811016 | tf_op jit(solution)/shard_map/left_1/ppermute | solution.py:29
  32.0 6.5 %collective-permute-start.12 = (bf16[384,256]{1,0:T(8,128)(2,1)S(1)}, bf16[384,256]{1,0:T(8,128)(2,1)S(1)}, u32[]{:S(2)}, u32[]{:S(2)}) collective-permute-start(bf16[384,256]{1,0:T(8,128)(2,1)S(1)} %collective-permute-done.1.refs_0_), channel_id=1, source_target_pairs={{0,16},{8,24},{16,0},{24,8},{1,17},{9,25},{17,1},{25,9},{2,18},{10... | collective-permute-start | bytes 589832 | tf_op jit(solution)/shard_map/right_2/ppermute | solution.py:29
  32.5 12.0 %collective-permute-start.11 = (bf16[384,256]{1,0:T(8,128)(2,1)S(1)}, bf16[384,256]{1,0:T(8,128)(2,1)S(1)}, u32[]{:S(2)}, u32[]{:S(2)}) collective-permute-start(bf16[384,256]{1,0:T(8,128)(2,1)S(1)} %collective-permute-done.1.refs_0_), channel_id=1, source_target_pairs={{0,8},{8,0},{16,24},{24,16},{1,9},{9,1},{17,25},{25,17},{2,10},{10... | collective-permute-start | bytes 589832 | tf_op jit(solution)/shard_map/right_1/ppermute | solution.py:29
  33.0 8.4 %collective-permute-start.16 = (bf16[256,256]{1,0:T(8,128)(2,1)S(1)}, bf16[256,256]{1,0:T(8,128)(2,1)S(1)}, u32[]{:S(2)}, u32[]{:S(2)}) collective-permute-start(bf16[256,256]{1,0:T(8,128)(2,1)S(1)} %slice.17), channel_id=1, source_target_pairs={{0,8},{8,0},{16,24},{24,16},{1,9},{9,1},{17,25},{25,17},{2,10},{10... | collective-permute-start | bytes 393224 | tf_op jit(solution)/shard_map/left_3b/ppermute | solution.py:29
  34.6 6.7 %collective-permute-start.15 = (bf16[256,256]{1,0:T(8,128)(2,1)S(1)}, bf16[256,256]{1,0:T(8,128)(2,1)S(1)}, u32[]{:S(2)}, u32[]{:S(2)}) collective-permute-start(bf16[256,256]{1,0:T(8,128)(2,1)S(1)} %slice.16), channel_id=1, source_target_pairs={{0,16},{8,24},{16,0},{24,8},{1,17},{9,25},{17,1},{25,9},{2,18},{10... | collective-permute-start | bytes 393224 | tf_op jit(solution)/shard_map/left_3a/ppermute | solution.py:29
  36.2 15.2 %collective-permute-start.10 = (bf16[528,256]{1,0:T(8,128)(2,1)S(1)}, bf16[528,256]{1,0:T(8,128)(2,1)S(1)}, u32[]{:S(2)}, u32[]{:S(2)}) collective-permute-start(bf16[528,256]{1,0:T(8,128)(2,1)S(1)} %get-tuple-element.45), channel_id=1, source_target_pairs={{0,4},{1,5},{2,6},{3,7},{4,0},{5,1},{6,2},{7,3},{8,12},{9,13},{10,... | collective-permute-start | bytes 811016 | tf_op jit(solution)/shard_map/corners/ppermute | solution.py:23
  38.5 7.5 %collective-permute-start.14 = (bf16[192,256]{1,0:T(8,128)(2,1)S(1)}, bf16[192,256]{1,0:T(8,128)(2,1)S(1)}, u32[]{:S(2)}, u32[]{:S(2)}) collective-permute-start(bf16[192,256]{1,0:T(8,128)(2,1)S(1)} %slice.19), channel_id=1, source_target_pairs={{0,8},{8,0},{16,24},{24,16},{1,9},{9,1},{17,25},{25,17},{2,10},{10... | collective-permute-start | bytes 294920 | tf_op jit(solution)/shard_map/right_3b/ppermute | solution.py:29
  42.4 8.9 %collective-permute-start.17 = (bf16[256,256]{1,0:T(8,128)(2,1)S(1)}, bf16[256,256]{1,0:T(8,128)(2,1)S(1)}, u32[]{:S(2)}, u32[]{:S(2)}) collective-permute-start(bf16[256,256]{1,0:T(8,128)(2,1)S(1)} %get-tuple-element.52), channel_id=1, source_target_pairs={{0,8},{8,0},{16,24},{24,16},{1,9},{9,1},{17,25},{25,17},{2,10},{10... | collective-permute-start | bytes 393224 | tf_op jit(solution)/shard_map/strip_1/ppermute | solution.py:29
  43.0 8.3 %collective-permute-start.18 = (bf16[256,256]{1,0:T(8,128)(2,1)S(1)}, bf16[256,256]{1,0:T(8,128)(2,1)S(1)}, u32[]{:S(2)}, u32[]{:S(2)}) collective-permute-start(bf16[256,256]{1,0:T(8,128)(2,1)S(1)} %get-tuple-element.53), channel_id=1, source_target_pairs={{0,16},{8,24},{16,0},{24,8},{1,17},{9,25},{17,1},{25,9},{2,18},{10... | collective-permute-start | bytes 393224 | tf_op jit(solution)/shard_map/strip_2/ppermute | solution.py:29
  44.5 6.9 %collective-permute-start.19 = (bf16[256,256]{1,0:T(8,128)(2,1)S(1)}, bf16[256,256]{1,0:T(8,128)(2,1)S(1)}, u32[]{:S(2)}, u32[]{:S(2)}) collective-permute-start(bf16[256,256]{1,0:T(8,128)(2,1)S(1)} %get-tuple-element.54), channel_id=1, source_target_pairs={{0,24},{8,16},{16,8},{24,0},{1,25},{9,17},{17,9},{25,1},{2,26},{10... | collective-permute-start | bytes 393224 | tf_op jit(solution)/shard_map/strip_3/ppermute | solution.py:29
  46.0 5.4 %collective-permute-start.13 = (bf16[192,256]{1,0:T(8,128)(2,1)S(1)}, bf16[192,256]{1,0:T(8,128)(2,1)S(1)}, u32[]{:S(2)}, u32[]{:S(2)}) collective-permute-start(bf16[192,256]{1,0:T(8,128)(2,1)S(1)} %slice.18), channel_id=1, source_target_pairs={{0,16},{8,24},{16,0},{24,8},{1,17},{9,25},{17,1},{25,9},{2,18},{10... | collective-permute-start | bytes 294920 | tf_op jit(solution)/shard_map/right_3a/ppermute | solution.py:29

commit v7 on v6

v7 whole, which is shorter than its diff:
```python
import functools

import jax
import jax.numpy as jnp
from jax import lax
from jax.experimental import pallas as pl
from jax.experimental.pallas import tpu as pltpu
from jax.sharding import PartitionSpec as P

TILE = 256
EXTRA = 16
VMEM = 24 * 1024 * 1024
SMEM_SPEC = pl.BlockSpec(memory_space=pltpu.SMEM)
VMEM_SPEC = pl.BlockSpec(memory_space=pltpu.VMEM)
HBM_SPEC = pl.BlockSpec(memory_space=pltpu.HBM)
BF16 = jnp.bfloat16
F32 = jnp.float32


def shifted(value, name):
    count = lax.axis_size("shard")
    with jax.named_scope(name):
        return lax.ppermute(value, "shard", [(source, (source + count // 2) % count) for source in range(count)])


def swapped(value, flip, name):
    count = lax.axis_size("dp")
    with jax.named_scope(name):
        return lax.ppermute(value, "dp", [(source, source ^ flip) for source in range(count)])


def after(value, *earlier):
    return lax.optimization_barrier((value, *earlier))[0]


def block(index):
    return pl.ds(index * TILE, TILE)


def strip_of(index, size):
    return pl.ds(pl.multiple_of(index * size, size), size)


def cost(flops, bytes_accessed):
    return pl.CostEstimate(flops=flops, bytes_accessed=bytes_accessed, transcendentals=0)


def below(tiles):
    return [(i, j) for j in range(tiles) for i in range(j + 1, tiles)]


def pick_copies(wanted, me, grad_ref, outs, sems):
    copies = []
    for parts, out in zip(wanted, outs):
        half, strip = out.shape[0] // len(parts), out.shape[1]
        for part, (flip, h) in enumerate(parts):
            source = grad_ref.at[0, 0, pl.ds(h * half, half), strip_of(jnp.bitwise_xor(me, flip), strip)]
            copies.append(
                pltpu.make_async_copy(source, out.at[pl.ds(part * half, half), :], sems.at[len(copies)])
            )
    return copies


def picked_shapes(wanted, width, groups):
    return [pltpu.VMEM((len(parts) * (width // 2), width // groups), BF16) for parts in wanted]


def strip_copies(me, root_ref, strip, out, sems):
    return [
        pltpu.make_async_copy(
            root_ref.at[0, pl.ds(pl.multiple_of(i * TILE + me * strip, strip), strip), block(j)],
            out.at[pl.ds(k * strip, strip), :],
            sems.at[k],
        )
        for k, (i, j) in enumerate(below(root_ref.shape[1] // TILE))
    ]


def corner_copies(root_ref, corners, sems):
    return [
        pltpu.make_async_copy(root_ref.at[0, block(i), block(i)], corners.at[i], sems.at[i])
        for i in range(corners.shape[0])
    ]


def fold_corners(corners, start, strip, out, base):
    tiles = corners.shape[0]
    row = lax.broadcasted_iota(jnp.int32, (strip, TILE), 0) + start
    column = lax.broadcasted_iota(jnp.int32, (strip, TILE), 1)
    on_diag = lax.broadcasted_iota(jnp.int32, (TILE, TILE), 0) == lax.broadcasted_iota(jnp.int32, (TILE, TILE), 1)
    rows = pl.ds(pl.multiple_of(start, strip), strip) if strip < TILE else pl.ds(0, TILE)
    lines = []
    for pair in range(tiles // 2):
        even, odd = 2 * pair, 2 * pair + 1
        out[pl.ds(base + pair * strip, strip), :] = jnp.where(
            row >= column, corners[even, rows, :], corners[odd, rows, :]
        )
        lines.append(jnp.sum(jnp.where(on_diag, corners[odd].astype(F32), 0.0), axis=0, keepdims=True))
    lines.append(jnp.zeros((EXTRA - len(lines), TILE), F32))
    out[pl.ds(base + tiles // 2 * strip, EXTRA), :] = jnp.concatenate(lines, axis=0).astype(BF16)


def messages_kernel(wanted, quarter, me_ref, grad_ref, root_ref, *refs):
    outs, (*folded, corners, pick_sems, strip_sems, corner_sems) = refs[: len(wanted)], refs[len(wanted) :]
    me = me_ref[0]
    tiles = corners.shape[0]
    low = len(below(tiles))
    strip = quarter
    strips = strip_copies(me, root_ref, strip, folded[0], strip_sems)
    cornered = corner_copies(root_ref, corners, corner_sems)
    copies = pick_copies(wanted, me, grad_ref, outs, pick_sems)
    for copy in cornered + strips + copies:
        copy.start()
    for copy in cornered:
        copy.wait()
    if len(folded) == 1:
        fold_corners(corners, me * strip, strip, folded[0], low * strip)
    else:
        fold_corners(corners, 0, TILE, folded[1], 0)
    for copy in strips + copies:
        copy.wait()


def messages(me, grads, root, groups, wanted, apart, name):
    width = grads.shape[-1]
    strip, tiles = TILE // groups, width // TILE
    count = sum(len(parts) for parts in wanted)
    low = len(below(tiles)) * strip
    if apart:
        rows = [low, tiles // 2 * TILE + EXTRA]
    else:
        rows = [low + tiles // 2 * strip + EXTRA]
    return pl.pallas_call(
        functools.partial(messages_kernel, wanted, strip),
        in_specs=[SMEM_SPEC] + [HBM_SPEC] * 2,
        out_specs=[VMEM_SPEC] * (len(wanted) + len(rows)),
        out_shape=picked_shapes(wanted, width, groups) + [pltpu.VMEM((number, TILE), BF16) for number in rows],
        scratch_shapes=[
            pltpu.VMEM((tiles, TILE, TILE), BF16),
            pltpu.SemaphoreType.DMA((max(count, 1),)),
            pltpu.SemaphoreType.DMA((len(below(tiles)),)),
            pltpu.SemaphoreType.DMA((tiles,)),
        ],
        compiler_params=pltpu.CompilerParams(vmem_limit_bytes=VMEM),
        name=name,
    )(me, grads, root)


def unfold_below(pieces, me, root):
    tiles = root.shape[0] // TILE
    strip = TILE // len(pieces)
    blocks = below(tiles)
    for flip, parts in enumerate(pieces):
        other = jnp.bitwise_xor(me, flip)
        for k, (i, j) in enumerate(blocks):
            part, row = 0, k * strip
            while row >= parts[part].shape[0]:
                row -= parts[part].shape[0]
                part += 1
            at = pl.ds(pl.multiple_of(i * TILE + other * strip, strip), strip)
            root[at, block(j)] = parts[part][pl.ds(row, strip), :]
    for i, j in blocks:
        root[block(j), block(i)] = root[block(i), block(j)].T


def unfold_corners(folded, lines, root):
    row = lax.broadcasted_iota(jnp.int32, (TILE, TILE), 0)
    column = lax.broadcasted_iota(jnp.int32, (TILE, TILE), 1)
    lines = lines.astype(F32)
    for i in range(root.shape[0] // TILE):
        value = folded[block(i // 2), :].astype(F32)
        value = jnp.where(row >= column if i % 2 == 0 else row < column, value, value.T)
        if i % 2:
            line = jnp.broadcast_to(lines[i // 2 : i // 2 + 1, :], (TILE, TILE))
            value = jnp.where(row == column, line, value)
        root[block(i), block(i)] = value.astype(BF16)


def unfold(pieces, me, root, folded):
    tiles = root.shape[0] // TILE
    strip = TILE // len(pieces)
    unfold_below(pieces, me, root)
    base = len(below(tiles)) * strip
    for flip, parts in enumerate(pieces):
        other = jnp.bitwise_xor(me, flip)
        for pair in range(tiles // 2):
            part, row = 0, base + pair * strip
            while row >= parts[part].shape[0]:
                row -= parts[part].shape[0]
                part += 1
            at = pl.ds(pl.multiple_of(pair * TILE + other * strip, strip), strip)
            folded[at, :] = parts[part][pl.ds(row, strip), :]
    unfold_corners(folded, pieces[0][0][pl.ds(base + tiles // 2 * strip, EXTRA), :], root)


def dealt(refs, counts):
    lists = []
    for count in counts:
        lists.append(refs[:count])
        refs = refs[count:]
    return lists, refs


def columns_kernel(groups, held, split, me_ref, rows_ref, cols_ref, *refs):
    pieces, refs = dealt(refs, held)
    terms, refs = dealt(refs, split)
    out, left, folded, masked = refs
    me = me_ref[0]
    width, strip = masked.shape
    unfold(pieces, me, left, folded)
    part = width // len(terms)
    column = lax.broadcasted_iota(jnp.int32, (part, strip), 1) + me * strip
    row = lax.broadcasted_iota(jnp.int32, (part, strip), 0)
    for index, used in enumerate(terms):
        total = functools.reduce(lambda a, b: a + b, [term[pl.ds(0, part), :].astype(F32) for term in used])
        keep = (row + index * part < rows_ref[0]) & (column < cols_ref[0])
        masked[pl.ds(index * part, part), :] = jnp.where(keep, total, 0.0).astype(BF16)
    out[...] = jnp.dot(left[...], masked[...], preferred_element_type=F32).astype(BF16)


def left_columns(me, rows_valid, cols_valid, pieces, terms, width):
    groups = len(pieces)
    strip = width // groups
    flat = [array for part in (*pieces, *terms) for array in part]
    return pl.pallas_call(
        functools.partial(columns_kernel, groups, [len(part) for part in pieces], [len(part) for part in terms]),
        in_specs=[SMEM_SPEC] * 3 + [VMEM_SPEC] * len(flat),
        out_specs=VMEM_SPEC,
        out_shape=pltpu.VMEM((width, strip), BF16),
        scratch_shapes=[
            pltpu.VMEM((width, width), BF16),
            pltpu.VMEM((width // 2, TILE), BF16),
            pltpu.VMEM((width, strip), BF16),
        ],
        compiler_params=pltpu.CompilerParams(vmem_limit_bytes=VMEM),
        cost_estimate=cost(2 * strip * width**2, 4 * width**2),
        name="left_columns",
    )(me, rows_valid, cols_valid, *flat)


def whole_right_kernel(held, me_ref, corners_ref, *refs):
    pieces, (right,) = dealt(refs, held)
    unfold_below(pieces, me_ref[0], right)
    unfold_corners(corners_ref, corners_ref[pl.ds(right.shape[0] // 2, EXTRA), :], right)


def whole_right(me, corners, pieces, width):
    flat = [array for part in pieces for array in part]
    return pl.pallas_call(
        functools.partial(whole_right_kernel, [len(part) for part in pieces]),
        in_specs=[SMEM_SPEC] + [VMEM_SPEC] * (1 + len(flat)),
        out_specs=VMEM_SPEC,
        out_shape=pltpu.VMEM((width, width), BF16),
        compiler_params=pltpu.CompilerParams(vmem_limit_bytes=VMEM),
        cost_estimate=cost(width**2, 4 * width**2),
        name="whole_right",
    )(me, corners, *flat)


def rows_kernel(me_ref, rows_ref, cols_ref, strips_ref, right, out, mixed):
    groups, strip, _ = strips_ref.shape
    width = right.shape[0]
    for k in range(groups):
        mixed[:, pl.ds(k * strip, strip)] = strips_ref[k]
    value = jnp.dot(mixed[...], right[...], preferred_element_type=F32)
    column = lax.broadcasted_iota(jnp.int32, (strip, width), 1)
    row = lax.broadcasted_iota(jnp.int32, (strip, width), 0) + me_ref[0] * strip
    out[0] = jnp.where((row < rows_ref[0]) & (column < cols_ref[0]), value, 0.0).astype(BF16)


def update_rows(me, rows_valid, cols_valid, strips, right):
    width = right.shape[0]
    strip = strips.shape[1]
    return pl.pallas_call(
        rows_kernel,
        in_specs=[SMEM_SPEC] * 3 + [VMEM_SPEC] * 2,
        out_specs=VMEM_SPEC,
        out_shape=jax.ShapeDtypeStruct((1, strip, width), BF16),
        scratch_shapes=[pltpu.VMEM((strip, width), BF16)],
        compiler_params=pltpu.CompilerParams(vmem_limit_bytes=VMEM),
        cost_estimate=cost(2 * strip * width**2, 4 * width**2),
        name="update_rows",
    )(me, rows_valid, cols_valid, strips, right)


def added(*terms):
    return functools.reduce(lambda a, b: a + b, [term.astype(F32) for term in terms])


def on_device(grads, left_roots, right_roots, rows_valid, cols_valid):
    groups = lax.axis_size("dp")
    me = lax.axis_index("dp").astype(jnp.int32).reshape(1)
    width = grads.shape[-1]
    half, strip = width // 2, width // groups
    plain = grads
    grads, left_roots, right_roots = (
        pltpu.with_memory_space_constraint(array, pltpu.HBM) for array in (grads, left_roots, right_roots)
    )

    if groups == 4:
        far_0, far_1, near_0, near_1, left = messages(
            me, grads, left_roots, groups, [[(3, 0)], [(3, 1)], [(1, 0)], [(2, 1)]], False, "sent_first"
        )
        far_0, far_1 = swapped(far_0, 1, "far_0"), swapped(far_1, 2, "far_1")
        near_0, near_1 = swapped(near_0, 1, "near_0"), swapped(near_1, 2, "near_1")
        left = shifted(left, "left")
        *kept, right, corners = messages(
            me, grads, right_roots, groups, [[(2, 0)], [(1, 1)], [(0, 0)], [(0, 1)]], True, "sent_later"
        )
        via_0, via_1 = added(kept[0], far_0).astype(BF16), added(kept[1], far_1).astype(BF16)
        right = shifted(after(right, left), "right")
        left = after(left, via_0, via_1, near_0, near_1)
        via_0, via_1 = swapped(via_0, 2, "via_0"), swapped(via_1, 1, "via_1")
        left_1, left_2 = swapped(left, 1, "left_1"), swapped(left, 2, "left_2")
        cut = (left.shape[0] - EXTRA) // 2
        left_3a, left_3b = left_1[:cut], left_2[cut : 2 * cut]
        corners = shifted(after(corners, right, left_3a, left_3b), "corners")
        left_3 = [swapped(left_3a, 2, "left_3a"), swapped(left_3b, 1, "left_3b")]
        mixed = left_columns(
            me,
            rows_valid,
            cols_valid,
            [[left], [left_1], [left_2], left_3],
            [[kept[2], near_0, via_0], [kept[3], near_1, via_1]],
            width,
        )
        right = after(right, via_0, via_1)
        right_1, right_2 = swapped(right, 1, "right_1"), swapped(right, 2, "right_2")
        cut = right.shape[0] // 2
        right_3 = [swapped(right_1[:cut], 2, "right_3a"), swapped(right_2[cut:], 1, "right_3b")]
        rights = [[right], [right_1], [right_2], right_3]
    else:
        (left,) = messages(me, grads, left_roots, groups, [], False, "sent_first")
        right, corners = messages(me, grads, right_roots, groups, [], True, "sent_later")
        left, right, corners = shifted(left, "left"), shifted(right, "right"), shifted(corners, "corners")
        parts = [
            lax.dynamic_slice_in_dim(plain[0, 0], jnp.bitwise_xor(me[0], flip) * strip, strip, 1)
            for flip in range(groups)
        ]
        terms = [parts[:1] + [swapped(parts[flip], flip, "grad") for flip in range(1, groups)]]
        lefts = [[left]] + [[swapped(left, flip, "left")] for flip in range(1, groups)]
        mixed = left_columns(me, rows_valid, cols_valid, lefts, terms, width)
        rights = [[right]] + [[swapped(right, flip, "right")] for flip in range(1, groups)]
    whole = whole_right(me, corners, rights, width)
    with jax.named_scope("strips"):
        strips = lax.all_to_all(mixed.reshape(groups, strip, strip), "dp", 0, 0)
    return update_rows(me, rows_valid, cols_valid, strips, whole)


def solution(mesh):
    placed = (
        P("dp", "shard", None, None),
        P("shard", None, None),
        P("shard", None, None),
        P("shard"),
        P("shard"),
    )
    return jax.shard_map(
        on_device, mesh=mesh, in_specs=placed, out_specs=P("shard", "dp", None), check_vma=False
    )
```

time: 53.4 us -> 61.4 us (1.15); the launches traced: 53.2 us -> 60.5 us
  waiting for transfers between devices: 18.4 us -> 27.7 us
  starting transfers between devices: 26.9 us -> 24.1 us
  Pallas kernels: 6.33 us -> 7.08 us
    ppermute x17 -> x14, waiting for transfers between devices: 7.85 us -> 22.5 us  [swapped(): lax.ppermute(value, 'dp', [(source, source ^ flip) for source in range(co...]
    ppermute x3, waiting for transfers between devices: 10.5 us -> 5.19 us  [shifted(): lax.ppermute(value, 'shard', [(source, (source + count // 2) % count) for...]
    ppermute x17 -> x14, starting transfers between devices: 22 us -> 17.7 us  [swapped(): lax.ppermute(value, 'dp', [(source, source ^ flip) for source in range(co...]
    all_to_all x0 -> x1, starting transfers between devices: none -> 3.47 us  [on_device(): strips = lax.all_to_all(mixed.reshape(groups, strip, strip), 'dp', 0, 0)]
    ppermute x3, starting transfers between devices: 4.87 us -> 2.98 us  [shifted(): lax.ppermute(value, 'shard', [(source, (source + count // 2) % count) for...]
    pallas_call x1, Pallas kernels: 1.05 us -> 1.79 us  [left_columns(): pl.pallas_call(functools.partial(columns_kernel, groups, [len(part) for p...]
    pallas_call x3 -> x4, Pallas kernels: 5.28 us -> 5.29 us  [the longest x2 3.25 us: messages(): pl.pallas_call(functools.partial(messages_kernel, wanted, strip), in_spec...]
  transfers between devices with their start and end apart: 20 -> 18, of which waited for: 5 -> 11; matrix products, arithmetic and copies ran while one was open for 0% -> 0% of each run, Pallas kernels for 4% -> 7%
where the time goes in v7:
time: 61.4 us; the launch traced here: 60.5 us
  waiting for transfers between devices  27.7 us (45%)
  starting transfers between devices  24.1 us (39%)
  Pallas kernels  7.08 us (12%)
  between operations  1.39 us (2%)
    ppermute x14, waiting for transfers between devices, swapped(): lax.ppermute(value, 'dp', [(source, source ^ flip) for source in range(co...  22.5 us
    ppermute x14, starting transfers between devices, swapped(): lax.ppermute(value, 'dp', [(source, source ^ flip) for source in range(co...  17.7 us
    ppermute x3, waiting for transfers between devices, shifted(): lax.ppermute(value, 'shard', [(source, (source + count // 2) % count) for...  5.19 us
    all_to_all x1, starting transfers between devices, on_device(): strips = lax.all_to_all(mixed.reshape(groups, strip, strip), 'dp', 0, 0)  3.47 us
    pallas_call x2, Pallas kernels, messages(): pl.pallas_call(functools.partial(messages_kernel, wanted, strip), in_spec...  3.25 us
    ppermute x3, starting transfers between devices, shifted(): lax.ppermute(value, 'shard', [(source, (source + count // 2) % count) for...  2.98 us
    pallas_call x1, Pallas kernels, left_columns(): pl.pallas_call(functools.partial(columns_kernel, groups, [len(part) for p...  1.79 us
    pallas_call x1, Pallas kernels, update_rows(): pl.pallas_call(rows_kernel, in_specs=[SMEM_SPEC] * 3 + [VMEM_SPEC] * 2, o...  1.51 us
  transfers between devices with their start and end apart: 18, of which 11 were waited for; matrix products, arithmetic and copies ran while one was open for 0% of the time, Pallas kernels for 7%

profile of v7, /device:TPU:0, one launch (start us, length us, event | category | flops | bytes accessed | tf_op | source)
XLA Modules:
  0.0 60.5 jit_solution(8020612403131680941)
XLA Ops:
  0.0 1.6 %sent_first.1 = (bf16[512,256]{1,0:T(8,128)(2,1)S(1)}, bf16[512,256]{1,0:T(8,128)(2,1)S(1)}, bf16[512,256]{1,0:T(8,128)(2,1)S(1)}, bf16[512,256]{1,0:T(8,128)(2,1)S(1)}, bf16[528,256]{1,0:T(8,128)(2,1)S(1)}) custom-call(s32[1]{0:T(128)} %bitcast.me_ref, bf16[1,1,1024,1024]{3,2,1,0:T(8,128)(2,1)} %grad_ref.3, bf16[1,1024,1024]{2,1,0:T(8,128)(2,1)} %root_ref.2), custom_call_target="tpu_custom_call" | custom-call | tf_op jit(solution)/shard_map/sent_first/pallas_call | solution.py:133
  1.6 3.0 %collective-permute-start.1 = (bf16[512,256]{1,0:T(8,128)(2,1)S(1)}, bf16[512,256]{1,0:T(8,128)(2,1)S(1)}, u32[]{:S(2)}, u32[]{:S(2)}) collective-permute-start(bf16[512,256]{1,0:T(8,128)(2,1)S(1)} %get-tuple-element.22), channel_id=1, source_target_pairs={{0,8},{8,0},{16,24},{24,16},{1,9},{9,1},{17,25},{25,17},{2,10},{10... | collective-permute-start | bytes 786440 | tf_op jit(solution)/shard_map/far_0/ppermute | solution.py:29
  4.6 1.5 %collective-permute-start.2 = (bf16[512,256]{1,0:T(8,128)(2,1)S(1)}, bf16[512,256]{1,0:T(8,128)(2,1)S(1)}, u32[]{:S(2)}, u32[]{:S(2)}) collective-permute-start(bf16[512,256]{1,0:T(8,128)(2,1)S(1)} %get-tuple-element.24), channel_id=1, source_target_pairs={{0,16},{8,24},{16,0},{24,8},{1,17},{9,25},{17,1},{25,9},{2,18},{10... | collective-permute-start | bytes 786440 | tf_op jit(solution)/shard_map/far_1/ppermute | solution.py:29
  6.2 2.6 %collective-permute-start = (bf16[528,256]{1,0:T(8,128)(2,1)S(1)}, bf16[528,256]{1,0:T(8,128)(2,1)S(1)}, u32[]{:S(2)}, u32[]{:S(2)}) collective-permute-start(bf16[528,256]{1,0:T(8,128)(2,1)S(1)} %get-tuple-element.20), channel_id=1, source_target_pairs={{0,4},{1,5},{2,6},{3,7},{4,0},{5,1},{6,2},{7,3},{8,12},{9,13},{10,... | collective-permute-start | bytes 811016 | tf_op jit(solution)/shard_map/left/ppermute | solution.py:23
  8.7 0.5 collective-permute-start.3
  9.3 0.5 collective-permute-start.4
  9.8 1.6 %sent_later.1 = (bf16[512,256]{1,0:T(8,128)(2,1)S(1)}, bf16[512,256]{1,0:T(8,128)(2,1)S(1)}, bf16[512,256]{1,0:T(8,128)(2,1)S(1)}, bf16[512,256]{1,0:T(8,128)(2,...) custom-call(s32[1]{0:T(128)} %bitcast.me_ref, bf16[1,1,1024,1024]{3,2,1,0:T(8,128)(2,1)} %grad_ref.3, ...), custom_call_target="tpu_custom_call" | custom-call | tf_op jit(solution)/shard_map/sent_later/pallas_call | solution.py:133
  11.6 2.3 %collective-permute-done.2 = bf16[512,256]{1,0:T(8,128)(2,1)S(1)} collective-permute-done((bf16[512,256]{1,0:T(8,128)(2,1)S(1)}, bf16[512,256]{1,0:T(8,128)(2,1)S(1)}, u32[]{:S(2)}, u32[]{:S(2)}) %collective-permute-start.2) | collective-permute-done | bytes 262176 | tf_op jit(solution)/shard_map/far_1/ppermute | solution.py:29
  13.9 2.6 %collective-permute-done.3.refs_6_ = bf16[512,256]{1,0:T(8,128)(2,1)S(1)} collective-permute-done((bf16[512,256]{1,0:T(8,128)(2,1)S(1)}, bf16[512,256]{1,0:T(8,128)(2,1)S(1)}, u32[]{:S(2)}, u32[]{:S(2)}) %collective-permute-start.3) | collective-permute-done | bytes 262176 | tf_op jit(solution)/shard_map/near_0/ppermute | solution.py:29
  16.6 1.5 %collective-permute-done.4.refs_9_ = bf16[512,256]{1,0:T(8,128)(2,1)S(1)} collective-permute-done((bf16[512,256]{1,0:T(8,128)(2,1)S(1)}, bf16[512,256]{1,0:T(8,128)(2,1)S(1)}, u32[]{:S(2)}, u32[]{:S(2)}) %collective-permute-start.4) | collective-permute-done | bytes 262176 | tf_op jit(solution)/shard_map/near_1/ppermute | solution.py:29
  18.0 2.5 %collective-permute-done.refs_0_ = bf16[528,256]{1,0:T(8,128)(2,1)S(1)} collective-permute-done((bf16[528,256]{1,0:T(8,128)(2,1)S(1)}, bf16[528,256]{1,0:T(8,128)(2,1)S(1)}, u32[]{:S(2)}, u32[]{:S(2)}) %collective-permute-start) | collective-permute-done | bytes 270368 | tf_op jit(solution)/shard_map/left/ppermute | solution.py:23
  20.5 0.5 collective-permute-start.5
  21.0 0.5 collective-permute-start.6
  21.5 1.6 %collective-permute-start.9 = (bf16[512,256]{1,0:T(8,128)(2,1)S(1)}, bf16[512,256]{1,0:T(8,128)(2,1)S(1)}, u32[]{:S(2)}, u32[]{:S(2)}) collective-permute-start(bf16[512,256]{1,0:T(8,128)(2,1)S(1)} %add_convert_fusion.1), channel_id=1, source_target_pairs={{0,16},{8,24},{16,0},{24,8},{1,17},{9,25},{17,1},{25,9},{2,18},{10... | collective-permute-start | bytes 786440 | tf_op jit(solution)/shard_map/via_0/ppermute | solution.py:29
  23.1 1.5 %collective-permute-start.10 = (bf16[512,256]{1,0:T(8,128)(2,1)S(1)}, bf16[512,256]{1,0:T(8,128)(2,1)S(1)}, u32[]{:S(2)}, u32[]{:S(2)}) collective-permute-start(bf16[512,256]{1,0:T(8,128)(2,1)S(1)} %add_convert_fusion), channel_id=1, source_target_pairs={{0,8},{8,0},{16,24},{24,16},{1,9},{9,1},{17,25},{25,17},{2,10},{10... | collective-permute-start | bytes 786440 | tf_op jit(solution)/shard_map/via_1/ppermute | solution.py:29
  24.6 5.4 %collective-permute-done.5.refs_1_ = bf16[528,256]{1,0:T(8,128)(2,1)S(1)} collective-permute-done((bf16[528,256]{1,0:T(8,128)(2,1)S(1)}, bf16[528,256]{1,0:T(8,128)(2,1)S(1)}, u32[]{:S(2)}, u32[]{:S(2)}) %collective-permute-start.5) | collective-permute-done | bytes 270368 | tf_op jit(solution)/shard_map/left_1/ppermute | solution.py:29
  29.9 0.6 collective-permute-start.7
  30.5 1.5 %collective-permute-start.8 = (bf16[256,256]{1,0:T(8,128)(2,1)S(1)}, bf16[256,256]{1,0:T(8,128)(2,1)S(1)}, u32[]{:S(2)}, u32[]{:S(2)}) collective-permute-start(bf16[256,256]{1,0:T(8,128)(2,1)S(1)} %slice.17), channel_id=1, source_target_pairs={{0,8},{8,0},{16,24},{24,16},{1,9},{9,1},{17,25},{25,17},{2,10},{10... | collective-permute-start | bytes 393224 | tf_op jit(solution)/shard_map/left_3b/ppermute | solution.py:29
  32.0 0.2 collective-permute-start.11
  33.6 1.6 %collective-permute-done.9.refs_7_ = bf16[512,256]{1,0:T(8,128)(2,1)S(1)} collective-permute-done((bf16[512,256]{1,0:T(8,128)(2,1)S(1)}, bf16[512,256]{1,0:T(8,128)(2,1)S(1)}, u32[]{:S(2)}, u32[]{:S(2)}) %collective-permute-start.9) | collective-permute-done | bytes 262176 | tf_op jit(solution)/shard_map/via_0/ppermute | solution.py:29
  35.1 1.4 %collective-permute-done.7.refs_3_ = bf16[256,256]{1,0:T(8,128)(2,1)S(1)} collective-permute-done((bf16[256,256]{1,0:T(8,128)(2,1)S(1)}, bf16[256,256]{1,0:T(8,128)(2,1)S(1)}, u32[]{:S(2)}, u32[]{:S(2)}) %collective-permute-start.7) | collective-permute-done | bytes 131104 | tf_op jit(solution)/shard_map/left_3a/ppermute | solution.py:29
  36.5 1.8 %left_columns.1 = bf16[1024,256]{1,0:T(8,128)(2,1)} custom-call(s32[1]{0:T(128)} %bitcast.me_ref, s32[1]{0:T(128)S(6)} %copy.6.rows_ref, s32[1]{0:T(128)S(6)} %copy.7.cols_ref, bf16[528,256]{1,0:T(8,128)(2,1)S(1)} %collective-permute-done.refs_0_, bf16[528,256]{1,0:T(8,128)(2,1)S(1)} %collective-permute-done.5.refs_1_, ...), custom_call_target="tpu_custom_call" | custom-call | flops 536870912 | bytes 4194304 | tf_op jit(solution)/shard_map/left_columns/pallas_call | solution.py:225
  38.3 3.5 %all-to-all-start = ((bf16[4,256,256]{2,1,0:T(8,128)(2,1)}), bf16[4,256,256]{2,1,0:T(8,128)(2,1)S(1)}, u32[]{:S(2)}, u32[]{:S(2)}) async-start(bf16[4,256,256]{2,1,0:T(8,128)(2,1)} %bitcast.1), calls=%async_computation | async-start | bytes 1048576 | tf_op jit(solution)/shard_map/strips/all_to_all | solution.py:346
  41.8 2.0 %collective-permute-start.13 = (bf16[384,256]{1,0:T(8,128)(2,1)S(1)}, bf16[384,256]{1,0:T(8,128)(2,1)S(1)}, u32[]{:S(2)}, u32[]{:S(2)}) collective-permute-start(bf16[384,256]{1,0:T(8,128)(2,1)S(1)} %collective-permute-done.11.refs_0_), channel_id=1, source_target_pairs={{0,8},{8,0},{16,24},{24,16},{1,9},{9,1},{17,25},{25,17},{2,10},{10... | collective-permute-start | bytes 589832 | tf_op jit(solution)/shard_map/right_1/ppermute | solution.py:29
  43.8 1.5 %collective-permute-start.14 = (bf16[384,256]{1,0:T(8,128)(2,1)S(1)}, bf16[384,256]{1,0:T(8,128)(2,1)S(1)}, u32[]{:S(2)}, u32[]{:S(2)}) collective-permute-start(bf16[384,256]{1,0:T(8,128)(2,1)S(1)} %collective-permute-done.11.refs_0_), channel_id=1, source_target_pairs={{0,16},{8,24},{16,0},{24,8},{1,17},{9,25},{17,1},{25,9},{2,18},{10... | collective-permute-start | bytes 589832 | tf_op jit(solution)/shard_map/right_2/ppermute | solution.py:29
  45.4 6.8 %collective-permute-done.13.refs_1_ = bf16[384,256]{1,0:T(8,128)(2,1)S(1)} collective-permute-done((bf16[384,256]{1,0:T(8,128)(2,1)S(1)}, bf16[384,256]{1,0:T(8,128)(2,1)S(1)}, u32[]{:S(2)}, u32[]{:S(2)}) %collective-permute-start.13) | collective-permute-done | bytes 196640 | tf_op jit(solution)/shard_map/right_1/ppermute | solution.py:29
  52.2 1.5 %collective-permute-start.15 = (bf16[192,256]{1,0:T(8,128)(2,1)S(1)}, bf16[192,256]{1,0:T(8,128)(2,1)S(1)}, u32[]{:S(2)}, u32[]{:S(2)}) collective-permute-start(bf16[192,256]{1,0:T(8,128)(2,1)S(1)} %slice.18), channel_id=1, source_target_pairs={{0,16},{8,24},{16,0},{24,8},{1,17},{9,25},{17,1},{25,9},{2,18},{10... | collective-permute-start | bytes 294920 | tf_op jit(solution)/shard_map/right_3a/ppermute | solution.py:29
  53.8 1.0 %collective-permute-start.16 = (bf16[192,256]{1,0:T(8,128)(2,1)S(1)}, bf16[192,256]{1,0:T(8,128)(2,1)S(1)}, u32[]{:S(2)}, u32[]{:S(2)}) collective-permute-start(bf16[192,256]{1,0:T(8,128)(2,1)S(1)} %slice.19), channel_id=1, source_target_pairs={{0,8},{8,0},{16,24},{24,16},{1,9},{9,1},{17,25},{25,17},{2,10},{10... | collective-permute-start | bytes 294920 | tf_op jit(solution)/shard_map/right_3b/ppermute | solution.py:29
  54.7 2.7 %collective-permute-done.12.corners_ref = bf16[528,256]{1,0:T(8,128)(2,1)S(1)} collective-permute-done((bf16[528,256]{1,0:T(8,128)(2,1)S(1)}, bf16[528,256]{1,0:T(8,128)(2,1)S(1)}, u32[]{:S(2)}, u32[]{:S(2)}) %collective-permute-start.12) | collective-permute-done | bytes 270368 | tf_op jit(solution)/shard_map/corners/ppermute | solution.py:23
  57.5 1.0 %collective-permute-done.16.refs_4_ = bf16[192,256]{1,0:T(8,128)(2,1)S(1)} collective-permute-done((bf16[192,256]{1,0:T(8,128)(2,1)S(1)}, bf16[192,256]{1,0:T(8,128)(2,1)S(1)}, u32[]{:S(2)}, u32[]{:S(2)}) %collective-permute-start.16) | collective-permute-done | bytes 98336 | tf_op jit(solution)/shard_map/right_3b/ppermute | solution.py:29
  58.4 0.5 whole_right.1.right
  59.0 1.5 %update_rows.1 = bf16[1,256,1024]{2,1,0:T(8,128)(2,1)} custom-call(s32[1]{0:T(128)} %bitcast.me_ref, s32[1]{0:T(128)S(6)} %copy.6.rows_ref, s32[1]{0:T(128)S(6)} %copy.7.cols_ref, bf16[4,256,256]{2,1,0:T(8,128)(2,1)S(1)} %all-to-all-done.strips_ref, bf16[1024,1024]{1,0:T(8,128)(2,1)S(1)} %whole_right.1.right), custom_call_target="tpu_custom_call" | custom-call | flops 536870912 | bytes 4194304 | tf_op jit(solution)/shard_map/update_rows/pallas_call | solution.py:274
  (15 shorter events, 0.4 us)
Async XLA Ops:
  1.6 9.8 %collective-permute-start.1 = (bf16[512,256]{1,0:T(8,128)(2,1)S(1)}, bf16[512,256]{1,0:T(8,128)(2,1)S(1)}, u32[]{:S(2)}, u32[]{:S(2)}) collective-permute-start(bf16[512,256]{1,0:T(8,128)(2,1)S(1)} %get-tuple-element.22), channel_id=1, source_target_pairs={{0,8},{8,0},{16,24},{24,16},{1,9},{9,1},{17,25},{25,17},{2,10},{10... | collective-permute-start | bytes 786440 | tf_op jit(solution)/shard_map/far_0/ppermute | solution.py:29
  4.6 9.2 %collective-permute-start.2 = (bf16[512,256]{1,0:T(8,128)(2,1)S(1)}, bf16[512,256]{1,0:T(8,128)(2,1)S(1)}, u32[]{:S(2)}, u32[]{:S(2)}) collective-permute-start(bf16[512,256]{1,0:T(8,128)(2,1)S(1)} %get-tuple-element.24), channel_id=1, source_target_pairs={{0,16},{8,24},{16,0},{24,8},{1,17},{9,25},{17,1},{25,9},{2,18},{10... | collective-permute-start | bytes 786440 | tf_op jit(solution)/shard_map/far_1/ppermute | solution.py:29
  6.2 14.4 %collective-permute-start = (bf16[528,256]{1,0:T(8,128)(2,1)S(1)}, bf16[528,256]{1,0:T(8,128)(2,1)S(1)}, u32[]{:S(2)}, u32[]{:S(2)}) collective-permute-start(bf16[528,256]{1,0:T(8,128)(2,1)S(1)} %get-tuple-element.20), channel_id=1, source_target_pairs={{0,4},{1,5},{2,6},{3,7},{4,0},{5,1},{6,2},{7,3},{8,12},{9,13},{10,... | collective-permute-start | bytes 811016 | tf_op jit(solution)/shard_map/left/ppermute | solution.py:23
  8.7 7.8 %collective-permute-start.3 = (bf16[512,256]{1,0:T(8,128)(2,1)S(1)}, bf16[512,256]{1,0:T(8,128)(2,1)S(1)}, u32[]{:S(2)}, u32[]{:S(2)}) collective-permute-start(bf16[512,256]{1,0:T(8,128)(2,1)S(1)} %get-tuple-element.25), channel_id=1, source_target_pairs={{0,8},{8,0},{16,24},{24,16},{1,9},{9,1},{17,25},{25,17},{2,10},{10... | collective-permute-start | bytes 786440 | tf_op jit(solution)/shard_map/near_0/ppermute | solution.py:29
  9.3 8.7 %collective-permute-start.4 = (bf16[512,256]{1,0:T(8,128)(2,1)S(1)}, bf16[512,256]{1,0:T(8,128)(2,1)S(1)}, u32[]{:S(2)}, u32[]{:S(2)}) collective-permute-start(bf16[512,256]{1,0:T(8,128)(2,1)S(1)} %get-tuple-element.26), channel_id=1, source_target_pairs={{0,16},{8,24},{16,0},{24,8},{1,17},{9,25},{17,1},{25,9},{2,18},{10... | collective-permute-start | bytes 786440 | tf_op jit(solution)/shard_map/near_1/ppermute | solution.py:29
  20.5 9.4 %collective-permute-start.5 = (bf16[528,256]{1,0:T(8,128)(2,1)S(1)}, bf16[528,256]{1,0:T(8,128)(2,1)S(1)}, u32[]{:S(2)}, u32[]{:S(2)}) collective-permute-start(bf16[528,256]{1,0:T(8,128)(2,1)S(1)} %collective-permute-done.refs_0_), channel_id=1, source_target_pairs={{0,8},{8,0},{16,24},{24,16},{1,9},{9,1},{17,25},{25,17},{2,10},{10... | collective-permute-start | bytes 811016 | tf_op jit(solution)/shard_map/left_1/ppermute | solution.py:29
  21.0 9.5 %collective-permute-start.6 = (bf16[528,256]{1,0:T(8,128)(2,1)S(1)}, bf16[528,256]{1,0:T(8,128)(2,1)S(1)}, u32[]{:S(2)}, u32[]{:S(2)}) collective-permute-start(bf16[528,256]{1,0:T(8,128)(2,1)S(1)} %collective-permute-done.refs_0_), channel_id=1, source_target_pairs={{0,16},{8,24},{16,0},{24,8},{1,17},{9,25},{17,1},{25,9},{2,18},{10... | collective-permute-start | bytes 811016 | tf_op jit(solution)/shard_map/left_2/ppermute | solution.py:29
  21.5 13.6 %collective-permute-start.9 = (bf16[512,256]{1,0:T(8,128)(2,1)S(1)}, bf16[512,256]{1,0:T(8,128)(2,1)S(1)}, u32[]{:S(2)}, u32[]{:S(2)}) collective-permute-start(bf16[512,256]{1,0:T(8,128)(2,1)S(1)} %add_convert_fusion.1), channel_id=1, source_target_pairs={{0,16},{8,24},{16,0},{24,8},{1,17},{9,25},{17,1},{25,9},{2,18},{10... | collective-permute-start | bytes 786440 | tf_op jit(solution)/shard_map/via_0/ppermute | solution.py:29
  23.1 12.0 %collective-permute-start.10 = (bf16[512,256]{1,0:T(8,128)(2,1)S(1)}, bf16[512,256]{1,0:T(8,128)(2,1)S(1)}, u32[]{:S(2)}, u32[]{:S(2)}) collective-permute-start(bf16[512,256]{1,0:T(8,128)(2,1)S(1)} %add_convert_fusion), channel_id=1, source_target_pairs={{0,8},{8,0},{16,24},{24,16},{1,9},{9,1},{17,25},{25,17},{2,10},{10... | collective-permute-start | bytes 786440 | tf_op jit(solution)/shard_map/via_1/ppermute | solution.py:29
  29.9 6.6 %collective-permute-start.7 = (bf16[256,256]{1,0:T(8,128)(2,1)S(1)}, bf16[256,256]{1,0:T(8,128)(2,1)S(1)}, u32[]{:S(2)}, u32[]{:S(2)}) collective-permute-start(bf16[256,256]{1,0:T(8,128)(2,1)S(1)} %slice.16), channel_id=1, source_target_pairs={{0,16},{8,24},{16,0},{24,8},{1,17},{9,25},{17,1},{25,9},{2,18},{10... | collective-permute-start | bytes 393224 | tf_op jit(solution)/shard_map/left_3a/ppermute | solution.py:29
  30.5 6.0 %collective-permute-start.8 = (bf16[256,256]{1,0:T(8,128)(2,1)S(1)}, bf16[256,256]{1,0:T(8,128)(2,1)S(1)}, u32[]{:S(2)}, u32[]{:S(2)}) collective-permute-start(bf16[256,256]{1,0:T(8,128)(2,1)S(1)} %slice.17), channel_id=1, source_target_pairs={{0,8},{8,0},{16,24},{24,16},{1,9},{9,1},{17,25},{25,17},{2,10},{10... | collective-permute-start | bytes 393224 | tf_op jit(solution)/shard_map/left_3b/ppermute | solution.py:29
  32.0 9.8 %collective-permute-start.11 = (bf16[384,256]{1,0:T(8,128)(2,1)S(1)}, bf16[384,256]{1,0:T(8,128)(2,1)S(1)}, u32[]{:S(2)}, u32[]{:S(2)}) collective-permute-start(bf16[384,256]{1,0:T(8,128)(2,1)S(1)} %get-tuple-element.32), channel_id=1, source_target_pairs={{0,4},{1,5},{2,6},{3,7},{4,0},{5,1},{6,2},{7,3},{8,12},{9,13},{10,... | collective-permute-start | bytes 589832 | tf_op jit(solution)/shard_map/right/ppermute | solution.py:23
  38.3 20.7 %all-to-all-start = ((bf16[4,256,256]{2,1,0:T(8,128)(2,1)}), bf16[4,256,256]{2,1,0:T(8,128)(2,1)S(1)}, u32[]{:S(2)}, u32[]{:S(2)}) async-start(bf16[4,256,256]{2,1,0:T(8,128)(2,1)} %bitcast.1), calls=%async_computation | async-start | bytes 1048576 | tf_op jit(solution)/shard_map/strips/all_to_all | solution.py:346
  41.8 10.4 %collective-permute-start.13 = (bf16[384,256]{1,0:T(8,128)(2,1)S(1)}, bf16[384,256]{1,0:T(8,128)(2,1)S(1)}, u32[]{:S(2)}, u32[]{:S(2)}) collective-permute-start(bf16[384,256]{1,0:T(8,128)(2,1)S(1)} %collective-permute-done.11.refs_0_), channel_id=1, source_target_pairs={{0,8},{8,0},{16,24},{24,16},{1,9},{9,1},{17,25},{25,17},{2,10},{10... | collective-permute-start | bytes 589832 | tf_op jit(solution)/shard_map/right_1/ppermute | solution.py:29
  43.8 10.0 %collective-permute-start.14 = (bf16[384,256]{1,0:T(8,128)(2,1)S(1)}, bf16[384,256]{1,0:T(8,128)(2,1)S(1)}, u32[]{:S(2)}, u32[]{:S(2)}) collective-permute-start(bf16[384,256]{1,0:T(8,128)(2,1)S(1)} %collective-permute-done.11.refs_0_), channel_id=1, source_target_pairs={{0,16},{8,24},{16,0},{24,8},{1,17},{9,25},{17,1},{25,9},{2,18},{10... | collective-permute-start | bytes 589832 | tf_op jit(solution)/shard_map/right_2/ppermute | solution.py:29
  45.3 12.2 %collective-permute-start.12 = (bf16[528,256]{1,0:T(8,128)(2,1)S(1)}, bf16[528,256]{1,0:T(8,128)(2,1)S(1)}, u32[]{:S(2)}, u32[]{:S(2)}) collective-permute-start(bf16[528,256]{1,0:T(8,128)(2,1)S(1)} %get-tuple-element.33), channel_id=1, source_target_pairs={{0,4},{1,5},{2,6},{3,7},{4,0},{5,1},{6,2},{7,3},{8,12},{9,13},{10,... | collective-permute-start | bytes 811016 | tf_op jit(solution)/shard_map/corners/ppermute | solution.py:23
  52.2 5.2 %collective-permute-start.15 = (bf16[192,256]{1,0:T(8,128)(2,1)S(1)}, bf16[192,256]{1,0:T(8,128)(2,1)S(1)}, u32[]{:S(2)}, u32[]{:S(2)}) collective-permute-start(bf16[192,256]{1,0:T(8,128)(2,1)S(1)} %slice.18), channel_id=1, source_target_pairs={{0,16},{8,24},{16,0},{24,8},{1,17},{9,25},{17,1},{25,9},{2,18},{10... | collective-permute-start | bytes 294920 | tf_op jit(solution)/shard_map/right_3a/ppermute | solution.py:29
  53.8 4.7 %collective-permute-start.16 = (bf16[192,256]{1,0:T(8,128)(2,1)S(1)}, bf16[192,256]{1,0:T(8,128)(2,1)S(1)}, u32[]{:S(2)}, u32[]{:S(2)}) collective-permute-start(bf16[192,256]{1,0:T(8,128)(2,1)S(1)} %slice.19), channel_id=1, source_target_pairs={{0,8},{8,0},{16,24},{24,16},{1,9},{9,1},{17,25},{25,17},{2,10},{10... | collective-permute-start | bytes 294920 | tf_op jit(solution)/shard_map/right_3b/ppermute | solution.py:29

commit v8 on v7

--- a/solution.py
+++ b/solution.py
@@ -204,7 +204,7 @@
 def columns_kernel(groups, held, split, me_ref, rows_ref, cols_ref, *refs):
     pieces, refs = dealt(refs, held)
     terms, refs = dealt(refs, split)
-    out, left, folded, masked = refs
+    outs, (left, folded, masked, mixed) = refs[:groups], refs[groups:]
     me = me_ref[0]
     width, strip = masked.shape
     unfold(pieces, me, left, folded)
@@ -215,7 +215,9 @@
         total = functools.reduce(lambda a, b: a + b, [term[pl.ds(0, part), :].astype(F32) for term in used])
         keep = (row + index * part < rows_ref[0]) & (column < cols_ref[0])
         masked[pl.ds(index * part, part), :] = jnp.where(keep, total, 0.0).astype(BF16)
-    out[...] = jnp.dot(left[...], masked[...], preferred_element_type=F32).astype(BF16)
+    mixed[...] = jnp.dot(left[...], masked[...], preferred_element_type=F32).astype(BF16)
+    for flip, out in enumerate(outs):
+        out[...] = mixed[strip_of(jnp.bitwise_xor(me, flip), strip), :]
 
 
 def left_columns(me, rows_valid, cols_valid, pieces, terms, width):
@@ -225,11 +227,12 @@
     return pl.pallas_call(
         functools.partial(columns_kernel, groups, [len(part) for part in pieces], [len(part) for part in terms]),
         in_specs=[SMEM_SPEC] * 3 + [VMEM_SPEC] * len(flat),
-        out_specs=VMEM_SPEC,
-        out_shape=pltpu.VMEM((width, strip), BF16),
+        out_specs=[VMEM_SPEC] * groups,
+        out_shape=[pltpu.VMEM((strip, strip), BF16)] * groups,
         scratch_shapes=[
             pltpu.VMEM((width, width), BF16),
             pltpu.VMEM((width // 2, TILE), BF16),
+            pltpu.VMEM((width, strip), BF16),
             pltpu.VMEM((width, strip), BF16),
         ],
         compiler_params=pltpu.CompilerParams(vmem_limit_bytes=VMEM),
@@ -257,30 +260,37 @@
     )(me, corners, *flat)
 
 
-def rows_kernel(me_ref, rows_ref, cols_ref, strips_ref, right, out, mixed):
-    groups, strip, _ = strips_ref.shape
-    width = right.shape[0]
-    for k in range(groups):
-        mixed[:, pl.ds(k * strip, strip)] = strips_ref[k]
-    value = jnp.dot(mixed[...], right[...], preferred_element_type=F32)
+def rows_kernel(groups, me_ref, rows_ref, cols_ref, *refs):
+    strips, (right, out, mixed) = refs[:groups], refs[groups:]
+    me = me_ref[0]
+    strip, width = mixed.shape
+    if strip % 128 == 0:
+        for flip, part in enumerate(strips):
+            mixed[:, strip_of(jnp.bitwise_xor(me, flip), strip)] = part[...]
+        value = jnp.dot(mixed[...], right[...], preferred_element_type=F32)
+    else:
+        value = 0.0
+        for flip, part in enumerate(strips):
+            rows = right[strip_of(jnp.bitwise_xor(me, flip), strip), :]
+            value += jnp.dot(part[...], rows, preferred_element_type=F32)
     column = lax.broadcasted_iota(jnp.int32, (strip, width), 1)
-    row = lax.broadcasted_iota(jnp.int32, (strip, width), 0) + me_ref[0] * strip
+    row = lax.broadcasted_iota(jnp.int32, (strip, width), 0) + me * strip
     out[0] = jnp.where((row < rows_ref[0]) & (column < cols_ref[0]), value, 0.0).astype(BF16)
 
 
 def update_rows(me, rows_valid, cols_valid, strips, right):
     width = right.shape[0]
-    strip = strips.shape[1]
+    groups, strip = len(strips), strips[0].shape[0]
     return pl.pallas_call(
-        rows_kernel,
-        in_specs=[SMEM_SPEC] * 3 + [VMEM_SPEC] * 2,
+        functools.partial(rows_kernel, groups),
+        in_specs=[SMEM_SPEC] * 3 + [VMEM_SPEC] * (groups + 1),
         out_specs=VMEM_SPEC,
         out_shape=jax.ShapeDtypeStruct((1, strip, width), BF16),
         scratch_shapes=[pltpu.VMEM((strip, width), BF16)],
         compiler_params=pltpu.CompilerParams(vmem_limit_bytes=VMEM),
         cost_estimate=cost(2 * strip * width**2, 4 * width**2),
         name="update_rows",
-    )(me, rows_valid, cols_valid, strips, right)
+    )(me, rows_valid, cols_valid, *strips, right)
 
 
 def added(*terms):
@@ -311,7 +321,7 @@
         right = shifted(after(right, left), "right")
         left = after(left, via_0, via_1, near_0, near_1)
         via_0, via_1 = swapped(via_0, 2, "via_0"), swapped(via_1, 1, "via_1")
-        left_1, left_2 = swapped(left, 1, "left_1"), swapped(left, 2, "left_2")
+        left_1, left_2 = swapped(left, 1, "left_1"), swapped(after(left, via_0), 2, "left_2")
         cut = (left.shape[0] - EXTRA) // 2
         left_3a, left_3b = left_1[:cut], left_2[cut : 2 * cut]
         corners = shifted(after(corners, right, left_3a, left_3b), "corners")
@@ -342,8 +352,7 @@
         mixed = left_columns(me, rows_valid, cols_valid, lefts, terms, width)
         rights = [[right]] + [[swapped(right, flip, "right")] for flip in range(1, groups)]
     whole = whole_right(me, corners, rights, width)
-    with jax.named_scope("strips"):
-        strips = lax.all_to_all(mixed.reshape(groups, strip, strip), "dp", 0, 0)
+    strips = [mixed[0]] + [swapped(mixed[flip], flip, "strip_%d" % flip) for flip in range(1, groups)]
     return update_rows(me, rows_valid, cols_valid, strips, whole)
 
 

time: 61.4 us -> 52.8 us (0.86); the launches traced: 60.5 us -> 52.6 us
  waiting for transfers between devices: 27.7 us -> 19.8 us
  starting transfers between devices: 24.1 us -> 24.8 us
  Pallas kernels: 7.08 us -> 6.41 us
    ppermute x14 -> x17, waiting for transfers between devices: 22.5 us -> 8.69 us  [swapped(): lax.ppermute(value, 'dp', [(source, source ^ flip) for source in range(co...]
    ppermute x3, waiting for transfers between devices: 5.19 us -> 11.1 us  [shifted(): lax.ppermute(value, 'shard', [(source, (source + count // 2) % count) for...]
    ppermute x14 -> x17, starting transfers between devices: 17.7 us -> 21.5 us  [swapped(): lax.ppermute(value, 'dp', [(source, source ^ flip) for source in range(co...]
    all_to_all x1 -> x0, starting transfers between devices: 3.47 us -> none  [on_device(): strips = lax.all_to_all(mixed.reshape(groups, strip, strip), 'dp', 0, 0)]
    pallas_call x1, Pallas kernels: 1.79 us -> 1.05 us  [left_columns(): pl.pallas_call(functools.partial(columns_kernel, groups, [len(part) for p...]
  transfers between devices with their start and end apart: 18 -> 20, of which waited for: 11 -> 7; matrix products, arithmetic and copies ran while one was open for 0% -> 0% of each run, Pallas kernels for 7% -> 6%
where the time goes in v8:
time: 52.8 us; the launch traced here: 52.6 us
  starting transfers between devices  24.8 us (47%)
  waiting for transfers between devices  19.8 us (38%)
  Pallas kernels  6.41 us (12%)
  between operations  1.4 us (3%)
    ppermute x17, starting transfers between devices, swapped(): lax.ppermute(value, 'dp', [(source, source ^ flip) for source in range(co...  21.5 us
    ppermute x3, waiting for transfers between devices, shifted(): lax.ppermute(value, 'shard', [(source, (source + count // 2) % count) for...  11.1 us
    ppermute x17, waiting for transfers between devices, swapped(): lax.ppermute(value, 'dp', [(source, source ^ flip) for source in range(co...  8.69 us
    ppermute x3, starting transfers between devices, shifted(): lax.ppermute(value, 'shard', [(source, (source + count // 2) % count) for...  3.26 us
    pallas_call x2, Pallas kernels, messages(): pl.pallas_call(functools.partial(messages_kernel, wanted, strip), in_spec...  3.25 us
    pallas_call x1, Pallas kernels, update_rows(): pl.pallas_call(functools.partial(rows_kernel, groups), in_specs=[SMEM_SPE...  1.58 us
  transfers between devices with their start and end apart: 20, of which 7 were waited for; matrix products, arithmetic and copies ran while one was open for 0% of the time, Pallas kernels for 6%

profile of v8, /device:TPU:0, one launch (start us, length us, event | category | flops | bytes accessed | tf_op | source)
XLA Modules:
  0.0 52.6 jit_solution(8989658028000255495)
XLA Ops:
  0.0 1.6 %sent_first.1 = (bf16[512,256]{1,0:T(8,128)(2,1)S(1)}, bf16[512,256]{1,0:T(8,128)(2,1)S(1)}, bf16[512,256]{1,0:T(8,128)(2,1)S(1)}, bf16[512,256]{1,0:T(8,128)(2,1)S(1)}, bf16[528,256]{1,0:T(8,128)(2,1)S(1)}) custom-call(s32[1]{0:T(128)} %bitcast.me_ref, bf16[1,1,1024,1024]{3,2,1,0:T(8,128)(2,1)} %grad_ref.3, bf16[1,1024,1024]{2,1,0:T(8,128)(2,1)} %root_ref.2), custom_call_target="tpu_custom_call" | custom-call | tf_op jit(solution)/shard_map/sent_first/pallas_call | solution.py:133
  1.6 3.0 %collective-permute-start.1 = (bf16[512,256]{1,0:T(8,128)(2,1)S(1)}, bf16[512,256]{1,0:T(8,128)(2,1)S(1)}, u32[]{:S(2)}, u32[]{:S(2)}) collective-permute-start(bf16[512,256]{1,0:T(8,128)(2,1)S(1)} %get-tuple-element.27), channel_id=1, source_target_pairs={{0,8},{8,0},{16,24},{24,16},{1,9},{9,1},{17,25},{25,17},{2,10},{10... | collective-permute-start | bytes 786440 | tf_op jit(solution)/shard_map/far_0/ppermute | solution.py:29
  4.6 1.5 %collective-permute-start.2 = (bf16[512,256]{1,0:T(8,128)(2,1)S(1)}, bf16[512,256]{1,0:T(8,128)(2,1)S(1)}, u32[]{:S(2)}, u32[]{:S(2)}) collective-permute-start(bf16[512,256]{1,0:T(8,128)(2,1)S(1)} %get-tuple-element.29), channel_id=1, source_target_pairs={{0,16},{8,24},{16,0},{24,8},{1,17},{9,25},{17,1},{25,9},{2,18},{10... | collective-permute-start | bytes 786440 | tf_op jit(solution)/shard_map/far_1/ppermute | solution.py:29
  6.2 2.6 %collective-permute-start = (bf16[528,256]{1,0:T(8,128)(2,1)S(1)}, bf16[528,256]{1,0:T(8,128)(2,1)S(1)}, u32[]{:S(2)}, u32[]{:S(2)}) collective-permute-start(bf16[528,256]{1,0:T(8,128)(2,1)S(1)} %get-tuple-element.25), channel_id=1, source_target_pairs={{0,4},{1,5},{2,6},{3,7},{4,0},{5,1},{6,2},{7,3},{8,12},{9,13},{10,... | collective-permute-start | bytes 811016 | tf_op jit(solution)/shard_map/left/ppermute | solution.py:23
  8.7 0.5 %collective-permute-start.3 = (bf16[512,256]{1,0:T(8,128)(2,1)S(1)}, bf16[512,256]{1,0:T(8,128)(2,1)S(1)}, u32[]{:S(2)}, u32[]{:S(2)}) collective-permute-start(bf16[512,256]{1,0:T(8,128)(2,1)S(1)} %get-tuple-element.30), channel_id=1, source_target_pairs={{0,8},{8,0},{16,24},{24,16},{1,9},{9,1},{17,25},{25,17},{2,10},{10... | collective-permute-start | bytes 786440 | tf_op jit(solution)/shard_map/near_0/ppermute | solution.py:29
  9.3 0.5 collective-permute-start.4
  9.8 1.6 %sent_later.1 = (bf16[512,256]{1,0:T(8,128)(2,1)S(1)}, bf16[512,256]{1,0:T(8,128)(2,1)S(1)}, bf16[512,256]{1,0:T(8,128)(2,1)S(1)}, bf16[512,256]{1,0:T(8,128)(2,...) custom-call(s32[1]{0:T(128)} %bitcast.me_ref, bf16[1,1,1024,1024]{3,2,1,0:T(8,128)(2,1)} %grad_ref.3, ...), custom_call_target="tpu_custom_call" | custom-call | tf_op jit(solution)/shard_map/sent_later/pallas_call | solution.py:133
  11.5 0.1 add_convert_fusion.1
  11.6 2.4 %collective-permute-start.6 = (bf16[512,256]{1,0:T(8,128)(2,1)S(1)}, bf16[512,256]{1,0:T(8,128)(2,1)S(1)}, u32[]{:S(2)}, u32[]{:S(2)}) collective-permute-start(bf16[512,256]{1,0:T(8,128)(2,1)S(1)} %add_convert_fusion.1), channel_id=1, source_target_pairs={{0,16},{8,24},{16,0},{24,8},{1,17},{9,25},{17,1},{25,9},{2,18},{10... | collective-permute-start | bytes 786440 | tf_op jit(solution)/shard_map/via_0/ppermute | solution.py:29
  14.0 0.1 add_convert_fusion
  14.1 1.6 %collective-permute-start.10 = (bf16[512,256]{1,0:T(8,128)(2,1)S(1)}, bf16[512,256]{1,0:T(8,128)(2,1)S(1)}, u32[]{:S(2)}, u32[]{:S(2)}) collective-permute-start(bf16[512,256]{1,0:T(8,128)(2,1)S(1)} %add_convert_fusion), channel_id=1, source_target_pairs={{0,8},{8,0},{16,24},{24,16},{1,9},{9,1},{17,25},{25,17},{2,10},{10... | collective-permute-start | bytes 786440 | tf_op jit(solution)/shard_map/via_1/ppermute | solution.py:29
  15.6 4.9 %collective-permute-done.refs_0_ = bf16[528,256]{1,0:T(8,128)(2,1)S(1)} collective-permute-done((bf16[528,256]{1,0:T(8,128)(2,1)S(1)}, bf16[528,256]{1,0:T(8,128)(2,1)S(1)}, u32[]{:S(2)}, u32[]{:S(2)}) %collective-permute-start) | collective-permute-done | bytes 270368 | tf_op jit(solution)/shard_map/left/ppermute | solution.py:23
  20.5 0.6 %collective-permute-start.5 = (bf16[528,256]{1,0:T(8,128)(2,1)S(1)}, bf16[528,256]{1,0:T(8,128)(2,1)S(1)}, u32[]{:S(2)}, u32[]{:S(2)}) collective-permute-start(bf16[528,256]{1,0:T(8,128)(2,1)S(1)} %collective-permute-done.refs_0_), channel_id=1, source_target_pairs={{0,8},{8,0},{16,24},{24,16},{1,9},{9,1},{17,25},{25,17},{2,10},{10... | collective-permute-start | bytes 811016 | tf_op jit(solution)/shard_map/left_1/ppermute | solution.py:29
  21.1 2.5 %collective-permute-done.6.refs_7_ = bf16[512,256]{1,0:T(8,128)(2,1)S(1)} collective-permute-done((bf16[512,256]{1,0:T(8,128)(2,1)S(1)}, bf16[512,256]{1,0:T(8,128)(2,1)S(1)}, u32[]{:S(2)}, u32[]{:S(2)}) %collective-permute-start.6) | collective-permute-done | bytes 262176 | tf_op jit(solution)/shard_map/via_0/ppermute | solution.py:29
  23.6 1.5 %collective-permute-start.7 = (bf16[528,256]{1,0:T(8,128)(2,1)S(1)}, bf16[528,256]{1,0:T(8,128)(2,1)S(1)}, u32[]{:S(2)}, u32[]{:S(2)}) collective-permute-start(bf16[528,256]{1,0:T(8,128)(2,1)S(1)} %collective-permute-done.refs_0_), channel_id=1, source_target_pairs={{0,16},{8,24},{16,0},{24,8},{1,17},{9,25},{17,1},{25,9},{2,18},{10... | collective-permute-start | bytes 811016 | tf_op jit(solution)/shard_map/left_2/ppermute | solution.py:29
  25.2 6.2 %collective-permute-done.14.refs_0_ = bf16[384,256]{1,0:T(8,128)(2,1)S(1)} collective-permute-done((bf16[384,256]{1,0:T(8,128)(2,1)S(1)}, bf16[384,256]{1,0:T(8,128)(2,1)S(1)}, u32[]{:S(2)}, u32[]{:S(2)}) %collective-permute-start.14) | collective-permute-done | bytes 196640 | tf_op jit(solution)/shard_map/right/ppermute | solution.py:23
  31.4 0.5 %collective-permute-start.16 = (bf16[384,256]{1,0:T(8,128)(2,1)S(1)}, bf16[384,256]{1,0:T(8,128)(2,1)S(1)}, u32[]{:S(2)}, u32[]{:S(2)}) collective-permute-start(bf16[384,256]{1,0:T(8,128)(2,1)S(1)} %collective-permute-done.14.refs_0_), channel_id=1, source_target_pairs={{0,8},{8,0},{16,24},{24,16},{1,9},{9,1},{17,25},{25,17},{2,10},{10... | collective-permute-start | bytes 589832 | tf_op jit(solution)/shard_map/right_1/ppermute | solution.py:29
  31.9 0.4 collective-permute-start.17
  32.3 1.7 %collective-permute-start.8 = (bf16[256,256]{1,0:T(8,128)(2,1)S(1)}, bf16[256,256]{1,0:T(8,128)(2,1)S(1)}, u32[]{:S(2)}, u32[]{:S(2)}) collective-permute-start(bf16[256,256]{1,0:T(8,128)(2,1)S(1)} %slice.16), channel_id=1, source_target_pairs={{0,16},{8,24},{16,0},{24,8},{1,17},{9,25},{17,1},{25,9},{2,18},{10... | collective-permute-start | bytes 393224 | tf_op jit(solution)/shard_map/left_3a/ppermute | solution.py:29
  34.0 1.6 %collective-permute-start.9 = (bf16[256,256]{1,0:T(8,128)(2,1)S(1)}, bf16[256,256]{1,0:T(8,128)(2,1)S(1)}, u32[]{:S(2)}, u32[]{:S(2)}) collective-permute-start(bf16[256,256]{1,0:T(8,128)(2,1)S(1)} %slice.17), channel_id=1, source_target_pairs={{0,8},{8,0},{16,24},{24,16},{1,9},{9,1},{17,25},{25,17},{2,10},{10... | collective-permute-start | bytes 393224 | tf_op jit(solution)/shard_map/left_3b/ppermute | solution.py:29
  35.6 0.7 %collective-permute-start.15 = (bf16[528,256]{1,0:T(8,128)(2,1)S(1)}, bf16[528,256]{1,0:T(8,128)(2,1)S(1)}, u32[]{:S(2)}, u32[]{:S(2)}) collective-permute-start(bf16[528,256]{1,0:T(8,128)(2,1)S(1)} %get-tuple-element.43), channel_id=1, source_target_pairs={{0,4},{1,5},{2,6},{3,7},{4,0},{5,1},{6,2},{7,3},{8,12},{9,13},{10,... | collective-permute-start | bytes 811016 | tf_op jit(solution)/shard_map/corners/ppermute | solution.py:23
  36.3 1.3 %collective-permute-done.16.refs_1_ = bf16[384,256]{1,0:T(8,128)(2,1)S(1)} collective-permute-done((bf16[384,256]{1,0:T(8,128)(2,1)S(1)}, bf16[384,256]{1,0:T(8,128)(2,1)S(1)}, u32[]{:S(2)}, u32[]{:S(2)}) %collective-permute-start.16) | collective-permute-done | bytes 196640 | tf_op jit(solution)/shard_map/right_1/ppermute | solution.py:29
  37.6 0.6 %collective-permute-start.18 = (bf16[192,256]{1,0:T(8,128)(2,1)S(1)}, bf16[192,256]{1,0:T(8,128)(2,1)S(1)}, u32[]{:S(2)}, u32[]{:S(2)}) collective-permute-start(bf16[192,256]{1,0:T(8,128)(2,1)S(1)} %slice.18), channel_id=1, source_target_pairs={{0,16},{8,24},{16,0},{24,8},{1,17},{9,25},{17,1},{25,9},{2,18},{10... | collective-permute-start | bytes 294920 | tf_op jit(solution)/shard_map/right_3a/ppermute | solution.py:29
  39.5 0.8 %collective-permute-done.8.refs_3_ = bf16[256,256]{1,0:T(8,128)(2,1)S(1)} collective-permute-done((bf16[256,256]{1,0:T(8,128)(2,1)S(1)}, bf16[256,256]{1,0:T(8,128)(2,1)S(1)}, u32[]{:S(2)}, u32[]{:S(2)}) %collective-permute-start.8) | collective-permute-done | bytes 131104 | tf_op jit(solution)/shard_map/left_3a/ppermute | solution.py:29
  40.3 1.1 %left_columns.1 = (bf16[256,256]{1,0:T(8,128)(2,1)S(1)}, bf16[256,256]{1,0:T(8,128)(2,1)S(1)}, bf16[256,256]{1,0:T(8,128)(2,1)S(1)}, bf16[256,256]{1,0:T(8,128)(2,1)S(1)}) custom-call(s32[1]{0:T(128)} %bitcast.me_ref, s32[1]{0:T(128)S(6)} %copy.6.rows_ref, s32[1]{0:T(128)S(6)} %copy.7.cols_ref, bf16[528,256]{1,0:T(8,128)(2,1)S(1)} %collective-permute-done.refs_0_, ...), custom_call_target="tpu_custom_call" | custom-call | flops 536870912 | bytes 4194304 | tf_op jit(solution)/shard_map/left_columns/pallas_call | solution.py:227
  41.4 1.5 %collective-permute-start.11 = (bf16[256,256]{1,0:T(8,128)(2,1)S(1)}, bf16[256,256]{1,0:T(8,128)(2,1)S(1)}, u32[]{:S(2)}, u32[]{:S(2)}) collective-permute-start(bf16[256,256]{1,0:T(8,128)(2,1)S(1)} %get-tuple-element.37), channel_id=1, source_target_pairs={{0,8},{8,0},{16,24},{24,16},{1,9},{9,1},{17,25},{25,17},{2,10},{10... | collective-permute-start | bytes 393224 | tf_op jit(solution)/shard_map/strip_1/ppermute | solution.py:29
  42.9 0.5 collective-permute-start.12
  43.5 1.5 %collective-permute-start.13 = (bf16[256,256]{1,0:T(8,128)(2,1)S(1)}, bf16[256,256]{1,0:T(8,128)(2,1)S(1)}, u32[]{:S(2)}, u32[]{:S(2)}) collective-permute-start(bf16[256,256]{1,0:T(8,128)(2,1)S(1)} %get-tuple-element.39), channel_id=1, source_target_pairs={{0,24},{8,16},{16,8},{24,0},{1,25},{9,17},{17,9},{25,1},{2,26},{10... | collective-permute-start | bytes 393224 | tf_op jit(solution)/shard_map/strip_3/ppermute | solution.py:29
  45.0 1.5 %collective-permute-start.19 = (bf16[192,256]{1,0:T(8,128)(2,1)S(1)}, bf16[192,256]{1,0:T(8,128)(2,1)S(1)}, u32[]{:S(2)}, u32[]{:S(2)}) collective-permute-start(bf16[192,256]{1,0:T(8,128)(2,1)S(1)} %slice.19), channel_id=1, source_target_pairs={{0,8},{8,0},{16,24},{24,16},{1,9},{9,1},{17,25},{25,17},{2,10},{10... | collective-permute-start | bytes 294920 | tf_op jit(solution)/shard_map/right_3b/ppermute | solution.py:29
  46.5 3.9 %collective-permute-done.19.refs_4_ = bf16[192,256]{1,0:T(8,128)(2,1)S(1)} collective-permute-done((bf16[192,256]{1,0:T(8,128)(2,1)S(1)}, bf16[192,256]{1,0:T(8,128)(2,1)S(1)}, u32[]{:S(2)}, u32[]{:S(2)}) %collective-permute-start.19) | collective-permute-done | bytes 98336 | tf_op jit(solution)/shard_map/right_3b/ppermute | solution.py:29
  50.4 0.5 whole_right.1.refs_4_
  51.0 1.6 %update_rows.1 = bf16[1,256,1024]{2,1,0:T(8,128)(2,1)} custom-call(s32[1]{0:T(128)} %bitcast.me_ref, s32[1]{0:T(128)S(6)} %copy.6.rows_ref, s32[1]{0:T(128)S(6)} %copy.7.cols_ref, bf16[256,256]{1,0:T(8,128)(2,1)S(1)} %get-tuple-element.36.refs_0_, bf16[256,256]{1,0:T(8,128)(2,1)S(1)} %collective-permute-done.11.refs_1_, ...), custom_call_target="tpu_custom_call" | custom-call | flops 536870912 | bytes 4194304 | tf_op jit(solution)/shard_map/update_rows/pallas_call | solution.py:284
  (19 shorter events, 0.1 us)
Async XLA Ops:
  1.6 9.8 %collective-permute-start.1 = (bf16[512,256]{1,0:T(8,128)(2,1)S(1)}, bf16[512,256]{1,0:T(8,128)(2,1)S(1)}, u32[]{:S(2)}, u32[]{:S(2)}) collective-permute-start(bf16[512,256]{1,0:T(8,128)(2,1)S(1)} %get-tuple-element.27), channel_id=1, source_target_pairs={{0,8},{8,0},{16,24},{24,16},{1,9},{9,1},{17,25},{25,17},{2,10},{10... | collective-permute-start | bytes 786440 | tf_op jit(solution)/shard_map/far_0/ppermute | solution.py:29
  4.6 9.4 %collective-permute-start.2 = (bf16[512,256]{1,0:T(8,128)(2,1)S(1)}, bf16[512,256]{1,0:T(8,128)(2,1)S(1)}, u32[]{:S(2)}, u32[]{:S(2)}) collective-permute-start(bf16[512,256]{1,0:T(8,128)(2,1)S(1)} %get-tuple-element.29), channel_id=1, source_target_pairs={{0,16},{8,24},{16,0},{24,8},{1,17},{9,25},{17,1},{25,9},{2,18},{10... | collective-permute-start | bytes 786440 | tf_op jit(solution)/shard_map/far_1/ppermute | solution.py:29
  6.2 14.4 %collective-permute-start = (bf16[528,256]{1,0:T(8,128)(2,1)S(1)}, bf16[528,256]{1,0:T(8,128)(2,1)S(1)}, u32[]{:S(2)}, u32[]{:S(2)}) collective-permute-start(bf16[528,256]{1,0:T(8,128)(2,1)S(1)} %get-tuple-element.25), channel_id=1, source_target_pairs={{0,4},{1,5},{2,6},{3,7},{4,0},{5,1},{6,2},{7,3},{8,12},{9,13},{10,... | collective-permute-start | bytes 811016 | tf_op jit(solution)/shard_map/left/ppermute | solution.py:23
  8.7 11.8 %collective-permute-start.3 = (bf16[512,256]{1,0:T(8,128)(2,1)S(1)}, bf16[512,256]{1,0:T(8,128)(2,1)S(1)}, u32[]{:S(2)}, u32[]{:S(2)}) collective-permute-start(bf16[512,256]{1,0:T(8,128)(2,1)S(1)} %get-tuple-element.30), channel_id=1, source_target_pairs={{0,8},{8,0},{16,24},{24,16},{1,9},{9,1},{17,25},{25,17},{2,10},{10... | collective-permute-start | bytes 786440 | tf_op jit(solution)/shard_map/near_0/ppermute | solution.py:29
  9.3 11.2 %collective-permute-start.4 = (bf16[512,256]{1,0:T(8,128)(2,1)S(1)}, bf16[512,256]{1,0:T(8,128)(2,1)S(1)}, u32[]{:S(2)}, u32[]{:S(2)}) collective-permute-start(bf16[512,256]{1,0:T(8,128)(2,1)S(1)} %get-tuple-element.31), channel_id=1, source_target_pairs={{0,16},{8,24},{16,0},{24,8},{1,17},{9,25},{17,1},{25,9},{2,18},{10... | collective-permute-start | bytes 786440 | tf_op jit(solution)/shard_map/near_1/ppermute | solution.py:29
  11.6 12.1 %collective-permute-start.6 = (bf16[512,256]{1,0:T(8,128)(2,1)S(1)}, bf16[512,256]{1,0:T(8,128)(2,1)S(1)}, u32[]{:S(2)}, u32[]{:S(2)}) collective-permute-start(bf16[512,256]{1,0:T(8,128)(2,1)S(1)} %add_convert_fusion.1), channel_id=1, source_target_pairs={{0,16},{8,24},{16,0},{24,8},{1,17},{9,25},{17,1},{25,9},{2,18},{10... | collective-permute-start | bytes 786440 | tf_op jit(solution)/shard_map/via_0/ppermute | solution.py:29
  14.1 17.3 %collective-permute-start.10 = (bf16[512,256]{1,0:T(8,128)(2,1)S(1)}, bf16[512,256]{1,0:T(8,128)(2,1)S(1)}, u32[]{:S(2)}, u32[]{:S(2)}) collective-permute-start(bf16[512,256]{1,0:T(8,128)(2,1)S(1)} %add_convert_fusion), channel_id=1, source_target_pairs={{0,8},{8,0},{16,24},{24,16},{1,9},{9,1},{17,25},{25,17},{2,10},{10... | collective-permute-start | bytes 786440 | tf_op jit(solution)/shard_map/via_1/ppermute | solution.py:29
  20.5 10.9 %collective-permute-start.14 = (bf16[384,256]{1,0:T(8,128)(2,1)S(1)}, bf16[384,256]{1,0:T(8,128)(2,1)S(1)}, u32[]{:S(2)}, u32[]{:S(2)}) collective-permute-start(bf16[384,256]{1,0:T(8,128)(2,1)S(1)} %get-tuple-element.42), channel_id=1, source_target_pairs={{0,4},{1,5},{2,6},{3,7},{4,0},{5,1},{6,2},{7,3},{8,12},{9,13},{10,... | collective-permute-start | bytes 589832 | tf_op jit(solution)/shard_map/right/ppermute | solution.py:23
  20.5 11.8 %collective-permute-start.5 = (bf16[528,256]{1,0:T(8,128)(2,1)S(1)}, bf16[528,256]{1,0:T(8,128)(2,1)S(1)}, u32[]{:S(2)}, u32[]{:S(2)}) collective-permute-start(bf16[528,256]{1,0:T(8,128)(2,1)S(1)} %collective-permute-done.refs_0_), channel_id=1, source_target_pairs={{0,8},{8,0},{16,24},{24,16},{1,9},{9,1},{17,25},{25,17},{2,10},{10... | collective-permute-start | bytes 811016 | tf_op jit(solution)/shard_map/left_1/ppermute | solution.py:29
  23.6 10.4 %collective-permute-start.7 = (bf16[528,256]{1,0:T(8,128)(2,1)S(1)}, bf16[528,256]{1,0:T(8,128)(2,1)S(1)}, u32[]{:S(2)}, u32[]{:S(2)}) collective-permute-start(bf16[528,256]{1,0:T(8,128)(2,1)S(1)} %collective-permute-done.refs_0_), channel_id=1, source_target_pairs={{0,16},{8,24},{16,0},{24,8},{1,17},{9,25},{17,1},{25,9},{2,18},{10... | collective-permute-start | bytes 811016 | tf_op jit(solution)/shard_map/left_2/ppermute | solution.py:29
  31.4 6.2 %collective-permute-start.16 = (bf16[384,256]{1,0:T(8,128)(2,1)S(1)}, bf16[384,256]{1,0:T(8,128)(2,1)S(1)}, u32[]{:S(2)}, u32[]{:S(2)}) collective-permute-start(bf16[384,256]{1,0:T(8,128)(2,1)S(1)} %collective-permute-done.14.refs_0_), channel_id=1, source_target_pairs={{0,8},{8,0},{16,24},{24,16},{1,9},{9,1},{17,25},{25,17},{2,10},{10... | collective-permute-start | bytes 589832 | tf_op jit(solution)/shard_map/right_1/ppermute | solution.py:29
  31.9 11.5 %collective-permute-start.17 = (bf16[384,256]{1,0:T(8,128)(2,1)S(1)}, bf16[384,256]{1,0:T(8,128)(2,1)S(1)}, u32[]{:S(2)}, u32[]{:S(2)}) collective-permute-start(bf16[384,256]{1,0:T(8,128)(2,1)S(1)} %collective-permute-done.14.refs_0_), channel_id=1, source_target_pairs={{0,16},{8,24},{16,0},{24,8},{1,17},{9,25},{17,1},{25,9},{2,18},{10... | collective-permute-start | bytes 589832 | tf_op jit(solution)/shard_map/right_2/ppermute | solution.py:29
  32.3 8.0 %collective-permute-start.8 = (bf16[256,256]{1,0:T(8,128)(2,1)S(1)}, bf16[256,256]{1,0:T(8,128)(2,1)S(1)}, u32[]{:S(2)}, u32[]{:S(2)}) collective-permute-start(bf16[256,256]{1,0:T(8,128)(2,1)S(1)} %slice.16), channel_id=1, source_target_pairs={{0,16},{8,24},{16,0},{24,8},{1,17},{9,25},{17,1},{25,9},{2,18},{10... | collective-permute-start | bytes 393224 | tf_op jit(solution)/shard_map/left_3a/ppermute | solution.py:29
  34.0 6.3 %collective-permute-start.9 = (bf16[256,256]{1,0:T(8,128)(2,1)S(1)}, bf16[256,256]{1,0:T(8,128)(2,1)S(1)}, u32[]{:S(2)}, u32[]{:S(2)}) collective-permute-start(bf16[256,256]{1,0:T(8,128)(2,1)S(1)} %slice.17), channel_id=1, source_target_pairs={{0,8},{8,0},{16,24},{24,16},{1,9},{9,1},{17,25},{25,17},{2,10},{10... | collective-permute-start | bytes 393224 | tf_op jit(solution)/shard_map/left_3b/ppermute | solution.py:29
  35.6 14.8 %collective-permute-start.15 = (bf16[528,256]{1,0:T(8,128)(2,1)S(1)}, bf16[528,256]{1,0:T(8,128)(2,1)S(1)}, u32[]{:S(2)}, u32[]{:S(2)}) collective-permute-start(bf16[528,256]{1,0:T(8,128)(2,1)S(1)} %get-tuple-element.43), channel_id=1, source_target_pairs={{0,4},{1,5},{2,6},{3,7},{4,0},{5,1},{6,2},{7,3},{8,12},{9,13},{10,... | collective-permute-start | bytes 811016 | tf_op jit(solution)/shard_map/corners/ppermute | solution.py:23
  37.6 7.3 %collective-permute-start.18 = (bf16[192,256]{1,0:T(8,128)(2,1)S(1)}, bf16[192,256]{1,0:T(8,128)(2,1)S(1)}, u32[]{:S(2)}, u32[]{:S(2)}) collective-permute-start(bf16[192,256]{1,0:T(8,128)(2,1)S(1)} %slice.18), channel_id=1, source_target_pairs={{0,16},{8,24},{16,0},{24,8},{1,17},{9,25},{17,1},{25,9},{2,18},{10... | collective-permute-start | bytes 294920 | tf_op jit(solution)/shard_map/right_3a/ppermute | solution.py:29
  41.4 9.6 %collective-permute-start.11 = (bf16[256,256]{1,0:T(8,128)(2,1)S(1)}, bf16[256,256]{1,0:T(8,128)(2,1)S(1)}, u32[]{:S(2)}, u32[]{:S(2)}) collective-permute-start(bf16[256,256]{1,0:T(8,128)(2,1)S(1)} %get-tuple-element.37), channel_id=1, source_target_pairs={{0,8},{8,0},{16,24},{24,16},{1,9},{9,1},{17,25},{25,17},{2,10},{10... | collective-permute-start | bytes 393224 | tf_op jit(solution)/shard_map/strip_1/ppermute | solution.py:29
  42.9 8.0 %collective-permute-start.12 = (bf16[256,256]{1,0:T(8,128)(2,1)S(1)}, bf16[256,256]{1,0:T(8,128)(2,1)S(1)}, u32[]{:S(2)}, u32[]{:S(2)}) collective-permute-start(bf16[256,256]{1,0:T(8,128)(2,1)S(1)} %get-tuple-element.38), channel_id=1, source_target_pairs={{0,16},{8,24},{16,0},{24,8},{1,17},{9,25},{17,1},{25,9},{2,18},{10... | collective-permute-start | bytes 393224 | tf_op jit(solution)/shard_map/strip_2/ppermute | solution.py:29
  43.5 7.5 %collective-permute-start.13 = (bf16[256,256]{1,0:T(8,128)(2,1)S(1)}, bf16[256,256]{1,0:T(8,128)(2,1)S(1)}, u32[]{:S(2)}, u32[]{:S(2)}) collective-permute-start(bf16[256,256]{1,0:T(8,128)(2,1)S(1)} %get-tuple-element.39), channel_id=1, source_target_pairs={{0,24},{8,16},{16,8},{24,0},{1,25},{9,17},{17,9},{25,1},{2,26},{10... | collective-permute-start | bytes 393224 | tf_op jit(solution)/shard_map/strip_3/ppermute | solution.py:29
  45.0 5.5 %collective-permute-start.19 = (bf16[192,256]{1,0:T(8,128)(2,1)S(1)}, bf16[192,256]{1,0:T(8,128)(2,1)S(1)}, u32[]{:S(2)}, u32[]{:S(2)}) collective-permute-start(bf16[192,256]{1,0:T(8,128)(2,1)S(1)} %slice.19), channel_id=1, source_target_pairs={{0,8},{8,0},{16,24},{24,16},{1,9},{9,1},{17,25},{25,17},{2,10},{10... | collective-permute-start | bytes 294920 | tf_op jit(solution)/shard_map/right_3b/ppermute | solution.py:29

commit v9 on v8

--- a/solution.py
+++ b/solution.py
@@ -321,24 +321,19 @@
         right = shifted(after(right, left), "right")
         left = after(left, via_0, via_1, near_0, near_1)
         via_0, via_1 = swapped(via_0, 2, "via_0"), swapped(via_1, 1, "via_1")
-        left_1, left_2 = swapped(left, 1, "left_1"), swapped(after(left, via_0), 2, "left_2")
-        cut = (left.shape[0] - EXTRA) // 2
-        left_3a, left_3b = left_1[:cut], left_2[cut : 2 * cut]
-        corners = shifted(after(corners, right, left_3a, left_3b), "corners")
-        left_3 = [swapped(left_3a, 2, "left_3a"), swapped(left_3b, 1, "left_3b")]
+        left_1, left_2, left_3 = [swapped(left if flip < 3 else after(left, via_0), flip, "left_%d" % flip) for flip in (1, 2, 3)]
+        corners = shifted(after(corners, right, left_1, left_2), "corners")
         mixed = left_columns(
             me,
             rows_valid,
             cols_valid,
-            [[left], [left_1], [left_2], left_3],
+            [[left], [left_1], [left_2], [left_3]],
             [[kept[2], near_0, via_0], [kept[3], near_1, via_1]],
             width,
         )
         right = after(right, via_0, via_1)
-        right_1, right_2 = swapped(right, 1, "right_1"), swapped(right, 2, "right_2")
-        cut = right.shape[0] // 2
-        right_3 = [swapped(right_1[:cut], 2, "right_3a"), swapped(right_2[cut:], 1, "right_3b")]
-        rights = [[right], [right_1], [right_2], right_3]
+        right_1, right_2, right_3 = [swapped(right, flip, "right_%d" % flip) for flip in (1, 2, 3)]
+        rights = [[right], [right_1], [right_2], [right_3]]
     else:
         (left,) = messages(me, grads, left_roots, groups, [], False, "sent_first")
         right, corners = messages(me, grads, right_roots, groups, [], True, "sent_later")

time: 52.8 us -> 52.8 us (level)
  starting transfers between devices: 24.8 us -> 29.9 us
  waiting for transfers between devices: 19.8 us -> 14.9 us
    ppermute x3, starting transfers between devices: 3.26 us -> 9.59 us  [shifted(): lax.ppermute(value, 'shard', [(source, (source + count // 2) % count) for...]
    ppermute x3, waiting for transfers between devices: 11.1 us -> 7.03 us  [shifted(): lax.ppermute(value, 'shard', [(source, (source + count // 2) % count) for...]
    ppermute x17 -> x15, starting transfers between devices: 21.5 us -> 20.3 us  [swapped(): lax.ppermute(value, 'dp', [(source, source ^ flip) for source in range(co...]
    ppermute x17 -> x15, waiting for transfers between devices: 8.69 us -> 7.83 us  [swapped(): lax.ppermute(value, 'dp', [(source, source ^ flip) for source in range(co...]
  transfers between devices with their start and end apart: 20 -> 18, of which waited for: 7 -> 10; matrix products, arithmetic and copies ran while one was open for 0% -> 0% of each run, Pallas kernels for 6% -> 6%
where the time goes in v9:
time: 52.8 us; the launch traced here: 52.6 us
  starting transfers between devices  29.9 us (57%)
  waiting for transfers between devices  14.9 us (28%)
  Pallas kernels  6.39 us (12%)
  between operations  1.37 us (3%)
    ppermute x15, starting transfers between devices, swapped(): lax.ppermute(value, 'dp', [(source, source ^ flip) for source in range(co...  20.3 us
    ppermute x3, starting transfers between devices, shifted(): lax.ppermute(value, 'shard', [(source, (source + count // 2) % count) for...  9.59 us
    ppermute x15, waiting for transfers between devices, swapped(): lax.ppermute(value, 'dp', [(source, source ^ flip) for source in range(co...  7.83 us
    ppermute x3, waiting for transfers between devices, shifted(): lax.ppermute(value, 'shard', [(source, (source + count // 2) % count) for...  7.03 us
    pallas_call x2, Pallas kernels, messages(): pl.pallas_call(functools.partial(messages_kernel, wanted, strip), in_spec...  3.25 us
    pallas_call x1, Pallas kernels, update_rows(): pl.pallas_call(functools.partial(rows_kernel, groups), in_specs=[SMEM_SPE...  1.57 us
  transfers between devices with their start and end apart: 18, of which 10 were waited for; matrix products, arithmetic and copies ran while one was open for 0% of the time, Pallas kernels for 6%

profile of v9, /device:TPU:0, one launch (start us, length us, event | category | flops | bytes accessed | tf_op | source)
XLA Modules:
  0.0 52.6 jit_solution(7740043469365999170)
XLA Ops:
  0.0 1.6 %sent_first.1 = (bf16[512,256]{1,0:T(8,128)(2,1)S(1)}, bf16[512,256]{1,0:T(8,128)(2,1)S(1)}, bf16[512,256]{1,0:T(8,128)(2,1)S(1)}, bf16[512,256]{1,0:T(8,128)(2,1)S(1)}, bf16[528,256]{1,0:T(8,128)(2,1)S(1)}) custom-call(s32[1]{0:T(128)} %bitcast.me_ref, bf16[1,1,1024,1024]{3,2,1,0:T(8,128)(2,1)} %grad_ref.3, bf16[1,1024,1024]{2,1,0:T(8,128)(2,1)} %root_ref.2), custom_call_target="tpu_custom_call" | custom-call | tf_op jit(solution)/shard_map/sent_first/pallas_call | solution.py:133
  1.6 3.0 %collective-permute-start.1 = (bf16[512,256]{1,0:T(8,128)(2,1)S(1)}, bf16[512,256]{1,0:T(8,128)(2,1)S(1)}, u32[]{:S(2)}, u32[]{:S(2)}) collective-permute-start(bf16[512,256]{1,0:T(8,128)(2,1)S(1)} %get-tuple-element.27), channel_id=1, source_target_pairs={{0,8},{8,0},{16,24},{24,16},{1,9},{9,1},{17,25},{25,17},{2,10},{10... | collective-permute-start | bytes 786440 | tf_op jit(solution)/shard_map/far_0/ppermute | solution.py:29
  4.6 1.5 %collective-permute-start.2 = (bf16[512,256]{1,0:T(8,128)(2,1)S(1)}, bf16[512,256]{1,0:T(8,128)(2,1)S(1)}, u32[]{:S(2)}, u32[]{:S(2)}) collective-permute-start(bf16[512,256]{1,0:T(8,128)(2,1)S(1)} %get-tuple-element.29), channel_id=1, source_target_pairs={{0,16},{8,24},{16,0},{24,8},{1,17},{9,25},{17,1},{25,9},{2,18},{10... | collective-permute-start | bytes 786440 | tf_op jit(solution)/shard_map/far_1/ppermute | solution.py:29
  6.2 2.6 %collective-permute-start = (bf16[528,256]{1,0:T(8,128)(2,1)S(1)}, bf16[528,256]{1,0:T(8,128)(2,1)S(1)}, u32[]{:S(2)}, u32[]{:S(2)}) collective-permute-start(bf16[528,256]{1,0:T(8,128)(2,1)S(1)} %get-tuple-element.25), channel_id=1, source_target_pairs={{0,4},{1,5},{2,6},{3,7},{4,0},{5,1},{6,2},{7,3},{8,12},{9,13},{10,... | collective-permute-start | bytes 811016 | tf_op jit(solution)/shard_map/left/ppermute | solution.py:23
  8.7 0.5 %collective-permute-start.3 = (bf16[512,256]{1,0:T(8,128)(2,1)S(1)}, bf16[512,256]{1,0:T(8,128)(2,1)S(1)}, u32[]{:S(2)}, u32[]{:S(2)}) collective-permute-start(bf16[512,256]{1,0:T(8,128)(2,1)S(1)} %get-tuple-element.30), channel_id=1, source_target_pairs={{0,8},{8,0},{16,24},{24,16},{1,9},{9,1},{17,25},{25,17},{2,10},{10... | collective-permute-start | bytes 786440 | tf_op jit(solution)/shard_map/near_0/ppermute | solution.py:29
  9.3 0.5 collective-permute-start.4
  9.8 1.6 %sent_later.1 = (bf16[512,256]{1,0:T(8,128)(2,1)S(1)}, bf16[512,256]{1,0:T(8,128)(2,1)S(1)}, bf16[512,256]{1,0:T(8,128)(2,1)S(1)}, bf16[512,256]{1,0:T(8,128)(2,...) custom-call(s32[1]{0:T(128)} %bitcast.me_ref, bf16[1,1,1024,1024]{3,2,1,0:T(8,128)(2,1)} %grad_ref.3, ...), custom_call_target="tpu_custom_call" | custom-call | tf_op jit(solution)/shard_map/sent_later/pallas_call | solution.py:133
  11.6 2.4 %collective-permute-start.7 = (bf16[512,256]{1,0:T(8,128)(2,1)S(1)}, bf16[512,256]{1,0:T(8,128)(2,1)S(1)}, u32[]{:S(2)}, u32[]{:S(2)}) collective-permute-start(bf16[512,256]{1,0:T(8,128)(2,1)S(1)} %add_convert_fusion.1), channel_id=1, source_target_pairs={{0,16},{8,24},{16,0},{24,8},{1,17},{9,25},{17,1},{25,9},{2,18},{10... | collective-permute-start | bytes 786440 | tf_op jit(solution)/shard_map/via_0/ppermute | solution.py:29
  14.1 1.6 %collective-permute-start.9 = (bf16[512,256]{1,0:T(8,128)(2,1)S(1)}, bf16[512,256]{1,0:T(8,128)(2,1)S(1)}, u32[]{:S(2)}, u32[]{:S(2)}) collective-permute-start(bf16[512,256]{1,0:T(8,128)(2,1)S(1)} %add_convert_fusion), channel_id=1, source_target_pairs={{0,8},{8,0},{16,24},{24,16},{1,9},{9,1},{17,25},{25,17},{2,10},{10... | collective-permute-start | bytes 786440 | tf_op jit(solution)/shard_map/via_1/ppermute | solution.py:29
  15.6 2.4 %collective-permute-done.3.refs_5_ = bf16[512,256]{1,0:T(8,128)(2,1)S(1)} collective-permute-done((bf16[512,256]{1,0:T(8,128)(2,1)S(1)}, bf16[512,256]{1,0:T(8,128)(2,1)S(1)}, u32[]{:S(2)}, u32[]{:S(2)}) %collective-permute-start.3) | collective-permute-done | bytes 262176 | tf_op jit(solution)/shard_map/near_0/ppermute | solution.py:29
  18.0 1.5 %collective-permute-done.4.refs_8_ = bf16[512,256]{1,0:T(8,128)(2,1)S(1)} collective-permute-done((bf16[512,256]{1,0:T(8,128)(2,1)S(1)}, bf16[512,256]{1,0:T(8,128)(2,1)S(1)}, u32[]{:S(2)}, u32[]{:S(2)}) %collective-permute-start.4) | collective-permute-done | bytes 262176 | tf_op jit(solution)/shard_map/near_1/ppermute | solution.py:29
  19.5 1.0 %collective-permute-done.refs_0_ = bf16[528,256]{1,0:T(8,128)(2,1)S(1)} collective-permute-done((bf16[528,256]{1,0:T(8,128)(2,1)S(1)}, bf16[528,256]{1,0:T(8,128)(2,1)S(1)}, u32[]{:S(2)}, u32[]{:S(2)}) %collective-permute-start) | collective-permute-done | bytes 270368 | tf_op jit(solution)/shard_map/left/ppermute | solution.py:23
  20.5 0.5 %collective-permute-start.5 = (bf16[528,256]{1,0:T(8,128)(2,1)S(1)}, bf16[528,256]{1,0:T(8,128)(2,1)S(1)}, u32[]{:S(2)}, u32[]{:S(2)}) collective-permute-start(bf16[528,256]{1,0:T(8,128)(2,1)S(1)} %collective-permute-done.refs_0_), channel_id=1, source_target_pairs={{0,8},{8,0},{16,24},{24,16},{1,9},{9,1},{17,25},{25,17},{2,10},{10... | collective-permute-start | bytes 811016 | tf_op jit(solution)/shard_map/left_1/ppermute | solution.py:29
  21.0 0.5 collective-permute-start.6
  21.5 2.6 %collective-permute-start.13 = (bf16[384,256]{1,0:T(8,128)(2,1)S(1)}, bf16[384,256]{1,0:T(8,128)(2,1)S(1)}, u32[]{:S(2)}, u32[]{:S(2)}) collective-permute-start(bf16[384,256]{1,0:T(8,128)(2,1)S(1)} %get-tuple-element.42), channel_id=1, source_target_pairs={{0,4},{1,5},{2,6},{3,7},{4,0},{5,1},{6,2},{7,3},{8,12},{9,13},{10,... | collective-permute-start | bytes 589832 | tf_op jit(solution)/shard_map/right/ppermute | solution.py:23
  24.1 0.8 %collective-permute-done.7.refs_6_ = bf16[512,256]{1,0:T(8,128)(2,1)S(1)} collective-permute-done((bf16[512,256]{1,0:T(8,128)(2,1)S(1)}, bf16[512,256]{1,0:T(8,128)(2,1)S(1)}, u32[]{:S(2)}, u32[]{:S(2)}) %collective-permute-start.7) | collective-permute-done | bytes 262176 | tf_op jit(solution)/shard_map/via_0/ppermute | solution.py:29
  24.9 1.6 %collective-permute-start.8 = (bf16[528,256]{1,0:T(8,128)(2,1)S(1)}, bf16[528,256]{1,0:T(8,128)(2,1)S(1)}, u32[]{:S(2)}, u32[]{:S(2)}) collective-permute-start(bf16[528,256]{1,0:T(8,128)(2,1)S(1)} %collective-permute-done.refs_0_), channel_id=1, source_target_pairs={{0,24},{8,16},{16,8},{24,0},{1,25},{9,17},{17,9},{25,1},{2,26},{10... | collective-permute-start | bytes 811016 | tf_op jit(solution)/shard_map/left_3/ppermute | solution.py:29
  26.5 5.3 %collective-permute-done.13.refs_0_ = bf16[384,256]{1,0:T(8,128)(2,1)S(1)} collective-permute-done((bf16[384,256]{1,0:T(8,128)(2,1)S(1)}, bf16[384,256]{1,0:T(8,128)(2,1)S(1)}, u32[]{:S(2)}, u32[]{:S(2)}) %collective-permute-start.13) | collective-permute-done | bytes 196640 | tf_op jit(solution)/shard_map/right/ppermute | solution.py:23
  31.8 1.6 %collective-permute-start.15 = (bf16[384,256]{1,0:T(8,128)(2,1)S(1)}, bf16[384,256]{1,0:T(8,128)(2,1)S(1)}, u32[]{:S(2)}, u32[]{:S(2)}) collective-permute-start(bf16[384,256]{1,0:T(8,128)(2,1)S(1)} %collective-permute-done.13.refs_0_), channel_id=1, source_target_pairs={{0,8},{8,0},{16,24},{24,16},{1,9},{9,1},{17,25},{25,17},{2,10},{10... | collective-permute-start | bytes 589832 | tf_op jit(solution)/shard_map/right_1/ppermute | solution.py:29
  33.3 1.5 %collective-permute-start.16 = (bf16[384,256]{1,0:T(8,128)(2,1)S(1)}, bf16[384,256]{1,0:T(8,128)(2,1)S(1)}, u32[]{:S(2)}, u32[]{:S(2)}) collective-permute-start(bf16[384,256]{1,0:T(8,128)(2,1)S(1)} %collective-permute-done.13.refs_0_), channel_id=1, source_target_pairs={{0,16},{8,24},{16,0},{24,8},{1,17},{9,25},{17,1},{25,9},{2,18},{10... | collective-permute-start | bytes 589832 | tf_op jit(solution)/shard_map/right_2/ppermute | solution.py:29
  34.9 4.4 %collective-permute-start.14 = (bf16[528,256]{1,0:T(8,128)(2,1)S(1)}, bf16[528,256]{1,0:T(8,128)(2,1)S(1)}, u32[]{:S(2)}, u32[]{:S(2)}) collective-permute-start(bf16[528,256]{1,0:T(8,128)(2,1)S(1)} %get-tuple-element.43), channel_id=1, source_target_pairs={{0,4},{1,5},{2,6},{3,7},{4,0},{5,1},{6,2},{7,3},{8,12},{9,13},{10,... | collective-permute-start | bytes 811016 | tf_op jit(solution)/shard_map/corners/ppermute | solution.py:23
  39.3 1.5 %collective-permute-start.17 = (bf16[384,256]{1,0:T(8,128)(2,1)S(1)}, bf16[384,256]{1,0:T(8,128)(2,1)S(1)}, u32[]{:S(2)}, u32[]{:S(2)}) collective-permute-start(bf16[384,256]{1,0:T(8,128)(2,1)S(1)} %collective-permute-done.13.refs_0_), channel_id=1, source_target_pairs={{0,24},{8,16},{16,8},{24,0},{1,25},{9,17},{17,9},{25,1},{2,26},{10... | collective-permute-start | bytes 589832 | tf_op jit(solution)/shard_map/right_3/ppermute | solution.py:29
  42.1 1.0 %left_columns.1 = (bf16[256,256]{1,0:T(8,128)(2,1)S(1)}, bf16[256,256]{1,0:T(8,128)(2,1)S(1)}, bf16[256,256]{1,0:T(8,128)(2,1)S(1)}, bf16[256,256]{1,0:T(8,128)(2,1)S(1)}) custom-call(s32[1]{0:T(128)} %bitcast.me_ref, s32[1]{0:T(128)S(6)} %copy.6.rows_ref, s32[1]{0:T(128)S(6)} %copy.7.cols_ref, bf16[528,256]{1,0:T(8,128)(2,1)S(1)} %collective-permute-done.refs_0_, ...), custom_call_target="tpu_custom_call" | custom-call | flops 536870912 | bytes 4194304 | tf_op jit(solution)/shard_map/left_columns/pallas_call | solution.py:227
  43.1 1.6 %collective-permute-start.10 = (bf16[256,256]{1,0:T(8,128)(2,1)S(1)}, bf16[256,256]{1,0:T(8,128)(2,1)S(1)}, u32[]{:S(2)}, u32[]{:S(2)}) collective-permute-start(bf16[256,256]{1,0:T(8,128)(2,1)S(1)} %get-tuple-element.37), channel_id=1, source_target_pairs={{0,8},{8,0},{16,24},{24,16},{1,9},{9,1},{17,25},{25,17},{2,10},{10... | collective-permute-start | bytes 393224 | tf_op jit(solution)/shard_map/strip_1/ppermute | solution.py:29
  44.7 0.5 collective-permute-start.11
  45.2 1.5 %collective-permute-start.12 = (bf16[256,256]{1,0:T(8,128)(2,1)S(1)}, bf16[256,256]{1,0:T(8,128)(2,1)S(1)}, u32[]{:S(2)}, u32[]{:S(2)}) collective-permute-start(bf16[256,256]{1,0:T(8,128)(2,1)S(1)} %get-tuple-element.39), channel_id=1, source_target_pairs={{0,24},{8,16},{16,8},{24,0},{1,25},{9,17},{17,9},{25,1},{2,26},{10... | collective-permute-start | bytes 393224 | tf_op jit(solution)/shard_map/strip_3/ppermute | solution.py:29
  46.7 0.7 %collective-permute-done.14.corners_ref = bf16[528,256]{1,0:T(8,128)(2,1)S(1)} collective-permute-done((bf16[528,256]{1,0:T(8,128)(2,1)S(1)}, bf16[528,256]{1,0:T(8,128)(2,1)S(1)}, u32[]{:S(2)}, u32[]{:S(2)}) %collective-permute-start.14) | collective-permute-done | bytes 270368 | tf_op jit(solution)/shard_map/corners/ppermute | solution.py:23
  47.4 0.5 whole_right.1.refs_4_
  47.9 0.2 collective-permute-done.10.refs_1_
  48.2 1.5 %collective-permute-done.11.refs_2_ = bf16[256,256]{1,0:T(8,128)(2,1)S(1)} collective-permute-done((bf16[256,256]{1,0:T(8,128)(2,1)S(1)}, bf16[256,256]{1,0:T(8,128)(2,1)S(1)}, u32[]{:S(2)}, u32[]{:S(2)}) %collective-permute-start.11) | collective-permute-done | bytes 131104 | tf_op jit(solution)/shard_map/strip_2/ppermute | solution.py:29
  49.7 1.4 %collective-permute-done.12.refs_3_ = bf16[256,256]{1,0:T(8,128)(2,1)S(1)} collective-permute-done((bf16[256,256]{1,0:T(8,128)(2,1)S(1)}, bf16[256,256]{1,0:T(8,128)(2,1)S(1)}, u32[]{:S(2)}, u32[]{:S(2)}) %collective-permute-start.12) | collective-permute-done | bytes 131104 | tf_op jit(solution)/shard_map/strip_3/ppermute | solution.py:29
  51.1 1.6 %update_rows.1 = bf16[1,256,1024]{2,1,0:T(8,128)(2,1)} custom-call(s32[1]{0:T(128)} %bitcast.me_ref, s32[1]{0:T(128)S(6)} %copy.6.rows_ref, s32[1]{0:T(128)S(6)} %copy.7.cols_ref, bf16[256,256]{1,0:T(8,128)(2,1)S(1)} %get-tuple-element.36.refs_0_, bf16[256,256]{1,0:T(8,128)(2,1)S(1)} %collective-permute-done.10.refs_1_, ...), custom_call_target="tpu_custom_call" | custom-call | flops 536870912 | bytes 4194304 | tf_op jit(solution)/shard_map/update_rows/pallas_call | solution.py:284
  (11 shorter events, 0.2 us)
Async XLA Ops:
  1.6 9.8 %collective-permute-start.1 = (bf16[512,256]{1,0:T(8,128)(2,1)S(1)}, bf16[512,256]{1,0:T(8,128)(2,1)S(1)}, u32[]{:S(2)}, u32[]{:S(2)}) collective-permute-start(bf16[512,256]{1,0:T(8,128)(2,1)S(1)} %get-tuple-element.27), channel_id=1, source_target_pairs={{0,8},{8,0},{16,24},{24,16},{1,9},{9,1},{17,25},{25,17},{2,10},{10... | collective-permute-start | bytes 786440 | tf_op jit(solution)/shard_map/far_0/ppermute | solution.py:29
  4.6 9.4 %collective-permute-start.2 = (bf16[512,256]{1,0:T(8,128)(2,1)S(1)}, bf16[512,256]{1,0:T(8,128)(2,1)S(1)}, u32[]{:S(2)}, u32[]{:S(2)}) collective-permute-start(bf16[512,256]{1,0:T(8,128)(2,1)S(1)} %get-tuple-element.29), channel_id=1, source_target_pairs={{0,16},{8,24},{16,0},{24,8},{1,17},{9,25},{17,1},{25,9},{2,18},{10... | collective-permute-start | bytes 786440 | tf_op jit(solution)/shard_map/far_1/ppermute | solution.py:29
  6.2 14.4 %collective-permute-start = (bf16[528,256]{1,0:T(8,128)(2,1)S(1)}, bf16[528,256]{1,0:T(8,128)(2,1)S(1)}, u32[]{:S(2)}, u32[]{:S(2)}) collective-permute-start(bf16[528,256]{1,0:T(8,128)(2,1)S(1)} %get-tuple-element.25), channel_id=1, source_target_pairs={{0,4},{1,5},{2,6},{3,7},{4,0},{5,1},{6,2},{7,3},{8,12},{9,13},{10,... | collective-permute-start | bytes 811016 | tf_op jit(solution)/shard_map/left/ppermute | solution.py:23
  8.7 9.2 %collective-permute-start.3 = (bf16[512,256]{1,0:T(8,128)(2,1)S(1)}, bf16[512,256]{1,0:T(8,128)(2,1)S(1)}, u32[]{:S(2)}, u32[]{:S(2)}) collective-permute-start(bf16[512,256]{1,0:T(8,128)(2,1)S(1)} %get-tuple-element.30), channel_id=1, source_target_pairs={{0,8},{8,0},{16,24},{24,16},{1,9},{9,1},{17,25},{25,17},{2,10},{10... | collective-permute-start | bytes 786440 | tf_op jit(solution)/shard_map/near_0/ppermute | solution.py:29
  9.3 10.2 %collective-permute-start.4 = (bf16[512,256]{1,0:T(8,128)(2,1)S(1)}, bf16[512,256]{1,0:T(8,128)(2,1)S(1)}, u32[]{:S(2)}, u32[]{:S(2)}) collective-permute-start(bf16[512,256]{1,0:T(8,128)(2,1)S(1)} %get-tuple-element.31), channel_id=1, source_target_pairs={{0,16},{8,24},{16,0},{24,8},{1,17},{9,25},{17,1},{25,9},{2,18},{10... | collective-permute-start | bytes 786440 | tf_op jit(solution)/shard_map/near_1/ppermute | solution.py:29
  11.6 13.4 %collective-permute-start.7 = (bf16[512,256]{1,0:T(8,128)(2,1)S(1)}, bf16[512,256]{1,0:T(8,128)(2,1)S(1)}, u32[]{:S(2)}, u32[]{:S(2)}) collective-permute-start(bf16[512,256]{1,0:T(8,128)(2,1)S(1)} %add_convert_fusion.1), channel_id=1, source_target_pairs={{0,16},{8,24},{16,0},{24,8},{1,17},{9,25},{17,1},{25,9},{2,18},{10... | collective-permute-start | bytes 786440 | tf_op jit(solution)/shard_map/via_0/ppermute | solution.py:29
  14.1 17.7 %collective-permute-start.9 = (bf16[512,256]{1,0:T(8,128)(2,1)S(1)}, bf16[512,256]{1,0:T(8,128)(2,1)S(1)}, u32[]{:S(2)}, u32[]{:S(2)}) collective-permute-start(bf16[512,256]{1,0:T(8,128)(2,1)S(1)} %add_convert_fusion), channel_id=1, source_target_pairs={{0,8},{8,0},{16,24},{24,16},{1,9},{9,1},{17,25},{25,17},{2,10},{10... | collective-permute-start | bytes 786440 | tf_op jit(solution)/shard_map/via_1/ppermute | solution.py:29
  20.5 14.4 %collective-permute-start.5 = (bf16[528,256]{1,0:T(8,128)(2,1)S(1)}, bf16[528,256]{1,0:T(8,128)(2,1)S(1)}, u32[]{:S(2)}, u32[]{:S(2)}) collective-permute-start(bf16[528,256]{1,0:T(8,128)(2,1)S(1)} %collective-permute-done.refs_0_), channel_id=1, source_target_pairs={{0,8},{8,0},{16,24},{24,16},{1,9},{9,1},{17,25},{25,17},{2,10},{10... | collective-permute-start | bytes 811016 | tf_op jit(solution)/shard_map/left_1/ppermute | solution.py:29
  21.0 13.8 %collective-permute-start.6 = (bf16[528,256]{1,0:T(8,128)(2,1)S(1)}, bf16[528,256]{1,0:T(8,128)(2,1)S(1)}, u32[]{:S(2)}, u32[]{:S(2)}) collective-permute-start(bf16[528,256]{1,0:T(8,128)(2,1)S(1)} %collective-permute-done.refs_0_), channel_id=1, source_target_pairs={{0,16},{8,24},{16,0},{24,8},{1,17},{9,25},{17,1},{25,9},{2,18},{10... | collective-permute-start | bytes 811016 | tf_op jit(solution)/shard_map/left_2/ppermute | solution.py:29
  21.5 10.2 %collective-permute-start.13 = (bf16[384,256]{1,0:T(8,128)(2,1)S(1)}, bf16[384,256]{1,0:T(8,128)(2,1)S(1)}, u32[]{:S(2)}, u32[]{:S(2)}) collective-permute-start(bf16[384,256]{1,0:T(8,128)(2,1)S(1)} %get-tuple-element.42), channel_id=1, source_target_pairs={{0,4},{1,5},{2,6},{3,7},{4,0},{5,1},{6,2},{7,3},{8,12},{9,13},{10,... | collective-permute-start | bytes 589832 | tf_op jit(solution)/shard_map/right/ppermute | solution.py:23
  24.9 17.2 %collective-permute-start.8 = (bf16[528,256]{1,0:T(8,128)(2,1)S(1)}, bf16[528,256]{1,0:T(8,128)(2,1)S(1)}, u32[]{:S(2)}, u32[]{:S(2)}) collective-permute-start(bf16[528,256]{1,0:T(8,128)(2,1)S(1)} %collective-permute-done.refs_0_), channel_id=1, source_target_pairs={{0,24},{8,16},{16,8},{24,0},{1,25},{9,17},{17,9},{25,1},{2,26},{10... | collective-permute-start | bytes 811016 | tf_op jit(solution)/shard_map/left_3/ppermute | solution.py:29
  31.8 12.9 %collective-permute-start.15 = (bf16[384,256]{1,0:T(8,128)(2,1)S(1)}, bf16[384,256]{1,0:T(8,128)(2,1)S(1)}, u32[]{:S(2)}, u32[]{:S(2)}) collective-permute-start(bf16[384,256]{1,0:T(8,128)(2,1)S(1)} %collective-permute-done.13.refs_0_), channel_id=1, source_target_pairs={{0,8},{8,0},{16,24},{24,16},{1,9},{9,1},{17,25},{25,17},{2,10},{10... | collective-permute-start | bytes 589832 | tf_op jit(solution)/shard_map/right_1/ppermute | solution.py:29
  33.3 11.9 %collective-permute-start.16 = (bf16[384,256]{1,0:T(8,128)(2,1)S(1)}, bf16[384,256]{1,0:T(8,128)(2,1)S(1)}, u32[]{:S(2)}, u32[]{:S(2)}) collective-permute-start(bf16[384,256]{1,0:T(8,128)(2,1)S(1)} %collective-permute-done.13.refs_0_), channel_id=1, source_target_pairs={{0,16},{8,24},{16,0},{24,8},{1,17},{9,25},{17,1},{25,9},{2,18},{10... | collective-permute-start | bytes 589832 | tf_op jit(solution)/shard_map/right_2/ppermute | solution.py:29
  34.9 12.5 %collective-permute-start.14 = (bf16[528,256]{1,0:T(8,128)(2,1)S(1)}, bf16[528,256]{1,0:T(8,128)(2,1)S(1)}, u32[]{:S(2)}, u32[]{:S(2)}) collective-permute-start(bf16[528,256]{1,0:T(8,128)(2,1)S(1)} %get-tuple-element.43), channel_id=1, source_target_pairs={{0,4},{1,5},{2,6},{3,7},{4,0},{5,1},{6,2},{7,3},{8,12},{9,13},{10,... | collective-permute-start | bytes 811016 | tf_op jit(solution)/shard_map/corners/ppermute | solution.py:23
  39.3 7.4 %collective-permute-start.17 = (bf16[384,256]{1,0:T(8,128)(2,1)S(1)}, bf16[384,256]{1,0:T(8,128)(2,1)S(1)}, u32[]{:S(2)}, u32[]{:S(2)}) collective-permute-start(bf16[384,256]{1,0:T(8,128)(2,1)S(1)} %collective-permute-done.13.refs_0_), channel_id=1, source_target_pairs={{0,24},{8,16},{16,8},{24,0},{1,25},{9,17},{17,9},{25,1},{2,26},{10... | collective-permute-start | bytes 589832 | tf_op jit(solution)/shard_map/right_3/ppermute | solution.py:29
  43.1 5.0 %collective-permute-start.10 = (bf16[256,256]{1,0:T(8,128)(2,1)S(1)}, bf16[256,256]{1,0:T(8,128)(2,1)S(1)}, u32[]{:S(2)}, u32[]{:S(2)}) collective-permute-start(bf16[256,256]{1,0:T(8,128)(2,1)S(1)} %get-tuple-element.37), channel_id=1, source_target_pairs={{0,8},{8,0},{16,24},{24,16},{1,9},{9,1},{17,25},{25,17},{2,10},{10... | collective-permute-start | bytes 393224 | tf_op jit(solution)/shard_map/strip_1/ppermute | solution.py:29
  44.7 5.0 %collective-permute-start.11 = (bf16[256,256]{1,0:T(8,128)(2,1)S(1)}, bf16[256,256]{1,0:T(8,128)(2,1)S(1)}, u32[]{:S(2)}, u32[]{:S(2)}) collective-permute-start(bf16[256,256]{1,0:T(8,128)(2,1)S(1)} %get-tuple-element.38), channel_id=1, source_target_pairs={{0,16},{8,24},{16,0},{24,8},{1,17},{9,25},{17,1},{25,9},{2,18},{10... | collective-permute-start | bytes 393224 | tf_op jit(solution)/shard_map/strip_2/ppermute | solution.py:29
  45.2 5.9 %collective-permute-start.12 = (bf16[256,256]{1,0:T(8,128)(2,1)S(1)}, bf16[256,256]{1,0:T(8,128)(2,1)S(1)}, u32[]{:S(2)}, u32[]{:S(2)}) collective-permute-start(bf16[256,256]{1,0:T(8,128)(2,1)S(1)} %get-tuple-element.39), channel_id=1, source_target_pairs={{0,24},{8,16},{16,8},{24,0},{1,25},{9,17},{17,9},{25,1},{2,26},{10... | collective-permute-start | bytes 393224 | tf_op jit(solution)/shard_map/strip_3/ppermute | solution.py:29

commit v10 on v9

--- a/solution.py
+++ b/solution.py
@@ -204,7 +204,7 @@
 def columns_kernel(groups, held, split, me_ref, rows_ref, cols_ref, *refs):
     pieces, refs = dealt(refs, held)
     terms, refs = dealt(refs, split)
-    outs, (left, folded, masked, mixed) = refs[:groups], refs[groups:]
+    outs, (left, folded, masked) = refs[:groups], refs[groups:]
     me = me_ref[0]
     width, strip = masked.shape
     unfold(pieces, me, left, folded)
@@ -215,9 +215,9 @@
         total = functools.reduce(lambda a, b: a + b, [term[pl.ds(0, part), :].astype(F32) for term in used])
         keep = (row + index * part < rows_ref[0]) & (column < cols_ref[0])
         masked[pl.ds(index * part, part), :] = jnp.where(keep, total, 0.0).astype(BF16)
-    mixed[...] = jnp.dot(left[...], masked[...], preferred_element_type=F32).astype(BF16)
     for flip, out in enumerate(outs):
-        out[...] = mixed[strip_of(jnp.bitwise_xor(me, flip), strip), :]
+        rows = left[strip_of(jnp.bitwise_xor(me, flip), strip), :]
+        out[...] = jnp.dot(rows, masked[...], preferred_element_type=F32).astype(BF16)
 
 
 def left_columns(me, rows_valid, cols_valid, pieces, terms, width):
@@ -233,7 +233,6 @@
             pltpu.VMEM((width, width), BF16),
             pltpu.VMEM((width // 2, TILE), BF16),
             pltpu.VMEM((width, strip), BF16),
-            pltpu.VMEM((width, strip), BF16),
         ],
         compiler_params=pltpu.CompilerParams(vmem_limit_bytes=VMEM),
         cost_estimate=cost(2 * strip * width**2, 4 * width**2),
@@ -261,21 +260,30 @@
 
 
 def rows_kernel(groups, me_ref, rows_ref, cols_ref, *refs):
-    strips, (right, out, mixed) = refs[:groups], refs[groups:]
+    strips, (right, out, mixed, staged, sems) = refs[:groups], refs[groups:]
     me = me_ref[0]
     strip, width = mixed.shape
-    if strip % 128 == 0:
+    joined = strip % 128 == 0
+    if joined:
         for flip, part in enumerate(strips):
             mixed[:, strip_of(jnp.bitwise_xor(me, flip), strip)] = part[...]
-        value = jnp.dot(mixed[...], right[...], preferred_element_type=F32)
-    else:
-        value = 0.0
-        for flip, part in enumerate(strips):
-            rows = right[strip_of(jnp.bitwise_xor(me, flip), strip), :]
-            value += jnp.dot(part[...], rows, preferred_element_type=F32)
-    column = lax.broadcasted_iota(jnp.int32, (strip, width), 1)
-    row = lax.broadcasted_iota(jnp.int32, (strip, width), 0) + me * strip
-    out[0] = jnp.where((row < rows_ref[0]) & (column < cols_ref[0]), value, 0.0).astype(BF16)
+    row = lax.broadcasted_iota(jnp.int32, (strip, TILE), 0) + me * strip
+    copies = []
+    for tile in range(width // TILE):
+        if joined:
+            value = jnp.dot(mixed[...], right[:, block(tile)], preferred_element_type=F32)
+        else:
+            value = 0.0
+            for flip, part in enumerate(strips):
+                rows = right[strip_of(jnp.bitwise_xor(me, flip), strip), block(tile)]
+                value += jnp.dot(part[...], rows, preferred_element_type=F32)
+        column = lax.broadcasted_iota(jnp.int32, (strip, TILE), 1) + tile * TILE
+        keep = (row < rows_ref[0]) & (column < cols_ref[0])
+        staged[:, block(tile)] = jnp.where(keep, value, 0.0).astype(BF16)
+        copies.append(pltpu.make_async_copy(staged.at[:, block(tile)], out.at[0, :, block(tile)], sems.at[tile]))
+        copies[-1].start()
+    for copy in copies:
+        copy.wait()
 
 
 def update_rows(me, rows_valid, cols_valid, strips, right):
@@ -284,9 +292,13 @@
     return pl.pallas_call(
         functools.partial(rows_kernel, groups),
         in_specs=[SMEM_SPEC] * 3 + [VMEM_SPEC] * (groups + 1),
-        out_specs=VMEM_SPEC,
+        out_specs=HBM_SPEC,
         out_shape=jax.ShapeDtypeStruct((1, strip, width), BF16),
-        scratch_shapes=[pltpu.VMEM((strip, width), BF16)],
+        scratch_shapes=[
+            pltpu.VMEM((strip, width), BF16),
+            pltpu.VMEM((strip, width), BF16),
+            pltpu.SemaphoreType.DMA((width // TILE,)),
+        ],
         compiler_params=pltpu.CompilerParams(vmem_limit_bytes=VMEM),
         cost_estimate=cost(2 * strip * width**2, 4 * width**2),
         name="update_rows",

time: 52.8 us -> 53 us (level)
  no operation moved by 1% of the time
where the time goes in v10:
time: 53 us; the launch traced here: 52.8 us
  starting transfers between devices  29.9 us (56%)
  waiting for transfers between devices  14.9 us (28%)
  Pallas kernels  6.53 us (12%)
  between operations  1.37 us (3%)
    ppermute x15, starting transfers between devices, swapped(): lax.ppermute(value, 'dp', [(source, source ^ flip) for source in range(co...  20.3 us
    ppermute x3, starting transfers between devices, shifted(): lax.ppermute(value, 'shard', [(source, (source + count // 2) % count) for...  9.59 us
    ppermute x15, waiting for transfers between devices, swapped(): lax.ppermute(value, 'dp', [(source, source ^ flip) for source in range(co...  8.02 us
    ppermute x3, waiting for transfers between devices, shifted(): lax.ppermute(value, 'shard', [(source, (source + count // 2) % count) for...  6.85 us
    pallas_call x2, Pallas kernels, messages(): pl.pallas_call(functools.partial(messages_kernel, wanted, strip), in_spec...  3.25 us
    pallas_call x1, Pallas kernels, update_rows(): pl.pallas_call(functools.partial(rows_kernel, groups), in_specs=[SMEM_SPE...  1.53 us
    pallas_call x1, Pallas kernels, left_columns(): pl.pallas_call(functools.partial(columns_kernel, groups, [len(part) for p...  1.23 us
  transfers between devices with their start and end apart: 18, of which 10 were waited for; matrix products, arithmetic and copies ran while one was open for 0% of the time, Pallas kernels for 6%

profile of v10, /device:TPU:0, one launch (start us, length us, event | category | flops | bytes accessed | tf_op | source)
XLA Modules:
  0.0 52.8 jit_solution(12968579246734707387)
XLA Ops:
  0.0 1.6 %sent_first.1 = (bf16[512,256]{1,0:T(8,128)(2,1)S(1)}, bf16[512,256]{1,0:T(8,128)(2,1)S(1)}, bf16[512,256]{1,0:T(8,128)(2,1)S(1)}, bf16[512,256]{1,0:T(8,128)(2,1)S(1)}, bf16[528,256]{1,0:T(8,128)(2,1)S(1)}) custom-call(s32[1]{0:T(128)} %bitcast.me_ref, bf16[1,1,1024,1024]{3,2,1,0:T(8,128)(2,1)} %grad_ref.3, bf16[1,1024,1024]{2,1,0:T(8,128)(2,1)} %root_ref.2), custom_call_target="tpu_custom_call" | custom-call | tf_op jit(solution)/shard_map/sent_first/pallas_call | solution.py:133
  1.6 3.0 %collective-permute-start.1 = (bf16[512,256]{1,0:T(8,128)(2,1)S(1)}, bf16[512,256]{1,0:T(8,128)(2,1)S(1)}, u32[]{:S(2)}, u32[]{:S(2)}) collective-permute-start(bf16[512,256]{1,0:T(8,128)(2,1)S(1)} %get-tuple-element.27), channel_id=1, source_target_pairs={{0,8},{8,0},{16,24},{24,16},{1,9},{9,1},{17,25},{25,17},{2,10},{10... | collective-permute-start | bytes 786440 | tf_op jit(solution)/shard_map/far_0/ppermute | solution.py:29
  4.6 1.5 %collective-permute-start.2 = (bf16[512,256]{1,0:T(8,128)(2,1)S(1)}, bf16[512,256]{1,0:T(8,128)(2,1)S(1)}, u32[]{:S(2)}, u32[]{:S(2)}) collective-permute-start(bf16[512,256]{1,0:T(8,128)(2,1)S(1)} %get-tuple-element.29), channel_id=1, source_target_pairs={{0,16},{8,24},{16,0},{24,8},{1,17},{9,25},{17,1},{25,9},{2,18},{10... | collective-permute-start | bytes 786440 | tf_op jit(solution)/shard_map/far_1/ppermute | solution.py:29
  6.2 2.6 %collective-permute-start = (bf16[528,256]{1,0:T(8,128)(2,1)S(1)}, bf16[528,256]{1,0:T(8,128)(2,1)S(1)}, u32[]{:S(2)}, u32[]{:S(2)}) collective-permute-start(bf16[528,256]{1,0:T(8,128)(2,1)S(1)} %get-tuple-element.25), channel_id=1, source_target_pairs={{0,4},{1,5},{2,6},{3,7},{4,0},{5,1},{6,2},{7,3},{8,12},{9,13},{10,... | collective-permute-start | bytes 811016 | tf_op jit(solution)/shard_map/left/ppermute | solution.py:23
  8.7 0.5 %collective-permute-start.3 = (bf16[512,256]{1,0:T(8,128)(2,1)S(1)}, bf16[512,256]{1,0:T(8,128)(2,1)S(1)}, u32[]{:S(2)}, u32[]{:S(2)}) collective-permute-start(bf16[512,256]{1,0:T(8,128)(2,1)S(1)} %get-tuple-element.30), channel_id=1, source_target_pairs={{0,8},{8,0},{16,24},{24,16},{1,9},{9,1},{17,25},{25,17},{2,10},{10... | collective-permute-start | bytes 786440 | tf_op jit(solution)/shard_map/near_0/ppermute | solution.py:29
  9.3 0.5 collective-permute-start.4
  9.8 1.6 %sent_later.1 = (bf16[512,256]{1,0:T(8,128)(2,1)S(1)}, bf16[512,256]{1,0:T(8,128)(2,1)S(1)}, bf16[512,256]{1,0:T(8,128)(2,1)S(1)}, bf16[512,256]{1,0:T(8,128)(2,...) custom-call(s32[1]{0:T(128)} %bitcast.me_ref, bf16[1,1,1024,1024]{3,2,1,0:T(8,128)(2,1)} %grad_ref.3, ...), custom_call_target="tpu_custom_call" | custom-call | tf_op jit(solution)/shard_map/sent_later/pallas_call | solution.py:133
  11.6 2.4 %collective-permute-start.7 = (bf16[512,256]{1,0:T(8,128)(2,1)S(1)}, bf16[512,256]{1,0:T(8,128)(2,1)S(1)}, u32[]{:S(2)}, u32[]{:S(2)}) collective-permute-start(bf16[512,256]{1,0:T(8,128)(2,1)S(1)} %add_convert_fusion.1), channel_id=1, source_target_pairs={{0,16},{8,24},{16,0},{24,8},{1,17},{9,25},{17,1},{25,9},{2,18},{10... | collective-permute-start | bytes 786440 | tf_op jit(solution)/shard_map/via_0/ppermute | solution.py:29
  14.1 1.6 %collective-permute-start.9 = (bf16[512,256]{1,0:T(8,128)(2,1)S(1)}, bf16[512,256]{1,0:T(8,128)(2,1)S(1)}, u32[]{:S(2)}, u32[]{:S(2)}) collective-permute-start(bf16[512,256]{1,0:T(8,128)(2,1)S(1)} %add_convert_fusion), channel_id=1, source_target_pairs={{0,8},{8,0},{16,24},{24,16},{1,9},{9,1},{17,25},{25,17},{2,10},{10... | collective-permute-start | bytes 786440 | tf_op jit(solution)/shard_map/via_1/ppermute | solution.py:29
  15.6 2.4 %collective-permute-done.3.refs_5_ = bf16[512,256]{1,0:T(8,128)(2,1)S(1)} collective-permute-done((bf16[512,256]{1,0:T(8,128)(2,1)S(1)}, bf16[512,256]{1,0:T(8,128)(2,1)S(1)}, u32[]{:S(2)}, u32[]{:S(2)}) %collective-permute-start.3) | collective-permute-done | bytes 262176 | tf_op jit(solution)/shard_map/near_0/ppermute | solution.py:29
  18.0 1.5 %collective-permute-done.4.refs_8_ = bf16[512,256]{1,0:T(8,128)(2,1)S(1)} collective-permute-done((bf16[512,256]{1,0:T(8,128)(2,1)S(1)}, bf16[512,256]{1,0:T(8,128)(2,1)S(1)}, u32[]{:S(2)}, u32[]{:S(2)}) %collective-permute-start.4) | collective-permute-done | bytes 262176 | tf_op jit(solution)/shard_map/near_1/ppermute | solution.py:29
  19.5 1.0 %collective-permute-done.refs_0_ = bf16[528,256]{1,0:T(8,128)(2,1)S(1)} collective-permute-done((bf16[528,256]{1,0:T(8,128)(2,1)S(1)}, bf16[528,256]{1,0:T(8,128)(2,1)S(1)}, u32[]{:S(2)}, u32[]{:S(2)}) %collective-permute-start) | collective-permute-done | bytes 270368 | tf_op jit(solution)/shard_map/left/ppermute | solution.py:23
  20.5 0.5 %collective-permute-start.5 = (bf16[528,256]{1,0:T(8,128)(2,1)S(1)}, bf16[528,256]{1,0:T(8,128)(2,1)S(1)}, u32[]{:S(2)}, u32[]{:S(2)}) collective-permute-start(bf16[528,256]{1,0:T(8,128)(2,1)S(1)} %collective-permute-done.refs_0_), channel_id=1, source_target_pairs={{0,8},{8,0},{16,24},{24,16},{1,9},{9,1},{17,25},{25,17},{2,10},{10... | collective-permute-start | bytes 811016 | tf_op jit(solution)/shard_map/left_1/ppermute | solution.py:29
  21.0 0.5 collective-permute-start.6
  21.5 2.6 %collective-permute-start.13 = (bf16[384,256]{1,0:T(8,128)(2,1)S(1)}, bf16[384,256]{1,0:T(8,128)(2,1)S(1)}, u32[]{:S(2)}, u32[]{:S(2)}) collective-permute-start(bf16[384,256]{1,0:T(8,128)(2,1)S(1)} %get-tuple-element.42), channel_id=1, source_target_pairs={{0,4},{1,5},{2,6},{3,7},{4,0},{5,1},{6,2},{7,3},{8,12},{9,13},{10,... | collective-permute-start | bytes 589832 | tf_op jit(solution)/shard_map/right/ppermute | solution.py:23
  24.1 0.8 %collective-permute-done.7.refs_6_ = bf16[512,256]{1,0:T(8,128)(2,1)S(1)} collective-permute-done((bf16[512,256]{1,0:T(8,128)(2,1)S(1)}, bf16[512,256]{1,0:T(8,128)(2,1)S(1)}, u32[]{:S(2)}, u32[]{:S(2)}) %collective-permute-start.7) | collective-permute-done | bytes 262176 | tf_op jit(solution)/shard_map/via_0/ppermute | solution.py:29
  24.9 1.6 %collective-permute-start.8 = (bf16[528,256]{1,0:T(8,128)(2,1)S(1)}, bf16[528,256]{1,0:T(8,128)(2,1)S(1)}, u32[]{:S(2)}, u32[]{:S(2)}) collective-permute-start(bf16[528,256]{1,0:T(8,128)(2,1)S(1)} %collective-permute-done.refs_0_), channel_id=1, source_target_pairs={{0,24},{8,16},{16,8},{24,0},{1,25},{9,17},{17,9},{25,1},{2,26},{10... | collective-permute-start | bytes 811016 | tf_op jit(solution)/shard_map/left_3/ppermute | solution.py:29
  26.5 5.3 %collective-permute-done.13.refs_0_ = bf16[384,256]{1,0:T(8,128)(2,1)S(1)} collective-permute-done((bf16[384,256]{1,0:T(8,128)(2,1)S(1)}, bf16[384,256]{1,0:T(8,128)(2,1)S(1)}, u32[]{:S(2)}, u32[]{:S(2)}) %collective-permute-start.13) | collective-permute-done | bytes 196640 | tf_op jit(solution)/shard_map/right/ppermute | solution.py:23
  31.8 1.6 %collective-permute-start.15 = (bf16[384,256]{1,0:T(8,128)(2,1)S(1)}, bf16[384,256]{1,0:T(8,128)(2,1)S(1)}, u32[]{:S(2)}, u32[]{:S(2)}) collective-permute-start(bf16[384,256]{1,0:T(8,128)(2,1)S(1)} %collective-permute-done.13.refs_0_), channel_id=1, source_target_pairs={{0,8},{8,0},{16,24},{24,16},{1,9},{9,1},{17,25},{25,17},{2,10},{10... | collective-permute-start | bytes 589832 | tf_op jit(solution)/shard_map/right_1/ppermute | solution.py:29
  33.3 1.5 %collective-permute-start.16 = (bf16[384,256]{1,0:T(8,128)(2,1)S(1)}, bf16[384,256]{1,0:T(8,128)(2,1)S(1)}, u32[]{:S(2)}, u32[]{:S(2)}) collective-permute-start(bf16[384,256]{1,0:T(8,128)(2,1)S(1)} %collective-permute-done.13.refs_0_), channel_id=1, source_target_pairs={{0,16},{8,24},{16,0},{24,8},{1,17},{9,25},{17,1},{25,9},{2,18},{10... | collective-permute-start | bytes 589832 | tf_op jit(solution)/shard_map/right_2/ppermute | solution.py:29
  34.9 4.4 %collective-permute-start.14 = (bf16[528,256]{1,0:T(8,128)(2,1)S(1)}, bf16[528,256]{1,0:T(8,128)(2,1)S(1)}, u32[]{:S(2)}, u32[]{:S(2)}) collective-permute-start(bf16[528,256]{1,0:T(8,128)(2,1)S(1)} %get-tuple-element.43), channel_id=1, source_target_pairs={{0,4},{1,5},{2,6},{3,7},{4,0},{5,1},{6,2},{7,3},{8,12},{9,13},{10,... | collective-permute-start | bytes 811016 | tf_op jit(solution)/shard_map/corners/ppermute | solution.py:23
  39.3 1.5 %collective-permute-start.17 = (bf16[384,256]{1,0:T(8,128)(2,1)S(1)}, bf16[384,256]{1,0:T(8,128)(2,1)S(1)}, u32[]{:S(2)}, u32[]{:S(2)}) collective-permute-start(bf16[384,256]{1,0:T(8,128)(2,1)S(1)} %collective-permute-done.13.refs_0_), channel_id=1, source_target_pairs={{0,24},{8,16},{16,8},{24,0},{1,25},{9,17},{17,9},{25,1},{2,26},{10... | collective-permute-start | bytes 589832 | tf_op jit(solution)/shard_map/right_3/ppermute | solution.py:29
  42.1 1.2 %left_columns.1 = (bf16[256,256]{1,0:T(8,128)(2,1)S(1)}, bf16[256,256]{1,0:T(8,128)(2,1)S(1)}, bf16[256,256]{1,0:T(8,128)(2,1)S(1)}, bf16[256,256]{1,0:T(8,128)(2,1)S(1)}) custom-call(s32[1]{0:T(128)} %bitcast.me_ref, s32[1]{0:T(128)S(6)} %copy.6.rows_ref, s32[1]{0:T(128)S(6)} %copy.7.cols_ref, bf16[528,256]{1,0:T(8,128)(2,1)S(1)} %collective-permute-done.refs_0_, ...), custom_call_target="tpu_custom_call" | custom-call | flops 536870912 | bytes 4194304 | tf_op jit(solution)/shard_map/left_columns/pallas_call | solution.py:227
  43.3 1.6 %collective-permute-start.10 = (bf16[256,256]{1,0:T(8,128)(2,1)S(1)}, bf16[256,256]{1,0:T(8,128)(2,1)S(1)}, u32[]{:S(2)}, u32[]{:S(2)}) collective-permute-start(bf16[256,256]{1,0:T(8,128)(2,1)S(1)} %get-tuple-element.37), channel_id=1, source_target_pairs={{0,8},{8,0},{16,24},{24,16},{1,9},{9,1},{17,25},{25,17},{2,10},{10... | collective-permute-start | bytes 393224 | tf_op jit(solution)/shard_map/strip_1/ppermute | solution.py:29
  44.9 0.5 collective-permute-start.11
  45.4 1.5 %collective-permute-start.12 = (bf16[256,256]{1,0:T(8,128)(2,1)S(1)}, bf16[256,256]{1,0:T(8,128)(2,1)S(1)}, u32[]{:S(2)}, u32[]{:S(2)}) collective-permute-start(bf16[256,256]{1,0:T(8,128)(2,1)S(1)} %get-tuple-element.39), channel_id=1, source_target_pairs={{0,24},{8,16},{16,8},{24,0},{1,25},{9,17},{17,9},{25,1},{2,26},{10... | collective-permute-start | bytes 393224 | tf_op jit(solution)/shard_map/strip_3/ppermute | solution.py:29
  46.9 0.5 %collective-permute-done.14.corners_ref = bf16[528,256]{1,0:T(8,128)(2,1)S(1)} collective-permute-done((bf16[528,256]{1,0:T(8,128)(2,1)S(1)}, bf16[528,256]{1,0:T(8,128)(2,1)S(1)}, u32[]{:S(2)}, u32[]{:S(2)}) %collective-permute-start.14) | collective-permute-done | bytes 270368 | tf_op jit(solution)/shard_map/corners/ppermute | solution.py:23
  47.4 0.5 whole_right.1.refs_4_
  47.9 0.4 collective-permute-done.10.refs_1_
  48.3 1.5 %collective-permute-done.11.refs_2_ = bf16[256,256]{1,0:T(8,128)(2,1)S(1)} collective-permute-done((bf16[256,256]{1,0:T(8,128)(2,1)S(1)}, bf16[256,256]{1,0:T(8,128)(2,1)S(1)}, u32[]{:S(2)}, u32[]{:S(2)}) %collective-permute-start.11) | collective-permute-done | bytes 131104 | tf_op jit(solution)/shard_map/strip_2/ppermute | solution.py:29
  49.9 1.4 %collective-permute-done.12.refs_3_ = bf16[256,256]{1,0:T(8,128)(2,1)S(1)} collective-permute-done((bf16[256,256]{1,0:T(8,128)(2,1)S(1)}, bf16[256,256]{1,0:T(8,128)(2,1)S(1)}, u32[]{:S(2)}, u32[]{:S(2)}) %collective-permute-start.12) | collective-permute-done | bytes 131104 | tf_op jit(solution)/shard_map/strip_3/ppermute | solution.py:29
  51.3 1.5 %update_rows.1 = bf16[1,256,1024]{2,1,0:T(8,128)(2,1)} custom-call(s32[1]{0:T(128)} %bitcast.me_ref, s32[1]{0:T(128)S(6)} %copy.6.rows_ref, s32[1]{0:T(128)S(6)} %copy.7.cols_ref, bf16[256,256]{1,0:T(8,128)(2,1)S(1)} %get-tuple-element.36.refs_0_, bf16[256,256]{1,0:T(8,128)(2,1)S(1)} %collective-permute-done.10.refs_1_, ...), custom_call_target="tpu_custom_call" | custom-call | flops 536870912 | bytes 4194304 | tf_op jit(solution)/shard_map/update_rows/pallas_call | solution.py:292
  (11 shorter events, 0.2 us)
Async XLA Ops:
  1.6 9.8 %collective-permute-start.1 = (bf16[512,256]{1,0:T(8,128)(2,1)S(1)}, bf16[512,256]{1,0:T(8,128)(2,1)S(1)}, u32[]{:S(2)}, u32[]{:S(2)}) collective-permute-start(bf16[512,256]{1,0:T(8,128)(2,1)S(1)} %get-tuple-element.27), channel_id=1, source_target_pairs={{0,8},{8,0},{16,24},{24,16},{1,9},{9,1},{17,25},{25,17},{2,10},{10... | collective-permute-start | bytes 786440 | tf_op jit(solution)/shard_map/far_0/ppermute | solution.py:29
  4.6 9.4 %collective-permute-start.2 = (bf16[512,256]{1,0:T(8,128)(2,1)S(1)}, bf16[512,256]{1,0:T(8,128)(2,1)S(1)}, u32[]{:S(2)}, u32[]{:S(2)}) collective-permute-start(bf16[512,256]{1,0:T(8,128)(2,1)S(1)} %get-tuple-element.29), channel_id=1, source_target_pairs={{0,16},{8,24},{16,0},{24,8},{1,17},{9,25},{17,1},{25,9},{2,18},{10... | collective-permute-start | bytes 786440 | tf_op jit(solution)/shard_map/far_1/ppermute | solution.py:29
  6.2 14.4 %collective-permute-start = (bf16[528,256]{1,0:T(8,128)(2,1)S(1)}, bf16[528,256]{1,0:T(8,128)(2,1)S(1)}, u32[]{:S(2)}, u32[]{:S(2)}) collective-permute-start(bf16[528,256]{1,0:T(8,128)(2,1)S(1)} %get-tuple-element.25), channel_id=1, source_target_pairs={{0,4},{1,5},{2,6},{3,7},{4,0},{5,1},{6,2},{7,3},{8,12},{9,13},{10,... | collective-permute-start | bytes 811016 | tf_op jit(solution)/shard_map/left/ppermute | solution.py:23
  8.7 9.2 %collective-permute-start.3 = (bf16[512,256]{1,0:T(8,128)(2,1)S(1)}, bf16[512,256]{1,0:T(8,128)(2,1)S(1)}, u32[]{:S(2)}, u32[]{:S(2)}) collective-permute-start(bf16[512,256]{1,0:T(8,128)(2,1)S(1)} %get-tuple-element.30), channel_id=1, source_target_pairs={{0,8},{8,0},{16,24},{24,16},{1,9},{9,1},{17,25},{25,17},{2,10},{10... | collective-permute-start | bytes 786440 | tf_op jit(solution)/shard_map/near_0/ppermute | solution.py:29
  9.3 10.2 %collective-permute-start.4 = (bf16[512,256]{1,0:T(8,128)(2,1)S(1)}, bf16[512,256]{1,0:T(8,128)(2,1)S(1)}, u32[]{:S(2)}, u32[]{:S(2)}) collective-permute-start(bf16[512,256]{1,0:T(8,128)(2,1)S(1)} %get-tuple-element.31), channel_id=1, source_target_pairs={{0,16},{8,24},{16,0},{24,8},{1,17},{9,25},{17,1},{25,9},{2,18},{10... | collective-permute-start | bytes 786440 | tf_op jit(solution)/shard_map/near_1/ppermute | solution.py:29
  11.6 13.4 %collective-permute-start.7 = (bf16[512,256]{1,0:T(8,128)(2,1)S(1)}, bf16[512,256]{1,0:T(8,128)(2,1)S(1)}, u32[]{:S(2)}, u32[]{:S(2)}) collective-permute-start(bf16[512,256]{1,0:T(8,128)(2,1)S(1)} %add_convert_fusion.1), channel_id=1, source_target_pairs={{0,16},{8,24},{16,0},{24,8},{1,17},{9,25},{17,1},{25,9},{2,18},{10... | collective-permute-start | bytes 786440 | tf_op jit(solution)/shard_map/via_0/ppermute | solution.py:29
  14.1 17.7 %collective-permute-start.9 = (bf16[512,256]{1,0:T(8,128)(2,1)S(1)}, bf16[512,256]{1,0:T(8,128)(2,1)S(1)}, u32[]{:S(2)}, u32[]{:S(2)}) collective-permute-start(bf16[512,256]{1,0:T(8,128)(2,1)S(1)} %add_convert_fusion), channel_id=1, source_target_pairs={{0,8},{8,0},{16,24},{24,16},{1,9},{9,1},{17,25},{25,17},{2,10},{10... | collective-permute-start | bytes 786440 | tf_op jit(solution)/shard_map/via_1/ppermute | solution.py:29
  20.5 14.4 %collective-permute-start.5 = (bf16[528,256]{1,0:T(8,128)(2,1)S(1)}, bf16[528,256]{1,0:T(8,128)(2,1)S(1)}, u32[]{:S(2)}, u32[]{:S(2)}) collective-permute-start(bf16[528,256]{1,0:T(8,128)(2,1)S(1)} %collective-permute-done.refs_0_), channel_id=1, source_target_pairs={{0,8},{8,0},{16,24},{24,16},{1,9},{9,1},{17,25},{25,17},{2,10},{10... | collective-permute-start | bytes 811016 | tf_op jit(solution)/shard_map/left_1/ppermute | solution.py:29
  21.0 13.8 %collective-permute-start.6 = (bf16[528,256]{1,0:T(8,128)(2,1)S(1)}, bf16[528,256]{1,0:T(8,128)(2,1)S(1)}, u32[]{:S(2)}, u32[]{:S(2)}) collective-permute-start(bf16[528,256]{1,0:T(8,128)(2,1)S(1)} %collective-permute-done.refs_0_), channel_id=1, source_target_pairs={{0,16},{8,24},{16,0},{24,8},{1,17},{9,25},{17,1},{25,9},{2,18},{10... | collective-permute-start | bytes 811016 | tf_op jit(solution)/shard_map/left_2/ppermute | solution.py:29
  21.5 10.2 %collective-permute-start.13 = (bf16[384,256]{1,0:T(8,128)(2,1)S(1)}, bf16[384,256]{1,0:T(8,128)(2,1)S(1)}, u32[]{:S(2)}, u32[]{:S(2)}) collective-permute-start(bf16[384,256]{1,0:T(8,128)(2,1)S(1)} %get-tuple-element.42), channel_id=1, source_target_pairs={{0,4},{1,5},{2,6},{3,7},{4,0},{5,1},{6,2},{7,3},{8,12},{9,13},{10,... | collective-permute-start | bytes 589832 | tf_op jit(solution)/shard_map/right/ppermute | solution.py:23
  24.9 17.2 %collective-permute-start.8 = (bf16[528,256]{1,0:T(8,128)(2,1)S(1)}, bf16[528,256]{1,0:T(8,128)(2,1)S(1)}, u32[]{:S(2)}, u32[]{:S(2)}) collective-permute-start(bf16[528,256]{1,0:T(8,128)(2,1)S(1)} %collective-permute-done.refs_0_), channel_id=1, source_target_pairs={{0,24},{8,16},{16,8},{24,0},{1,25},{9,17},{17,9},{25,1},{2,26},{10... | collective-permute-start | bytes 811016 | tf_op jit(solution)/shard_map/left_3/ppermute | solution.py:29
  31.8 13.1 %collective-permute-start.15 = (bf16[384,256]{1,0:T(8,128)(2,1)S(1)}, bf16[384,256]{1,0:T(8,128)(2,1)S(1)}, u32[]{:S(2)}, u32[]{:S(2)}) collective-permute-start(bf16[384,256]{1,0:T(8,128)(2,1)S(1)} %collective-permute-done.13.refs_0_), channel_id=1, source_target_pairs={{0,8},{8,0},{16,24},{24,16},{1,9},{9,1},{17,25},{25,17},{2,10},{10... | collective-permute-start | bytes 589832 | tf_op jit(solution)/shard_map/right_1/ppermute | solution.py:29
  33.3 12.0 %collective-permute-start.16 = (bf16[384,256]{1,0:T(8,128)(2,1)S(1)}, bf16[384,256]{1,0:T(8,128)(2,1)S(1)}, u32[]{:S(2)}, u32[]{:S(2)}) collective-permute-start(bf16[384,256]{1,0:T(8,128)(2,1)S(1)} %collective-permute-done.13.refs_0_), channel_id=1, source_target_pairs={{0,16},{8,24},{16,0},{24,8},{1,17},{9,25},{17,1},{25,9},{2,18},{10... | collective-permute-start | bytes 589832 | tf_op jit(solution)/shard_map/right_2/ppermute | solution.py:29
  34.9 12.5 %collective-permute-start.14 = (bf16[528,256]{1,0:T(8,128)(2,1)S(1)}, bf16[528,256]{1,0:T(8,128)(2,1)S(1)}, u32[]{:S(2)}, u32[]{:S(2)}) collective-permute-start(bf16[528,256]{1,0:T(8,128)(2,1)S(1)} %get-tuple-element.43), channel_id=1, source_target_pairs={{0,4},{1,5},{2,6},{3,7},{4,0},{5,1},{6,2},{7,3},{8,12},{9,13},{10,... | collective-permute-start | bytes 811016 | tf_op jit(solution)/shard_map/corners/ppermute | solution.py:23
  39.3 7.6 %collective-permute-start.17 = (bf16[384,256]{1,0:T(8,128)(2,1)S(1)}, bf16[384,256]{1,0:T(8,128)(2,1)S(1)}, u32[]{:S(2)}, u32[]{:S(2)}) collective-permute-start(bf16[384,256]{1,0:T(8,128)(2,1)S(1)} %collective-permute-done.13.refs_0_), channel_id=1, source_target_pairs={{0,24},{8,16},{16,8},{24,0},{1,25},{9,17},{17,9},{25,1},{2,26},{10... | collective-permute-start | bytes 589832 | tf_op jit(solution)/shard_map/right_3/ppermute | solution.py:29
  43.3 5.0 %collective-permute-start.10 = (bf16[256,256]{1,0:T(8,128)(2,1)S(1)}, bf16[256,256]{1,0:T(8,128)(2,1)S(1)}, u32[]{:S(2)}, u32[]{:S(2)}) collective-permute-start(bf16[256,256]{1,0:T(8,128)(2,1)S(1)} %get-tuple-element.37), channel_id=1, source_target_pairs={{0,8},{8,0},{16,24},{24,16},{1,9},{9,1},{17,25},{25,17},{2,10},{10... | collective-permute-start | bytes 393224 | tf_op jit(solution)/shard_map/strip_1/ppermute | solution.py:29
  44.9 5.0 %collective-permute-start.11 = (bf16[256,256]{1,0:T(8,128)(2,1)S(1)}, bf16[256,256]{1,0:T(8,128)(2,1)S(1)}, u32[]{:S(2)}, u32[]{:S(2)}) collective-permute-start(bf16[256,256]{1,0:T(8,128)(2,1)S(1)} %get-tuple-element.38), channel_id=1, source_target_pairs={{0,16},{8,24},{16,0},{24,8},{1,17},{9,25},{17,1},{25,9},{2,18},{10... | collective-permute-start | bytes 393224 | tf_op jit(solution)/shard_map/strip_2/ppermute | solution.py:29
  45.4 5.9 %collective-permute-start.12 = (bf16[256,256]{1,0:T(8,128)(2,1)S(1)}, bf16[256,256]{1,0:T(8,128)(2,1)S(1)}, u32[]{:S(2)}, u32[]{:S(2)}) collective-permute-start(bf16[256,256]{1,0:T(8,128)(2,1)S(1)} %get-tuple-element.39), channel_id=1, source_target_pairs={{0,24},{8,16},{16,8},{24,0},{1,25},{9,17},{17,9},{25,1},{2,26},{10... | collective-permute-start | bytes 393224 | tf_op jit(solution)/shard_map/strip_3/ppermute | solution.py:29

commit v11 on v8

--- a/solution.py
+++ b/solution.py
@@ -308,15 +308,21 @@
     )
 
     if groups == 4:
-        far_0, far_1, near_0, near_1, left = messages(
-            me, grads, left_roots, groups, [[(3, 0)], [(3, 1)], [(1, 0)], [(2, 1)]], False, "sent_first"
+        far_0, far_1, left = messages(
+            me, grads, left_roots, groups, [[(3, 0)], [(3, 1)]], False, "sent_first"
         )
         far_0, far_1 = swapped(far_0, 1, "far_0"), swapped(far_1, 2, "far_1")
+        left = shifted(left, "left")
+        near_0, near_1, *kept, right, corners = messages(
+            me,
+            grads,
+            right_roots,
+            groups,
+            [[(1, 0)], [(2, 1)], [(2, 0)], [(1, 1)], [(0, 0)], [(0, 1)]],
+            True,
+            "sent_later",
+        )
         near_0, near_1 = swapped(near_0, 1, "near_0"), swapped(near_1, 2, "near_1")
-        left = shifted(left, "left")
-        *kept, right, corners = messages(
-            me, grads, right_roots, groups, [[(2, 0)], [(1, 1)], [(0, 0)], [(0, 1)]], True, "sent_later"
-        )
         via_0, via_1 = added(kept[0], far_0).astype(BF16), added(kept[1], far_1).astype(BF16)
         right = shifted(after(right, left), "right")
         left = after(left, via_0, via_1, near_0, near_1)

time: 52.8 us -> 52.6 us (level)
  waiting for transfers between devices: 19.8 us -> 19.2 us
    ppermute x17, waiting for transfers between devices: 8.69 us -> 7.93 us  [swapped(): lax.ppermute(value, 'dp', [(source, source ^ flip) for source in range(co...]
  transfers between devices with their start and end apart: 20 -> 20, of which waited for: 7 -> 6; matrix products, arithmetic and copies ran while one was open for 0% -> 0% of each run, Pallas kernels for 6% -> 6%
where the time goes in v11:
time: 52.6 us; the launch traced here: 52.4 us
  starting transfers between devices  25.2 us (48%)
  waiting for transfers between devices  19.2 us (37%)
  Pallas kernels  6.37 us (12%)
  between operations  1.4 us (3%)
    ppermute x17, starting transfers between devices, swapped(): lax.ppermute(value, 'dp', [(source, source ^ flip) for source in range(co...  22 us
    ppermute x3, waiting for transfers between devices, shifted(): lax.ppermute(value, 'shard', [(source, (source + count // 2) % count) for...  11.3 us
    ppermute x17, waiting for transfers between devices, swapped(): lax.ppermute(value, 'dp', [(source, source ^ flip) for source in range(co...  7.93 us
    ppermute x3, starting transfers between devices, shifted(): lax.ppermute(value, 'shard', [(source, (source + count // 2) % count) for...  3.26 us
    pallas_call x2, Pallas kernels, messages(): pl.pallas_call(functools.partial(messages_kernel, wanted, strip), in_spec...  3.23 us
    pallas_call x1, Pallas kernels, update_rows(): pl.pallas_call(functools.partial(rows_kernel, groups), in_specs=[SMEM_SPE...  1.57 us
  transfers between devices with their start and end apart: 20, of which 6 were waited for; matrix products, arithmetic and copies ran while one was open for 0% of the time, Pallas kernels for 6%

profile of v11, /device:TPU:0, one launch (start us, length us, event | category | flops | bytes accessed | tf_op | source)
XLA Modules:
  0.0 52.4 jit_solution(4635909598297095514)
XLA Ops:
  0.0 1.5 %sent_first.1 = (bf16[512,256]{1,0:T(8,128)(2,1)S(1)}, bf16[512,256]{1,0:T(8,128)(2,1)S(1)}, bf16[528,256]{1,0:T(8,128)(2,1)S(1)}) custom-call(s32[1]{0:T(128)} %bitcast.me_ref, bf16[1,1,1024,1024]{3,2,1,0:T(8,128)(2,1)} %grad_ref.3, bf16[1,1024,1024]{2,1,0:T(8,128)(2,1)} %root_ref.2), custom_call_target="tpu_custom_call" | custom-call | tf_op jit(solution)/shard_map/sent_first/pallas_call | solution.py:133
  1.5 3.0 %collective-permute-start.1 = (bf16[512,256]{1,0:T(8,128)(2,1)S(1)}, bf16[512,256]{1,0:T(8,128)(2,1)S(1)}, u32[]{:S(2)}, u32[]{:S(2)}) collective-permute-start(bf16[512,256]{1,0:T(8,128)(2,1)S(1)} %get-tuple-element.27), channel_id=1, source_target_pairs={{0,8},{8,0},{16,24},{24,16},{1,9},{9,1},{17,25},{25,17},{2,10},{10... | collective-permute-start | bytes 786440 | tf_op jit(solution)/shard_map/far_0/ppermute | solution.py:29
  4.5 1.5 %collective-permute-start.2 = (bf16[512,256]{1,0:T(8,128)(2,1)S(1)}, bf16[512,256]{1,0:T(8,128)(2,1)S(1)}, u32[]{:S(2)}, u32[]{:S(2)}) collective-permute-start(bf16[512,256]{1,0:T(8,128)(2,1)S(1)} %get-tuple-element.29), channel_id=1, source_target_pairs={{0,16},{8,24},{16,0},{24,8},{1,17},{9,25},{17,1},{25,9},{2,18},{10... | collective-permute-start | bytes 786440 | tf_op jit(solution)/shard_map/far_1/ppermute | solution.py:29
  6.0 2.6 %collective-permute-start = (bf16[528,256]{1,0:T(8,128)(2,1)S(1)}, bf16[528,256]{1,0:T(8,128)(2,1)S(1)}, u32[]{:S(2)}, u32[]{:S(2)}) collective-permute-start(bf16[528,256]{1,0:T(8,128)(2,1)S(1)} %get-tuple-element.25), channel_id=1, source_target_pairs={{0,4},{1,5},{2,6},{3,7},{4,0},{5,1},{6,2},{7,3},{8,12},{9,13},{10,... | collective-permute-start | bytes 811016 | tf_op jit(solution)/shard_map/left/ppermute | solution.py:23
  8.6 1.8 %sent_later.1 = (bf16[512,256]{1,0:T(8,128)(2,1)S(1)}, bf16[512,256]{1,0:T(8,128)(2,1)S(1)}, bf16[512,256]{1,0:T(8,128)(2,1)S(1)}, bf16[512,256]{1,0:T(8,128)(2,...) custom-call(s32[1]{0:T(128)} %bitcast.me_ref, ...), custom_call_target="tpu_custom_call" | custom-call | tf_op jit(solution)/shard_map/sent_later/pallas_call | solution.py:133
  10.4 0.6 %collective-permute-start.3 = (bf16[512,256]{1,0:T(8,128)(2,1)S(1)}, bf16[512,256]{1,0:T(8,128)(2,1)S(1)}, u32[]{:S(2)}, u32[]{:S(2)}) collective-permute-start(bf16[512,256]{1,0:T(8,128)(2,1)S(1)} %get-tuple-element.30), channel_id=1, source_target_pairs={{0,8},{8,0},{16,24},{24,16},{1,9},{9,1},{17,25},{25,17},{2,10},{10... | collective-permute-start | bytes 786440 | tf_op jit(solution)/shard_map/near_0/ppermute | solution.py:29
  11.0 0.5 collective-permute-start.4
  11.5 0.1 add_convert_fusion.1
  11.5 1.6 %collective-permute-start.6 = (bf16[512,256]{1,0:T(8,128)(2,1)S(1)}, bf16[512,256]{1,0:T(8,128)(2,1)S(1)}, u32[]{:S(2)}, u32[]{:S(2)}) collective-permute-start(bf16[512,256]{1,0:T(8,128)(2,1)S(1)} %add_convert_fusion.1), channel_id=1, source_target_pairs={{0,16},{8,24},{16,0},{24,8},{1,17},{9,25},{17,1},{25,9},{2,18},{10... | collective-permute-start | bytes 786440 | tf_op jit(solution)/shard_map/via_0/ppermute | solution.py:29
  13.1 0.1 add_convert_fusion
  13.2 2.1 %collective-permute-start.10 = (bf16[512,256]{1,0:T(8,128)(2,1)S(1)}, bf16[512,256]{1,0:T(8,128)(2,1)S(1)}, u32[]{:S(2)}, u32[]{:S(2)}) collective-permute-start(bf16[512,256]{1,0:T(8,128)(2,1)S(1)} %add_convert_fusion), channel_id=1, source_target_pairs={{0,8},{8,0},{16,24},{24,16},{1,9},{9,1},{17,25},{25,17},{2,10},{10... | collective-permute-start | bytes 786440 | tf_op jit(solution)/shard_map/via_1/ppermute | solution.py:29
  15.3 5.1 %collective-permute-done.refs_0_ = bf16[528,256]{1,0:T(8,128)(2,1)S(1)} collective-permute-done((bf16[528,256]{1,0:T(8,128)(2,1)S(1)}, bf16[528,256]{1,0:T(8,128)(2,1)S(1)}, u32[]{:S(2)}, u32[]{:S(2)}) %collective-permute-start) | collective-permute-done | bytes 270368 | tf_op jit(solution)/shard_map/left/ppermute | solution.py:23
  20.4 1.3 %collective-permute-start.5 = (bf16[528,256]{1,0:T(8,128)(2,1)S(1)}, bf16[528,256]{1,0:T(8,128)(2,1)S(1)}, u32[]{:S(2)}, u32[]{:S(2)}) collective-permute-start(bf16[528,256]{1,0:T(8,128)(2,1)S(1)} %collective-permute-done.refs_0_), channel_id=1, source_target_pairs={{0,8},{8,0},{16,24},{24,16},{1,9},{9,1},{17,25},{25,17},{2,10},{10... | collective-permute-start | bytes 811016 | tf_op jit(solution)/shard_map/left_1/ppermute | solution.py:29
  21.7 1.8 %collective-permute-done.6.refs_7_ = bf16[512,256]{1,0:T(8,128)(2,1)S(1)} collective-permute-done((bf16[512,256]{1,0:T(8,128)(2,1)S(1)}, bf16[512,256]{1,0:T(8,128)(2,1)S(1)}, u32[]{:S(2)}, u32[]{:S(2)}) %collective-permute-start.6) | collective-permute-done | bytes 262176 | tf_op jit(solution)/shard_map/via_0/ppermute | solution.py:29
  23.5 1.5 %collective-permute-start.7 = (bf16[528,256]{1,0:T(8,128)(2,1)S(1)}, bf16[528,256]{1,0:T(8,128)(2,1)S(1)}, u32[]{:S(2)}, u32[]{:S(2)}) collective-permute-start(bf16[528,256]{1,0:T(8,128)(2,1)S(1)} %collective-permute-done.refs_0_), channel_id=1, source_target_pairs={{0,16},{8,24},{16,0},{24,8},{1,17},{9,25},{17,1},{25,9},{2,18},{10... | collective-permute-start | bytes 811016 | tf_op jit(solution)/shard_map/left_2/ppermute | solution.py:29
  25.0 6.2 %collective-permute-done.14.refs_0_ = bf16[384,256]{1,0:T(8,128)(2,1)S(1)} collective-permute-done((bf16[384,256]{1,0:T(8,128)(2,1)S(1)}, bf16[384,256]{1,0:T(8,128)(2,1)S(1)}, u32[]{:S(2)}, u32[]{:S(2)}) %collective-permute-start.14) | collective-permute-done | bytes 196640 | tf_op jit(solution)/shard_map/right/ppermute | solution.py:23
  31.2 0.5 %collective-permute-start.16 = (bf16[384,256]{1,0:T(8,128)(2,1)S(1)}, bf16[384,256]{1,0:T(8,128)(2,1)S(1)}, u32[]{:S(2)}, u32[]{:S(2)}) collective-permute-start(bf16[384,256]{1,0:T(8,128)(2,1)S(1)} %collective-permute-done.14.refs_0_), channel_id=1, source_target_pairs={{0,8},{8,0},{16,24},{24,16},{1,9},{9,1},{17,25},{25,17},{2,10},{10... | collective-permute-start | bytes 589832 | tf_op jit(solution)/shard_map/right_1/ppermute | solution.py:29
  31.8 0.4 collective-permute-start.17
  32.2 1.7 %collective-permute-start.8 = (bf16[256,256]{1,0:T(8,128)(2,1)S(1)}, bf16[256,256]{1,0:T(8,128)(2,1)S(1)}, u32[]{:S(2)}, u32[]{:S(2)}) collective-permute-start(bf16[256,256]{1,0:T(8,128)(2,1)S(1)} %slice.16), channel_id=1, source_target_pairs={{0,16},{8,24},{16,0},{24,8},{1,17},{9,25},{17,1},{25,9},{2,18},{10... | collective-permute-start | bytes 393224 | tf_op jit(solution)/shard_map/left_3a/ppermute | solution.py:29
  33.9 1.6 %collective-permute-start.9 = (bf16[256,256]{1,0:T(8,128)(2,1)S(1)}, bf16[256,256]{1,0:T(8,128)(2,1)S(1)}, u32[]{:S(2)}, u32[]{:S(2)}) collective-permute-start(bf16[256,256]{1,0:T(8,128)(2,1)S(1)} %slice.17), channel_id=1, source_target_pairs={{0,8},{8,0},{16,24},{24,16},{1,9},{9,1},{17,25},{25,17},{2,10},{10... | collective-permute-start | bytes 393224 | tf_op jit(solution)/shard_map/left_3b/ppermute | solution.py:29
  35.4 0.7 %collective-permute-start.15 = (bf16[528,256]{1,0:T(8,128)(2,1)S(1)}, bf16[528,256]{1,0:T(8,128)(2,1)S(1)}, u32[]{:S(2)}, u32[]{:S(2)}) collective-permute-start(bf16[528,256]{1,0:T(8,128)(2,1)S(1)} %get-tuple-element.43), channel_id=1, source_target_pairs={{0,4},{1,5},{2,6},{3,7},{4,0},{5,1},{6,2},{7,3},{8,12},{9,13},{10,... | collective-permute-start | bytes 811016 | tf_op jit(solution)/shard_map/corners/ppermute | solution.py:23
  36.1 1.3 %collective-permute-done.16.refs_1_ = bf16[384,256]{1,0:T(8,128)(2,1)S(1)} collective-permute-done((bf16[384,256]{1,0:T(8,128)(2,1)S(1)}, bf16[384,256]{1,0:T(8,128)(2,1)S(1)}, u32[]{:S(2)}, u32[]{:S(2)}) %collective-permute-start.16) | collective-permute-done | bytes 196640 | tf_op jit(solution)/shard_map/right_1/ppermute | solution.py:29
  37.5 0.6 %collective-permute-start.18 = (bf16[192,256]{1,0:T(8,128)(2,1)S(1)}, bf16[192,256]{1,0:T(8,128)(2,1)S(1)}, u32[]{:S(2)}, u32[]{:S(2)}) collective-permute-start(bf16[192,256]{1,0:T(8,128)(2,1)S(1)} %slice.18), channel_id=1, source_target_pairs={{0,16},{8,24},{16,0},{24,8},{1,17},{9,25},{17,1},{25,9},{2,18},{10... | collective-permute-start | bytes 294920 | tf_op jit(solution)/shard_map/right_3a/ppermute | solution.py:29
  39.3 0.8 %collective-permute-done.8.refs_3_ = bf16[256,256]{1,0:T(8,128)(2,1)S(1)} collective-permute-done((bf16[256,256]{1,0:T(8,128)(2,1)S(1)}, bf16[256,256]{1,0:T(8,128)(2,1)S(1)}, u32[]{:S(2)}, u32[]{:S(2)}) %collective-permute-start.8) | collective-permute-done | bytes 131104 | tf_op jit(solution)/shard_map/left_3a/ppermute | solution.py:29
  40.2 1.0 %left_columns.1 = (bf16[256,256]{1,0:T(8,128)(2,1)S(1)}, bf16[256,256]{1,0:T(8,128)(2,1)S(1)}, bf16[256,256]{1,0:T(8,128)(2,1)S(1)}, bf16[256,256]{1,0:T(8,128)(2,1)S(1)}) custom-call(s32[1]{0:T(128)} %bitcast.me_ref, s32[1]{0:T(128)S(6)} %copy.6.rows_ref, s32[1]{0:T(128)S(6)} %copy.7.cols_ref, bf16[528,256]{1,0:T(8,128)(2,1)S(1)} %collective-permute-done.refs_0_, ...), custom_call_target="tpu_custom_call" | custom-call | flops 536870912 | bytes 4194304 | tf_op jit(solution)/shard_map/left_columns/pallas_call | solution.py:227
  41.2 1.6 %collective-permute-start.11 = (bf16[256,256]{1,0:T(8,128)(2,1)S(1)}, bf16[256,256]{1,0:T(8,128)(2,1)S(1)}, u32[]{:S(2)}, u32[]{:S(2)}) collective-permute-start(bf16[256,256]{1,0:T(8,128)(2,1)S(1)} %get-tuple-element.37), channel_id=1, source_target_pairs={{0,8},{8,0},{16,24},{24,16},{1,9},{9,1},{17,25},{25,17},{2,10},{10... | collective-permute-start | bytes 393224 | tf_op jit(solution)/shard_map/strip_1/ppermute | solution.py:29
  42.8 0.5 collective-permute-start.12
  43.3 1.5 %collective-permute-start.13 = (bf16[256,256]{1,0:T(8,128)(2,1)S(1)}, bf16[256,256]{1,0:T(8,128)(2,1)S(1)}, u32[]{:S(2)}, u32[]{:S(2)}) collective-permute-start(bf16[256,256]{1,0:T(8,128)(2,1)S(1)} %get-tuple-element.39), channel_id=1, source_target_pairs={{0,24},{8,16},{16,8},{24,0},{1,25},{9,17},{17,9},{25,1},{2,26},{10... | collective-permute-start | bytes 393224 | tf_op jit(solution)/shard_map/strip_3/ppermute | solution.py:29
  44.8 1.6 %collective-permute-start.19 = (bf16[192,256]{1,0:T(8,128)(2,1)S(1)}, bf16[192,256]{1,0:T(8,128)(2,1)S(1)}, u32[]{:S(2)}, u32[]{:S(2)}) collective-permute-start(bf16[192,256]{1,0:T(8,128)(2,1)S(1)} %slice.19), channel_id=1, source_target_pairs={{0,8},{8,0},{16,24},{24,16},{1,9},{9,1},{17,25},{25,17},{2,10},{10... | collective-permute-start | bytes 294920 | tf_op jit(solution)/shard_map/right_3b/ppermute | solution.py:29
  46.4 3.9 %collective-permute-done.19.refs_4_ = bf16[192,256]{1,0:T(8,128)(2,1)S(1)} collective-permute-done((bf16[192,256]{1,0:T(8,128)(2,1)S(1)}, bf16[192,256]{1,0:T(8,128)(2,1)S(1)}, u32[]{:S(2)}, u32[]{:S(2)}) %collective-permute-start.19) | collective-permute-done | bytes 98336 | tf_op jit(solution)/shard_map/right_3b/ppermute | solution.py:29
  50.3 0.5 %whole_right.1.refs_4_ = bf16[1024,1024]{1,0:T(8,128)(2,1)S(1)} custom-call(s32[1]{0:T(128)} %bitcast.me_ref, bf16[528,256]{1,0:T(8,128)(2,1)S(1)} %collective-permute-done.15.corners_ref, bf16[384,256]{1,0:T(8,128)(2,1)S(1)} %collective-permute-done.14.refs_0_, bf16[384,256]{1,0:T(8,128)(2,1)S(1)} %collective-permute-done.16.refs_1_, ...), custom_call_target="tpu_custom_call" | custom-call | flops 1048576 | bytes 4194304 | tf_op jit(solution)/shard_map/whole_right/pallas_call | solution.py:252
  50.8 1.6 %update_rows.1 = bf16[1,256,1024]{2,1,0:T(8,128)(2,1)} custom-call(s32[1]{0:T(128)} %bitcast.me_ref, s32[1]{0:T(128)S(6)} %copy.6.rows_ref, s32[1]{0:T(128)S(6)} %copy.7.cols_ref, bf16[256,256]{1,0:T(8,128)(2,1)S(1)} %get-tuple-element.36.refs_0_, bf16[256,256]{1,0:T(8,128)(2,1)S(1)} %collective-permute-done.11.refs_1_, ...), custom_call_target="tpu_custom_call" | custom-call | flops 536870912 | bytes 4194304 | tf_op jit(solution)/shard_map/update_rows/pallas_call | solution.py:284
  (19 shorter events, 0.1 us)
Async XLA Ops:
  1.5 10.0 %collective-permute-start.1 = (bf16[512,256]{1,0:T(8,128)(2,1)S(1)}, bf16[512,256]{1,0:T(8,128)(2,1)S(1)}, u32[]{:S(2)}, u32[]{:S(2)}) collective-permute-start(bf16[512,256]{1,0:T(8,128)(2,1)S(1)} %get-tuple-element.27), channel_id=1, source_target_pairs={{0,8},{8,0},{16,24},{24,16},{1,9},{9,1},{17,25},{25,17},{2,10},{10... | collective-permute-start | bytes 786440 | tf_op jit(solution)/shard_map/far_0/ppermute | solution.py:29
  4.5 8.6 %collective-permute-start.2 = (bf16[512,256]{1,0:T(8,128)(2,1)S(1)}, bf16[512,256]{1,0:T(8,128)(2,1)S(1)}, u32[]{:S(2)}, u32[]{:S(2)}) collective-permute-start(bf16[512,256]{1,0:T(8,128)(2,1)S(1)} %get-tuple-element.29), channel_id=1, source_target_pairs={{0,16},{8,24},{16,0},{24,8},{1,17},{9,25},{17,1},{25,9},{2,18},{10... | collective-permute-start | bytes 786440 | tf_op jit(solution)/shard_map/far_1/ppermute | solution.py:29
  6.0 14.4 %collective-permute-start = (bf16[528,256]{1,0:T(8,128)(2,1)S(1)}, bf16[528,256]{1,0:T(8,128)(2,1)S(1)}, u32[]{:S(2)}, u32[]{:S(2)}) collective-permute-start(bf16[528,256]{1,0:T(8,128)(2,1)S(1)} %get-tuple-element.25), channel_id=1, source_target_pairs={{0,4},{1,5},{2,6},{3,7},{4,0},{5,1},{6,2},{7,3},{8,12},{9,13},{10,... | collective-permute-start | bytes 811016 | tf_op jit(solution)/shard_map/left/ppermute | solution.py:23
  10.4 10.0 %collective-permute-start.3 = (bf16[512,256]{1,0:T(8,128)(2,1)S(1)}, bf16[512,256]{1,0:T(8,128)(2,1)S(1)}, u32[]{:S(2)}, u32[]{:S(2)}) collective-permute-start(bf16[512,256]{1,0:T(8,128)(2,1)S(1)} %get-tuple-element.30), channel_id=1, source_target_pairs={{0,8},{8,0},{16,24},{24,16},{1,9},{9,1},{17,25},{25,17},{2,10},{10... | collective-permute-start | bytes 786440 | tf_op jit(solution)/shard_map/near_0/ppermute | solution.py:29
  11.0 9.4 %collective-permute-start.4 = (bf16[512,256]{1,0:T(8,128)(2,1)S(1)}, bf16[512,256]{1,0:T(8,128)(2,1)S(1)}, u32[]{:S(2)}, u32[]{:S(2)}) collective-permute-start(bf16[512,256]{1,0:T(8,128)(2,1)S(1)} %get-tuple-element.31), channel_id=1, source_target_pairs={{0,16},{8,24},{16,0},{24,8},{1,17},{9,25},{17,1},{25,9},{2,18},{10... | collective-permute-start | bytes 786440 | tf_op jit(solution)/shard_map/near_1/ppermute | solution.py:29
  11.5 12.0 %collective-permute-start.6 = (bf16[512,256]{1,0:T(8,128)(2,1)S(1)}, bf16[512,256]{1,0:T(8,128)(2,1)S(1)}, u32[]{:S(2)}, u32[]{:S(2)}) collective-permute-start(bf16[512,256]{1,0:T(8,128)(2,1)S(1)} %add_convert_fusion.1), channel_id=1, source_target_pairs={{0,16},{8,24},{16,0},{24,8},{1,17},{9,25},{17,1},{25,9},{2,18},{10... | collective-permute-start | bytes 786440 | tf_op jit(solution)/shard_map/via_0/ppermute | solution.py:29
  13.2 18.0 %collective-permute-start.10 = (bf16[512,256]{1,0:T(8,128)(2,1)S(1)}, bf16[512,256]{1,0:T(8,128)(2,1)S(1)}, u32[]{:S(2)}, u32[]{:S(2)}) collective-permute-start(bf16[512,256]{1,0:T(8,128)(2,1)S(1)} %add_convert_fusion), channel_id=1, source_target_pairs={{0,8},{8,0},{16,24},{24,16},{1,9},{9,1},{17,25},{25,17},{2,10},{10... | collective-permute-start | bytes 786440 | tf_op jit(solution)/shard_map/via_1/ppermute | solution.py:29
  20.4 10.9 %collective-permute-start.14 = (bf16[384,256]{1,0:T(8,128)(2,1)S(1)}, bf16[384,256]{1,0:T(8,128)(2,1)S(1)}, u32[]{:S(2)}, u32[]{:S(2)}) collective-permute-start(bf16[384,256]{1,0:T(8,128)(2,1)S(1)} %get-tuple-element.42), channel_id=1, source_target_pairs={{0,4},{1,5},{2,6},{3,7},{4,0},{5,1},{6,2},{7,3},{8,12},{9,13},{10,... | collective-permute-start | bytes 589832 | tf_op jit(solution)/shard_map/right/ppermute | solution.py:23
  20.4 11.8 %collective-permute-start.5 = (bf16[528,256]{1,0:T(8,128)(2,1)S(1)}, bf16[528,256]{1,0:T(8,128)(2,1)S(1)}, u32[]{:S(2)}, u32[]{:S(2)}) collective-permute-start(bf16[528,256]{1,0:T(8,128)(2,1)S(1)} %collective-permute-done.refs_0_), channel_id=1, source_target_pairs={{0,8},{8,0},{16,24},{24,16},{1,9},{9,1},{17,25},{25,17},{2,10},{10... | collective-permute-start | bytes 811016 | tf_op jit(solution)/shard_map/left_1/ppermute | solution.py:29
  23.5 10.4 %collective-permute-start.7 = (bf16[528,256]{1,0:T(8,128)(2,1)S(1)}, bf16[528,256]{1,0:T(8,128)(2,1)S(1)}, u32[]{:S(2)}, u32[]{:S(2)}) collective-permute-start(bf16[528,256]{1,0:T(8,128)(2,1)S(1)} %collective-permute-done.refs_0_), channel_id=1, source_target_pairs={{0,16},{8,24},{16,0},{24,8},{1,17},{9,25},{17,1},{25,9},{2,18},{10... | collective-permute-start | bytes 811016 | tf_op jit(solution)/shard_map/left_2/ppermute | solution.py:29
  31.2 6.2 %collective-permute-start.16 = (bf16[384,256]{1,0:T(8,128)(2,1)S(1)}, bf16[384,256]{1,0:T(8,128)(2,1)S(1)}, u32[]{:S(2)}, u32[]{:S(2)}) collective-permute-start(bf16[384,256]{1,0:T(8,128)(2,1)S(1)} %collective-permute-done.14.refs_0_), channel_id=1, source_target_pairs={{0,8},{8,0},{16,24},{24,16},{1,9},{9,1},{17,25},{25,17},{2,10},{10... | collective-permute-start | bytes 589832 | tf_op jit(solution)/shard_map/right_1/ppermute | solution.py:29
  31.8 11.5 %collective-permute-start.17 = (bf16[384,256]{1,0:T(8,128)(2,1)S(1)}, bf16[384,256]{1,0:T(8,128)(2,1)S(1)}, u32[]{:S(2)}, u32[]{:S(2)}) collective-permute-start(bf16[384,256]{1,0:T(8,128)(2,1)S(1)} %collective-permute-done.14.refs_0_), channel_id=1, source_target_pairs={{0,16},{8,24},{16,0},{24,8},{1,17},{9,25},{17,1},{25,9},{2,18},{10... | collective-permute-start | bytes 589832 | tf_op jit(solution)/shard_map/right_2/ppermute | solution.py:29
  32.2 8.0 %collective-permute-start.8 = (bf16[256,256]{1,0:T(8,128)(2,1)S(1)}, bf16[256,256]{1,0:T(8,128)(2,1)S(1)}, u32[]{:S(2)}, u32[]{:S(2)}) collective-permute-start(bf16[256,256]{1,0:T(8,128)(2,1)S(1)} %slice.16), channel_id=1, source_target_pairs={{0,16},{8,24},{16,0},{24,8},{1,17},{9,25},{17,1},{25,9},{2,18},{10... | collective-permute-start | bytes 393224 | tf_op jit(solution)/shard_map/left_3a/ppermute | solution.py:29
  33.9 6.3 %collective-permute-start.9 = (bf16[256,256]{1,0:T(8,128)(2,1)S(1)}, bf16[256,256]{1,0:T(8,128)(2,1)S(1)}, u32[]{:S(2)}, u32[]{:S(2)}) collective-permute-start(bf16[256,256]{1,0:T(8,128)(2,1)S(1)} %slice.17), channel_id=1, source_target_pairs={{0,8},{8,0},{16,24},{24,16},{1,9},{9,1},{17,25},{25,17},{2,10},{10... | collective-permute-start | bytes 393224 | tf_op jit(solution)/shard_map/left_3b/ppermute | solution.py:29
  35.4 14.8 %collective-permute-start.15 = (bf16[528,256]{1,0:T(8,128)(2,1)S(1)}, bf16[528,256]{1,0:T(8,128)(2,1)S(1)}, u32[]{:S(2)}, u32[]{:S(2)}) collective-permute-start(bf16[528,256]{1,0:T(8,128)(2,1)S(1)} %get-tuple-element.43), channel_id=1, source_target_pairs={{0,4},{1,5},{2,6},{3,7},{4,0},{5,1},{6,2},{7,3},{8,12},{9,13},{10,... | collective-permute-start | bytes 811016 | tf_op jit(solution)/shard_map/corners/ppermute | solution.py:23
  37.5 7.3 %collective-permute-start.18 = (bf16[192,256]{1,0:T(8,128)(2,1)S(1)}, bf16[192,256]{1,0:T(8,128)(2,1)S(1)}, u32[]{:S(2)}, u32[]{:S(2)}) collective-permute-start(bf16[192,256]{1,0:T(8,128)(2,1)S(1)} %slice.18), channel_id=1, source_target_pairs={{0,16},{8,24},{16,0},{24,8},{1,17},{9,25},{17,1},{25,9},{2,18},{10... | collective-permute-start | bytes 294920 | tf_op jit(solution)/shard_map/right_3a/ppermute | solution.py:29
  41.2 9.6 %collective-permute-start.11 = (bf16[256,256]{1,0:T(8,128)(2,1)S(1)}, bf16[256,256]{1,0:T(8,128)(2,1)S(1)}, u32[]{:S(2)}, u32[]{:S(2)}) collective-permute-start(bf16[256,256]{1,0:T(8,128)(2,1)S(1)} %get-tuple-element.37), channel_id=1, source_target_pairs={{0,8},{8,0},{16,24},{24,16},{1,9},{9,1},{17,25},{25,17},{2,10},{10... | collective-permute-start | bytes 393224 | tf_op jit(solution)/shard_map/strip_1/ppermute | solution.py:29
  42.8 8.0 %collective-permute-start.12 = (bf16[256,256]{1,0:T(8,128)(2,1)S(1)}, bf16[256,256]{1,0:T(8,128)(2,1)S(1)}, u32[]{:S(2)}, u32[]{:S(2)}) collective-permute-start(bf16[256,256]{1,0:T(8,128)(2,1)S(1)} %get-tuple-element.38), channel_id=1, source_target_pairs={{0,16},{8,24},{16,0},{24,8},{1,17},{9,25},{17,1},{25,9},{2,18},{10... | collective-permute-start | bytes 393224 | tf_op jit(solution)/shard_map/strip_2/ppermute | solution.py:29
  43.3 7.5 %collective-permute-start.13 = (bf16[256,256]{1,0:T(8,128)(2,1)S(1)}, bf16[256,256]{1,0:T(8,128)(2,1)S(1)}, u32[]{:S(2)}, u32[]{:S(2)}) collective-permute-start(bf16[256,256]{1,0:T(8,128)(2,1)S(1)} %get-tuple-element.39), channel_id=1, source_target_pairs={{0,24},{8,16},{16,8},{24,0},{1,25},{9,17},{17,9},{25,1},{2,26},{10... | collective-permute-start | bytes 393224 | tf_op jit(solution)/shard_map/strip_3/ppermute | solution.py:29
  44.8 5.5 %collective-permute-start.19 = (bf16[192,256]{1,0:T(8,128)(2,1)S(1)}, bf16[192,256]{1,0:T(8,128)(2,1)S(1)}, u32[]{:S(2)}, u32[]{:S(2)}) collective-permute-start(bf16[192,256]{1,0:T(8,128)(2,1)S(1)} %slice.19), channel_id=1, source_target_pairs={{0,8},{8,0},{16,24},{24,16},{1,9},{9,1},{17,25},{25,17},{2,10},{10... | collective-permute-start | bytes 294920 | tf_op jit(solution)/shard_map/right_3b/ppermute | solution.py:29

commit v12 on v11

--- a/solution.py
+++ b/solution.py
@@ -342,8 +342,7 @@
         )
         right = after(right, via_0, via_1)
         right_1, right_2 = swapped(right, 1, "right_1"), swapped(right, 2, "right_2")
-        cut = right.shape[0] // 2
-        right_3 = [swapped(right_1[:cut], 2, "right_3a"), swapped(right_2[cut:], 1, "right_3b")]
+        right_3 = [swapped(right_1, 2, "right_3")]
         rights = [[right], [right_1], [right_2], right_3]
     else:
         (left,) = messages(me, grads, left_roots, groups, [], False, "sent_first")

time: 52.6 us -> 54.2 us (1.030)
  waiting for transfers between devices: 19.2 us -> 20.7 us
    ppermute x17 -> x16, waiting for transfers between devices: 7.93 us -> 9.43 us  [swapped(): lax.ppermute(value, 'dp', [(source, source ^ flip) for source in range(co...]
    ppermute x17 -> x16, starting transfers between devices: 22 us -> 22.1 us  [swapped(): lax.ppermute(value, 'dp', [(source, source ^ flip) for source in range(co...]
  transfers between devices with their start and end apart: 20 -> 19, of which waited for: 6 -> 7; matrix products, arithmetic and copies ran while one was open for 0% -> 0% of each run, Pallas kernels for 6% -> 6%
where the time goes in v12:
time: 54.2 us; the launch traced here: 54 us
  starting transfers between devices  25.4 us (47%)
  waiting for transfers between devices  20.7 us (38%)
  Pallas kernels  6.35 us (12%)
  between operations  1.37 us (3%)
    ppermute x16, starting transfers between devices, swapped(): lax.ppermute(value, 'dp', [(source, source ^ flip) for source in range(co...  22.1 us
    ppermute x3, waiting for transfers between devices, shifted(): lax.ppermute(value, 'shard', [(source, (source + count // 2) % count) for...  11.3 us
    ppermute x16, waiting for transfers between devices, swapped(): lax.ppermute(value, 'dp', [(source, source ^ flip) for source in range(co...  9.43 us
    ppermute x3, starting transfers between devices, shifted(): lax.ppermute(value, 'shard', [(source, (source + count // 2) % count) for...  3.26 us
    pallas_call x2, Pallas kernels, messages(): pl.pallas_call(functools.partial(messages_kernel, wanted, strip), in_spec...  3.23 us
    pallas_call x1, Pallas kernels, update_rows(): pl.pallas_call(functools.partial(rows_kernel, groups), in_specs=[SMEM_SPE...  1.57 us
  transfers between devices with their start and end apart: 19, of which 7 were waited for; matrix products, arithmetic and copies ran while one was open for 0% of the time, Pallas kernels for 6%

profile of v12, /device:TPU:0, one launch (start us, length us, event | category | flops | bytes accessed | tf_op | source)
XLA Modules:
  0.0 54.0 jit_solution(3862481004430882980)
XLA Ops:
  0.0 1.5 %sent_first.1 = (bf16[512,256]{1,0:T(8,128)(2,1)S(1)}, bf16[512,256]{1,0:T(8,128)(2,1)S(1)}, bf16[528,256]{1,0:T(8,128)(2,1)S(1)}) custom-call(s32[1]{0:T(128)} %bitcast.me_ref, bf16[1,1,1024,1024]{3,2,1,0:T(8,128)(2,1)} %grad_ref.3, bf16[1,1024,1024]{2,1,0:T(8,128)(2,1)} %root_ref.2), custom_call_target="tpu_custom_call" | custom-call | tf_op jit(solution)/shard_map/sent_first/pallas_call | solution.py:133
  1.5 3.0 %collective-permute-start.1 = (bf16[512,256]{1,0:T(8,128)(2,1)S(1)}, bf16[512,256]{1,0:T(8,128)(2,1)S(1)}, u32[]{:S(2)}, u32[]{:S(2)}) collective-permute-start(bf16[512,256]{1,0:T(8,128)(2,1)S(1)} %get-tuple-element.27), channel_id=1, source_target_pairs={{0,8},{8,0},{16,24},{24,16},{1,9},{9,1},{17,25},{25,17},{2,10},{10... | collective-permute-start | bytes 786440 | tf_op jit(solution)/shard_map/far_0/ppermute | solution.py:29
  4.5 1.5 %collective-permute-start.2 = (bf16[512,256]{1,0:T(8,128)(2,1)S(1)}, bf16[512,256]{1,0:T(8,128)(2,1)S(1)}, u32[]{:S(2)}, u32[]{:S(2)}) collective-permute-start(bf16[512,256]{1,0:T(8,128)(2,1)S(1)} %get-tuple-element.29), channel_id=1, source_target_pairs={{0,16},{8,24},{16,0},{24,8},{1,17},{9,25},{17,1},{25,9},{2,18},{10... | collective-permute-start | bytes 786440 | tf_op jit(solution)/shard_map/far_1/ppermute | solution.py:29
  6.0 2.6 %collective-permute-start = (bf16[528,256]{1,0:T(8,128)(2,1)S(1)}, bf16[528,256]{1,0:T(8,128)(2,1)S(1)}, u32[]{:S(2)}, u32[]{:S(2)}) collective-permute-start(bf16[528,256]{1,0:T(8,128)(2,1)S(1)} %get-tuple-element.25), channel_id=1, source_target_pairs={{0,4},{1,5},{2,6},{3,7},{4,0},{5,1},{6,2},{7,3},{8,12},{9,13},{10,... | collective-permute-start | bytes 811016 | tf_op jit(solution)/shard_map/left/ppermute | solution.py:23
  8.6 1.8 %sent_later.1 = (bf16[512,256]{1,0:T(8,128)(2,1)S(1)}, bf16[512,256]{1,0:T(8,128)(2,1)S(1)}, bf16[512,256]{1,0:T(8,128)(2,1)S(1)}, bf16[512,256]{1,0:T(8,128)(2,...) custom-call(s32[1]{0:T(128)} %bitcast.me_ref, ...), custom_call_target="tpu_custom_call" | custom-call | tf_op jit(solution)/shard_map/sent_later/pallas_call | solution.py:133
  10.4 0.6 %collective-permute-start.3 = (bf16[512,256]{1,0:T(8,128)(2,1)S(1)}, bf16[512,256]{1,0:T(8,128)(2,1)S(1)}, u32[]{:S(2)}, u32[]{:S(2)}) collective-permute-start(bf16[512,256]{1,0:T(8,128)(2,1)S(1)} %get-tuple-element.30), channel_id=1, source_target_pairs={{0,8},{8,0},{16,24},{24,16},{1,9},{9,1},{17,25},{25,17},{2,10},{10... | collective-permute-start | bytes 786440 | tf_op jit(solution)/shard_map/near_0/ppermute | solution.py:29
  11.0 0.5 collective-permute-start.4
  11.5 0.0 collective-permute-done.1
  11.5 0.1 add_convert_fusion.1
  11.5 1.6 %collective-permute-start.6 = (bf16[512,256]{1,0:T(8,128)(2,1)S(1)}, bf16[512,256]{1,0:T(8,128)(2,1)S(1)}, u32[]{:S(2)}, u32[]{:S(2)}) collective-permute-start(bf16[512,256]{1,0:T(8,128)(2,1)S(1)} %add_convert_fusion.1), channel_id=1, source_target_pairs={{0,16},{8,24},{16,0},{24,8},{1,17},{9,25},{17,1},{25,9},{2,18},{10... | collective-permute-start | bytes 786440 | tf_op jit(solution)/shard_map/via_0/ppermute | solution.py:29
  13.1 0.1 add_convert_fusion
  13.2 2.1 %collective-permute-start.10 = (bf16[512,256]{1,0:T(8,128)(2,1)S(1)}, bf16[512,256]{1,0:T(8,128)(2,1)S(1)}, u32[]{:S(2)}, u32[]{:S(2)}) collective-permute-start(bf16[512,256]{1,0:T(8,128)(2,1)S(1)} %add_convert_fusion), channel_id=1, source_target_pairs={{0,8},{8,0},{16,24},{24,16},{1,9},{9,1},{17,25},{25,17},{2,10},{10... | collective-permute-start | bytes 786440 | tf_op jit(solution)/shard_map/via_1/ppermute | solution.py:29
  15.3 5.1 %collective-permute-done.refs_0_ = bf16[528,256]{1,0:T(8,128)(2,1)S(1)} collective-permute-done((bf16[528,256]{1,0:T(8,128)(2,1)S(1)}, bf16[528,256]{1,0:T(8,128)(2,1)S(1)}, u32[]{:S(2)}, u32[]{:S(2)}) %collective-permute-start) | collective-permute-done | bytes 270368 | tf_op jit(solution)/shard_map/left/ppermute | solution.py:23
  20.4 1.3 %collective-permute-start.5 = (bf16[528,256]{1,0:T(8,128)(2,1)S(1)}, bf16[528,256]{1,0:T(8,128)(2,1)S(1)}, u32[]{:S(2)}, u32[]{:S(2)}) collective-permute-start(bf16[528,256]{1,0:T(8,128)(2,1)S(1)} %collective-permute-done.refs_0_), channel_id=1, source_target_pairs={{0,8},{8,0},{16,24},{24,16},{1,9},{9,1},{17,25},{25,17},{2,10},{10... | collective-permute-start | bytes 811016 | tf_op jit(solution)/shard_map/left_1/ppermute | solution.py:29
  21.7 1.8 %collective-permute-done.6.refs_7_ = bf16[512,256]{1,0:T(8,128)(2,1)S(1)} collective-permute-done((bf16[512,256]{1,0:T(8,128)(2,1)S(1)}, bf16[512,256]{1,0:T(8,128)(2,1)S(1)}, u32[]{:S(2)}, u32[]{:S(2)}) %collective-permute-start.6) | collective-permute-done | bytes 262176 | tf_op jit(solution)/shard_map/via_0/ppermute | solution.py:29
  23.5 1.5 %collective-permute-start.7 = (bf16[528,256]{1,0:T(8,128)(2,1)S(1)}, bf16[528,256]{1,0:T(8,128)(2,1)S(1)}, u32[]{:S(2)}, u32[]{:S(2)}) collective-permute-start(bf16[528,256]{1,0:T(8,128)(2,1)S(1)} %collective-permute-done.refs_0_), channel_id=1, source_target_pairs={{0,16},{8,24},{16,0},{24,8},{1,17},{9,25},{17,1},{25,9},{2,18},{10... | collective-permute-start | bytes 811016 | tf_op jit(solution)/shard_map/left_2/ppermute | solution.py:29
  25.0 6.2 %collective-permute-done.14.refs_0_ = bf16[384,256]{1,0:T(8,128)(2,1)S(1)} collective-permute-done((bf16[384,256]{1,0:T(8,128)(2,1)S(1)}, bf16[384,256]{1,0:T(8,128)(2,1)S(1)}, u32[]{:S(2)}, u32[]{:S(2)}) %collective-permute-start.14) | collective-permute-done | bytes 196640 | tf_op jit(solution)/shard_map/right/ppermute | solution.py:23
  31.2 0.5 collective-permute-start.16
  31.8 0.4 collective-permute-start.17
  32.2 1.7 %collective-permute-start.8 = (bf16[256,256]{1,0:T(8,128)(2,1)S(1)}, bf16[256,256]{1,0:T(8,128)(2,1)S(1)}, u32[]{:S(2)}, u32[]{:S(2)}) collective-permute-start(bf16[256,256]{1,0:T(8,128)(2,1)S(1)} %slice.8), channel_id=1, source_target_pairs={{0,16},{8,24},{16,0},{24,8},{1,17},{9,25},{17,1},{25,9},{2,18},{10... | collective-permute-start | bytes 393224 | tf_op jit(solution)/shard_map/left_3a/ppermute | solution.py:29
  33.9 1.6 %collective-permute-start.9 = (bf16[256,256]{1,0:T(8,128)(2,1)S(1)}, bf16[256,256]{1,0:T(8,128)(2,1)S(1)}, u32[]{:S(2)}, u32[]{:S(2)}) collective-permute-start(bf16[256,256]{1,0:T(8,128)(2,1)S(1)} %slice.9), channel_id=1, source_target_pairs={{0,8},{8,0},{16,24},{24,16},{1,9},{9,1},{17,25},{25,17},{2,10},{10... | collective-permute-start | bytes 393224 | tf_op jit(solution)/shard_map/left_3b/ppermute | solution.py:29
  35.4 0.7 %collective-permute-start.15 = (bf16[528,256]{1,0:T(8,128)(2,1)S(1)}, bf16[528,256]{1,0:T(8,128)(2,1)S(1)}, u32[]{:S(2)}, u32[]{:S(2)}) collective-permute-start(bf16[528,256]{1,0:T(8,128)(2,1)S(1)} %get-tuple-element.43), channel_id=1, source_target_pairs={{0,4},{1,5},{2,6},{3,7},{4,0},{5,1},{6,2},{7,3},{8,12},{9,13},{10,... | collective-permute-start | bytes 811016 | tf_op jit(solution)/shard_map/corners/ppermute | solution.py:23
  36.1 1.3 %collective-permute-done.16.refs_1_ = bf16[384,256]{1,0:T(8,128)(2,1)S(1)} collective-permute-done((bf16[384,256]{1,0:T(8,128)(2,1)S(1)}, bf16[384,256]{1,0:T(8,128)(2,1)S(1)}, u32[]{:S(2)}, u32[]{:S(2)}) %collective-permute-start.16) | collective-permute-done | bytes 196640 | tf_op jit(solution)/shard_map/right_1/ppermute | solution.py:29
  37.5 0.5 collective-permute-start.18
  39.3 2.0 %collective-permute-done.8.refs_3_ = bf16[256,256]{1,0:T(8,128)(2,1)S(1)} collective-permute-done((bf16[256,256]{1,0:T(8,128)(2,1)S(1)}, bf16[256,256]{1,0:T(8,128)(2,1)S(1)}, u32[]{:S(2)}, u32[]{:S(2)}) %collective-permute-start.8) | collective-permute-done | bytes 131104 | tf_op jit(solution)/shard_map/left_3a/ppermute | solution.py:29
  41.2 1.0 %left_columns.1 = (bf16[256,256]{1,0:T(8,128)(2,1)S(1)}, bf16[256,256]{1,0:T(8,128)(2,1)S(1)}, bf16[256,256]{1,0:T(8,128)(2,1)S(1)}, bf16[256,256]{1,0:T(8,128)(2,1)S(1)}) custom-call(s32[1]{0:T(128)} %bitcast.me_ref, s32[1]{0:T(128)S(6)} %copy.6.rows_ref, s32[1]{0:T(128)S(6)} %copy.7.cols_ref, bf16[528,256]{1,0:T(8,128)(2,1)S(1)} %collective-permute-done.refs_0_, ...), custom_call_target="tpu_custom_call" | custom-call | flops 536870912 | bytes 4194304 | tf_op jit(solution)/shard_map/left_columns/pallas_call | solution.py:227
  42.3 3.8 %collective-permute-start.11 = (bf16[256,256]{1,0:T(8,128)(2,1)S(1)}, bf16[256,256]{1,0:T(8,128)(2,1)S(1)}, u32[]{:S(2)}, u32[]{:S(2)}) collective-permute-start(bf16[256,256]{1,0:T(8,128)(2,1)S(1)} %get-tuple-element.37), channel_id=1, source_target_pairs={{0,8},{8,0},{16,24},{24,16},{1,9},{9,1},{17,25},{25,17},{2,10},{10... | collective-permute-start | bytes 393224 | tf_op jit(solution)/shard_map/strip_1/ppermute | solution.py:29
  46.1 1.5 %collective-permute-start.13 = (bf16[256,256]{1,0:T(8,128)(2,1)S(1)}, bf16[256,256]{1,0:T(8,128)(2,1)S(1)}, u32[]{:S(2)}, u32[]{:S(2)}) collective-permute-start(bf16[256,256]{1,0:T(8,128)(2,1)S(1)} %get-tuple-element.39), channel_id=1, source_target_pairs={{0,24},{8,16},{16,8},{24,0},{1,25},{9,17},{17,9},{25,1},{2,26},{10... | collective-permute-start | bytes 393224 | tf_op jit(solution)/shard_map/strip_3/ppermute | solution.py:29
  47.6 0.5 whole_right.1.refs_4_
  48.1 0.9 %collective-permute-done.11.refs_1_ = bf16[256,256]{1,0:T(8,128)(2,1)S(1)} collective-permute-done((bf16[256,256]{1,0:T(8,128)(2,1)S(1)}, bf16[256,256]{1,0:T(8,128)(2,1)S(1)}, u32[]{:S(2)}, u32[]{:S(2)}) %collective-permute-start.11) | collective-permute-done | bytes 131104 | tf_op jit(solution)/shard_map/strip_1/ppermute | solution.py:29
  49.0 3.4 %collective-permute-done.12.refs_2_ = bf16[256,256]{1,0:T(8,128)(2,1)S(1)} collective-permute-done((bf16[256,256]{1,0:T(8,128)(2,1)S(1)}, bf16[256,256]{1,0:T(8,128)(2,1)S(1)}, u32[]{:S(2)}, u32[]{:S(2)}) %collective-permute-start.12) | collective-permute-done | bytes 131104 | tf_op jit(solution)/shard_map/strip_2/ppermute | solution.py:29
  52.4 1.6 %update_rows.1 = bf16[1,256,1024]{2,1,0:T(8,128)(2,1)} custom-call(s32[1]{0:T(128)} %bitcast.me_ref, s32[1]{0:T(128)S(6)} %copy.6.rows_ref, s32[1]{0:T(128)S(6)} %copy.7.cols_ref, bf16[256,256]{1,0:T(8,128)(2,1)S(1)} %get-tuple-element.36.refs_0_, bf16[256,256]{1,0:T(8,128)(2,1)S(1)} %collective-permute-done.11.refs_1_, ...), custom_call_target="tpu_custom_call" | custom-call | flops 536870912 | bytes 4194304 | tf_op jit(solution)/shard_map/update_rows/pallas_call | solution.py:284
  (15 shorter events, 0.1 us)
Async XLA Ops:
  1.5 10.0 %collective-permute-start.1 = (bf16[512,256]{1,0:T(8,128)(2,1)S(1)}, bf16[512,256]{1,0:T(8,128)(2,1)S(1)}, u32[]{:S(2)}, u32[]{:S(2)}) collective-permute-start(bf16[512,256]{1,0:T(8,128)(2,1)S(1)} %get-tuple-element.27), channel_id=1, source_target_pairs={{0,8},{8,0},{16,24},{24,16},{1,9},{9,1},{17,25},{25,17},{2,10},{10... | collective-permute-start | bytes 786440 | tf_op jit(solution)/shard_map/far_0/ppermute | solution.py:29
  4.5 8.6 %collective-permute-start.2 = (bf16[512,256]{1,0:T(8,128)(2,1)S(1)}, bf16[512,256]{1,0:T(8,128)(2,1)S(1)}, u32[]{:S(2)}, u32[]{:S(2)}) collective-permute-start(bf16[512,256]{1,0:T(8,128)(2,1)S(1)} %get-tuple-element.29), channel_id=1, source_target_pairs={{0,16},{8,24},{16,0},{24,8},{1,17},{9,25},{17,1},{25,9},{2,18},{10... | collective-permute-start | bytes 786440 | tf_op jit(solution)/shard_map/far_1/ppermute | solution.py:29
  6.0 14.4 %collective-permute-start = (bf16[528,256]{1,0:T(8,128)(2,1)S(1)}, bf16[528,256]{1,0:T(8,128)(2,1)S(1)}, u32[]{:S(2)}, u32[]{:S(2)}) collective-permute-start(bf16[528,256]{1,0:T(8,128)(2,1)S(1)} %get-tuple-element.25), channel_id=1, source_target_pairs={{0,4},{1,5},{2,6},{3,7},{4,0},{5,1},{6,2},{7,3},{8,12},{9,13},{10,... | collective-permute-start | bytes 811016 | tf_op jit(solution)/shard_map/left/ppermute | solution.py:23
  10.4 10.0 %collective-permute-start.3 = (bf16[512,256]{1,0:T(8,128)(2,1)S(1)}, bf16[512,256]{1,0:T(8,128)(2,1)S(1)}, u32[]{:S(2)}, u32[]{:S(2)}) collective-permute-start(bf16[512,256]{1,0:T(8,128)(2,1)S(1)} %get-tuple-element.30), channel_id=1, source_target_pairs={{0,8},{8,0},{16,24},{24,16},{1,9},{9,1},{17,25},{25,17},{2,10},{10... | collective-permute-start | bytes 786440 | tf_op jit(solution)/shard_map/near_0/ppermute | solution.py:29
  11.0 9.4 %collective-permute-start.4 = (bf16[512,256]{1,0:T(8,128)(2,1)S(1)}, bf16[512,256]{1,0:T(8,128)(2,1)S(1)}, u32[]{:S(2)}, u32[]{:S(2)}) collective-permute-start(bf16[512,256]{1,0:T(8,128)(2,1)S(1)} %get-tuple-element.31), channel_id=1, source_target_pairs={{0,16},{8,24},{16,0},{24,8},{1,17},{9,25},{17,1},{25,9},{2,18},{10... | collective-permute-start | bytes 786440 | tf_op jit(solution)/shard_map/near_1/ppermute | solution.py:29
  11.5 12.0 %collective-permute-start.6 = (bf16[512,256]{1,0:T(8,128)(2,1)S(1)}, bf16[512,256]{1,0:T(8,128)(2,1)S(1)}, u32[]{:S(2)}, u32[]{:S(2)}) collective-permute-start(bf16[512,256]{1,0:T(8,128)(2,1)S(1)} %add_convert_fusion.1), channel_id=1, source_target_pairs={{0,16},{8,24},{16,0},{24,8},{1,17},{9,25},{17,1},{25,9},{2,18},{10... | collective-permute-start | bytes 786440 | tf_op jit(solution)/shard_map/via_0/ppermute | solution.py:29
  13.2 18.0 %collective-permute-start.10 = (bf16[512,256]{1,0:T(8,128)(2,1)S(1)}, bf16[512,256]{1,0:T(8,128)(2,1)S(1)}, u32[]{:S(2)}, u32[]{:S(2)}) collective-permute-start(bf16[512,256]{1,0:T(8,128)(2,1)S(1)} %add_convert_fusion), channel_id=1, source_target_pairs={{0,8},{8,0},{16,24},{24,16},{1,9},{9,1},{17,25},{25,17},{2,10},{10... | collective-permute-start | bytes 786440 | tf_op jit(solution)/shard_map/via_1/ppermute | solution.py:29
  20.4 10.9 %collective-permute-start.14 = (bf16[384,256]{1,0:T(8,128)(2,1)S(1)}, bf16[384,256]{1,0:T(8,128)(2,1)S(1)}, u32[]{:S(2)}, u32[]{:S(2)}) collective-permute-start(bf16[384,256]{1,0:T(8,128)(2,1)S(1)} %get-tuple-element.42), channel_id=1, source_target_pairs={{0,4},{1,5},{2,6},{3,7},{4,0},{5,1},{6,2},{7,3},{8,12},{9,13},{10,... | collective-permute-start | bytes 589832 | tf_op jit(solution)/shard_map/right/ppermute | solution.py:23
  20.4 11.8 %collective-permute-start.5 = (bf16[528,256]{1,0:T(8,128)(2,1)S(1)}, bf16[528,256]{1,0:T(8,128)(2,1)S(1)}, u32[]{:S(2)}, u32[]{:S(2)}) collective-permute-start(bf16[528,256]{1,0:T(8,128)(2,1)S(1)} %collective-permute-done.refs_0_), channel_id=1, source_target_pairs={{0,8},{8,0},{16,24},{24,16},{1,9},{9,1},{17,25},{25,17},{2,10},{10... | collective-permute-start | bytes 811016 | tf_op jit(solution)/shard_map/left_1/ppermute | solution.py:29
  23.5 10.4 %collective-permute-start.7 = (bf16[528,256]{1,0:T(8,128)(2,1)S(1)}, bf16[528,256]{1,0:T(8,128)(2,1)S(1)}, u32[]{:S(2)}, u32[]{:S(2)}) collective-permute-start(bf16[528,256]{1,0:T(8,128)(2,1)S(1)} %collective-permute-done.refs_0_), channel_id=1, source_target_pairs={{0,16},{8,24},{16,0},{24,8},{1,17},{9,25},{17,1},{25,9},{2,18},{10... | collective-permute-start | bytes 811016 | tf_op jit(solution)/shard_map/left_2/ppermute | solution.py:29
  31.2 6.2 %collective-permute-start.16 = (bf16[384,256]{1,0:T(8,128)(2,1)S(1)}, bf16[384,256]{1,0:T(8,128)(2,1)S(1)}, u32[]{:S(2)}, u32[]{:S(2)}) collective-permute-start(bf16[384,256]{1,0:T(8,128)(2,1)S(1)} %collective-permute-done.14.refs_0_), channel_id=1, source_target_pairs={{0,8},{8,0},{16,24},{24,16},{1,9},{9,1},{17,25},{25,17},{2,10},{10... | collective-permute-start | bytes 589832 | tf_op jit(solution)/shard_map/right_1/ppermute | solution.py:29
  31.8 14.3 %collective-permute-start.17 = (bf16[384,256]{1,0:T(8,128)(2,1)S(1)}, bf16[384,256]{1,0:T(8,128)(2,1)S(1)}, u32[]{:S(2)}, u32[]{:S(2)}) collective-permute-start(bf16[384,256]{1,0:T(8,128)(2,1)S(1)} %collective-permute-done.14.refs_0_), channel_id=1, source_target_pairs={{0,16},{8,24},{16,0},{24,8},{1,17},{9,25},{17,1},{25,9},{2,18},{10... | collective-permute-start | bytes 589832 | tf_op jit(solution)/shard_map/right_2/ppermute | solution.py:29
  32.2 9.0 %collective-permute-start.8 = (bf16[256,256]{1,0:T(8,128)(2,1)S(1)}, bf16[256,256]{1,0:T(8,128)(2,1)S(1)}, u32[]{:S(2)}, u32[]{:S(2)}) collective-permute-start(bf16[256,256]{1,0:T(8,128)(2,1)S(1)} %slice.8), channel_id=1, source_target_pairs={{0,16},{8,24},{16,0},{24,8},{1,17},{9,25},{17,1},{25,9},{2,18},{10... | collective-permute-start | bytes 393224 | tf_op jit(solution)/shard_map/left_3a/ppermute | solution.py:29
  33.9 7.3 %collective-permute-start.9 = (bf16[256,256]{1,0:T(8,128)(2,1)S(1)}, bf16[256,256]{1,0:T(8,128)(2,1)S(1)}, u32[]{:S(2)}, u32[]{:S(2)}) collective-permute-start(bf16[256,256]{1,0:T(8,128)(2,1)S(1)} %slice.9), channel_id=1, source_target_pairs={{0,8},{8,0},{16,24},{24,16},{1,9},{9,1},{17,25},{25,17},{2,10},{10... | collective-permute-start | bytes 393224 | tf_op jit(solution)/shard_map/left_3b/ppermute | solution.py:29
  35.4 12.2 %collective-permute-start.15 = (bf16[528,256]{1,0:T(8,128)(2,1)S(1)}, bf16[528,256]{1,0:T(8,128)(2,1)S(1)}, u32[]{:S(2)}, u32[]{:S(2)}) collective-permute-start(bf16[528,256]{1,0:T(8,128)(2,1)S(1)} %get-tuple-element.43), channel_id=1, source_target_pairs={{0,4},{1,5},{2,6},{3,7},{4,0},{5,1},{6,2},{7,3},{8,12},{9,13},{10,... | collective-permute-start | bytes 811016 | tf_op jit(solution)/shard_map/corners/ppermute | solution.py:23
  37.5 10.2 %collective-permute-start.18 = (bf16[384,256]{1,0:T(8,128)(2,1)S(1)}, bf16[384,256]{1,0:T(8,128)(2,1)S(1)}, u32[]{:S(2)}, u32[]{:S(2)}) collective-permute-start(bf16[384,256]{1,0:T(8,128)(2,1)S(1)} %collective-permute-done.16.refs_1_), channel_id=1, source_target_pairs={{0,16},{8,24},{16,0},{24,8},{1,17},{9,25},{17,1},{25,9},{2,18},{10... | collective-permute-start | bytes 589832 | tf_op jit(solution)/shard_map/right_3/ppermute | solution.py:29
  42.3 6.7 %collective-permute-start.11 = (bf16[256,256]{1,0:T(8,128)(2,1)S(1)}, bf16[256,256]{1,0:T(8,128)(2,1)S(1)}, u32[]{:S(2)}, u32[]{:S(2)}) collective-permute-start(bf16[256,256]{1,0:T(8,128)(2,1)S(1)} %get-tuple-element.37), channel_id=1, source_target_pairs={{0,8},{8,0},{16,24},{24,16},{1,9},{9,1},{17,25},{25,17},{2,10},{10... | collective-permute-start | bytes 393224 | tf_op jit(solution)/shard_map/strip_1/ppermute | solution.py:29
  46.1 6.4 %collective-permute-start.12 = (bf16[256,256]{1,0:T(8,128)(2,1)S(1)}, bf16[256,256]{1,0:T(8,128)(2,1)S(1)}, u32[]{:S(2)}, u32[]{:S(2)}) collective-permute-start(bf16[256,256]{1,0:T(8,128)(2,1)S(1)} %get-tuple-element.38), channel_id=1, source_target_pairs={{0,16},{8,24},{16,0},{24,8},{1,17},{9,25},{17,1},{25,9},{2,18},{10... | collective-permute-start | bytes 393224 | tf_op jit(solution)/shard_map/strip_2/ppermute | solution.py:29
  46.1 6.4 %collective-permute-start.13 = (bf16[256,256]{1,0:T(8,128)(2,1)S(1)}, bf16[256,256]{1,0:T(8,128)(2,1)S(1)}, u32[]{:S(2)}, u32[]{:S(2)}) collective-permute-start(bf16[256,256]{1,0:T(8,128)(2,1)S(1)} %get-tuple-element.39), channel_id=1, source_target_pairs={{0,24},{8,16},{16,8},{24,0},{1,25},{9,17},{17,9},{25,1},{2,26},{10... | collective-permute-start | bytes 393224 | tf_op jit(solution)/shard_map/strip_3/ppermute | solution.py:29

commit v13 on v11

--- a/solution.py
+++ b/solution.py
@@ -342,7 +342,7 @@
         )
         right = after(right, via_0, via_1)
         right_1, right_2 = swapped(right, 1, "right_1"), swapped(right, 2, "right_2")
-        cut = right.shape[0] // 2
+        cut = TILE
         right_3 = [swapped(right_1[:cut], 2, "right_3a"), swapped(right_2[cut:], 1, "right_3b")]
         rights = [[right], [right_1], [right_2], right_3]
     else:

time: 52.6 us -> 51.7 us (0.983)
  waiting for transfers between devices: 19.2 us -> 18.6 us
    ppermute x17, waiting for transfers between devices: 7.93 us -> 5.57 us  [swapped(): lax.ppermute(value, 'dp', [(source, source ^ flip) for source in range(co...]
    ppermute x3, waiting for transfers between devices: 11.3 us -> 13.1 us  [shifted(): lax.ppermute(value, 'shard', [(source, (source + count // 2) % count) for...]
  transfers between devices with their start and end apart: 20 -> 20, of which waited for: 6 -> 7; matrix products, arithmetic and copies ran while one was open for 0% -> 0% of each run, Pallas kernels for 6% -> 6%
where the time goes in v13:
time: 51.7 us; the launch traced here: 51.5 us
  starting transfers between devices  24.9 us (48%)
  waiting for transfers between devices  18.6 us (36%)
  Pallas kernels  6.36 us (12%)
  between operations  1.4 us (3%)
    ppermute x17, starting transfers between devices, swapped(): lax.ppermute(value, 'dp', [(source, source ^ flip) for source in range(co...  21.6 us
    ppermute x3, waiting for transfers between devices, shifted(): lax.ppermute(value, 'shard', [(source, (source + count // 2) % count) for...  13.1 us
    ppermute x17, waiting for transfers between devices, swapped(): lax.ppermute(value, 'dp', [(source, source ^ flip) for source in range(co...  5.57 us
    ppermute x3, starting transfers between devices, shifted(): lax.ppermute(value, 'shard', [(source, (source + count // 2) % count) for...  3.26 us
    pallas_call x2, Pallas kernels, messages(): pl.pallas_call(functools.partial(messages_kernel, wanted, strip), in_spec...  3.23 us
    pallas_call x1, Pallas kernels, update_rows(): pl.pallas_call(functools.partial(rows_kernel, groups), in_specs=[SMEM_SPE...  1.57 us
    pallas_call x1, Pallas kernels, left_columns(): pl.pallas_call(functools.partial(columns_kernel, groups, [len(part) for p...  1.04 us
  transfers between devices with their start and end apart: 20, of which 7 were waited for; matrix products, arithmetic and copies ran while one was open for 0% of the time, Pallas kernels for 6%

profile of v13, /device:TPU:0, one launch (start us, length us, event | category | flops | bytes accessed | tf_op | source)
XLA Modules:
  0.0 51.5 jit_solution(89568412529307509)
XLA Ops:
  0.0 1.5 %sent_first.1 = (bf16[512,256]{1,0:T(8,128)(2,1)S(1)}, bf16[512,256]{1,0:T(8,128)(2,1)S(1)}, bf16[528,256]{1,0:T(8,128)(2,1)S(1)}) custom-call(s32[1]{0:T(128)} %bitcast.me_ref, bf16[1,1,1024,1024]{3,2,1,0:T(8,128)(2,1)} %grad_ref.3, bf16[1,1024,1024]{2,1,0:T(8,128)(2,1)} %root_ref.2), custom_call_target="tpu_custom_call" | custom-call | tf_op jit(solution)/shard_map/sent_first/pallas_call | solution.py:133
  1.5 3.0 %collective-permute-start.1 = (bf16[512,256]{1,0:T(8,128)(2,1)S(1)}, bf16[512,256]{1,0:T(8,128)(2,1)S(1)}, u32[]{:S(2)}, u32[]{:S(2)}) collective-permute-start(bf16[512,256]{1,0:T(8,128)(2,1)S(1)} %get-tuple-element.27), channel_id=1, source_target_pairs={{0,8},{8,0},{16,24},{24,16},{1,9},{9,1},{17,25},{25,17},{2,10},{10... | collective-permute-start | bytes 786440 | tf_op jit(solution)/shard_map/far_0/ppermute | solution.py:29
  4.5 1.5 %collective-permute-start.2 = (bf16[512,256]{1,0:T(8,128)(2,1)S(1)}, bf16[512,256]{1,0:T(8,128)(2,1)S(1)}, u32[]{:S(2)}, u32[]{:S(2)}) collective-permute-start(bf16[512,256]{1,0:T(8,128)(2,1)S(1)} %get-tuple-element.29), channel_id=1, source_target_pairs={{0,16},{8,24},{16,0},{24,8},{1,17},{9,25},{17,1},{25,9},{2,18},{10... | collective-permute-start | bytes 786440 | tf_op jit(solution)/shard_map/far_1/ppermute | solution.py:29
  6.0 2.6 %collective-permute-start = (bf16[528,256]{1,0:T(8,128)(2,1)S(1)}, bf16[528,256]{1,0:T(8,128)(2,1)S(1)}, u32[]{:S(2)}, u32[]{:S(2)}) collective-permute-start(bf16[528,256]{1,0:T(8,128)(2,1)S(1)} %get-tuple-element.25), channel_id=1, source_target_pairs={{0,4},{1,5},{2,6},{3,7},{4,0},{5,1},{6,2},{7,3},{8,12},{9,13},{10,... | collective-permute-start | bytes 811016 | tf_op jit(solution)/shard_map/left/ppermute | solution.py:23
  8.6 1.8 %sent_later.1 = (bf16[512,256]{1,0:T(8,128)(2,1)S(1)}, bf16[512,256]{1,0:T(8,128)(2,1)S(1)}, bf16[512,256]{1,0:T(8,128)(2,1)S(1)}, bf16[512,256]{1,0:T(8,128)(2,...) custom-call(s32[1]{0:T(128)} %bitcast.me_ref, ...), custom_call_target="tpu_custom_call" | custom-call | tf_op jit(solution)/shard_map/sent_later/pallas_call | solution.py:133
  10.4 0.6 %collective-permute-start.3 = (bf16[512,256]{1,0:T(8,128)(2,1)S(1)}, bf16[512,256]{1,0:T(8,128)(2,1)S(1)}, u32[]{:S(2)}, u32[]{:S(2)}) collective-permute-start(bf16[512,256]{1,0:T(8,128)(2,1)S(1)} %get-tuple-element.30), channel_id=1, source_target_pairs={{0,8},{8,0},{16,24},{24,16},{1,9},{9,1},{17,25},{25,17},{2,10},{10... | collective-permute-start | bytes 786440 | tf_op jit(solution)/shard_map/near_0/ppermute | solution.py:29
  11.0 0.5 collective-permute-start.4
  11.5 1.6 %collective-permute-start.6 = (bf16[512,256]{1,0:T(8,128)(2,1)S(1)}, bf16[512,256]{1,0:T(8,128)(2,1)S(1)}, u32[]{:S(2)}, u32[]{:S(2)}) collective-permute-start(bf16[512,256]{1,0:T(8,128)(2,1)S(1)} %add_convert_fusion.1), channel_id=1, source_target_pairs={{0,16},{8,24},{16,0},{24,8},{1,17},{9,25},{17,1},{25,9},{2,18},{10... | collective-permute-start | bytes 786440 | tf_op jit(solution)/shard_map/via_0/ppermute | solution.py:29
  13.1 0.1 add_convert_fusion
  13.2 2.1 %collective-permute-start.10 = (bf16[512,256]{1,0:T(8,128)(2,1)S(1)}, bf16[512,256]{1,0:T(8,128)(2,1)S(1)}, u32[]{:S(2)}, u32[]{:S(2)}) collective-permute-start(bf16[512,256]{1,0:T(8,128)(2,1)S(1)} %add_convert_fusion), channel_id=1, source_target_pairs={{0,8},{8,0},{16,24},{24,16},{1,9},{9,1},{17,25},{25,17},{2,10},{10... | collective-permute-start | bytes 786440 | tf_op jit(solution)/shard_map/via_1/ppermute | solution.py:29
  15.3 5.1 %collective-permute-done.refs_0_ = bf16[528,256]{1,0:T(8,128)(2,1)S(1)} collective-permute-done((bf16[528,256]{1,0:T(8,128)(2,1)S(1)}, bf16[528,256]{1,0:T(8,128)(2,1)S(1)}, u32[]{:S(2)}, u32[]{:S(2)}) %collective-permute-start) | collective-permute-done | bytes 270368 | tf_op jit(solution)/shard_map/left/ppermute | solution.py:23
  20.4 1.3 %collective-permute-start.5 = (bf16[528,256]{1,0:T(8,128)(2,1)S(1)}, bf16[528,256]{1,0:T(8,128)(2,1)S(1)}, u32[]{:S(2)}, u32[]{:S(2)}) collective-permute-start(bf16[528,256]{1,0:T(8,128)(2,1)S(1)} %collective-permute-done.refs_0_), channel_id=1, source_target_pairs={{0,8},{8,0},{16,24},{24,16},{1,9},{9,1},{17,25},{25,17},{2,10},{10... | collective-permute-start | bytes 811016 | tf_op jit(solution)/shard_map/left_1/ppermute | solution.py:29
  21.7 1.8 %collective-permute-done.6.refs_7_ = bf16[512,256]{1,0:T(8,128)(2,1)S(1)} collective-permute-done((bf16[512,256]{1,0:T(8,128)(2,1)S(1)}, bf16[512,256]{1,0:T(8,128)(2,1)S(1)}, u32[]{:S(2)}, u32[]{:S(2)}) %collective-permute-start.6) | collective-permute-done | bytes 262176 | tf_op jit(solution)/shard_map/via_0/ppermute | solution.py:29
  23.5 1.5 %collective-permute-start.7 = (bf16[528,256]{1,0:T(8,128)(2,1)S(1)}, bf16[528,256]{1,0:T(8,128)(2,1)S(1)}, u32[]{:S(2)}, u32[]{:S(2)}) collective-permute-start(bf16[528,256]{1,0:T(8,128)(2,1)S(1)} %collective-permute-done.refs_0_), channel_id=1, source_target_pairs={{0,16},{8,24},{16,0},{24,8},{1,17},{9,25},{17,1},{25,9},{2,18},{10... | collective-permute-start | bytes 811016 | tf_op jit(solution)/shard_map/left_2/ppermute | solution.py:29
  25.0 6.2 %collective-permute-done.14.refs_0_ = bf16[384,256]{1,0:T(8,128)(2,1)S(1)} collective-permute-done((bf16[384,256]{1,0:T(8,128)(2,1)S(1)}, bf16[384,256]{1,0:T(8,128)(2,1)S(1)}, u32[]{:S(2)}, u32[]{:S(2)}) %collective-permute-start.14) | collective-permute-done | bytes 196640 | tf_op jit(solution)/shard_map/right/ppermute | solution.py:23
  31.2 0.5 collective-permute-start.17
  31.7 0.4 collective-permute-start.16
  32.2 1.7 %collective-permute-start.8 = (bf16[256,256]{1,0:T(8,128)(2,1)S(1)}, bf16[256,256]{1,0:T(8,128)(2,1)S(1)}, u32[]{:S(2)}, u32[]{:S(2)}) collective-permute-start(bf16[256,256]{1,0:T(8,128)(2,1)S(1)} %slice.16), channel_id=1, source_target_pairs={{0,16},{8,24},{16,0},{24,8},{1,17},{9,25},{17,1},{25,9},{2,18},{10... | collective-permute-start | bytes 393224 | tf_op jit(solution)/shard_map/left_3a/ppermute | solution.py:29
  33.9 1.6 %collective-permute-start.9 = (bf16[256,256]{1,0:T(8,128)(2,1)S(1)}, bf16[256,256]{1,0:T(8,128)(2,1)S(1)}, u32[]{:S(2)}, u32[]{:S(2)}) collective-permute-start(bf16[256,256]{1,0:T(8,128)(2,1)S(1)} %slice.17), channel_id=1, source_target_pairs={{0,8},{8,0},{16,24},{24,16},{1,9},{9,1},{17,25},{25,17},{2,10},{10... | collective-permute-start | bytes 393224 | tf_op jit(solution)/shard_map/left_3b/ppermute | solution.py:29
  35.4 0.7 %collective-permute-start.15 = (bf16[528,256]{1,0:T(8,128)(2,1)S(1)}, bf16[528,256]{1,0:T(8,128)(2,1)S(1)}, u32[]{:S(2)}, u32[]{:S(2)}) collective-permute-start(bf16[528,256]{1,0:T(8,128)(2,1)S(1)} %get-tuple-element.43), channel_id=1, source_target_pairs={{0,4},{1,5},{2,6},{3,7},{4,0},{5,1},{6,2},{7,3},{8,12},{9,13},{10,... | collective-permute-start | bytes 811016 | tf_op jit(solution)/shard_map/corners/ppermute | solution.py:23
  36.1 1.3 %collective-permute-done.17.refs_2_ = bf16[384,256]{1,0:T(8,128)(2,1)S(1)} collective-permute-done((bf16[384,256]{1,0:T(8,128)(2,1)S(1)}, bf16[384,256]{1,0:T(8,128)(2,1)S(1)}, u32[]{:S(2)}, u32[]{:S(2)}) %collective-permute-start.17) | collective-permute-done | bytes 196640 | tf_op jit(solution)/shard_map/right_2/ppermute | solution.py:29
  37.5 0.5 %collective-permute-start.19 = (bf16[128,256]{1,0:T(8,128)(2,1)S(1)}, bf16[128,256]{1,0:T(8,128)(2,1)S(1)}, u32[]{:S(2)}, u32[]{:S(2)}) collective-permute-start(bf16[128,256]{1,0:T(8,128)(2,1)S(1)} %slice.19), channel_id=1, source_target_pairs={{0,8},{8,0},{16,24},{24,16},{1,9},{9,1},{17,25},{25,17},{2,10},{10... | collective-permute-start | bytes 196616 | tf_op jit(solution)/shard_map/right_3b/ppermute | solution.py:29
  39.3 1.3 %collective-permute-start.18 = (bf16[256,256]{1,0:T(8,128)(2,1)S(1)}, bf16[256,256]{1,0:T(8,128)(2,1)S(1)}, u32[]{:S(2)}, u32[]{:S(2)}) collective-permute-start(bf16[256,256]{1,0:T(8,128)(2,1)S(1)} %slice.18), channel_id=1, source_target_pairs={{0,16},{8,24},{16,0},{24,8},{1,17},{9,25},{17,1},{25,9},{2,18},{10... | collective-permute-start | bytes 393224 | tf_op jit(solution)/shard_map/right_3a/ppermute | solution.py:29
  40.6 1.0 %left_columns.1 = (bf16[256,256]{1,0:T(8,128)(2,1)S(1)}, bf16[256,256]{1,0:T(8,128)(2,1)S(1)}, bf16[256,256]{1,0:T(8,128)(2,1)S(1)}, bf16[256,256]{1,0:T(8,128)(2,1)S(1)}) custom-call(s32[1]{0:T(128)} %bitcast.me_ref, s32[1]{0:T(128)S(6)} %copy.6.rows_ref, s32[1]{0:T(128)S(6)} %copy.7.cols_ref, bf16[528,256]{1,0:T(8,128)(2,1)S(1)} %collective-permute-done.refs_0_, ...), custom_call_target="tpu_custom_call" | custom-call | flops 536870912 | bytes 4194304 | tf_op jit(solution)/shard_map/left_columns/pallas_call | solution.py:227
  41.6 0.9 %collective-permute-start.11 = (bf16[256,256]{1,0:T(8,128)(2,1)S(1)}, bf16[256,256]{1,0:T(8,128)(2,1)S(1)}, u32[]{:S(2)}, u32[]{:S(2)}) collective-permute-start(bf16[256,256]{1,0:T(8,128)(2,1)S(1)} %get-tuple-element.37), channel_id=1, source_target_pairs={{0,8},{8,0},{16,24},{24,16},{1,9},{9,1},{17,25},{25,17},{2,10},{10... | collective-permute-start | bytes 393224 | tf_op jit(solution)/shard_map/strip_1/ppermute | solution.py:29
  42.5 1.5 %collective-permute-start.12 = (bf16[256,256]{1,0:T(8,128)(2,1)S(1)}, bf16[256,256]{1,0:T(8,128)(2,1)S(1)}, u32[]{:S(2)}, u32[]{:S(2)}) collective-permute-start(bf16[256,256]{1,0:T(8,128)(2,1)S(1)} %get-tuple-element.38), channel_id=1, source_target_pairs={{0,16},{8,24},{16,0},{24,8},{1,17},{9,25},{17,1},{25,9},{2,18},{10... | collective-permute-start | bytes 393224 | tf_op jit(solution)/shard_map/strip_2/ppermute | solution.py:29
  44.0 1.2 %collective-permute-start.13 = (bf16[256,256]{1,0:T(8,128)(2,1)S(1)}, bf16[256,256]{1,0:T(8,128)(2,1)S(1)}, u32[]{:S(2)}, u32[]{:S(2)}) collective-permute-start(bf16[256,256]{1,0:T(8,128)(2,1)S(1)} %get-tuple-element.39), channel_id=1, source_target_pairs={{0,24},{8,16},{16,8},{24,0},{1,25},{9,17},{17,9},{25,1},{2,26},{10... | collective-permute-start | bytes 393224 | tf_op jit(solution)/shard_map/strip_3/ppermute | solution.py:29
  45.2 0.5 collective-permute-done.18.refs_3_
  45.7 1.8 %collective-permute-done.15.corners_ref = bf16[528,256]{1,0:T(8,128)(2,1)S(1)} collective-permute-done((bf16[528,256]{1,0:T(8,128)(2,1)S(1)}, bf16[528,256]{1,0:T(8,128)(2,1)S(1)}, u32[]{:S(2)}, u32[]{:S(2)}) %collective-permute-start.15) | collective-permute-done | bytes 270368 | tf_op jit(solution)/shard_map/corners/ppermute | solution.py:23
  47.4 0.5 %whole_right.1.refs_4_ = bf16[1024,1024]{1,0:T(8,128)(2,1)S(1)} custom-call(s32[1]{0:T(128)} %bitcast.me_ref, bf16[528,256]{1,0:T(8,128)(2,1)S(1)} %collective-permute-done.15.corners_ref, bf16[384,256]{1,0:T(8,128)(2,1)S(1)} %collective-permute-done.14.refs_0_, bf16[384,256]{1,0:T(8,128)(2,1)S(1)} %collective-permute-done.16.refs_1_, ...), custom_call_target="tpu_custom_call" | custom-call | flops 1048576 | bytes 4194304 | tf_op jit(solution)/shard_map/whole_right/pallas_call | solution.py:252
  48.0 1.9 %collective-permute-done.13.refs_3_ = bf16[256,256]{1,0:T(8,128)(2,1)S(1)} collective-permute-done((bf16[256,256]{1,0:T(8,128)(2,1)S(1)}, bf16[256,256]{1,0:T(8,128)(2,1)S(1)}, u32[]{:S(2)}, u32[]{:S(2)}) %collective-permute-start.13) | collective-permute-done | bytes 131104 | tf_op jit(solution)/shard_map/strip_3/ppermute | solution.py:29
  49.9 1.6 %update_rows.1 = bf16[1,256,1024]{2,1,0:T(8,128)(2,1)} custom-call(s32[1]{0:T(128)} %bitcast.me_ref, s32[1]{0:T(128)S(6)} %copy.6.rows_ref, s32[1]{0:T(128)S(6)} %copy.7.cols_ref, bf16[256,256]{1,0:T(8,128)(2,1)S(1)} %get-tuple-element.36.refs_0_, bf16[256,256]{1,0:T(8,128)(2,1)S(1)} %collective-permute-done.11.refs_1_, ...), custom_call_target="tpu_custom_call" | custom-call | flops 536870912 | bytes 4194304 | tf_op jit(solution)/shard_map/update_rows/pallas_call | solution.py:284
  (19 shorter events, 0.1 us)
Async XLA Ops:
  1.5 10.0 %collective-permute-start.1 = (bf16[512,256]{1,0:T(8,128)(2,1)S(1)}, bf16[512,256]{1,0:T(8,128)(2,1)S(1)}, u32[]{:S(2)}, u32[]{:S(2)}) collective-permute-start(bf16[512,256]{1,0:T(8,128)(2,1)S(1)} %get-tuple-element.27), channel_id=1, source_target_pairs={{0,8},{8,0},{16,24},{24,16},{1,9},{9,1},{17,25},{25,17},{2,10},{10... | collective-permute-start | bytes 786440 | tf_op jit(solution)/shard_map/far_0/ppermute | solution.py:29
  4.5 8.6 %collective-permute-start.2 = (bf16[512,256]{1,0:T(8,128)(2,1)S(1)}, bf16[512,256]{1,0:T(8,128)(2,1)S(1)}, u32[]{:S(2)}, u32[]{:S(2)}) collective-permute-start(bf16[512,256]{1,0:T(8,128)(2,1)S(1)} %get-tuple-element.29), channel_id=1, source_target_pairs={{0,16},{8,24},{16,0},{24,8},{1,17},{9,25},{17,1},{25,9},{2,18},{10... | collective-permute-start | bytes 786440 | tf_op jit(solution)/shard_map/far_1/ppermute | solution.py:29
  6.0 14.4 %collective-permute-start = (bf16[528,256]{1,0:T(8,128)(2,1)S(1)}, bf16[528,256]{1,0:T(8,128)(2,1)S(1)}, u32[]{:S(2)}, u32[]{:S(2)}) collective-permute-start(bf16[528,256]{1,0:T(8,128)(2,1)S(1)} %get-tuple-element.25), channel_id=1, source_target_pairs={{0,4},{1,5},{2,6},{3,7},{4,0},{5,1},{6,2},{7,3},{8,12},{9,13},{10,... | collective-permute-start | bytes 811016 | tf_op jit(solution)/shard_map/left/ppermute | solution.py:23
  10.4 10.0 %collective-permute-start.3 = (bf16[512,256]{1,0:T(8,128)(2,1)S(1)}, bf16[512,256]{1,0:T(8,128)(2,1)S(1)}, u32[]{:S(2)}, u32[]{:S(2)}) collective-permute-start(bf16[512,256]{1,0:T(8,128)(2,1)S(1)} %get-tuple-element.30), channel_id=1, source_target_pairs={{0,8},{8,0},{16,24},{24,16},{1,9},{9,1},{17,25},{25,17},{2,10},{10... | collective-permute-start | bytes 786440 | tf_op jit(solution)/shard_map/near_0/ppermute | solution.py:29
  11.0 9.4 %collective-permute-start.4 = (bf16[512,256]{1,0:T(8,128)(2,1)S(1)}, bf16[512,256]{1,0:T(8,128)(2,1)S(1)}, u32[]{:S(2)}, u32[]{:S(2)}) collective-permute-start(bf16[512,256]{1,0:T(8,128)(2,1)S(1)} %get-tuple-element.31), channel_id=1, source_target_pairs={{0,16},{8,24},{16,0},{24,8},{1,17},{9,25},{17,1},{25,9},{2,18},{10... | collective-permute-start | bytes 786440 | tf_op jit(solution)/shard_map/near_1/ppermute | solution.py:29
  11.5 12.0 %collective-permute-start.6 = (bf16[512,256]{1,0:T(8,128)(2,1)S(1)}, bf16[512,256]{1,0:T(8,128)(2,1)S(1)}, u32[]{:S(2)}, u32[]{:S(2)}) collective-permute-start(bf16[512,256]{1,0:T(8,128)(2,1)S(1)} %add_convert_fusion.1), channel_id=1, source_target_pairs={{0,16},{8,24},{16,0},{24,8},{1,17},{9,25},{17,1},{25,9},{2,18},{10... | collective-permute-start | bytes 786440 | tf_op jit(solution)/shard_map/via_0/ppermute | solution.py:29
  13.2 18.0 %collective-permute-start.10 = (bf16[512,256]{1,0:T(8,128)(2,1)S(1)}, bf16[512,256]{1,0:T(8,128)(2,1)S(1)}, u32[]{:S(2)}, u32[]{:S(2)}) collective-permute-start(bf16[512,256]{1,0:T(8,128)(2,1)S(1)} %add_convert_fusion), channel_id=1, source_target_pairs={{0,8},{8,0},{16,24},{24,16},{1,9},{9,1},{17,25},{25,17},{2,10},{10... | collective-permute-start | bytes 786440 | tf_op jit(solution)/shard_map/via_1/ppermute | solution.py:29
  20.4 10.9 %collective-permute-start.14 = (bf16[384,256]{1,0:T(8,128)(2,1)S(1)}, bf16[384,256]{1,0:T(8,128)(2,1)S(1)}, u32[]{:S(2)}, u32[]{:S(2)}) collective-permute-start(bf16[384,256]{1,0:T(8,128)(2,1)S(1)} %get-tuple-element.42), channel_id=1, source_target_pairs={{0,4},{1,5},{2,6},{3,7},{4,0},{5,1},{6,2},{7,3},{8,12},{9,13},{10,... | collective-permute-start | bytes 589832 | tf_op jit(solution)/shard_map/right/ppermute | solution.py:23
  20.4 11.8 %collective-permute-start.5 = (bf16[528,256]{1,0:T(8,128)(2,1)S(1)}, bf16[528,256]{1,0:T(8,128)(2,1)S(1)}, u32[]{:S(2)}, u32[]{:S(2)}) collective-permute-start(bf16[528,256]{1,0:T(8,128)(2,1)S(1)} %collective-permute-done.refs_0_), channel_id=1, source_target_pairs={{0,8},{8,0},{16,24},{24,16},{1,9},{9,1},{17,25},{25,17},{2,10},{10... | collective-permute-start | bytes 811016 | tf_op jit(solution)/shard_map/left_1/ppermute | solution.py:29
  23.5 10.4 %collective-permute-start.7 = (bf16[528,256]{1,0:T(8,128)(2,1)S(1)}, bf16[528,256]{1,0:T(8,128)(2,1)S(1)}, u32[]{:S(2)}, u32[]{:S(2)}) collective-permute-start(bf16[528,256]{1,0:T(8,128)(2,1)S(1)} %collective-permute-done.refs_0_), channel_id=1, source_target_pairs={{0,16},{8,24},{16,0},{24,8},{1,17},{9,25},{17,1},{25,9},{2,18},{10... | collective-permute-start | bytes 811016 | tf_op jit(solution)/shard_map/left_2/ppermute | solution.py:29
  31.2 6.2 %collective-permute-start.17 = (bf16[384,256]{1,0:T(8,128)(2,1)S(1)}, bf16[384,256]{1,0:T(8,128)(2,1)S(1)}, u32[]{:S(2)}, u32[]{:S(2)}) collective-permute-start(bf16[384,256]{1,0:T(8,128)(2,1)S(1)} %collective-permute-done.14.refs_0_), channel_id=1, source_target_pairs={{0,16},{8,24},{16,0},{24,8},{1,17},{9,25},{17,1},{25,9},{2,18},{10... | collective-permute-start | bytes 589832 | tf_op jit(solution)/shard_map/right_2/ppermute | solution.py:29
  31.7 7.6 %collective-permute-start.16 = (bf16[384,256]{1,0:T(8,128)(2,1)S(1)}, bf16[384,256]{1,0:T(8,128)(2,1)S(1)}, u32[]{:S(2)}, u32[]{:S(2)}) collective-permute-start(bf16[384,256]{1,0:T(8,128)(2,1)S(1)} %collective-permute-done.14.refs_0_), channel_id=1, source_target_pairs={{0,8},{8,0},{16,24},{24,16},{1,9},{9,1},{17,25},{25,17},{2,10},{10... | collective-permute-start | bytes 589832 | tf_op jit(solution)/shard_map/right_1/ppermute | solution.py:29
  32.2 8.4 %collective-permute-start.8 = (bf16[256,256]{1,0:T(8,128)(2,1)S(1)}, bf16[256,256]{1,0:T(8,128)(2,1)S(1)}, u32[]{:S(2)}, u32[]{:S(2)}) collective-permute-start(bf16[256,256]{1,0:T(8,128)(2,1)S(1)} %slice.16), channel_id=1, source_target_pairs={{0,16},{8,24},{16,0},{24,8},{1,17},{9,25},{17,1},{25,9},{2,18},{10... | collective-permute-start | bytes 393224 | tf_op jit(solution)/shard_map/left_3a/ppermute | solution.py:29
  33.9 6.7 %collective-permute-start.9 = (bf16[256,256]{1,0:T(8,128)(2,1)S(1)}, bf16[256,256]{1,0:T(8,128)(2,1)S(1)}, u32[]{:S(2)}, u32[]{:S(2)}) collective-permute-start(bf16[256,256]{1,0:T(8,128)(2,1)S(1)} %slice.17), channel_id=1, source_target_pairs={{0,8},{8,0},{16,24},{24,16},{1,9},{9,1},{17,25},{25,17},{2,10},{10... | collective-permute-start | bytes 393224 | tf_op jit(solution)/shard_map/left_3b/ppermute | solution.py:29
  35.4 12.0 %collective-permute-start.15 = (bf16[528,256]{1,0:T(8,128)(2,1)S(1)}, bf16[528,256]{1,0:T(8,128)(2,1)S(1)}, u32[]{:S(2)}, u32[]{:S(2)}) collective-permute-start(bf16[528,256]{1,0:T(8,128)(2,1)S(1)} %get-tuple-element.43), channel_id=1, source_target_pairs={{0,4},{1,5},{2,6},{3,7},{4,0},{5,1},{6,2},{7,3},{8,12},{9,13},{10,... | collective-permute-start | bytes 811016 | tf_op jit(solution)/shard_map/corners/ppermute | solution.py:23
  37.5 6.6 %collective-permute-start.19 = (bf16[128,256]{1,0:T(8,128)(2,1)S(1)}, bf16[128,256]{1,0:T(8,128)(2,1)S(1)}, u32[]{:S(2)}, u32[]{:S(2)}) collective-permute-start(bf16[128,256]{1,0:T(8,128)(2,1)S(1)} %slice.19), channel_id=1, source_target_pairs={{0,8},{8,0},{16,24},{24,16},{1,9},{9,1},{17,25},{25,17},{2,10},{10... | collective-permute-start | bytes 196616 | tf_op jit(solution)/shard_map/right_3b/ppermute | solution.py:29
  39.3 6.3 %collective-permute-start.18 = (bf16[256,256]{1,0:T(8,128)(2,1)S(1)}, bf16[256,256]{1,0:T(8,128)(2,1)S(1)}, u32[]{:S(2)}, u32[]{:S(2)}) collective-permute-start(bf16[256,256]{1,0:T(8,128)(2,1)S(1)} %slice.18), channel_id=1, source_target_pairs={{0,16},{8,24},{16,0},{24,8},{1,17},{9,25},{17,1},{25,9},{2,18},{10... | collective-permute-start | bytes 393224 | tf_op jit(solution)/shard_map/right_3a/ppermute | solution.py:29
  41.6 6.3 %collective-permute-start.11 = (bf16[256,256]{1,0:T(8,128)(2,1)S(1)}, bf16[256,256]{1,0:T(8,128)(2,1)S(1)}, u32[]{:S(2)}, u32[]{:S(2)}) collective-permute-start(bf16[256,256]{1,0:T(8,128)(2,1)S(1)} %get-tuple-element.37), channel_id=1, source_target_pairs={{0,8},{8,0},{16,24},{24,16},{1,9},{9,1},{17,25},{25,17},{2,10},{10... | collective-permute-start | bytes 393224 | tf_op jit(solution)/shard_map/strip_1/ppermute | solution.py:29
  42.5 5.5 %collective-permute-start.12 = (bf16[256,256]{1,0:T(8,128)(2,1)S(1)}, bf16[256,256]{1,0:T(8,128)(2,1)S(1)}, u32[]{:S(2)}, u32[]{:S(2)}) collective-permute-start(bf16[256,256]{1,0:T(8,128)(2,1)S(1)} %get-tuple-element.38), channel_id=1, source_target_pairs={{0,16},{8,24},{16,0},{24,8},{1,17},{9,25},{17,1},{25,9},{2,18},{10... | collective-permute-start | bytes 393224 | tf_op jit(solution)/shard_map/strip_2/ppermute | solution.py:29
  44.0 5.9 %collective-permute-start.13 = (bf16[256,256]{1,0:T(8,128)(2,1)S(1)}, bf16[256,256]{1,0:T(8,128)(2,1)S(1)}, u32[]{:S(2)}, u32[]{:S(2)}) collective-permute-start(bf16[256,256]{1,0:T(8,128)(2,1)S(1)} %get-tuple-element.39), channel_id=1, source_target_pairs={{0,24},{8,16},{16,8},{24,0},{1,25},{9,17},{17,9},{25,1},{2,26},{10... | collective-permute-start | bytes 393224 | tf_op jit(solution)/shard_map/strip_3/ppermute | solution.py:29

commit v14 on v13

--- a/solution.py
+++ b/solution.py
@@ -76,11 +76,17 @@
     ]
 
 
-def corner_copies(root_ref, corners, sems):
-    return [
-        pltpu.make_async_copy(root_ref.at[0, block(i), block(i)], corners.at[i], sems.at[i])
-        for i in range(corners.shape[0])
-    ]
+def corner_copies(me, strip, root_ref, corners, sems):
+    copies = []
+    for i in range(corners.shape[0]):
+        rows, size = (me * strip, strip) if i % 2 == 0 else (0, TILE)
+        if size < TILE:
+            source = root_ref.at[0, pl.ds(pl.multiple_of(i * TILE + rows, size), size), block(i)]
+            target = corners.at[i, pl.ds(pl.multiple_of(rows, size), size), :]
+        else:
+            source, target = root_ref.at[0, block(i), block(i)], corners.at[i]
+        copies.append(pltpu.make_async_copy(source, target, sems.at[i]))
+    return copies
 
 
 def fold_corners(corners, start, strip, out, base):
@@ -107,7 +113,7 @@
     low = len(below(tiles))
     strip = quarter
     strips = strip_copies(me, root_ref, strip, folded[0], strip_sems)
-    cornered = corner_copies(root_ref, corners, corner_sems)
+    cornered = corner_copies(me, strip if len(folded) == 1 else TILE, root_ref, corners, corner_sems)
     copies = pick_copies(wanted, me, grad_ref, outs, pick_sems)
     for copy in cornered + strips + copies:
         copy.start()

time: 51.7 us -> 51.6 us (level)
  no operation moved by 1% of the time
where the time goes in v14:
time: 51.6 us; the launch traced here: 51.4 us
  starting transfers between devices  24.9 us (48%)
  waiting for transfers between devices  18.6 us (36%)
  Pallas kernels  6.27 us (12%)
  between operations  1.4 us (3%)
    ppermute x17, starting transfers between devices, swapped(): lax.ppermute(value, 'dp', [(source, source ^ flip) for source in range(co...  21.6 us
    ppermute x3, waiting for transfers between devices, shifted(): lax.ppermute(value, 'shard', [(source, (source + count // 2) % count) for...  13.1 us
    ppermute x17, waiting for transfers between devices, swapped(): lax.ppermute(value, 'dp', [(source, source ^ flip) for source in range(co...  5.57 us
    ppermute x3, starting transfers between devices, shifted(): lax.ppermute(value, 'shard', [(source, (source + count // 2) % count) for...  3.26 us
    pallas_call x2, Pallas kernels, messages(): pl.pallas_call(functools.partial(messages_kernel, wanted, strip), in_spec...  3.13 us
    pallas_call x1, Pallas kernels, update_rows(): pl.pallas_call(functools.partial(rows_kernel, groups), in_specs=[SMEM_SPE...  1.57 us
    pallas_call x1, Pallas kernels, left_columns(): pl.pallas_call(functools.partial(columns_kernel, groups, [len(part) for p...  1.05 us
  transfers between devices with their start and end apart: 20, of which 7 were waited for; matrix products, arithmetic and copies ran while one was open for 0% of the time, Pallas kernels for 6%

profile of v14, /device:TPU:0, one launch (start us, length us, event | category | flops | bytes accessed | tf_op | source)
XLA Modules:
  0.0 51.4 jit_solution(9579686050611900577)
XLA Ops:
  0.0 1.4 %sent_first.1 = (bf16[512,256]{1,0:T(8,128)(2,1)S(1)}, bf16[512,256]{1,0:T(8,128)(2,1)S(1)}, bf16[528,256]{1,0:T(8,128)(2,1)S(1)}) custom-call(s32[1]{0:T(128)} %bitcast.me_ref, bf16[1,1,1024,1024]{3,2,1,0:T(8,128)(2,1)} %grad_ref.3, bf16[1,1024,1024]{2,1,0:T(8,128)(2,1)} %root_ref.2), custom_call_target="tpu_custom_call" | custom-call | tf_op jit(solution)/shard_map/sent_first/pallas_call | solution.py:139
  1.4 3.0 %collective-permute-start.1 = (bf16[512,256]{1,0:T(8,128)(2,1)S(1)}, bf16[512,256]{1,0:T(8,128)(2,1)S(1)}, u32[]{:S(2)}, u32[]{:S(2)}) collective-permute-start(bf16[512,256]{1,0:T(8,128)(2,1)S(1)} %get-tuple-element.27), channel_id=1, source_target_pairs={{0,8},{8,0},{16,24},{24,16},{1,9},{9,1},{17,25},{25,17},{2,10},{10... | collective-permute-start | bytes 786440 | tf_op jit(solution)/shard_map/far_0/ppermute | solution.py:29
  4.4 1.5 %collective-permute-start.2 = (bf16[512,256]{1,0:T(8,128)(2,1)S(1)}, bf16[512,256]{1,0:T(8,128)(2,1)S(1)}, u32[]{:S(2)}, u32[]{:S(2)}) collective-permute-start(bf16[512,256]{1,0:T(8,128)(2,1)S(1)} %get-tuple-element.29), channel_id=1, source_target_pairs={{0,16},{8,24},{16,0},{24,8},{1,17},{9,25},{17,1},{25,9},{2,18},{10... | collective-permute-start | bytes 786440 | tf_op jit(solution)/shard_map/far_1/ppermute | solution.py:29
  5.9 2.6 %collective-permute-start = (bf16[528,256]{1,0:T(8,128)(2,1)S(1)}, bf16[528,256]{1,0:T(8,128)(2,1)S(1)}, u32[]{:S(2)}, u32[]{:S(2)}) collective-permute-start(bf16[528,256]{1,0:T(8,128)(2,1)S(1)} %get-tuple-element.25), channel_id=1, source_target_pairs={{0,4},{1,5},{2,6},{3,7},{4,0},{5,1},{6,2},{7,3},{8,12},{9,13},{10,... | collective-permute-start | bytes 811016 | tf_op jit(solution)/shard_map/left/ppermute | solution.py:23
  8.5 1.8 %sent_later.1 = (bf16[512,256]{1,0:T(8,128)(2,1)S(1)}, bf16[512,256]{1,0:T(8,128)(2,1)S(1)}, bf16[512,256]{1,0:T(8,128)(2,1)S(1)}, bf16[512,256]{1,0:T(8,128)(2,...) custom-call(s32[1]{0:T(128)} %bitcast.me_ref, ...), custom_call_target="tpu_custom_call" | custom-call | tf_op jit(solution)/shard_map/sent_later/pallas_call | solution.py:139
  10.3 0.6 %collective-permute-start.3 = (bf16[512,256]{1,0:T(8,128)(2,1)S(1)}, bf16[512,256]{1,0:T(8,128)(2,1)S(1)}, u32[]{:S(2)}, u32[]{:S(2)}) collective-permute-start(bf16[512,256]{1,0:T(8,128)(2,1)S(1)} %get-tuple-element.30), channel_id=1, source_target_pairs={{0,8},{8,0},{16,24},{24,16},{1,9},{9,1},{17,25},{25,17},{2,10},{10... | collective-permute-start | bytes 786440 | tf_op jit(solution)/shard_map/near_0/ppermute | solution.py:29
  10.9 0.5 collective-permute-start.4
  11.4 0.1 add_convert_fusion.1
  11.5 1.6 %collective-permute-start.6 = (bf16[512,256]{1,0:T(8,128)(2,1)S(1)}, bf16[512,256]{1,0:T(8,128)(2,1)S(1)}, u32[]{:S(2)}, u32[]{:S(2)}) collective-permute-start(bf16[512,256]{1,0:T(8,128)(2,1)S(1)} %add_convert_fusion.1), channel_id=1, source_target_pairs={{0,16},{8,24},{16,0},{24,8},{1,17},{9,25},{17,1},{25,9},{2,18},{10... | collective-permute-start | bytes 786440 | tf_op jit(solution)/shard_map/via_0/ppermute | solution.py:29
  13.1 2.1 %collective-permute-start.10 = (bf16[512,256]{1,0:T(8,128)(2,1)S(1)}, bf16[512,256]{1,0:T(8,128)(2,1)S(1)}, u32[]{:S(2)}, u32[]{:S(2)}) collective-permute-start(bf16[512,256]{1,0:T(8,128)(2,1)S(1)} %add_convert_fusion), channel_id=1, source_target_pairs={{0,8},{8,0},{16,24},{24,16},{1,9},{9,1},{17,25},{25,17},{2,10},{10... | collective-permute-start | bytes 786440 | tf_op jit(solution)/shard_map/via_1/ppermute | solution.py:29
  15.2 5.1 %collective-permute-done.refs_0_ = bf16[528,256]{1,0:T(8,128)(2,1)S(1)} collective-permute-done((bf16[528,256]{1,0:T(8,128)(2,1)S(1)}, bf16[528,256]{1,0:T(8,128)(2,1)S(1)}, u32[]{:S(2)}, u32[]{:S(2)}) %collective-permute-start) | collective-permute-done | bytes 270368 | tf_op jit(solution)/shard_map/left/ppermute | solution.py:23
  20.3 1.3 %collective-permute-start.5 = (bf16[528,256]{1,0:T(8,128)(2,1)S(1)}, bf16[528,256]{1,0:T(8,128)(2,1)S(1)}, u32[]{:S(2)}, u32[]{:S(2)}) collective-permute-start(bf16[528,256]{1,0:T(8,128)(2,1)S(1)} %collective-permute-done.refs_0_), channel_id=1, source_target_pairs={{0,8},{8,0},{16,24},{24,16},{1,9},{9,1},{17,25},{25,17},{2,10},{10... | collective-permute-start | bytes 811016 | tf_op jit(solution)/shard_map/left_1/ppermute | solution.py:29
  21.6 1.8 %collective-permute-done.6.refs_7_ = bf16[512,256]{1,0:T(8,128)(2,1)S(1)} collective-permute-done((bf16[512,256]{1,0:T(8,128)(2,1)S(1)}, bf16[512,256]{1,0:T(8,128)(2,1)S(1)}, u32[]{:S(2)}, u32[]{:S(2)}) %collective-permute-start.6) | collective-permute-done | bytes 262176 | tf_op jit(solution)/shard_map/via_0/ppermute | solution.py:29
  23.4 1.5 %collective-permute-start.7 = (bf16[528,256]{1,0:T(8,128)(2,1)S(1)}, bf16[528,256]{1,0:T(8,128)(2,1)S(1)}, u32[]{:S(2)}, u32[]{:S(2)}) collective-permute-start(bf16[528,256]{1,0:T(8,128)(2,1)S(1)} %collective-permute-done.refs_0_), channel_id=1, source_target_pairs={{0,16},{8,24},{16,0},{24,8},{1,17},{9,25},{17,1},{25,9},{2,18},{10... | collective-permute-start | bytes 811016 | tf_op jit(solution)/shard_map/left_2/ppermute | solution.py:29
  24.9 6.2 %collective-permute-done.14.refs_0_ = bf16[384,256]{1,0:T(8,128)(2,1)S(1)} collective-permute-done((bf16[384,256]{1,0:T(8,128)(2,1)S(1)}, bf16[384,256]{1,0:T(8,128)(2,1)S(1)}, u32[]{:S(2)}, u32[]{:S(2)}) %collective-permute-start.14) | collective-permute-done | bytes 196640 | tf_op jit(solution)/shard_map/right/ppermute | solution.py:23
  31.1 0.5 collective-permute-start.17
  31.6 0.4 collective-permute-start.16
  32.1 1.7 %collective-permute-start.8 = (bf16[256,256]{1,0:T(8,128)(2,1)S(1)}, bf16[256,256]{1,0:T(8,128)(2,1)S(1)}, u32[]{:S(2)}, u32[]{:S(2)}) collective-permute-start(bf16[256,256]{1,0:T(8,128)(2,1)S(1)} %slice.16), channel_id=1, source_target_pairs={{0,16},{8,24},{16,0},{24,8},{1,17},{9,25},{17,1},{25,9},{2,18},{10... | collective-permute-start | bytes 393224 | tf_op jit(solution)/shard_map/left_3a/ppermute | solution.py:29
  33.8 1.6 %collective-permute-start.9 = (bf16[256,256]{1,0:T(8,128)(2,1)S(1)}, bf16[256,256]{1,0:T(8,128)(2,1)S(1)}, u32[]{:S(2)}, u32[]{:S(2)}) collective-permute-start(bf16[256,256]{1,0:T(8,128)(2,1)S(1)} %slice.17), channel_id=1, source_target_pairs={{0,8},{8,0},{16,24},{24,16},{1,9},{9,1},{17,25},{25,17},{2,10},{10... | collective-permute-start | bytes 393224 | tf_op jit(solution)/shard_map/left_3b/ppermute | solution.py:29
  35.3 0.7 %collective-permute-start.15 = (bf16[528,256]{1,0:T(8,128)(2,1)S(1)}, bf16[528,256]{1,0:T(8,128)(2,1)S(1)}, u32[]{:S(2)}, u32[]{:S(2)}) collective-permute-start(bf16[528,256]{1,0:T(8,128)(2,1)S(1)} %get-tuple-element.43), channel_id=1, source_target_pairs={{0,4},{1,5},{2,6},{3,7},{4,0},{5,1},{6,2},{7,3},{8,12},{9,13},{10,... | collective-permute-start | bytes 811016 | tf_op jit(solution)/shard_map/corners/ppermute | solution.py:23
  36.0 1.3 %collective-permute-done.17.refs_2_ = bf16[384,256]{1,0:T(8,128)(2,1)S(1)} collective-permute-done((bf16[384,256]{1,0:T(8,128)(2,1)S(1)}, bf16[384,256]{1,0:T(8,128)(2,1)S(1)}, u32[]{:S(2)}, u32[]{:S(2)}) %collective-permute-start.17) | collective-permute-done | bytes 196640 | tf_op jit(solution)/shard_map/right_2/ppermute | solution.py:29
  37.4 0.5 %collective-permute-start.19 = (bf16[128,256]{1,0:T(8,128)(2,1)S(1)}, bf16[128,256]{1,0:T(8,128)(2,1)S(1)}, u32[]{:S(2)}, u32[]{:S(2)}) collective-permute-start(bf16[128,256]{1,0:T(8,128)(2,1)S(1)} %slice.19), channel_id=1, source_target_pairs={{0,8},{8,0},{16,24},{24,16},{1,9},{9,1},{17,25},{25,17},{2,10},{10... | collective-permute-start | bytes 196616 | tf_op jit(solution)/shard_map/right_3b/ppermute | solution.py:29
  39.2 1.3 %collective-permute-start.18 = (bf16[256,256]{1,0:T(8,128)(2,1)S(1)}, bf16[256,256]{1,0:T(8,128)(2,1)S(1)}, u32[]{:S(2)}, u32[]{:S(2)}) collective-permute-start(bf16[256,256]{1,0:T(8,128)(2,1)S(1)} %slice.18), channel_id=1, source_target_pairs={{0,16},{8,24},{16,0},{24,8},{1,17},{9,25},{17,1},{25,9},{2,18},{10... | collective-permute-start | bytes 393224 | tf_op jit(solution)/shard_map/right_3a/ppermute | solution.py:29
  40.5 1.0 %left_columns.1 = (bf16[256,256]{1,0:T(8,128)(2,1)S(1)}, bf16[256,256]{1,0:T(8,128)(2,1)S(1)}, bf16[256,256]{1,0:T(8,128)(2,1)S(1)}, bf16[256,256]{1,0:T(8,128)(2,1)S(1)}) custom-call(s32[1]{0:T(128)} %bitcast.me_ref, s32[1]{0:T(128)S(6)} %copy.6.rows_ref, s32[1]{0:T(128)S(6)} %copy.7.cols_ref, bf16[528,256]{1,0:T(8,128)(2,1)S(1)} %collective-permute-done.refs_0_, ...), custom_call_target="tpu_custom_call" | custom-call | flops 536870912 | bytes 4194304 | tf_op jit(solution)/shard_map/left_columns/pallas_call | solution.py:233
  41.6 0.9 %collective-permute-start.11 = (bf16[256,256]{1,0:T(8,128)(2,1)S(1)}, bf16[256,256]{1,0:T(8,128)(2,1)S(1)}, u32[]{:S(2)}, u32[]{:S(2)}) collective-permute-start(bf16[256,256]{1,0:T(8,128)(2,1)S(1)} %get-tuple-element.37), channel_id=1, source_target_pairs={{0,8},{8,0},{16,24},{24,16},{1,9},{9,1},{17,25},{25,17},{2,10},{10... | collective-permute-start | bytes 393224 | tf_op jit(solution)/shard_map/strip_1/ppermute | solution.py:29
  42.4 1.5 %collective-permute-start.12 = (bf16[256,256]{1,0:T(8,128)(2,1)S(1)}, bf16[256,256]{1,0:T(8,128)(2,1)S(1)}, u32[]{:S(2)}, u32[]{:S(2)}) collective-permute-start(bf16[256,256]{1,0:T(8,128)(2,1)S(1)} %get-tuple-element.38), channel_id=1, source_target_pairs={{0,16},{8,24},{16,0},{24,8},{1,17},{9,25},{17,1},{25,9},{2,18},{10... | collective-permute-start | bytes 393224 | tf_op jit(solution)/shard_map/strip_2/ppermute | solution.py:29
  43.9 1.2 %collective-permute-start.13 = (bf16[256,256]{1,0:T(8,128)(2,1)S(1)}, bf16[256,256]{1,0:T(8,128)(2,1)S(1)}, u32[]{:S(2)}, u32[]{:S(2)}) collective-permute-start(bf16[256,256]{1,0:T(8,128)(2,1)S(1)} %get-tuple-element.39), channel_id=1, source_target_pairs={{0,24},{8,16},{16,8},{24,0},{1,25},{9,17},{17,9},{25,1},{2,26},{10... | collective-permute-start | bytes 393224 | tf_op jit(solution)/shard_map/strip_3/ppermute | solution.py:29
  45.1 0.5 collective-permute-done.18.refs_3_
  45.6 1.8 %collective-permute-done.15.corners_ref = bf16[528,256]{1,0:T(8,128)(2,1)S(1)} collective-permute-done((bf16[528,256]{1,0:T(8,128)(2,1)S(1)}, bf16[528,256]{1,0:T(8,128)(2,1)S(1)}, u32[]{:S(2)}, u32[]{:S(2)}) %collective-permute-start.15) | collective-permute-done | bytes 270368 | tf_op jit(solution)/shard_map/corners/ppermute | solution.py:23
  47.3 0.5 %whole_right.1.refs_4_ = bf16[1024,1024]{1,0:T(8,128)(2,1)S(1)} custom-call(s32[1]{0:T(128)} %bitcast.me_ref, bf16[528,256]{1,0:T(8,128)(2,1)S(1)} %collective-permute-done.15.corners_ref, bf16[384,256]{1,0:T(8,128)(2,1)S(1)} %collective-permute-done.14.refs_0_, bf16[384,256]{1,0:T(8,128)(2,1)S(1)} %collective-permute-done.16.refs_1_, ...), custom_call_target="tpu_custom_call" | custom-call | flops 1048576 | bytes 4194304 | tf_op jit(solution)/shard_map/whole_right/pallas_call | solution.py:258
  47.9 1.9 %collective-permute-done.13.refs_3_ = bf16[256,256]{1,0:T(8,128)(2,1)S(1)} collective-permute-done((bf16[256,256]{1,0:T(8,128)(2,1)S(1)}, bf16[256,256]{1,0:T(8,128)(2,1)S(1)}, u32[]{:S(2)}, u32[]{:S(2)}) %collective-permute-start.13) | collective-permute-done | bytes 131104 | tf_op jit(solution)/shard_map/strip_3/ppermute | solution.py:29
  49.8 1.6 %update_rows.1 = bf16[1,256,1024]{2,1,0:T(8,128)(2,1)} custom-call(s32[1]{0:T(128)} %bitcast.me_ref, s32[1]{0:T(128)S(6)} %copy.6.rows_ref, s32[1]{0:T(128)S(6)} %copy.7.cols_ref, bf16[256,256]{1,0:T(8,128)(2,1)S(1)} %get-tuple-element.36.refs_0_, bf16[256,256]{1,0:T(8,128)(2,1)S(1)} %collective-permute-done.11.refs_1_, ...), custom_call_target="tpu_custom_call" | custom-call | flops 536870912 | bytes 4194304 | tf_op jit(solution)/shard_map/update_rows/pallas_call | solution.py:290
  (19 shorter events, 0.1 us)
Async XLA Ops:
  1.4 10.0 %collective-permute-start.1 = (bf16[512,256]{1,0:T(8,128)(2,1)S(1)}, bf16[512,256]{1,0:T(8,128)(2,1)S(1)}, u32[]{:S(2)}, u32[]{:S(2)}) collective-permute-start(bf16[512,256]{1,0:T(8,128)(2,1)S(1)} %get-tuple-element.27), channel_id=1, source_target_pairs={{0,8},{8,0},{16,24},{24,16},{1,9},{9,1},{17,25},{25,17},{2,10},{10... | collective-permute-start | bytes 786440 | tf_op jit(solution)/shard_map/far_0/ppermute | solution.py:29
  4.4 8.6 %collective-permute-start.2 = (bf16[512,256]{1,0:T(8,128)(2,1)S(1)}, bf16[512,256]{1,0:T(8,128)(2,1)S(1)}, u32[]{:S(2)}, u32[]{:S(2)}) collective-permute-start(bf16[512,256]{1,0:T(8,128)(2,1)S(1)} %get-tuple-element.29), channel_id=1, source_target_pairs={{0,16},{8,24},{16,0},{24,8},{1,17},{9,25},{17,1},{25,9},{2,18},{10... | collective-permute-start | bytes 786440 | tf_op jit(solution)/shard_map/far_1/ppermute | solution.py:29
  5.9 14.4 %collective-permute-start = (bf16[528,256]{1,0:T(8,128)(2,1)S(1)}, bf16[528,256]{1,0:T(8,128)(2,1)S(1)}, u32[]{:S(2)}, u32[]{:S(2)}) collective-permute-start(bf16[528,256]{1,0:T(8,128)(2,1)S(1)} %get-tuple-element.25), channel_id=1, source_target_pairs={{0,4},{1,5},{2,6},{3,7},{4,0},{5,1},{6,2},{7,3},{8,12},{9,13},{10,... | collective-permute-start | bytes 811016 | tf_op jit(solution)/shard_map/left/ppermute | solution.py:23
  10.3 10.0 %collective-permute-start.3 = (bf16[512,256]{1,0:T(8,128)(2,1)S(1)}, bf16[512,256]{1,0:T(8,128)(2,1)S(1)}, u32[]{:S(2)}, u32[]{:S(2)}) collective-permute-start(bf16[512,256]{1,0:T(8,128)(2,1)S(1)} %get-tuple-element.30), channel_id=1, source_target_pairs={{0,8},{8,0},{16,24},{24,16},{1,9},{9,1},{17,25},{25,17},{2,10},{10... | collective-permute-start | bytes 786440 | tf_op jit(solution)/shard_map/near_0/ppermute | solution.py:29
  10.9 9.4 %collective-permute-start.4 = (bf16[512,256]{1,0:T(8,128)(2,1)S(1)}, bf16[512,256]{1,0:T(8,128)(2,1)S(1)}, u32[]{:S(2)}, u32[]{:S(2)}) collective-permute-start(bf16[512,256]{1,0:T(8,128)(2,1)S(1)} %get-tuple-element.31), channel_id=1, source_target_pairs={{0,16},{8,24},{16,0},{24,8},{1,17},{9,25},{17,1},{25,9},{2,18},{10... | collective-permute-start | bytes 786440 | tf_op jit(solution)/shard_map/near_1/ppermute | solution.py:29
  11.5 12.0 %collective-permute-start.6 = (bf16[512,256]{1,0:T(8,128)(2,1)S(1)}, bf16[512,256]{1,0:T(8,128)(2,1)S(1)}, u32[]{:S(2)}, u32[]{:S(2)}) collective-permute-start(bf16[512,256]{1,0:T(8,128)(2,1)S(1)} %add_convert_fusion.1), channel_id=1, source_target_pairs={{0,16},{8,24},{16,0},{24,8},{1,17},{9,25},{17,1},{25,9},{2,18},{10... | collective-permute-start | bytes 786440 | tf_op jit(solution)/shard_map/via_0/ppermute | solution.py:29
  13.1 18.0 %collective-permute-start.10 = (bf16[512,256]{1,0:T(8,128)(2,1)S(1)}, bf16[512,256]{1,0:T(8,128)(2,1)S(1)}, u32[]{:S(2)}, u32[]{:S(2)}) collective-permute-start(bf16[512,256]{1,0:T(8,128)(2,1)S(1)} %add_convert_fusion), channel_id=1, source_target_pairs={{0,8},{8,0},{16,24},{24,16},{1,9},{9,1},{17,25},{25,17},{2,10},{10... | collective-permute-start | bytes 786440 | tf_op jit(solution)/shard_map/via_1/ppermute | solution.py:29
  20.3 10.9 %collective-permute-start.14 = (bf16[384,256]{1,0:T(8,128)(2,1)S(1)}, bf16[384,256]{1,0:T(8,128)(2,1)S(1)}, u32[]{:S(2)}, u32[]{:S(2)}) collective-permute-start(bf16[384,256]{1,0:T(8,128)(2,1)S(1)} %get-tuple-element.42), channel_id=1, source_target_pairs={{0,4},{1,5},{2,6},{3,7},{4,0},{5,1},{6,2},{7,3},{8,12},{9,13},{10,... | collective-permute-start | bytes 589832 | tf_op jit(solution)/shard_map/right/ppermute | solution.py:23
  20.3 11.8 %collective-permute-start.5 = (bf16[528,256]{1,0:T(8,128)(2,1)S(1)}, bf16[528,256]{1,0:T(8,128)(2,1)S(1)}, u32[]{:S(2)}, u32[]{:S(2)}) collective-permute-start(bf16[528,256]{1,0:T(8,128)(2,1)S(1)} %collective-permute-done.refs_0_), channel_id=1, source_target_pairs={{0,8},{8,0},{16,24},{24,16},{1,9},{9,1},{17,25},{25,17},{2,10},{10... | collective-permute-start | bytes 811016 | tf_op jit(solution)/shard_map/left_1/ppermute | solution.py:29
  23.4 10.4 %collective-permute-start.7 = (bf16[528,256]{1,0:T(8,128)(2,1)S(1)}, bf16[528,256]{1,0:T(8,128)(2,1)S(1)}, u32[]{:S(2)}, u32[]{:S(2)}) collective-permute-start(bf16[528,256]{1,0:T(8,128)(2,1)S(1)} %collective-permute-done.refs_0_), channel_id=1, source_target_pairs={{0,16},{8,24},{16,0},{24,8},{1,17},{9,25},{17,1},{25,9},{2,18},{10... | collective-permute-start | bytes 811016 | tf_op jit(solution)/shard_map/left_2/ppermute | solution.py:29
  31.1 6.2 %collective-permute-start.17 = (bf16[384,256]{1,0:T(8,128)(2,1)S(1)}, bf16[384,256]{1,0:T(8,128)(2,1)S(1)}, u32[]{:S(2)}, u32[]{:S(2)}) collective-permute-start(bf16[384,256]{1,0:T(8,128)(2,1)S(1)} %collective-permute-done.14.refs_0_), channel_id=1, source_target_pairs={{0,16},{8,24},{16,0},{24,8},{1,17},{9,25},{17,1},{25,9},{2,18},{10... | collective-permute-start | bytes 589832 | tf_op jit(solution)/shard_map/right_2/ppermute | solution.py:29
  31.6 7.6 %collective-permute-start.16 = (bf16[384,256]{1,0:T(8,128)(2,1)S(1)}, bf16[384,256]{1,0:T(8,128)(2,1)S(1)}, u32[]{:S(2)}, u32[]{:S(2)}) collective-permute-start(bf16[384,256]{1,0:T(8,128)(2,1)S(1)} %collective-permute-done.14.refs_0_), channel_id=1, source_target_pairs={{0,8},{8,0},{16,24},{24,16},{1,9},{9,1},{17,25},{25,17},{2,10},{10... | collective-permute-start | bytes 589832 | tf_op jit(solution)/shard_map/right_1/ppermute | solution.py:29
  32.1 8.4 %collective-permute-start.8 = (bf16[256,256]{1,0:T(8,128)(2,1)S(1)}, bf16[256,256]{1,0:T(8,128)(2,1)S(1)}, u32[]{:S(2)}, u32[]{:S(2)}) collective-permute-start(bf16[256,256]{1,0:T(8,128)(2,1)S(1)} %slice.16), channel_id=1, source_target_pairs={{0,16},{8,24},{16,0},{24,8},{1,17},{9,25},{17,1},{25,9},{2,18},{10... | collective-permute-start | bytes 393224 | tf_op jit(solution)/shard_map/left_3a/ppermute | solution.py:29
  33.8 6.7 %collective-permute-start.9 = (bf16[256,256]{1,0:T(8,128)(2,1)S(1)}, bf16[256,256]{1,0:T(8,128)(2,1)S(1)}, u32[]{:S(2)}, u32[]{:S(2)}) collective-permute-start(bf16[256,256]{1,0:T(8,128)(2,1)S(1)} %slice.17), channel_id=1, source_target_pairs={{0,8},{8,0},{16,24},{24,16},{1,9},{9,1},{17,25},{25,17},{2,10},{10... | collective-permute-start | bytes 393224 | tf_op jit(solution)/shard_map/left_3b/ppermute | solution.py:29
  35.3 12.0 %collective-permute-start.15 = (bf16[528,256]{1,0:T(8,128)(2,1)S(1)}, bf16[528,256]{1,0:T(8,128)(2,1)S(1)}, u32[]{:S(2)}, u32[]{:S(2)}) collective-permute-start(bf16[528,256]{1,0:T(8,128)(2,1)S(1)} %get-tuple-element.43), channel_id=1, source_target_pairs={{0,4},{1,5},{2,6},{3,7},{4,0},{5,1},{6,2},{7,3},{8,12},{9,13},{10,... | collective-permute-start | bytes 811016 | tf_op jit(solution)/shard_map/corners/ppermute | solution.py:23
  37.4 6.6 %collective-permute-start.19 = (bf16[128,256]{1,0:T(8,128)(2,1)S(1)}, bf16[128,256]{1,0:T(8,128)(2,1)S(1)}, u32[]{:S(2)}, u32[]{:S(2)}) collective-permute-start(bf16[128,256]{1,0:T(8,128)(2,1)S(1)} %slice.19), channel_id=1, source_target_pairs={{0,8},{8,0},{16,24},{24,16},{1,9},{9,1},{17,25},{25,17},{2,10},{10... | collective-permute-start | bytes 196616 | tf_op jit(solution)/shard_map/right_3b/ppermute | solution.py:29
  39.2 6.3 %collective-permute-start.18 = (bf16[256,256]{1,0:T(8,128)(2,1)S(1)}, bf16[256,256]{1,0:T(8,128)(2,1)S(1)}, u32[]{:S(2)}, u32[]{:S(2)}) collective-permute-start(bf16[256,256]{1,0:T(8,128)(2,1)S(1)} %slice.18), channel_id=1, source_target_pairs={{0,16},{8,24},{16,0},{24,8},{1,17},{9,25},{17,1},{25,9},{2,18},{10... | collective-permute-start | bytes 393224 | tf_op jit(solution)/shard_map/right_3a/ppermute | solution.py:29
  41.6 6.3 %collective-permute-start.11 = (bf16[256,256]{1,0:T(8,128)(2,1)S(1)}, bf16[256,256]{1,0:T(8,128)(2,1)S(1)}, u32[]{:S(2)}, u32[]{:S(2)}) collective-permute-start(bf16[256,256]{1,0:T(8,128)(2,1)S(1)} %get-tuple-element.37), channel_id=1, source_target_pairs={{0,8},{8,0},{16,24},{24,16},{1,9},{9,1},{17,25},{25,17},{2,10},{10... | collective-permute-start | bytes 393224 | tf_op jit(solution)/shard_map/strip_1/ppermute | solution.py:29
  42.4 5.5 %collective-permute-start.12 = (bf16[256,256]{1,0:T(8,128)(2,1)S(1)}, bf16[256,256]{1,0:T(8,128)(2,1)S(1)}, u32[]{:S(2)}, u32[]{:S(2)}) collective-permute-start(bf16[256,256]{1,0:T(8,128)(2,1)S(1)} %get-tuple-element.38), channel_id=1, source_target_pairs={{0,16},{8,24},{16,0},{24,8},{1,17},{9,25},{17,1},{25,9},{2,18},{10... | collective-permute-start | bytes 393224 | tf_op jit(solution)/shard_map/strip_2/ppermute | solution.py:29
  43.9 5.9 %collective-permute-start.13 = (bf16[256,256]{1,0:T(8,128)(2,1)S(1)}, bf16[256,256]{1,0:T(8,128)(2,1)S(1)}, u32[]{:S(2)}, u32[]{:S(2)}) collective-permute-start(bf16[256,256]{1,0:T(8,128)(2,1)S(1)} %get-tuple-element.39), channel_id=1, source_target_pairs={{0,24},{8,16},{16,8},{24,0},{1,25},{9,17},{17,9},{25,1},{2,26},{10... | collective-permute-start | bytes 393224 | tf_op jit(solution)/shard_map/strip_3/ppermute | solution.py:29
